TPU v7x, 32 devices: a whole 2x2x4 slice. The times are simulated.
32 devices in a mesh: rep: 4 (over y, x), shard: 8 (over z, core).
Axes of the slice: x: 2, y: 2, z: 4, core: 2. Of those that a mesh axis runs over, the one named last changes fastest.
Arguments:
- tokens: bfloat16 [8192, 1024], P(('rep', 'shard')), may hold values from -6 to 6
- segments: int32 [8192], P('rep'), may hold values from 0 to 2047, as said below
- enc_states: bfloat16 [2048, 1024], P(('rep', 'shard')), may hold values from -6 to 6
- enc_lengths: int32 [4], P('rep'), may hold values from 128 to 512, as said below
- cotangent: bfloat16 [8192, 1024], P(('rep', 'shard')), may hold values from -6 to 6
- self_qkv: bfloat16 [1024, 3072], P('shard'), may hold values from -0.1875 to 0.1875
- self_out: bfloat16 [1024, 1024], P('shard'), may hold values from -3 to 3
- cross_query: bfloat16 [1024, 1024], P('shard'), may hold values from -0.1875 to 0.1875
- cross_memory: bfloat16 [1024, 2048], P('shard'), may hold values from -0.1875 to 0.1875
- cross_out: bfloat16 [1024, 1024], P('shard'), may hold values from -2 to 2
- expand_weight: bfloat16 [1024, 8192], P('shard'), may hold values from -0.1875 to 0.1875
- shrink_weight: bfloat16 [8192, 1024], P('shard'), may hold values from -0.0625 to 0.0625
- norm_gain: bfloat16 [3, 1024], P(None, 'shard'), may hold values from 0.5 to 1.5
- norm_bias: bfloat16 [3, 1024], P(None, 'shard'), may hold values from -2 to 2
- proj_bias: bfloat16 [7, 1024], P(None, 'shard'), may hold values from -2 to 2
- expand_bias: bfloat16 [8192], P('shard'), may hold values from -2 to 2
Outputs:
- output: bfloat16 [8192, 1024], P(('rep', 'shard'))
- tokens_grad: float32 [8192, 1024], P(('rep', 'shard'))
- enc_grad: float32 [2048, 1024], P(('rep', 'shard'))
- self_qkv_grad: float32 [1024, 3072], P('shard')
- self_out_grad: float32 [1024, 1024], P('shard')
- cross_query_grad: float32 [1024, 1024], P('shard')
- cross_memory_grad: float32 [1024, 2048], P('shard')
- cross_out_grad: float32 [1024, 1024], P('shard')
- expand_grad: float32 [1024, 8192], P('shard')
- shrink_grad: float32 [8192, 1024], P('shard')
- gain_grad: float32 [3, 1024], P(None, 'shard')
- shift_grad: float32 [3, 1024], P(None, 'shard')
- proj_bias_grad: float32 [7, 1024], P(None, 'shard')
- expand_bias_grad: float32 [8192], P('shard')
Inputs may be any that keep to these rules, and one draw needn't show every extreme that they name: `segments`: within each sequence of 2048 tokens the ids start at 0 and never fall, and its last token is a document of its own with id 2048 - 1; among the 1 sequence of each index of rep, one holds a document that starts within its first 256 tokens and ends within its last 256. `enc_lengths`: some sequence has all 512 states valid.
All inputs are finite; a program needn't handle non-finite values.
Results may differ from a plain program's by a relative error of at most 0.025.
Values may be sent and summed in bfloat16 or wider, within the bound.
No kernel may reach another device: no remote copies, remote signals or barrier semaphores. Data moves between devices by JAX's collectives and lax.ppermute only.
A program may use at most 256 MiB of HBM per device.

v0:
```python
import jax
import jax.numpy as jnp
from jax import lax
from jax.sharding import PartitionSpec as P

D = 1024
H = 16
HD = 64
SEQ = 2048


EPS = 1e-05
NEGATIVE = -1e30


def from_behind(value, axis, steps):
    count = lax.axis_size(axis)
    initial, last = (max(0, -steps), min(count, count - steps))
    return lax.ppermute(value, axis, [(source, source + steps) for source in range(initial, last)])


def from_partner(value, axis, bit):
    return lax.ppermute(value, axis, [(i, i ^ 1 << bit) for i in range(lax.axis_size(axis))])


def from_behind_2(block, axis, distance):
    devices = range(lax.axis_size(axis))
    route = [((i - distance) % len(devices), i) for i in devices]
    return lax.ppermute(block, axis, route)


def norm_apply(rows, gain, shift):
    mean_rows = jnp.mean(rows, axis=-1, keepdims=True)
    centered = rows - mean_rows
    inverse = lax.rsqrt(jnp.mean(centered * centered, axis=-1, keepdims=True) + EPS)
    return centered * inverse * gain + shift


def gelu_apply(values):
    return jax.nn.gelu(values, approximate=True)


def split_heads(rows):
    return rows.reshape(rows.shape[0], H, HD)


def column_sums(rows):
    return jnp.sum(rows, axis=0, dtype=jnp.float32)


def shards(
    tokens,
    segments,
    enc_states,
    enc_lengths,
    cotangent,
    self_qkv,
    self_out,
    cross_query,
    cross_memory,
    cross_out,
    expand_weight,
    shrink_weight,
    norm_gain,
    norm_bias,
    proj_bias,
    expand_bias,
):
    gathered = (
        lax.all_gather(self_qkv, "shard", axis=0, tiled=True),
        lax.all_gather(self_out, "shard", axis=0, tiled=True),
        lax.all_gather(cross_query, "shard", axis=0, tiled=True),
        lax.all_gather(cross_memory, "shard", axis=0, tiled=True),
        lax.all_gather(cross_out, "shard", axis=0, tiled=True),
        lax.all_gather(expand_weight, "shard", axis=0, tiled=True),
        lax.all_gather(shrink_weight, "shard", axis=0, tiled=True),
        lax.all_gather(norm_gain, "shard", axis=1, tiled=True),
        lax.all_gather(norm_bias, "shard", axis=1, tiled=True),
        lax.all_gather(proj_bias, "shard", axis=1, tiled=True),
        lax.all_gather(expand_bias, "shard", axis=0, tiled=True),
    )
    attn_in, attn_proj, query_in, memory_in, cross_proj, expand_full, shrink_full = gathered[:7]
    gain_rows = gathered[7].astype(jnp.float32)
    shift_rows = gathered[8].astype(jnp.float32)
    bias_rows = gathered[9].astype(jnp.float32)
    hidden_bias = gathered[10].astype(jnp.float32)
    row_count = tokens.shape[0]
    span = SEQ // row_count
    bit_count = span.bit_length() - 1
    score_scale = HD ** (-0.5)
    shard_pos = lax.axis_index("shard")
    local_pos = shard_pos % span
    local_seq = shard_pos // span
    query_pos = local_pos * row_count + jnp.arange(row_count, dtype=jnp.int32)
    query_seg = lax.dynamic_slice_in_dim(segments, shard_pos * row_count, row_count)

    def piece_mask(distance):
        key_pos = (local_pos - distance) * row_count + jnp.arange(row_count, dtype=jnp.int32)
        key_seg = lax.dynamic_slice_in_dim(
            segments, jnp.maximum(shard_pos - distance, 0) * row_count, row_count
        )
        return (key_pos[None, :] <= query_pos[:, None]) & (key_seg[None, :] == query_seg[:, None])

    def piece_used(distance):
        last_seg = lax.dynamic_slice_in_dim(
            segments, jnp.maximum(shard_pos - distance, 0) * row_count + row_count - 1, 1
        )[0]
        return (local_pos >= distance) & (last_seg >= query_seg[0])

    residual_in = tokens.astype(jnp.float32)
    input_one = norm_apply(residual_in, gain_rows[0], shift_rows[0]).astype(jnp.bfloat16)
    projected = jnp.dot(input_one, attn_in, preferred_element_type=jnp.float32)
    query = (projected[:, :D] + bias_rows[0]).astype(jnp.bfloat16)
    key_rows = projected[:, D : 2 * D].astype(jnp.bfloat16)
    value_rows = (projected[:, 2 * D :] + bias_rows[1]).astype(jnp.bfloat16)
    key_value = jnp.concatenate([key_rows, value_rows], axis=1)
    query_heads = split_heads(query)

    def attend_piece(state_now, piece, distance):

        def attend_update(state_in):
            top_old, total_old, acc_old = state_in
            key_heads = split_heads(piece[:, :D])
            value_heads = split_heads(piece[:, D:])
            scores = (
                jnp.einsum(
                    "qhd,khd->hqk", query_heads, key_heads, preferred_element_type=jnp.float32
                )
                * score_scale
            )
            keep_mask = piece_mask(distance)[None]
            top_new = jnp.maximum(top_old, jnp.max(jnp.where(keep_mask, scores, NEGATIVE), axis=-1))
            expo_rows = jnp.exp(jnp.where(keep_mask, scores - top_new[..., None], NEGATIVE))
            fade_factor = jnp.exp(top_old - top_new)
            total_new = total_old * fade_factor + jnp.sum(expo_rows, axis=-1)
            acc_new = acc_old * fade_factor.T[:, :, None] + jnp.einsum(
                "hqk,khd->qhd",
                expo_rows.astype(jnp.bfloat16),
                value_heads,
                preferred_element_type=jnp.float32,
            )
            return (top_new, total_new, acc_new)

        return lax.cond(piece_used(distance), attend_update, lambda untouched: untouched, state_now)

    start_state = (
        jnp.full((H, row_count), NEGATIVE, jnp.float32),
        jnp.zeros((H, row_count), jnp.float32),
        jnp.zeros((row_count, H, HD), jnp.float32),
    )
    own_state = attend_piece(start_state, key_value, 0)
    kept_start = jnp.zeros((0, row_count, 2 * D), jnp.bfloat16)

    def forward_turn(distance, carry):
        piece, state_now, kept = carry
        piece = from_behind(piece, "shard", 1)
        state_now = attend_piece(state_now, piece, distance)
        return (piece, state_now, kept)

    _, final_state, kept_all = lax.fori_loop(
        1, span, forward_turn, (key_value, own_state, kept_start)
    )
    top_all, total_all, acc_all = final_state
    attn_heads = acc_all / total_all.T[:, :, None]
    log_total = top_all + jnp.log(total_all)
    attn_low = attn_heads.reshape(row_count, D).astype(jnp.bfloat16)
    hidden_one = (
        residual_in
        + jnp.dot(attn_low, attn_proj, preferred_element_type=jnp.float32)
        + bias_rows[2]
    )
    input_two = norm_apply(hidden_one, gain_rows[1], shift_rows[1]).astype(jnp.bfloat16)
    cross_queries = (
        jnp.dot(input_two, query_in, preferred_element_type=jnp.float32) + bias_rows[3]
    ).astype(jnp.bfloat16)
    memory_rows = jnp.dot(enc_states, memory_in, preferred_element_type=jnp.float32)
    memory_pair = jnp.concatenate(
        [
            memory_rows[:, :D].astype(jnp.bfloat16),
            (memory_rows[:, D:] + bias_rows[4]).astype(jnp.bfloat16),
        ],
        axis=1,
    )
    for bit_index in range(bit_count):
        partner = from_partner(memory_pair, "shard", bit_index)
        high_side = shard_pos // 2**bit_index % 2 == 1
        memory_pair = jnp.where(
            high_side,
            jnp.concatenate([partner, memory_pair], axis=0),
            jnp.concatenate([memory_pair, partner], axis=0),
        )
    key_heads_all = split_heads(memory_pair[:, :D])
    value_heads_all = split_heads(memory_pair[:, D:])
    enc_count = lax.dynamic_slice_in_dim(enc_lengths, local_seq, 1)[0]
    memory_keep = (jnp.arange(memory_pair.shape[0], dtype=jnp.int32) < enc_count)[None, None, :]
    cross_heads = split_heads(cross_queries)
    cross_scores = (
        jnp.einsum("qhd,khd->hqk", cross_heads, key_heads_all, preferred_element_type=jnp.float32)
        * score_scale
    )
    cross_top = jnp.max(jnp.where(memory_keep, cross_scores, NEGATIVE), axis=-1, keepdims=True)
    cross_expo = jnp.exp(jnp.where(memory_keep, cross_scores - cross_top, NEGATIVE))
    cross_probs = cross_expo / jnp.sum(cross_expo, axis=-1, keepdims=True)
    cross_low = cross_probs.astype(jnp.bfloat16)
    context_low = (
        jnp.einsum("hqk,khd->qhd", cross_low, value_heads_all, preferred_element_type=jnp.float32)
        .reshape(row_count, D)
        .astype(jnp.bfloat16)
    )
    hidden_two = (
        hidden_one
        + jnp.dot(context_low, cross_proj, preferred_element_type=jnp.float32)
        + bias_rows[5]
    )
    input_three = norm_apply(hidden_two, gain_rows[2], shift_rows[2]).astype(jnp.bfloat16)
    pre_act = jnp.dot(input_three, expand_full, preferred_element_type=jnp.float32) + hidden_bias
    act_low = gelu_apply(pre_act).astype(jnp.bfloat16)
    result = (
        hidden_two
        + jnp.dot(act_low, shrink_full, preferred_element_type=jnp.float32)
        + bias_rows[6]
    )
    again = (
        lax.all_gather(self_qkv, "shard", axis=0, tiled=True),
        lax.all_gather(self_out, "shard", axis=0, tiled=True),
        lax.all_gather(cross_query, "shard", axis=0, tiled=True),
        lax.all_gather(cross_memory, "shard", axis=0, tiled=True),
        lax.all_gather(cross_out, "shard", axis=0, tiled=True),
        lax.all_gather(expand_weight, "shard", axis=0, tiled=True),
        lax.all_gather(shrink_weight, "shard", axis=0, tiled=True),
    )
    attn_in, attn_proj, query_in, memory_in, cross_proj, expand_full, shrink_full = again
    grad_out = cotangent.astype(jnp.float32)
    grad_bias_six = column_sums(cotangent)
    grad_shrink = jnp.einsum("tf,td->fd", act_low, cotangent, preferred_element_type=jnp.float32)
    grad_act = jnp.einsum("td,fd->tf", cotangent, shrink_full, preferred_element_type=jnp.float32)
    grad_pre = jax.vjp(gelu_apply, pre_act)[1](grad_act)[0].astype(jnp.bfloat16)
    grad_hidden_bias = column_sums(grad_pre)
    grad_expand = jnp.einsum("td,tf->df", input_three, grad_pre, preferred_element_type=jnp.float32)
    grad_in_three = jnp.einsum(
        "tf,df->td", grad_pre, expand_full, preferred_element_type=jnp.float32
    )
    norm_three = jax.vjp(norm_apply, hidden_two, gain_rows[2], shift_rows[2])[1](grad_in_three)
    grad_two = grad_out + norm_three[0]
    grad_two_low = grad_two.astype(jnp.bfloat16)
    grad_bias_five = column_sums(grad_two_low)
    grad_cross_proj = jnp.einsum(
        "td,te->de", context_low, grad_two_low, preferred_element_type=jnp.float32
    )
    grad_context = jnp.einsum(
        "te,de->td", grad_two_low, cross_proj, preferred_element_type=jnp.float32
    ).astype(jnp.bfloat16)
    grad_ctx_heads = split_heads(grad_context)
    grad_cross_probs = jnp.einsum(
        "qhd,khd->hqk", grad_ctx_heads, value_heads_all, preferred_element_type=jnp.float32
    )
    row_inner = jnp.sum(cross_probs * grad_cross_probs, axis=-1, keepdims=True)
    grad_cross_scores = (cross_probs * (grad_cross_probs - row_inner)).astype(jnp.bfloat16)
    grad_cross_q = (
        (
            jnp.einsum(
                "hqk,khd->qhd", grad_cross_scores, key_heads_all, preferred_element_type=jnp.float32
            )
            * score_scale
        )
        .reshape(row_count, D)
        .astype(jnp.bfloat16)
    )
    grad_mem_key = (
        jnp.einsum(
            "hqk,qhd->khd", grad_cross_scores, cross_heads, preferred_element_type=jnp.float32
        ).reshape(-1, D)
        * score_scale
    )
    grad_mem_value = jnp.einsum(
        "hqk,qhd->khd", cross_low, grad_ctx_heads, preferred_element_type=jnp.float32
    ).reshape(-1, D)
    mem_partial = jnp.concatenate([grad_mem_key, grad_mem_value], axis=1)
    for bit_index in reversed(range(bit_count)):
        half_rows = mem_partial.shape[0] // 2
        low_rows = mem_partial[:half_rows]
        high_rows = mem_partial[half_rows:]
        high_side = shard_pos // 2**bit_index % 2 == 1
        outgoing = jnp.where(high_side, low_rows, high_rows)
        staying = jnp.where(high_side, high_rows, low_rows)
        mem_partial = staying + from_partner(
            outgoing.astype(jnp.bfloat16), "shard", bit_index
        ).astype(outgoing.dtype)
    mem_grads = mem_partial.astype(jnp.bfloat16)
    grad_bias_four = column_sums(mem_grads[:, D:])
    grad_memory = jnp.einsum("td,te->de", enc_states, mem_grads, preferred_element_type=jnp.float32)
    grad_enc = jnp.einsum("te,de->td", mem_grads, memory_in, preferred_element_type=jnp.float32)
    grad_bias_three = column_sums(grad_cross_q)
    grad_query_in = jnp.einsum(
        "td,te->de", input_two, grad_cross_q, preferred_element_type=jnp.float32
    )
    grad_in_two = jnp.einsum(
        "te,de->td", grad_cross_q, query_in, preferred_element_type=jnp.float32
    )
    norm_two = jax.vjp(norm_apply, hidden_one, gain_rows[1], shift_rows[1])[1](grad_in_two)
    grad_one = grad_two + norm_two[0]
    grad_one_low = grad_one.astype(jnp.bfloat16)
    grad_bias_two = column_sums(grad_one_low)
    grad_attn_proj = jnp.einsum(
        "td,te->de", attn_low, grad_one_low, preferred_element_type=jnp.float32
    )
    grad_attn = jnp.einsum(
        "te,de->td", grad_one_low, attn_proj, preferred_element_type=jnp.float32
    ).astype(jnp.bfloat16)
    grad_attn_heads = split_heads(grad_attn)
    row_delta = jnp.sum(grad_attn_heads.astype(jnp.float32) * attn_heads, axis=-1).T

    def back_piece(grad_q_now, grad_kv_now, piece, distance):

        def back_update(state_in):
            grad_q_old, grad_kv_old = state_in
            key_heads = split_heads(piece[:, :D])
            value_heads = split_heads(piece[:, D:])
            scores = (
                jnp.einsum(
                    "qhd,khd->hqk", query_heads, key_heads, preferred_element_type=jnp.float32
                )
                * score_scale
            )
            keep_mask = piece_mask(distance)[None]
            probs = jnp.exp(jnp.where(keep_mask, scores - log_total[..., None], NEGATIVE))
            grad_probs = jnp.einsum(
                "qhd,khd->hqk", grad_attn_heads, value_heads, preferred_element_type=jnp.float32
            )
            grad_scores = (probs * (grad_probs - row_delta[..., None])).astype(jnp.bfloat16)
            grad_q_new = grad_q_old + jnp.einsum(
                "hqk,khd->qhd", grad_scores, key_heads, preferred_element_type=jnp.float32
            )
            grad_key = jnp.einsum(
                "hqk,qhd->khd", grad_scores, query_heads, preferred_element_type=jnp.float32
            ).reshape(row_count, D)
            grad_value = jnp.einsum(
                "hqk,qhd->khd",
                probs.astype(jnp.bfloat16),
                grad_attn_heads,
                preferred_element_type=jnp.float32,
            ).reshape(row_count, D)
            return (
                grad_q_new,
                grad_kv_old + jnp.concatenate([grad_key * score_scale, grad_value], axis=1),
            )

        return lax.cond(
            piece_used(distance),
            back_update,
            lambda untouched: untouched,
            (grad_q_now, grad_kv_now),
        )

    own_q, own_kv = back_piece(
        jnp.zeros((row_count, H, HD), jnp.float32),
        jnp.zeros((row_count, 2 * D), jnp.float32),
        key_value,
        0,
    )

    def backward_turn(distance, carry):
        piece, grad_q_now, grad_kv_now = carry
        grad_kv_now = from_behind_2(grad_kv_now.astype(jnp.bfloat16), "shard", 1).astype(
            grad_kv_now.dtype
        )
        piece = from_behind(piece, "shard", 1)
        grad_q_now, grad_kv_now = back_piece(grad_q_now, grad_kv_now, piece, distance)
        return (piece, grad_q_now, grad_kv_now)

    _, grad_q_heads, grad_kv_partial = lax.fori_loop(
        1, span, backward_turn, (key_value, own_q, own_kv)
    )
    key_value_sum = from_behind_2(grad_kv_partial.astype(jnp.bfloat16), "shard", 1 - span).astype(
        grad_kv_partial.dtype
    )
    grad_query = (grad_q_heads * score_scale).reshape(row_count, D).astype(jnp.bfloat16)
    grad_kv_low = key_value_sum.astype(jnp.bfloat16)
    grad_qkv = jnp.concatenate([grad_query, grad_kv_low], axis=1)
    grad_bias_zero = column_sums(grad_query)
    grad_bias_one = column_sums(grad_kv_low[:, D:])
    grad_attn_in = jnp.einsum("td,te->de", input_one, grad_qkv, preferred_element_type=jnp.float32)
    grad_in_one = jnp.einsum("te,de->td", grad_qkv, attn_in, preferred_element_type=jnp.float32)
    norm_one = jax.vjp(norm_apply, residual_in, gain_rows[0], shift_rows[0])[1](grad_in_one)
    grad_tokens = grad_one + norm_one[0]
    grad_gains = jnp.stack([norm_one[1], norm_two[1], norm_three[1]])
    grad_shifts = jnp.stack([norm_one[2], norm_two[2], norm_three[2]])
    grad_biases = jnp.stack(
        [
            grad_bias_zero,
            grad_bias_one,
            grad_bias_two,
            grad_bias_three,
            grad_bias_four,
            grad_bias_five,
            grad_bias_six,
        ]
    )
    owned = (
        lax.psum_scatter(
            grad_attn_in.astype(jnp.bfloat16), "shard", scatter_dimension=0, tiled=True
        ).astype(jnp.float32),
        lax.psum_scatter(
            grad_attn_proj.astype(jnp.bfloat16), "shard", scatter_dimension=0, tiled=True
        ).astype(jnp.float32),
        lax.psum_scatter(
            grad_query_in.astype(jnp.bfloat16), "shard", scatter_dimension=0, tiled=True
        ).astype(jnp.float32),
        lax.psum_scatter(
            grad_memory.astype(jnp.bfloat16), "shard", scatter_dimension=0, tiled=True
        ).astype(jnp.float32),
        lax.psum_scatter(
            grad_cross_proj.astype(jnp.bfloat16), "shard", scatter_dimension=0, tiled=True
        ).astype(jnp.float32),
        lax.psum_scatter(
            grad_expand.astype(jnp.bfloat16), "shard", scatter_dimension=0, tiled=True
        ).astype(jnp.float32),
        lax.psum_scatter(
            grad_shrink.astype(jnp.bfloat16), "shard", scatter_dimension=0, tiled=True
        ).astype(jnp.float32),
        lax.psum_scatter(
            grad_gains.astype(jnp.bfloat16), "shard", scatter_dimension=1, tiled=True
        ).astype(jnp.float32),
        lax.psum_scatter(
            grad_shifts.astype(jnp.bfloat16), "shard", scatter_dimension=1, tiled=True
        ).astype(jnp.float32),
        lax.psum_scatter(
            grad_biases.astype(jnp.bfloat16), "shard", scatter_dimension=1, tiled=True
        ).astype(jnp.float32),
        lax.psum_scatter(
            grad_hidden_bias.astype(jnp.bfloat16), "shard", scatter_dimension=0, tiled=True
        ).astype(jnp.float32),
    )
    totals = (
        lax.psum(owned[0].astype(jnp.bfloat16), "rep").astype(jnp.float32),
        lax.psum(owned[1].astype(jnp.bfloat16), "rep").astype(jnp.float32),
        lax.psum(owned[2].astype(jnp.bfloat16), "rep").astype(jnp.float32),
        lax.psum(owned[3].astype(jnp.bfloat16), "rep").astype(jnp.float32),
        lax.psum(owned[4].astype(jnp.bfloat16), "rep").astype(jnp.float32),
        lax.psum(owned[5].astype(jnp.bfloat16), "rep").astype(jnp.float32),
        lax.psum(owned[6].astype(jnp.bfloat16), "rep").astype(jnp.float32),
        lax.psum(owned[7].astype(jnp.bfloat16), "rep").astype(jnp.float32),
        lax.psum(owned[8].astype(jnp.bfloat16), "rep").astype(jnp.float32),
        lax.psum(owned[9].astype(jnp.bfloat16), "rep").astype(jnp.float32),
        lax.psum(owned[10].astype(jnp.bfloat16), "rep").astype(jnp.float32),
    )
    return (
        result.astype(jnp.bfloat16),
        grad_tokens,
        grad_enc,
        totals[0],
        totals[1],
        totals[2],
        totals[3],
        totals[4],
        totals[5],
        totals[6],
        totals[7],
        totals[8],
        totals[9],
        totals[10],
    )


def solution(mesh):
    return jax.shard_map(
        shards,
        mesh=mesh,
        in_specs=(
            P(("rep", "shard"), None),
            P("rep"),
            P(("rep", "shard"), None),
            P("rep"),
            P(("rep", "shard"), None),
            P("shard", None),
            P("shard", None),
            P("shard", None),
            P("shard", None),
            P("shard", None),
            P("shard", None),
            P("shard", None),
            P(None, "shard"),
            P(None, "shard"),
            P(None, "shard"),
            P("shard"),
        ),
        out_specs=(
            P(("rep", "shard"), None),
            P(("rep", "shard"), None),
            P(("rep", "shard"), None),
            P("shard", None),
            P("shard", None),
            P("shard", None),
            P("shard", None),
            P("shard", None),
            P("shard", None),
            P("shard", None),
            P(None, "shard"),
            P(None, "shard"),
            P(None, "shard"),
            P("shard"),
        ),
        check_vma=False,
    )
```

profile of v0, /device:TPU:12, one launch (start us, length us, event | category | flops | bytes accessed | tf_op | source)
XLA Modules:
  0.0 1801.9 jit_solution(9910110105213441028)
XLA Ops:
  25.7 30.7 %all-gather.12.cloned.1.call-done = bf16[1024,2048]{1,0:T(8,128)(2,1)} async-done(((bf16[128,2048]{1,0:T(8,128)(2,1)}), bf16[1024,2048]{1,0:T(8,128)(2,1)}) %all-gather.12.cloned.1.call-update) | async-done | bytes 4194320 | tf_op jit(solution)/shard_map/all_gather | solution.py:73
  65.3 41.8 %all_gather.41 = bf16[3,1024]{1,0:T(4,128)(2,1)S(1)} all-gather(bf16[3,128]{1,0:T(4,128)(2,1)S(1)} %copy-done.59), channel_id=1, replica_groups=mesh['rep'=4,'shard'=8] {'shard'}, dimensions={1}, use_global_device_ids=true | all-gather | bytes 6912 | tf_op jit(solution)/shard_map/all_gather | solution.py:78
  130.8 59.9 %collective-permute-done.5 = bf16[256,2048]{1,0:T(8,128)(2,1)S(1)} collective-permute-done((bf16[256,2048]{1,0:T(8,128)(2,1)S(1)}, bf16[256,2048]{1,0:T(8,128)(2,1)S(1)}, u32[]{:S(2)}, u32[]{:S(2)}) %collective-permute-start.5) | collective-permute-done | bytes 1048608 | tf_op jit(solution)/shard_map/ppermute | solution.py:23
  214.6 270.2 %while.46 = (s32[]{:T(128)}, bf16[256,2048]{0,1:T(8,128)(2,1)}, f32[16,256]{1,0:T(8,128)}, f32[16,256]{1,0:T(8,128)S(1)}, f32[256,16,64]{0,2,1:T(8,128)S(1)}, /*...) while((s32[]{:T(128)}, bf16[256,2048]{0,1:T(8,128)(2,1)}, ...), condition=%wide.region_11.12_spmd.clone, body=%wide.region_6.11_spmd.clone.sunk | while | flops 280703488 | bytes 25176640 | solution.py:160
  219.0 30.6 %collective-permute-done = bf16[256,2048]{0,1:T(8,128)(2,1)S(1)} collective-permute-done((bf16[256,2048]{0,1:T(8,128)(2,1)}, bf16[256,2048]{0,1:T(8,128)(2,1)S(1)}, u32[]{:S(2)}, u32[]{:S(2)}) %collective-permute-start) | collective-permute-done | bytes 1048608 | tf_op jit(solution)/shard_map/while/body/eval_jaxpr/ppermute | solution.py:19
  260.2 31.6 %collective-permute-done = bf16[256,2048]{0,1:T(8,128)(2,1)S(1)} collective-permute-done((bf16[256,2048]{0,1:T(8,128)(2,1)}, bf16[256,2048]{0,1:T(8,128)(2,1)S(1)}, u32[]{:S(2)}, u32[]{:S(2)}) %collective-permute-start) | collective-permute-done | bytes 1048608 | tf_op jit(solution)/shard_map/while/body/eval_jaxpr/ppermute | solution.py:19
  313.6 23.2 %collective-permute-done = bf16[256,2048]{0,1:T(8,128)(2,1)S(1)} collective-permute-done((bf16[256,2048]{0,1:T(8,128)(2,1)}, bf16[256,2048]{0,1:T(8,128)(2,1)S(1)}, u32[]{:S(2)}, u32[]{:S(2)}) %collective-permute-start) | collective-permute-done | bytes 1048608 | tf_op jit(solution)/shard_map/while/body/eval_jaxpr/ppermute | solution.py:19
  337.8 35.7 %collective-permute-start = (bf16[256,2048]{0,1:T(8,128)(2,1)}, bf16[256,2048]{0,1:T(8,128)(2,1)S(1)}, u32[]{:S(2)}, u32[]{:S(2)}) collective-permute-start(bf16[256,2048]{0,1:T(8,128)(2,1)} %get-tuple-element.1516), channel_id=1, source_target_pairs={{0,1},{1,2},{2,3},{3,4},{4,5},{5,6},{6,7},{8,9},{9,10},{10,11},{11... | collective-permute-start | bytes 3145736 | tf_op jit(solution)/shard_map/while/body/eval_jaxpr/ppermute | solution.py:19
  377.5 41.5 %collective-permute-start = (bf16[256,2048]{0,1:T(8,128)(2,1)}, bf16[256,2048]{0,1:T(8,128)(2,1)S(1)}, u32[]{:S(2)}, u32[]{:S(2)}) collective-permute-start(bf16[256,2048]{0,1:T(8,128)(2,1)} %get-tuple-element.1516), channel_id=1, source_target_pairs={{0,1},{1,2},{2,3},{3,4},{4,5},{5,6},{6,7},{8,9},{9,10},{10,11},{11... | collective-permute-start | bytes 3145736 | tf_op jit(solution)/shard_map/while/body/eval_jaxpr/ppermute | solution.py:19
  423.0 24.3 %collective-permute-start = (bf16[256,2048]{0,1:T(8,128)(2,1)}, bf16[256,2048]{0,1:T(8,128)(2,1)S(1)}, u32[]{:S(2)}, u32[]{:S(2)}) collective-permute-start(bf16[256,2048]{0,1:T(8,128)(2,1)} %get-tuple-element.1516), channel_id=1, source_target_pairs={{0,1},{1,2},{2,3},{3,4},{4,5},{5,6},{6,7},{8,9},{9,10},{10,11},{11... | collective-permute-start | bytes 3145736 | tf_op jit(solution)/shard_map/while/body/eval_jaxpr/ppermute | solution.py:19
  511.9 19.4 %fusion.140 = f32[256,8192]{1,0:T(8,128)} fusion(bf16[256,1024]{1,0:T(8,128)(2,1)S(1)} %copy-done.20, bf16[8192,1024]{1,0:T(8,128)(2,1)} %all-gather.20.cloned.1.call-done), kind=kOutput, calls=%fused_computation.228 | convolution fusion | flops 4294967296 | bytes 25690112 | tf_op jit(solution)/shard_map/td,fd->tf/dot_general | solution.py:236
  531.3 76.6 %all-gather.18.cloned.1.call-done = bf16[1024,8192]{1,0:T(8,128)(2,1)} async-done(((bf16[128,8192]{1,0:T(8,128)(2,1)}), bf16[1024,8192]{1,0:T(8,128)(2,1)}) %all-gather.18.cloned.1.call-update) | async-done | bytes 16777232 | tf_op jit(solution)/shard_map/all_gather | solution.py:75
  607.9 18.9 %fusion.120 = (bf16[8192]{0:T(1024)(128)(2,1)}, bf16[256,8192]{1,0:T(8,128)(2,1)}, f32[256,8192]{1,0:T(8,128)}) fusion(f32[256,8192]{1,0:T(8,128)} %fusion.140, f32[8192]{0:T(1024)S(1)} %convert_element_type.328, bf16[1024,8192]{1,0:T(8,128)(2,1)} %all-gather.18.cloned.1.call-done, f32[256,1024]{1,0:T(8,128)} %copy-done.6, f32[1024]{0:T(1024)S(1)} %bitcast.211, ...), kind=kOutput, calls=%fused_computation.210 | convolution fusion | flops 4342407168 | bytes 38856704 | tf_op jit(solution)/shard_map/dot_general | solution.py:216
  663.0 36.8 %collective-permute-start.7 = (bf16[256,2048]{0,1:T(8,128)(2,1)S(1)}, bf16[256,2048]{0,1:T(8,128)(2,1)S(1)}, u32[]{:S(2)}, u32[]{:S(2)}) collective-permute-start(bf16[256,2048]{0,1:T(8,128)(2,1)S(1)} %select_convert_fusion), channel_id=1, source_target_pairs={{0,4},{1,5},{2,6},{3,7},{4,0},{5,1},{6,2},{7,3},{8,12},{9,13},{10,... | collective-permute-start | bytes 3145736 | tf_op jit(solution)/shard_map/ppermute | solution.py:23
  699.8 22.1 %collective-permute-done.7 = bf16[256,2048]{0,1:T(8,128)(2,1)S(1)} collective-permute-done((bf16[256,2048]{0,1:T(8,128)(2,1)S(1)}, bf16[256,2048]{0,1:T(8,128)(2,1)S(1)}, u32[]{:S(2)}, u32[]{:S(2)}) %collective-permute-start.7) | collective-permute-done | bytes 1048608 | tf_op jit(solution)/shard_map/ppermute | solution.py:23
  783.5 295.0 %while.47 = (s32[]{:T(128)}, bf16[256,2048]{0,1:T(8,128)(2,1)}, f32[256,16,64]{0,2,1:T(8,128)}, f32[256,2048]{0,1:T(8,128)S(1)}, s32[]{:T(128)}, /*index=5*/s32[...) while((s32[]{:T(128)}, bf16[256,2048]{0,1:T(8,128)(2,1)}, ...), condition=%wide.region_29.30_spmd.clone, body=%wide.region_26.29_spmd.clone.sunk | while | flops 684392960 | bytes 71035560 | solution.py:371
  806.9 24.6 %collective-permute-done.1 = bf16[256,2048]{0,1:T(8,128)(2,1)} collective-permute-done((bf16[256,2048]{0,1:T(8,128)(2,1)}, bf16[256,2048]{0,1:T(8,128)(2,1)}, u32[]{:S(2)}, u32[]{:S(2)}) %collective-permute-start.1) | collective-permute-done | bytes 1048608 | tf_op jit(solution)/shard_map/while/body/eval_jaxpr/ppermute | solution.py:19
  854.7 25.8 %collective-permute-done.2 = bf16[256,2048]{0,1:T(8,128)(2,1)} collective-permute-done((bf16[256,2048]{0,1:T(8,128)(2,1)}, bf16[256,2048]{0,1:T(8,128)(2,1)}, u32[]{:S(2)}, u32[]{:S(2)}) %collective-permute-start.2) | collective-permute-done | bytes 1048608 | tf_op jit(solution)/shard_map/while/body/eval_jaxpr/ppermute | solution.py:29
  1136.1 65.0 %reduce-scatter.19.cloned.1.call-done = bf16[128,3072]{1,0:T(8,128)(2,1)} async-done(((bf16[1024,3072]{1,0:T(8,128)(2,1)}), bf16[128,3072]{1,0:T(8,128)(2,1)}) %reduce-scatter.19.cloned.1.call-update) | async-done | bytes 786448 | tf_op jit(solution)/shard_map/reduce_scatter | solution.py:400
  1201.2 169.0 %reduce-scatter.27.cloned.1.call-done = bf16[128,8192]{1,0:T(8,128)(2,1)} async-done(((bf16[1024,8192]{1,0:T(8,128)(2,1)}), bf16[128,8192]{1,0:T(8,128)(2,1)}) %reduce-scatter.27.cloned.1.call-update) | async-done | bytes 2097168 | tf_op jit(solution)/shard_map/reduce_scatter | solution.py:415
  1370.2 168.8 %reduce-scatter.29.cloned.1.call-done = bf16[1024,1024]{1,0:T(8,128)(2,1)} async-done(((bf16[8192,1024]{1,0:T(8,128)(2,1)}), bf16[1024,1024]{1,0:T(8,128)(2,1)}) %reduce-scatter.29.cloned.1.call-update) | async-done | bytes 2097168 | tf_op jit(solution)/shard_map/reduce_scatter | solution.py:418
  1540.3 25.6 %all-reduce = bf16[8192]{0:T(1024)(128)(2,1)S(1)} all-reduce(bf16[8192]{0:T(1024)(128)(2,1)S(1)} %copy-done.50), channel_id=12, replica_groups=mesh['rep'=4,'shard'=8] {'shard'}, use_global_device_ids=true, to_apply=%region_66.67.clone | all-reduce | flops 8192 | bytes 32768
  1606.1 26.1 %reduce-scatter.37.cloned.1.call-done = bf16[128,7]{1,0:T(8,128)(2,1)} async-done(((bf16[1024,7]{1,0:T(8,128)(2,1)}), bf16[128,7]{1,0:T(8,128)(2,1)}) %reduce-scatter.37.cloned.1.call-update) | async-done | bytes 1808
  1644.4 135.5 %all-reduce.5.cloned.1.call-done = (bf16[128,2048]{0,1:T(8,128)(2,1)}, bf16[128,3072]{1,0:T(8,128)(2,1)}, bf16[128,1024]{1,0:T(8,128)(2,1)}, bf16[128,1024]{1,0:...) async-done(((bf16[128,2048]{0,1:T(8,128)(2,1)}, bf16[128,3072]{1,0:T(8,128)(2,1)}, bf16[128,1024]{1,0:T(8,128)(2,1)}, ...) | async-done | bytes 6291472 | tf_op jit(solution)/shard_map/psum | solution.py:438
  (499 shorter events, 690.9 us)
Async XLA Ops:
  7.2 49.2 %all-gather.12.cloned.1.call-start = ((), (), s32[]{:S(2)}) async-start(), calls=%async_computation.12 | async-start | bytes 4718592 | tf_op jit(solution)/shard_map/all_gather | solution.py:73
  7.9 186.6 %all-gather.8.cloned.1.call-start = ((), (), s32[]{:S(2)}) async-start(), calls=%async_computation.10 | async-start | bytes 7077888 | tf_op jit(solution)/shard_map/all_gather | solution.py:70
  8.7 477.0 %all-gather.10.cloned.1.call-start = ((), (), s32[]{:S(2)}) async-start(), calls=%async_computation.11 | async-start | bytes 2359296 | tf_op jit(solution)/shard_map/all_gather | solution.py:71
  9.4 479.2 %all-gather.14.cloned.1.call-start = ((), (), s32[]{:S(2)}) async-start(), calls=%async_computation.13 | async-start | bytes 2359296 | tf_op jit(solution)/shard_map/all_gather | solution.py:72
  10.0 498.0 %all-gather.16.cloned.1.call-start = ((), (), s32[]{:S(2)}) async-start(), calls=%async_computation.14 | async-start | bytes 2359296 | tf_op jit(solution)/shard_map/all_gather | solution.py:74
  10.6 501.3 %all-gather.20.cloned.1.call-start = ((), (), s32[]{:S(2)}) async-start(), calls=%async_computation.16 | async-start | bytes 18874368 | tf_op jit(solution)/shard_map/all_gather | solution.py:76
  11.2 596.7 %all-gather.18.cloned.1.call-start = ((), (), s32[]{:S(2)}) async-start(), calls=%async_computation.15 | async-start | bytes 18874368 | tf_op jit(solution)/shard_map/all_gather | solution.py:75
  12.0 1122.1 %reduce-scatter.31.cloned.1.call-start = ((), (), s32[]{:S(2)}) async-start(), calls=%async_computation.23 | async-start | bytes 4718592
  61.2 65.9 %collective-permute-start.4 = (bf16[128,2048]{1,0:T(8,128)(2,1)S(1)}, bf16[128,2048]{1,0:T(8,128)(2,1)S(1)}, u32[]{:S(2)}, u32[]{:S(2)}) collective-permute-start(bf16[128,2048]{1,0:T(8,128)(2,1)S(1)} %maximum_select_fusion.2), channel_id=1, source_target_pairs={{0,2},{1,3},{2,0},{3,1},{4,6},{5,7},{6,4},{7,5},{8,10},{9,11},{10,... | collective-permute-start | bytes 1572872 | tf_op jit(solution)/shard_map/ppermute | solution.py:23
  127.4 63.3 %collective-permute-start.5 = (bf16[256,2048]{1,0:T(8,128)(2,1)S(1)}, bf16[256,2048]{1,0:T(8,128)(2,1)S(1)}, u32[]{:S(2)}, u32[]{:S(2)}) collective-permute-start(bf16[256,2048]{1,0:T(8,128)(2,1)S(1)} %maximum_select_fusion.1), channel_id=1, source_target_pairs={{0,4},{1,5},{2,6},{3,7},{4,0},{5,1},{6,2},{7,3},{8,12},{9,13},{10,... | collective-permute-start | bytes 3145736 | tf_op jit(solution)/shard_map/ppermute | solution.py:23
  377.5 44.4 %collective-permute-start = (bf16[256,2048]{0,1:T(8,128)(2,1)}, bf16[256,2048]{0,1:T(8,128)(2,1)S(1)}, u32[]{:S(2)}, u32[]{:S(2)}) collective-permute-start(bf16[256,2048]{0,1:T(8,128)(2,1)} %get-tuple-element.1516), channel_id=1, source_target_pairs={{0,1},{1,2},{2,3},{3,4},{4,5},{5,6},{6,7},{8,9},{9,10},{10,11},{11... | collective-permute-start | bytes 3145736 | tf_op jit(solution)/shard_map/while/body/eval_jaxpr/ppermute | solution.py:19
  663.0 59.0 %collective-permute-start.7 = (bf16[256,2048]{0,1:T(8,128)(2,1)S(1)}, bf16[256,2048]{0,1:T(8,128)(2,1)S(1)}, u32[]{:S(2)}, u32[]{:S(2)}) collective-permute-start(bf16[256,2048]{0,1:T(8,128)(2,1)S(1)} %select_convert_fusion), channel_id=1, source_target_pairs={{0,4},{1,5},{2,6},{3,7},{4,0},{5,1},{6,2},{7,3},{8,12},{9,13},{10,... | collective-permute-start | bytes 3145736 | tf_op jit(solution)/shard_map/ppermute | solution.py:23
  748.0 388.1 %reduce-scatter.21.cloned.1.call-start = ((), (), s32[]{:S(2)}) async-start(), calls=%async_computation.18 | async-start | bytes 2359296 | tf_op jit(solution)/shard_map/reduce_scatter | solution.py:403
  758.1 378.0 %reduce-scatter.23.cloned.1.call-start = ((), (), s32[]{:S(2)}) async-start(), calls=%async_computation.19 | async-start | bytes 2359296 | tf_op jit(solution)/shard_map/reduce_scatter | solution.py:406
  761.5 374.6 %reduce-scatter.25.cloned.1.call-start = ((), (), s32[]{:S(2)}) async-start(), calls=%async_computation.20 | async-start | bytes 2359296 | tf_op jit(solution)/shard_map/reduce_scatter | solution.py:412
  764.8 436.4 %reduce-scatter.19.cloned.1.call-start = ((), (), s32[]{:S(2)}) async-start(), calls=%async_computation.17 | async-start | bytes 7077888 | tf_op jit(solution)/shard_map/reduce_scatter | solution.py:400
  784.7 46.8 %collective-permute-start.1 = (bf16[256,2048]{0,1:T(8,128)(2,1)}, bf16[256,2048]{0,1:T(8,128)(2,1)}, u32[]{:S(2)}, u32[]{:S(2)}) collective-permute-start(bf16[256,2048]{0,1:T(8,128)(2,1)} %get-tuple-element.1570), channel_id=1, source_target_pairs={{0,1},{1,2},{2,3},{3,4},{4,5},{5,6},{6,7},{8,9},{9,10},{10,11},{11... | collective-permute-start | bytes 3145736 | tf_op jit(solution)/shard_map/while/body/eval_jaxpr/ppermute | solution.py:19
  848.8 45.9 %collective-permute-start.1 = (bf16[256,2048]{0,1:T(8,128)(2,1)}, bf16[256,2048]{0,1:T(8,128)(2,1)}, u32[]{:S(2)}, u32[]{:S(2)}) collective-permute-start(bf16[256,2048]{0,1:T(8,128)(2,1)} %get-tuple-element.1570), channel_id=1, source_target_pairs={{0,1},{1,2},{2,3},{3,4},{4,5},{5,6},{6,7},{8,9},{9,10},{10,11},{11... | collective-permute-start | bytes 3145736 | tf_op jit(solution)/shard_map/while/body/eval_jaxpr/ppermute | solution.py:19
  1098.6 271.5 %reduce-scatter.27.cloned.1.call-start = ((), (), s32[]{:S(2)}) async-start(), calls=%async_computation.21 | async-start | bytes 18874368 | tf_op jit(solution)/shard_map/reduce_scatter | solution.py:415
  1110.3 428.7 %reduce-scatter.29.cloned.1.call-start = ((), (), s32[]{:S(2)}) async-start(), calls=%async_computation.22 | async-start | bytes 18874368 | tf_op jit(solution)/shard_map/reduce_scatter | solution.py:418
  1122.8 458.9 %reduce-scatter.33.cloned.1.call-start = ((), (), s32[]{:S(2)}) async-start(), calls=%async_computation.24 | async-start | bytes 294912
  1130.5 470.4 %reduce-scatter.35.cloned.1.call-start = ((), (), s32[]{:S(2)}) async-start(), calls=%async_computation.25 | async-start | bytes 294912
  1132.8 499.3 %reduce-scatter.37.cloned.1.call-start = ((), (), s32[]{:S(2)}) async-start(), calls=%async_computation.26 | async-start | bytes 294912
  1134.0 645.9 %all-reduce.5.cloned.1.call-start = ((), (), s32[]{:S(2)}) async-start(), calls=%async_computation.27 | async-start | bytes 12582912 | tf_op jit(solution)/shard_map/psum | solution.py:438
  (88 other events, 2779.4 us)
Sparse Core Ops, SparseCore 0:
  9.6 46.7 all-gather.11
  58.1 71.0 all-gather.7
  130.8 49.3 all-gather.9
  181.6 31.7 all-gather.13
  214.9 35.6 all-gather.15
  252.1 198.0 all-gather.19
  451.8 156.1 all-gather.17
  748.1 49.0 reduce-scatter.30
  799.5 37.5 reduce-scatter.20
  839.2 39.4 reduce-scatter.22
  880.9 34.4 reduce-scatter.24
  1098.8 102.3 reduce-scatter.18
  1203.5 166.6 reduce-scatter.26
  1372.4 166.5 reduce-scatter.28
  1541.7 27.9 reduce-scatter.32
  1572.4 28.4 reduce-scatter.34
  1603.6 28.5 reduce-scatter.36
  1637.8 142.0 all-reduce.4
where the time goes:
time: 1820 us; the launch traced here: 1800 us
  waiting for transfers between devices  1030 us (57%)
  starting transfers between devices  275 us (15%)
  matrix products  205 us (11%)
  blocking collectives  110 us (6%)
  local copies, waits for them, and re-layouts  86 us (5%)
  other arithmetic  63.1 us (3%)
  loops' own time  19.6 us (1%)
  between operations  18.3 us (1%)
    ppermute x14, waiting for transfers between devices, from_behind(): lax.ppermute(value, axis, [(source, source + steps) for source in range(i...  177 us
    ppermute x14, starting transfers between devices, from_behind(): lax.ppermute(value, axis, [(source, source + steps) for source in range(i...  171 us
    reduce_scatter x1, waiting for transfers between devices, shards(): lax.psum_scatter(grad_expand.astype(jnp.bfloat16), 'shard', scatter_dimen...  169 us
    reduce_scatter x1, waiting for transfers between devices, shards(): lax.psum_scatter(grad_shrink.astype(jnp.bfloat16), 'shard', scatter_dimen...  169 us
    psum x1, waiting for transfers between devices, shards(): lax.psum(owned[3].astype(jnp.bfloat16), 'rep').astype(jnp.float32)  135 us
    ppermute x6, waiting for transfers between devices, from_partner(): lax.ppermute(value, axis, [(i, i ^ 1 << bit) for i in range(lax.axis_size...  98.1 us
    all_gather x1, waiting for transfers between devices, shards(): lax.all_gather(expand_weight, 'shard', axis=0, tiled=True)  76.6 us
    reduce_scatter x1, waiting for transfers between devices, shards(): lax.psum_scatter(grad_attn_in.astype(jnp.bfloat16), 'shard', scatter_dime...  65 us
  transfers between devices with their start and end apart: 46, of which 30 were waited for; matrix products, arithmetic and copies ran while one was open for 15% of the time, Pallas kernels for 0%

commit v1 on v0

v1 whole, which is shorter than its diff:
```python
import jax
import jax.numpy as jnp
from jax import lax
from jax.experimental import pallas as pl
from jax.experimental.pallas import tpu as pltpu
from jax.sharding import PartitionSpec as P

D = 1024
H = 16
HD = 64
SEQ = 2048
PAIR = 2 * HD

EPS = 1e-05
NEGATIVE = -1e30
SCALE = HD**-0.5
BLOCK = 512


def norm_apply(rows, gain, shift):
    mean_rows = jnp.mean(rows, axis=-1, keepdims=True)
    centered = rows - mean_rows
    inverse = lax.rsqrt(jnp.mean(centered * centered, axis=-1, keepdims=True) + EPS)
    return centered * inverse * gain + shift


def gelu_apply(values):
    return jax.nn.gelu(values, approximate=True)


def column_sums(rows):
    return jnp.sum(rows, axis=0, dtype=jnp.float32)


def low(values):
    return values.astype(jnp.bfloat16)


def dot(left, right):
    return jnp.dot(left, right, preferred_element_type=jnp.float32)


def dot_nt(left, right):
    return lax.dot_general(left, right, (((1,), (1,)), ((), ())), preferred_element_type=jnp.float32)


def dot_tn(left, right):
    return lax.dot_general(left, right, (((0,), (0,)), ((), ())), preferred_element_type=jnp.float32)


def head_halves(rows, scale=None):
    lane = lax.broadcasted_iota(jnp.int32, rows.shape, 1)
    if scale is not None:
        rows = rows * jnp.asarray(scale, rows.dtype)
    zero = jnp.zeros_like(rows)
    return jnp.where(lane < HD, rows, zero), jnp.where(lane < HD, zero, rows)


def self_forward_kernel(ends, q_ref, k_ref, v_ref, seg_col, seg_row, low_ref, full_ref, lse_ref):
    step = pl.program_id(0)
    rows = q_ref.shape[0]
    queries = head_halves(q_ref[...], SCALE)
    query_seg = seg_col[...]
    last_seg = ends[1, step]

    def piece(index, state, masked, diagonal):
        keys = k_ref[pl.ds(index * rows, rows), :]
        values = v_ref[pl.ds(index * rows, rows), :]
        keep = None
        if masked:
            keep = seg_row[:, pl.ds(index * rows, rows)] == query_seg
            if diagonal:
                key_pos = lax.broadcasted_iota(jnp.int32, (rows, rows), 1)
                query_pos = lax.broadcasted_iota(jnp.int32, (rows, rows), 0)
                keep = keep & (key_pos <= query_pos)
        after = []
        for head in range(2):
            top, total, acc = state[head]
            scores = dot_nt(queries[head], keys)
            if masked:
                scores = jnp.where(keep, scores, NEGATIVE)
            top_new = jnp.maximum(top, jnp.max(scores, axis=1, keepdims=True))
            expo = jnp.exp(scores - top_new)
            fade = jnp.exp(top - top_new)
            after.append(
                (
                    top_new,
                    total * fade + jnp.sum(expo, axis=1, keepdims=True),
                    acc * fade + dot(low(expo), values),
                )
            )
        return tuple(after)

    def before(index, state):
        return lax.cond(
            ends[0, index] == last_seg,
            lambda s: piece(index, s, False, False),
            lambda s: piece(index, s, True, False),
            state,
        )

    blank = (
        jnp.full((rows, 1), NEGATIVE, jnp.float32),
        jnp.zeros((rows, 1), jnp.float32),
        jnp.zeros((rows, PAIR), jnp.float32),
    )
    state = lax.fori_loop(0, step, before, (blank, blank))
    state = piece(step, state, True, True)
    lane = lax.broadcasted_iota(jnp.int32, (rows, PAIR), 1)
    joined = jnp.where(lane < HD, state[0][2] / state[0][1], state[1][2] / state[1][1])
    full_ref[...] = joined
    low_ref[...] = low(joined)
    lse_ref[:, 0:1] = state[0][0] + jnp.log(state[0][1])
    lse_ref[:, 1:2] = state[1][0] + jnp.log(state[1][1])


def block_ends(segments, rows):
    return jnp.stack([segments[::rows], segments[rows - 1 :: rows]])


def self_forward(qkv, segments):
    count = qkv.shape[0]
    rows = BLOCK
    col = segments[:, None]
    row = segments[None, :]
    grid_spec = pltpu.PrefetchScalarGridSpec(
        num_scalar_prefetch=1,
        grid=(count // rows,),
        in_specs=[
            pl.BlockSpec((rows, PAIR), lambda i, e: (i, 0)),
            pl.BlockSpec((count, PAIR), lambda i, e: (0, 1)),
            pl.BlockSpec((count, PAIR), lambda i, e: (0, 2)),
            pl.BlockSpec((rows, 1), lambda i, e: (i, 0)),
            pl.BlockSpec((1, count), lambda i, e: (0, 0)),
        ],
        out_specs=[
            pl.BlockSpec((rows, PAIR), lambda i, e: (i, 0)),
            pl.BlockSpec((rows, PAIR), lambda i, e: (i, 0)),
            pl.BlockSpec((rows, 2), lambda i, e: (i, 0)),
        ],
    )
    return pl.pallas_call(
        self_forward_kernel,
        grid_spec=grid_spec,
        out_shape=(
            jax.ShapeDtypeStruct((count, PAIR), jnp.bfloat16),
            jax.ShapeDtypeStruct((count, PAIR), jnp.float32),
            jax.ShapeDtypeStruct((count, 2), jnp.float32),
        ),
        compiler_params=pltpu.CompilerParams(vmem_limit_bytes=40 * 2**20),
        cost_estimate=pl.CostEstimate(
            flops=4 * count * count * PAIR, bytes_accessed=8 * count * PAIR, transcendentals=count * count
        ),
    )(block_ends(segments, rows), qkv, qkv, qkv, col, row)


def self_backward_kernel(
    ends, q_ref, k_ref, v_ref, go_ref, lse_ref, delta_ref, seg_col, seg_row, grad_ref, acc_q, acc_k, acc_v
):
    step = pl.program_id(0)
    blocks = pl.num_programs(0)
    rows = k_ref.shape[0]

    @pl.when(step == 0)
    def _():
        acc_q[...] = jnp.zeros_like(acc_q)

    keys = k_ref[...]
    values = v_ref[...]
    key_halves = head_halves(keys, SCALE)
    key_seg = seg_col[...]
    first_seg = ends[0, step]

    def piece(index, masked, diagonal):
        place = pl.ds(pl.multiple_of(index * rows, rows), rows)
        queries = head_halves(q_ref[place, :], SCALE)
        grads = head_halves(go_ref[place, :])
        keep = None
        if masked:
            keep = seg_row[:, place] == key_seg
            if diagonal:
                key_pos = lax.broadcasted_iota(jnp.int32, (rows, rows), 0)
                query_pos = lax.broadcasted_iota(jnp.int32, (rows, rows), 1)
                keep = keep & (key_pos <= query_pos)
        sum_q = sum_k = sum_v = None
        for head in range(2):
            scores = dot_nt(keys, queries[head])
            probs = jnp.exp(scores - lse_ref[head : head + 1, place])
            if masked:
                probs = jnp.where(keep, probs, 0.0)
            part_v = dot(low(probs), grads[head])
            grad_probs = dot_nt(values, grads[head])
            grad_scores = low(probs * (grad_probs - delta_ref[head : head + 1, place]))
            part_k = dot(grad_scores, queries[head])
            part_q = dot_tn(grad_scores, key_halves[head])
            sum_q = part_q if sum_q is None else sum_q + part_q
            sum_k = part_k if sum_k is None else sum_k + part_k
            sum_v = part_v if sum_v is None else sum_v + part_v
        acc_q[place, :] += sum_q
        if diagonal:
            acc_k[...] = sum_k
            acc_v[...] = sum_v
        else:
            acc_k[...] += sum_k
            acc_v[...] += sum_v

    piece(step, True, True)

    @pl.loop(step + 1, blocks)
    def _(index):
        whole = ends[1, index] == first_seg

        @pl.when(whole)
        def _():
            piece(index, False, False)

        @pl.when(jnp.logical_not(whole))
        def _():
            piece(index, True, False)

    own = pl.ds(pl.multiple_of(step * rows, rows), rows)
    grad_ref[own, 0:PAIR] = low(acc_q[own, :])
    grad_ref[own, PAIR : 2 * PAIR] = low(acc_k[...])
    grad_ref[own, 2 * PAIR : 3 * PAIR] = low(acc_v[...])


def self_backward(qkv, grad_att, lse, delta, segments):
    count = qkv.shape[0]
    rows = BLOCK
    col = segments[:, None]
    row = segments[None, :]
    whole = lambda i, e: (0, 0)
    grid_spec = pltpu.PrefetchScalarGridSpec(
        num_scalar_prefetch=1,
        grid=(count // rows,),
        in_specs=[
            pl.BlockSpec((count, PAIR), whole),
            pl.BlockSpec((rows, PAIR), lambda i, e: (i, 1)),
            pl.BlockSpec((rows, PAIR), lambda i, e: (i, 2)),
            pl.BlockSpec((count, PAIR), whole),
            pl.BlockSpec((2, count), whole),
            pl.BlockSpec((2, count), whole),
            pl.BlockSpec((rows, 1), lambda i, e: (i, 0)),
            pl.BlockSpec((1, count), whole),
        ],
        out_specs=pl.BlockSpec((count, 3 * PAIR), whole),
        scratch_shapes=[
            pltpu.VMEM((count, PAIR), jnp.float32),
            pltpu.VMEM((rows, PAIR), jnp.float32),
            pltpu.VMEM((rows, PAIR), jnp.float32),
        ],
    )
    return pl.pallas_call(
        self_backward_kernel,
        grid_spec=grid_spec,
        out_shape=jax.ShapeDtypeStruct((count, 3 * PAIR), jnp.bfloat16),
        compiler_params=pltpu.CompilerParams(vmem_limit_bytes=40 * 2**20),
        cost_estimate=pl.CostEstimate(
            flops=10 * count * count * PAIR, bytes_accessed=14 * count * PAIR, transcendentals=count * count
        ),
    )(block_ends(segments, rows), qkv, qkv, qkv, grad_att, lse, delta, col, row)


def cross_forward_kernel(length, q_ref, m_ref, out_ref):
    queries = head_halves(q_ref[...], SCALE)
    keys = m_ref[:, :PAIR]
    values = m_ref[:, PAIR:]
    shape = (q_ref.shape[0], m_ref.shape[0])
    keep = lax.broadcasted_iota(jnp.int32, shape, 1) < length[0]
    parts = []
    for head in range(2):
        scores = jnp.where(keep, dot_nt(queries[head], keys), NEGATIVE)
        expo = jnp.exp(scores - jnp.max(scores, axis=1, keepdims=True))
        parts.append(dot(low(expo), values) / jnp.sum(expo, axis=1, keepdims=True))
    lane = lax.broadcasted_iota(jnp.int32, parts[0].shape, 1)
    out_ref[...] = low(jnp.where(lane < HD, parts[0], parts[1]))


def cross_forward(queries, memory, length):
    count, states = queries.shape[0], memory.shape[0]
    grid_spec = pltpu.PrefetchScalarGridSpec(
        num_scalar_prefetch=1,
        grid=(D // PAIR,),
        in_specs=[
            pl.BlockSpec((count, PAIR), lambda i, e: (0, i)),
            pl.BlockSpec((states, 2 * PAIR), lambda i, e: (0, i)),
        ],
        out_specs=pl.BlockSpec((count, PAIR), lambda i, e: (0, i)),
    )
    return pl.pallas_call(
        cross_forward_kernel,
        grid_spec=grid_spec,
        out_shape=jax.ShapeDtypeStruct((count, D), jnp.bfloat16),
        cost_estimate=pl.CostEstimate(
            flops=8 * count * states * D, bytes_accessed=4 * count * D + 4 * states * D, transcendentals=count * states * H
        ),
    )(length, queries, memory)


def cross_backward_kernel(length, q_ref, m_ref, g_ref, dq_ref, dm_ref):
    queries = head_halves(q_ref[...], SCALE)
    grads = head_halves(g_ref[...])
    keys = m_ref[:, :PAIR]
    values = m_ref[:, PAIR:]
    key_halves = head_halves(keys, SCALE)
    shape = (m_ref.shape[0], q_ref.shape[0])
    keep = lax.broadcasted_iota(jnp.int32, shape, 0) < length[0]
    sum_q = sum_k = sum_v = None
    for head in range(2):
        scores = jnp.where(keep, dot_nt(keys, queries[head]), NEGATIVE)
        expo = jnp.exp(scores - jnp.max(scores, axis=0, keepdims=True))
        probs = expo * (1.0 / jnp.sum(expo, axis=0, keepdims=True))
        part_v = dot(low(probs), grads[head])
        grad_probs = dot_nt(values, grads[head])
        inner = jnp.sum(probs * grad_probs, axis=0, keepdims=True)
        grad_scores = low(probs * (grad_probs - inner))
        part_k = dot(grad_scores, queries[head])
        part_q = dot_tn(grad_scores, key_halves[head])
        sum_q = part_q if sum_q is None else sum_q + part_q
        sum_k = part_k if sum_k is None else sum_k + part_k
        sum_v = part_v if sum_v is None else sum_v + part_v
    dq_ref[...] = low(sum_q)
    dm_ref[:, :PAIR] = low(sum_k)
    dm_ref[:, PAIR:] = low(sum_v)


def cross_backward(queries, memory, grads, length):
    count, states = queries.shape[0], memory.shape[0]
    grid_spec = pltpu.PrefetchScalarGridSpec(
        num_scalar_prefetch=1,
        grid=(D // PAIR,),
        in_specs=[
            pl.BlockSpec((count, PAIR), lambda i, e: (0, i)),
            pl.BlockSpec((states, 2 * PAIR), lambda i, e: (0, i)),
            pl.BlockSpec((count, PAIR), lambda i, e: (0, i)),
        ],
        out_specs=[
            pl.BlockSpec((count, PAIR), lambda i, e: (0, i)),
            pl.BlockSpec((states, 2 * PAIR), lambda i, e: (0, i)),
        ],
    )
    return pl.pallas_call(
        cross_backward_kernel,
        grid_spec=grid_spec,
        out_shape=(
            jax.ShapeDtypeStruct((count, D), jnp.bfloat16),
            jax.ShapeDtypeStruct((states, 2 * D), jnp.bfloat16),
        ),
        cost_estimate=pl.CostEstimate(
            flops=20 * count * states * D, bytes_accessed=6 * count * D + 8 * states * D, transcendentals=count * states * H
        ),
    )(length, queries, memory, grads)


def shards(
    tokens,
    segments,
    enc_states,
    enc_lengths,
    cotangent,
    self_qkv,
    self_out,
    cross_query,
    cross_memory,
    cross_out,
    expand_weight,
    shrink_weight,
    norm_gain,
    norm_bias,
    proj_bias,
    expand_bias,
):
    row_count = tokens.shape[0]
    span = SEQ // row_count
    width = D // span
    count = lax.axis_size("shard")
    shard_pos = lax.axis_index("shard")
    local_pos = shard_pos % span
    local_seq = shard_pos // span
    groups = None
    if count != span:
        groups = [[g * span + i for i in range(span)] for g in range(count // span)]
    weight_rows = self_qkv.shape[0]
    hidden = expand_bias.shape[0]

    def gather(value, groups=None):
        return lax.all_gather(value, "shard", axis=0, tiled=True, axis_index_groups=groups)

    def scatter(value, groups=None):
        return lax.psum_scatter(value, "shard", scatter_dimension=0, tiled=True, axis_index_groups=groups)

    def swap(value):
        return lax.all_to_all(value, "shard", 0, 0, tiled=True)

    tokens_all = gather(tokens, groups)
    blocks = self_qkv.reshape(weight_rows, 3, span, width).transpose(2, 0, 1, 3)
    blocks = jnp.tile(blocks.reshape(span, weight_rows, 3 * width), (count // span, 1, 1))
    qkv_weight = swap(blocks).reshape(D, 3 * width)
    small = jnp.concatenate([norm_gain, norm_bias, proj_bias], axis=0)
    small_all = lax.all_gather(small, "shard", axis=1, tiled=True).astype(jnp.float32)
    gain_rows, shift_rows, bias_rows = small_all[:3], small_all[3:6], small_all[6:]
    memory_weight = cross_memory.reshape(weight_rows, 2, span, width).transpose(0, 2, 1, 3)
    memory_weight = memory_weight.reshape(weight_rows, 2 * D)
    pack = gather(jnp.concatenate([self_out, cross_query, cross_out, memory_weight], axis=1))
    attn_proj, query_in, cross_proj = pack[:, :D], pack[:, D : 2 * D], pack[:, 2 * D : 3 * D]
    memory_in = pack[:, 3 * D :]
    expand_local = swap(expand_weight.reshape(weight_rows, count, hidden).transpose(1, 0, 2)).reshape(D, hidden)

    seq_segments = lax.dynamic_slice_in_dim(segments, local_seq * SEQ, SEQ)
    x_all = tokens_all.astype(jnp.float32)
    input_one_all = low(norm_apply(x_all, gain_rows[0], shift_rows[0]))
    own_bias = lax.dynamic_slice_in_dim(bias_rows[:2], local_pos * width, width, axis=1)
    qkv_bias = jnp.concatenate([own_bias[0], jnp.zeros((width,), jnp.float32), own_bias[1]])
    qkv = low(dot(input_one_all, qkv_weight) + qkv_bias)
    att_low, att_full, lse = self_forward(qkv, seq_segments)
    attended = lax.all_to_all(att_low, "shard", 0, 1, tiled=True, axis_index_groups=groups)

    pair_bias = bias_rows[4].reshape(span, width)
    pair_bias = jnp.stack([jnp.zeros_like(pair_bias), pair_bias], axis=1).reshape(2 * D)
    memory_own = low(dot(enc_states, memory_in) + pair_bias)
    memory_all = gather(memory_own, groups)
    enc_count = lax.dynamic_slice_in_dim(enc_lengths, local_seq, 1)

    residual_in = tokens.astype(jnp.float32)
    hidden_one = residual_in + dot(attended, attn_proj) + bias_rows[2]
    input_two = low(norm_apply(hidden_one, gain_rows[1], shift_rows[1]))
    cross_q = low(dot(input_two, query_in) + bias_rows[3])
    context = cross_forward(cross_q, memory_all, enc_count)
    hidden_two = hidden_one + dot(context, cross_proj) + bias_rows[5]
    input_three = low(norm_apply(hidden_two, gain_rows[2], shift_rows[2]))

    grad_all = gather(cotangent)
    input_three_all = gather(input_three)
    pre_act = dot(input_three_all, expand_local) + expand_bias.astype(jnp.float32)
    act = low(gelu_apply(pre_act))
    grad_act = dot_nt(grad_all, shrink_weight)
    grad_pre = low(jax.vjp(gelu_apply, pre_act)[1](grad_act)[0])
    grad_in_three = scatter(low(dot_nt(grad_pre, expand_local))).astype(jnp.float32)
    result = hidden_two + scatter(low(dot(act, shrink_weight))).astype(jnp.float32) + bias_rows[6]
    grad_shrink = dot_tn(act, grad_all)
    grad_expand = dot_tn(input_three_all, grad_pre)
    grad_hidden_bias = column_sums(grad_pre)

    grad_out = cotangent.astype(jnp.float32)
    norm_three = jax.vjp(norm_apply, hidden_two, gain_rows[2], shift_rows[2])[1](grad_in_three)
    grad_two = grad_out + norm_three[0]
    grad_two_low = low(grad_two)
    grad_cross_proj = dot_tn(context, grad_two_low)
    grad_context = low(dot_nt(grad_two_low, cross_proj))
    grad_cross_q, memory_part = cross_backward(cross_q, memory_all, grad_context, enc_count)
    mem_grads = scatter(memory_part, groups)
    grad_memory = dot_tn(enc_states, mem_grads)
    grad_enc = dot_nt(mem_grads, memory_in)
    grad_query_in = dot_tn(input_two, grad_cross_q)
    grad_in_two = dot_nt(grad_cross_q, query_in)
    norm_two = jax.vjp(norm_apply, hidden_one, gain_rows[1], shift_rows[1])[1](grad_in_two)
    grad_one = grad_two + norm_two[0]
    grad_one_low = low(grad_one)
    grad_attn_proj = dot_tn(attended, grad_one_low)
    grad_attn = low(dot_nt(grad_one_low, attn_proj))

    grad_att_heads = lax.all_to_all(grad_attn, "shard", 1, 0, tiled=True, axis_index_groups=groups)
    delta = jnp.sum((grad_att_heads.astype(jnp.float32) * att_full).reshape(SEQ, 2, HD), axis=-1).T
    grad_qkv = self_backward(qkv, grad_att_heads, lse.T, delta, seq_segments)
    grad_in_one = scatter(low(dot_nt(grad_qkv, qkv_weight)), groups).astype(jnp.float32)
    grad_attn_in = low(dot_tn(input_one_all, grad_qkv))
    norm_one = jax.vjp(norm_apply, residual_in, gain_rows[0], shift_rows[0])[1](grad_in_one)
    grad_tokens = grad_one + norm_one[0]

    qkv_sums = column_sums(grad_qkv)
    zero_row = jnp.zeros((D,), jnp.float32)
    bias_zero = lax.dynamic_update_slice_in_dim(zero_row, qkv_sums[:width], local_pos * width, 0)
    bias_one = lax.dynamic_update_slice_in_dim(zero_row, qkv_sums[2 * width :], local_pos * width, 0)
    memory_sums = column_sums(mem_grads).reshape(span, 2, width)[:, 1].reshape(D)
    small_grads = jnp.stack(
        [
            norm_one[1],
            norm_two[1],
            norm_three[1],
            norm_one[2],
            norm_two[2],
            norm_three[2],
            bias_zero,
            bias_one,
            column_sums(grad_one_low),
            column_sums(grad_cross_q),
            memory_sums,
            column_sums(grad_two_low),
            column_sums(cotangent),
        ]
    )
    small_count = small_grads.shape[0]
    shard_width = D // count
    pack_width = 5 * D
    extra = 8
    small_rows = low(small_grads).reshape(small_count, count, shard_width).transpose(1, 0, 2)
    small_rows = small_rows.reshape(count, small_count * shard_width)
    small_rows = jnp.pad(small_rows, ((0, 0), (0, extra * pack_width - small_count * shard_width)))
    small_rows = small_rows.reshape(count, extra, pack_width)
    grad_pack = low(jnp.concatenate([grad_attn_proj, grad_query_in, grad_cross_proj, grad_memory], axis=1))
    grad_pack = jnp.concatenate([grad_pack.reshape(count, weight_rows, pack_width), small_rows], axis=1)
    owned_pack = scatter(grad_pack.reshape(count * (weight_rows + extra), pack_width))
    owned_qkv = swap(grad_attn_in.reshape(count, weight_rows, 3 * width))
    owned_qkv = owned_qkv.astype(jnp.float32).reshape(count // span, span, weight_rows, 3 * width)
    owned_qkv = low(jnp.sum(owned_qkv, axis=0))
    owned_expand = swap(low(grad_expand).reshape(count, weight_rows, hidden))
    total_shrink, total_hidden_bias = lax.psum((low(grad_shrink), low(grad_hidden_bias)), "rep")
    total_expand = lax.psum(owned_expand, "rep")
    total_pack, total_qkv = lax.psum((owned_pack, owned_qkv), "rep")
    total_expand = total_expand.transpose(1, 0, 2).reshape(weight_rows, count * hidden)
    total_qkv = total_qkv.reshape(span, weight_rows, 3, width).transpose(1, 2, 0, 3)
    total_qkv = total_qkv.reshape(weight_rows, 3 * D)
    total_memory = total_pack[:weight_rows, 3 * D :].reshape(weight_rows, span, 2, width)
    total_memory = total_memory.transpose(0, 2, 1, 3).reshape(weight_rows, 2 * D)
    total_small = total_pack[weight_rows:].reshape(-1)[: small_count * shard_width]
    total_small = total_small.reshape(small_count, shard_width)

    def wide(value):
        return value.astype(jnp.float32)

    return (
        low(result),
        grad_tokens,
        grad_enc,
        wide(total_qkv),
        wide(total_pack[:weight_rows, :D]),
        wide(total_pack[:weight_rows, D : 2 * D]),
        wide(total_memory),
        wide(total_pack[:weight_rows, 2 * D : 3 * D]),
        wide(total_expand),
        wide(total_shrink),
        wide(total_small[:3]),
        wide(total_small[3:6]),
        wide(total_small[6:]),
        wide(total_hidden_bias),
    )


def solution(mesh):
    return jax.shard_map(
        shards,
        mesh=mesh,
        in_specs=(
            P(("rep", "shard"), None),
            P("rep"),
            P(("rep", "shard"), None),
            P("rep"),
            P(("rep", "shard"), None),
            P("shard", None),
            P("shard", None),
            P("shard", None),
            P("shard", None),
            P("shard", None),
            P("shard", None),
            P("shard", None),
            P(None, "shard"),
            P(None, "shard"),
            P(None, "shard"),
            P("shard"),
        ),
        out_specs=(
            P(("rep", "shard"), None),
            P(("rep", "shard"), None),
            P(("rep", "shard"), None),
            P("shard", None),
            P("shard", None),
            P("shard", None),
            P("shard", None),
            P("shard", None),
            P("shard", None),
            P("shard", None),
            P(None, "shard"),
            P(None, "shard"),
            P(None, "shard"),
            P("shard"),
        ),
        check_vma=False,
    )
```

time: 1820 us -> 1000 us (0.55)
  waiting for transfers between devices: 1030 us -> 612 us
  starting transfers between devices: 275 us -> 44.5 us
  matrix products: 205 us -> 113 us
  Pallas kernels: 0 us -> 60.9 us
  blocking collectives: 110 us -> 53.4 us
  local copies, waits for them, and re-layouts: 86 us -> 45 us
  loops' own time: 19.6 us -> 0 us
    ppermute x28 -> x0, waiting for transfers between devices: 330 us -> none  [the longest x14 177 us: from_behind(): lax.ppermute(value, axis, [(source, source + steps) for source in range(i...]
    ppermute x28 -> x0, starting transfers between devices: 274 us -> none  [the longest x14 171 us: from_behind(): lax.ppermute(value, axis, [(source, source + steps) for source in range(i...]
    reduce_scatter x6 -> x5, waiting for transfers between devices: 403 us -> 152 us  [scatter(): lax.psum_scatter(value, 'shard', scatter_dimension=0, tiled=True, axis_in...]
    all_to_all x0 -> x6, waiting for transfers between devices: none -> 195 us  [the longest x4 165 us: swap(): return lax.all_to_all(value, 'shard', 0, 0, tiled=True)]
    dot_general x47 -> x21, matrix products: 197 us -> 113 us  [the longest x7 39.2 us: dot_tn(): lax.dot_general(left, right, (((0,), (0,)), ((), ())), preferred_element_...]
    pallas_call x0 -> x4, Pallas kernels: none -> 60.9 us  [the longest x1 19.1 us: self_backward(): pl.pallas_call(self_backward_kernel, grid_spec=grid_spec, out_shape=jax.S...]
    unnamed x22 -> x11, waiting for transfers between devices: 49.1 us -> 1.36 us
    all_to_all x0 -> x6, starting transfers between devices: none -> 43.3 us  [the longest x4 28.6 us: swap(): return lax.all_to_all(value, 'shard', 0, 0, tiled=True)]
  transfers between devices with their start and end apart: 46 -> 17, of which waited for: 30 -> 13; matrix products, arithmetic and copies ran while one was open for 15% -> 13% of each run, Pallas kernels for 0% -> 4%
where the time goes in v1:
time: 1000 us; the launch traced here: 992 us
  waiting for transfers between devices  612 us (61%)
  matrix products  113 us (11%)
  Pallas kernels  60.9 us (6%)
  blocking collectives  53.4 us (5%)
  other arithmetic  48.1 us (5%)
  local copies, waits for them, and re-layouts  45 us (4%)
  starting transfers between devices  44.5 us (4%)
  between operations  15.4 us (2%)
    all_to_all x4, waiting for transfers between devices, swap(): return lax.all_to_all(value, 'shard', 0, 0, tiled=True)  165 us
    reduce_scatter x5, waiting for transfers between devices, scatter(): lax.psum_scatter(value, 'shard', scatter_dimension=0, tiled=True, axis_in...  152 us
    psum x1, waiting for transfers between devices, shards(): total_pack, total_qkv = lax.psum((owned_pack, owned_qkv), 'rep')  136 us
    all_gather x5, waiting for transfers between devices, gather(): lax.all_gather(value, 'shard', axis=0, tiled=True, axis_index_groups=groups)  128 us
    all_gather x1, blocking collectives, shards(): lax.all_gather(small, 'shard', axis=1, tiled=True).astype(jnp.float32)  44.3 us
    dot_general x7, matrix products, dot_tn(): lax.dot_general(left, right, (((0,), (0,)), ((), ())), preferred_element_...  39.2 us
    dot_general x7, matrix products, dot(): return jnp.dot(left, right, preferred_element_type=jnp.float32)  37.5 us
    dot_general x7, matrix products, dot_nt(): lax.dot_general(left, right, (((1,), (1,)), ((), ())), preferred_element_...  35.8 us
  transfers between devices with their start and end apart: 17, of which 13 were waited for; matrix products, arithmetic and copies ran while one was open for 13% of the time, Pallas kernels for 4%

profile of v1, /device:TPU:12, one launch (start us, length us, event | category | flops | bytes accessed | tf_op | source)
XLA Modules:
  0.0 991.7 jit_solution(10670196660414916926)
XLA Ops:
  21.9 44.3 %all_gather.19 = bf16[13,1024]{1,0:T(8,128)(2,1)S(1)} all-gather(bf16[13,128]{1,0:T(8,128)(2,1)S(1)} %pad_maximum_fusion.2), channel_id=1, replica_groups=mesh['rep'=4,'shard'=8] {'shard'}, dimensions={1}, use_global_device_ids=true | all-gather | bytes 29952 | tf_op jit(solution)/shard_map/all_gather | solution.py:400
  75.9 96.9 %all-gather.8.cloned.1.call-done = bf16[1024,5120]{0,1:T(8,128)(2,1)} async-done(((bf16[128,5120]{0,1:T(8,128)(2,1)}), bf16[1024,5120]{0,1:T(8,128)(2,1)}) %all-gather.8.cloned.1.call-update) | async-done | bytes 10485776 | tf_op jit(solution)/shard_map/all_gather | solution.py:387
  183.0 18.5 %shard_map.263 = (bf16[2048,128]{1,0:T(8,128)(2,1)S(1)}, f32[2048,128]{1,0:T(8,128)S(1)}, f32[2048,2]{1,0:T(8,128)S(1)}) custom-call(s32[2,4]{1,0:T(2,128)S(1)} %pad_add_fusion.ends, bf16[2048,384]{1,0:T(8,128)(2,1)S(1)} %add_convert_fusion.q_ref.k_ref.v_ref, bf16[2048,384]{1,0:T(8,128)(2,1)S(1)} %add_convert_fusion.q_ref.k_ref.v_ref, ...), custom_call_target="tpu_custom_call" | custom-call | flops 2147483648 | bytes 2097152 | tf_op jit(solution)/shard_map/pallas_call | solution.py:142
  214.5 11.4 %all-to-all-done.1 = bf16[8,256,128]{1,2,0:T(8,128)(2,1)} async-done(((bf16[8,256,128]{1,2,0:T(8,128)(2,1)}), bf16[8,256,128]{1,2,0:T(8,128)(2,1)}, u32[]{:S(2)}, u32[]{:S(2)}) %all-to-all-start.1) | async-done | bytes 524320 | tf_op jit(solution)/shard_map/all_to_all | solution.py:416
  232.7 8.6 shard_map.264
  258.3 76.7 %all-to-all-done.2 = bf16[8,128,1024]{1,2,0:T(8,128)(2,1)} async-done(((bf16[8,128,1024]{1,2,0:T(8,128)(2,1)}), bf16[8,128,1024]{1,2,0:T(8,128)(2,1)}, u32[]{:S(2)}, u32[]{:S(2)}) %all-to-all-start.2) | async-done | bytes 2097184 | tf_op jit(solution)/shard_map/all_to_all | solution.py:393
  338.9 11.0 %fusion.94 = f32[2048,1024]{1,0:T(8,128)} fusion(bf16[2048,1024]{1,0:T(8,128)(2,1)} %all-gather.12.cloned.1.call-done, bf16[1024,1024]{1,0:T(8,128)(2,1)} %bitcast.171), kind=kOutput, calls=%fused_computation.158 | convolution fusion | flops 4294967296 | bytes 14680064 | tf_op jit(solution)/shard_map/dot_general | solution.py:40
  349.9 28.6 %all-gather.14.cloned.1.call-done = bf16[2048,1024]{1,0:T(8,128)(2,1)} async-done(((bf16[256,1024]{1,0:T(8,128)(2,1)}), bf16[2048,1024]{1,0:T(8,128)(2,1)}) %all-gather.14.cloned.1.call-update) | async-done | bytes 4194320 | tf_op jit(solution)/shard_map/all_gather | solution.py:387
  378.6 12.8 %fusion.85 = (bf16[1024]{0:T(1024)(128)(2,1)S(1)}, bf16[2048,1024]{1,0:T(8,128)(2,1)S(1)}) fusion(f32[2048,1024]{1,0:T(8,128)} %fusion.94, f32[1024]{0:T(1024)S(1)} %convert_element_type.180, bf16[2048,1024]{1,0:T(8,128)(2,1)} %all-gather.14.cloned.1.call-done, bf16[1024,1024]{1,0:T(8,128)(2,1)S(1)} %copy-done), kind=kOutput, calls=%fused_computation.151 | convolution fusion | flops 4341103616 | bytes 18880512 | tf_op jit(solution)/shard_map/dot_general | solution.py:44
  399.9 11.2 %convolution_convert_fusion.3 = bf16[2048,1024]{1,0:T(8,128)(2,1)} fusion(bf16[1024,1024]{1,0:T(8,128)(2,1)S(1)} %copy-done, f32[2048,1024]{1,0:T(8,128)} %fusion.94, f32[1024]{0:T(1024)S(1)} %convert_element_type.180), kind=kOutput, calls=%fused_computation.22 | convolution fusion | flops 4318035968 | bytes 14684160 | tf_op jit(solution)/shard_map/dot_general | solution.py:40
  411.1 35.5 %reduce-scatter.8.cloned.1.call-done = bf16[256,1024]{1,0:T(8,128)(2,1)} async-done(((bf16[2048,1024]{1,0:T(8,128)(2,1)}), bf16[256,1024]{1,0:T(8,128)(2,1)}) %reduce-scatter.8.cloned.1.call-update) | async-done | bytes 524304 | tf_op jit(solution)/shard_map/reduce_scatter | solution.py:390
  448.1 49.6 %reduce-scatter.6.cloned.1.call-done = bf16[256,1024]{1,0:T(8,128)(2,1)} async-done(((bf16[2048,1024]{1,0:T(8,128)(2,1)}), bf16[256,1024]{1,0:T(8,128)(2,1)}) %reduce-scatter.6.cloned.1.call-update) | async-done | bytes 524304 | tf_op jit(solution)/shard_map/reduce_scatter | solution.py:390
  505.7 14.6 %shard_map.265 = (bf16[256,1024]{1,0:T(8,128)(2,1)}, bf16[512,2048]{1,0:T(8,128)(2,1)}) custom-call(s32[1]{0:T(128)S(6)} %copy.101.length, bf16[256,1024]{1,0:T(8,128)(2,1)} %fusion.62.q_ref, bf16[512,2048]{1,0:T(8,128)(2,1)} %all-gather.10.cloned.1.call-done.m_ref, bf16[256,1024]{1,0:T(8,128)(2,1)} %fusion.59.g_ref), custom_call_target="tpu_custom_call" | custom-call | flops 2684354560 | bytes 5767168 | tf_op jit(solution)/shard_map/pallas_call | solution.py:342
  537.0 18.2 %all-to-all-done.3 = bf16[256,8,128]{2,0,1:T(8,128)(2,1)S(1)} async-done(((bf16[256,8,128]{2,0,1:T(8,128)(2,1)}), bf16[256,8,128]{2,0,1:T(8,128)(2,1)S(1)}, u32[]{:S(2)}, u32[]{:S(2)}) %all-to-all-start.3) | async-done | bytes 524320 | tf_op jit(solution)/shard_map/all_to_all | solution.py:462
  559.3 19.1 %shard_map.266 = bf16[2048,384]{1,0:T(8,128)(2,1)S(1)} custom-call(s32[2,4]{1,0:T(2,128)S(1)} %pad_add_fusion.ends, bf16[2048,384]{1,0:T(8,128)(2,1)S(1)} %copy-done.8, bf16[2048,384]{1,0:T(8,128)(2,1)S(1)} %copy-done.8, bf16[2048,384]{1,0:T(8,128)(2,1)S(1)} %copy-done.8, bf16[2048,128]{1,0:T(8,128)(2,1)S(1)} %bitcast.150, f32[2,2048]{1,0:T(2,128)S(1)} %bitcast.152, ...), custom_call_target="tpu_custom_call" | custom-call | flops 5368709120 | bytes 3670016 | tf_op jit(solution)/shard_map/pallas_call | solution.py:253
  601.1 30.7 %reduce-scatter.10.cloned.1.call-done = bf16[256,1024]{1,0:T(8,128)(2,1)} async-done(((bf16[2048,1024]{1,0:T(8,128)(2,1)}), bf16[256,1024]{1,0:T(8,128)(2,1)}) %reduce-scatter.10.cloned.1.call-update) | async-done | bytes 524304 | tf_op jit(solution)/shard_map/reduce_scatter | solution.py:390
  636.6 10.6 %pad_maximum_fusion = bf16[8,136,5120]{2,1,0:T(8,128)(2,1)} fusion(bf16[8,8,5120]{2,1,0:T(8,128)(2,1)S(1)} %bitcast.168, bf16[8,128,2048]{2,1,0:T(8,128)(2,1)} %bitcast.158, bf16[8,128,1024]{2,1,0:T(8,128)(2,1)} %bitcast.161, bf16[8,128,1024]{2,1,0:T(8,128)(2,1)} %bitcast.162, bf16[8,128,1024]{2,1,0:T(8,128)(2,1)} %convolution_convert_fusion.8), kind=kLoop, calls=%fused_computation.2 | loop fusion | flops 55705600 | bytes 22282240 | tf_op jit(solution)/shard_map/concatenate | solution.py:501
  647.2 9.4 convolution_convert_fusion.5
  670.7 73.3 %all-to-all-done.5 = bf16[8,128,1024]{2,1,0:T(8,128)(2,1)} async-done(((bf16[8,128,1024]{2,1,0:T(8,128)(2,1)}), bf16[8,128,1024]{2,1,0:T(8,128)(2,1)}, u32[]{:S(2)}, u32[]{:S(2)}) %all-to-all-start.5) | async-done | bytes 2097184 | tf_op jit(solution)/shard_map/all_to_all | solution.py:393
  751.5 12.0 %convolution_convert_fusion.4 = bf16[1024,1024]{1,0:T(8,128)(2,1)} fusion(bf16[2048,1024]{1,0:T(8,128)(2,1)} %all-gather.14.cloned.1.call-done, f32[2048,1024]{1,0:T(8,128)} %fusion.94, f32[1024]{0:T(1024)S(1)} %convert_element_type.180), kind=kOutput, calls=%fused_computation.32 | convolution fusion | flops 4316987392 | bytes 14684160 | tf_op jit(solution)/shard_map/dot_general | solution.py:48
  766.7 15.0 %all-to-all-done.4 = bf16[8,128,384]{1,2,0:T(8,128)(2,1)S(1)} async-done(((bf16[8,128,384]{1,2,0:T(8,128)(2,1)}), bf16[8,128,384]{1,2,0:T(8,128)(2,1)S(1)}, u32[]{:S(2)}, u32[]{:S(2)}) %all-to-all-start.4) | async-done | bytes 786464 | tf_op jit(solution)/shard_map/all_to_all | solution.py:393
  782.7 36.1 %reduce-scatter.14.cloned.1.call-done = bf16[136,5120]{1,0:T(8,128)(2,1)} async-done(((bf16[1088,5120]{1,0:T(8,128)(2,1)}), bf16[136,5120]{1,0:T(8,128)(2,1)}) %reduce-scatter.14.cloned.1.call-update) | async-done | bytes 1392656 | tf_op jit(solution)/shard_map/reduce_scatter | solution.py:390
  818.8 9.1 psum.39
  833.6 136.5 %all-reduce.5.cloned.1.call-done = (bf16[128,3072]{0,1:T(8,128)(2,1)}, bf16[136,5120]{1,0:T(8,128)(2,1)}, bf16[128,8192]{1,0:T(8,128)(2,1)}, bf16[1024,1024]{1,0:T(8,128)(2,1)}) async-done(((bf16[128,3072]{0,1:T(8,128)(2,1)}, bf16[136,5120]{1,0:T(8,128)(2,1)}, bf16[128,8192]{1,0:T(8,128)(2,1)}, bf16[1024,1024]{1,0:T(8,128)(2,1)}), (bf16[128,3072]{0,1:T(8,128)(2,1)}, bf16[136,5120]{1,0:T(8,128)(2,1)}, ...) | async-done | bytes 6373392 | tf_op jit(solution)/shard_map/psum | solution.py:509
  (228 shorter events, 186.5 us)
Async XLA Ops:
  7.2 371.4 %copy-start = (bf16[1024,1024]{1,0:T(8,128)(2,1)S(1)}, bf16[1024,1024]{1,0:T(8,128)(2,1)}, u32[]{:S(2)}) copy-start(bf16[1024,1024]{1,0:T(8,128)(2,1)} %param.27) | copy-start | bytes 6291460
  7.2 63.9 %all-gather.6.cloned.1.call-start = ((), (), s32[]{:S(2)}) async-start(), calls=%async_computation.11 | async-start | bytes 4718592 | tf_op jit(solution)/shard_map/all_gather | solution.py:387
  7.9 164.9 %all-gather.8.cloned.1.call-start = ((), (), s32[]{:S(2)}) async-start(), calls=%async_computation.12 | async-start | bytes 11796480 | tf_op jit(solution)/shard_map/all_gather | solution.py:387
  16.4 50.4 %all-to-all-start = ((bf16[8,128,384]{1,2,0:T(8,128)(2,1)}), bf16[8,128,384]{1,2,0:T(8,128)(2,1)}, u32[]{:S(2)}, u32[]{:S(2)}) async-start(bf16[8,128,384]{1,2,0:T(8,128)(2,1)} %bitcast.6), calls=%async_computation | async-start | bytes 1572864 | tf_op jit(solution)/shard_map/all_to_all | solution.py:393
  21.7 211.0 %all-gather.10.cloned.1.call-start = ((), (), s32[]{:S(2)}) async-start(), calls=%async_computation.13 | async-start | bytes 2359296 | tf_op jit(solution)/shard_map/all_gather | solution.py:387
  71.1 101.8 %copy-start.32 = (bf16[64,1024]{1,0:T(8,128)(2,1)S(1)}, bf16[64,1024]{1,0:T(8,128)(2,1)}, u32[]{:S(2)}) copy-start(bf16[64,1024]{1,0:T(8,128)(2,1)} %param.18) | copy-start | bytes 393220
  206.3 19.6 %all-to-all-start.1 = ((bf16[8,256,128]{1,2,0:T(8,128)(2,1)}), bf16[8,256,128]{1,2,0:T(8,128)(2,1)}, u32[]{:S(2)}, u32[]{:S(2)}) async-start(bf16[8,256,128]{1,2,0:T(8,128)(2,1)} %copy.52), calls=%async_computation.1 | async-start | bytes 1048576 | tf_op jit(solution)/shard_map/all_to_all | solution.py:416
  213.6 125.3 %all-gather.12.cloned.1.call-start = ((), (), s32[]{:S(2)}) async-start(), calls=%async_computation.14 | async-start | bytes 4718592 | tf_op jit(solution)/shard_map/all_gather | solution.py:387
  246.2 132.4 %all-gather.14.cloned.1.call-start = ((), (), s32[]{:S(2)}) async-start(), calls=%async_computation.16 | async-start | bytes 4718592 | tf_op jit(solution)/shard_map/all_gather | solution.py:387
  250.9 84.2 %all-to-all-start.2 = ((bf16[8,128,1024]{1,2,0:T(8,128)(2,1)}), bf16[8,128,1024]{1,2,0:T(8,128)(2,1)}, u32[]{:S(2)}, u32[]{:S(2)}) async-start(bf16[8,128,1024]{1,2,0:T(8,128)(2,1)} %bitcast.160), calls=%async_computation.2 | async-start | bytes 4194304 | tf_op jit(solution)/shard_map/all_to_all | solution.py:393
  258.3 188.3 %reduce-scatter.8.cloned.1.call-start = ((), (), s32[]{:S(2)}) async-start(), calls=%async_computation.17 | async-start | bytes 4718592 | tf_op jit(solution)/shard_map/reduce_scatter | solution.py:390
  399.6 98.1 %reduce-scatter.6.cloned.1.call-start = ((), (), s32[]{:S(2)}) async-start(), calls=%async_computation.15 | async-start | bytes 4718592 | tf_op jit(solution)/shard_map/reduce_scatter | solution.py:390
  411.0 35.6 %copy-start.11 = (f32[256,1024]{1,0:T(8,128)S(1)}, f32[256,1024]{1,0:T(8,128)}, u32[]{:S(2)}) copy-start(f32[256,1024]{1,0:T(8,128)} %copy-done.10) | copy-start | bytes 3145732
  411.1 184.8 %reduce-scatter.12.cloned.1.call-start = ((), (), s32[]{:S(2)}) async-start(), calls=%async_computation.19 | async-start | bytes 2359296 | tf_op jit(solution)/shard_map/reduce_scatter | solution.py:390
  500.2 20.2 %copy-start.18 = (f32[256,1024]{1,0:T(8,128)}, f32[256,1024]{1,0:T(8,128)S(1)}, u32[]{:S(2)}) copy-start(f32[256,1024]{1,0:T(8,128)S(1)} %get-tuple-element.60) | copy-start | bytes 3145732
  524.1 31.1 %copy-start.3 = (f32[2048,128]{1,0:T(8,128)S(1)}, f32[2048,128]{1,0:T(8,128)}, u32[]{:S(2)}) copy-start(f32[2048,128]{1,0:T(8,128)} %copy-done.2) | copy-start | bytes 3145732
  527.7 27.4 %all-to-all-start.3 = ((bf16[256,8,128]{2,0,1:T(8,128)(2,1)}), bf16[256,8,128]{2,0,1:T(8,128)(2,1)S(1)}, u32[]{:S(2)}, u32[]{:S(2)}) async-start(bf16[256,8,128]{2,0,1:T(8,128)(2,1)} %bitcast.174), calls=%async_computation.5 | async-start | bytes 1048576 | tf_op jit(solution)/shard_map/all_to_all | solution.py:462
  535.0 96.8 %reduce-scatter.10.cloned.1.call-start = ((), (), s32[]{:S(2)}) async-start(), calls=%async_computation.18 | async-start | bytes 4718592 | tf_op jit(solution)/shard_map/reduce_scatter | solution.py:390
  559.3 19.2 %copy-start.30 = (bf16[8,128,384]{2,1,0:T(8,128)(2,1)S(1)}, bf16[8,128,384]{2,1,0:T(8,128)(2,1)}, u32[]{:S(2)}) copy-start(bf16[8,128,384]{2,1,0:T(8,128)(2,1)} %copy.50) | copy-start | bytes 2359300
  582.9 235.8 %reduce-scatter.14.cloned.1.call-start = ((), (), s32[]{:S(2)}) async-start(), calls=%async_computation.20 | async-start | bytes 12533760 | tf_op jit(solution)/shard_map/reduce_scatter | solution.py:390
  656.6 87.5 %all-to-all-start.5 = ((bf16[8,128,1024]{2,1,0:T(8,128)(2,1)}), bf16[8,128,1024]{2,1,0:T(8,128)(2,1)}, u32[]{:S(2)}, u32[]{:S(2)}) async-start(bf16[8,128,1024]{2,1,0:T(8,128)(2,1)} %bitcast.173), calls=%async_computation.10 | async-start | bytes 4194304 | tf_op jit(solution)/shard_map/all_to_all | solution.py:393
  744.1 37.7 %all-to-all-start.4 = ((bf16[8,128,384]{1,2,0:T(8,128)(2,1)}), bf16[8,128,384]{1,2,0:T(8,128)(2,1)S(1)}, u32[]{:S(2)}, u32[]{:S(2)}) async-start(bf16[8,128,384]{1,2,0:T(8,128)(2,1)} %copy.65), calls=%async_computation.8 | async-start | bytes 1572864 | tf_op jit(solution)/shard_map/all_to_all | solution.py:393
  751.5 218.5 %all-reduce.5.cloned.1.call-start = ((), (), s32[]{:S(2)}) async-start(), calls=%async_computation.21 | async-start | bytes 12746752 | tf_op jit(solution)/shard_map/psum | solution.py:509
  766.7 61.8 %copy-start.23 = (bf16[64,2048]{1,0:T(8,128)(2,1)S(1)}, bf16[64,2048]{1,0:T(8,128)(2,1)}, u32[]{:S(2)}) copy-start(bf16[64,2048]{1,0:T(8,128)(2,1)} %reduce-scatter.12.cloned.1.call-done) | copy-start | bytes 786436
  (31 other events, 186.3 us)
Sparse Core Ops, SparseCore 0:
  9.6 61.4 all-gather.5
  73.2 99.5 all-gather.7
  177.3 30.0 all-gather.9
  246.3 81.7 all-gather.11
  329.6 48.9 all-gather.13
  399.7 46.8 reduce-scatter.7
  449.5 48.2 reduce-scatter.5
  520.5 41.8 reduce-scatter.11
  583.0 48.7 reduce-scatter.9
  647.4 171.3 reduce-scatter.13
  824.2 145.7 all-reduce.4

commit v2 on v1

--- a/solution.py
+++ b/solution.py
@@ -277,13 +277,13 @@
 
 
 def cross_forward(queries, memory, length):
-    count, states = queries.shape[0], memory.shape[0]
+    count, states = queries.shape[0], memory.shape[0] // (D // PAIR)
     grid_spec = pltpu.PrefetchScalarGridSpec(
         num_scalar_prefetch=1,
         grid=(D // PAIR,),
         in_specs=[
             pl.BlockSpec((count, PAIR), lambda i, e: (0, i)),
-            pl.BlockSpec((states, 2 * PAIR), lambda i, e: (0, i)),
+            pl.BlockSpec((states, 2 * PAIR), lambda i, e: (i, 0)),
         ],
         out_specs=pl.BlockSpec((count, PAIR), lambda i, e: (0, i)),
     )
@@ -325,18 +325,18 @@
 
 
 def cross_backward(queries, memory, grads, length):
-    count, states = queries.shape[0], memory.shape[0]
+    count, states = queries.shape[0], memory.shape[0] // (D // PAIR)
     grid_spec = pltpu.PrefetchScalarGridSpec(
         num_scalar_prefetch=1,
         grid=(D // PAIR,),
         in_specs=[
             pl.BlockSpec((count, PAIR), lambda i, e: (0, i)),
-            pl.BlockSpec((states, 2 * PAIR), lambda i, e: (0, i)),
+            pl.BlockSpec((states, 2 * PAIR), lambda i, e: (i, 0)),
             pl.BlockSpec((count, PAIR), lambda i, e: (0, i)),
         ],
         out_specs=[
             pl.BlockSpec((count, PAIR), lambda i, e: (0, i)),
-            pl.BlockSpec((states, 2 * PAIR), lambda i, e: (0, i)),
+            pl.BlockSpec((states, 2 * PAIR), lambda i, e: (i, 0)),
         ],
     )
     return pl.pallas_call(
@@ -344,12 +344,83 @@
         grid_spec=grid_spec,
         out_shape=(
             jax.ShapeDtypeStruct((count, D), jnp.bfloat16),
-            jax.ShapeDtypeStruct((states, 2 * D), jnp.bfloat16),
+            jax.ShapeDtypeStruct((states * (D // PAIR), 2 * PAIR), jnp.bfloat16),
         ),
         cost_estimate=pl.CostEstimate(
             flops=20 * count * states * D, bytes_accessed=6 * count * D + 8 * states * D, transcendentals=count * states * H
         ),
     )(length, queries, memory, grads)
+
+
+def rep_send(value, step):
+    size = lax.axis_size("rep")
+    return lax.ppermute(value, "rep", [(i, i ^ step) for i in range(size)])
+
+
+def rep_gather(value, axis):
+    size, me = lax.axis_size("rep"), lax.axis_index("rep")
+    parts = [value] + [rep_send(value, step) for step in range(1, size)]
+    shape = value.shape[:axis] + (size,) + value.shape[axis:]
+    out = jnp.zeros(shape, value.dtype)
+    for step, part in enumerate(parts):
+        out = lax.dynamic_update_slice_in_dim(out, jnp.expand_dims(part, axis), me ^ step, axis)
+    return out
+
+
+def rep_reduce(parts, axis):
+    size, me = lax.axis_size("rep"), lax.axis_index("rep")
+
+    def pick(step):
+        return lax.dynamic_index_in_dim(parts, me ^ step, axis, keepdims=False)
+
+    total = pick(0).astype(jnp.float32)
+    for step in range(1, size):
+        total = total + rep_send(low(pick(step)), step).astype(jnp.float32)
+    return low(total)
+
+
+def core_send(value):
+    size = lax.axis_size("shard")
+    return lax.ppermute(value, "shard", [(i, i ^ 1) for i in range(size)])
+
+
+def line_send(value, step):
+    size = lax.axis_size("shard")
+    return lax.ppermute(value, "shard", [(i, (i + 2 * step) % size) for i in range(size)])
+
+
+def gather_weights(piece):
+    kinds, rows, columns = piece.shape
+    chips = lax.axis_size("shard") // 2
+    chip, core = lax.axis_index("shard") // 2, lax.axis_index("shard") % 2
+    line = jnp.zeros((kinds, chips, rows, columns), piece.dtype)
+    for step in range(chips):
+        part = line_send(piece, step) if step else piece
+        line = lax.dynamic_update_slice_in_dim(line, part[:, None], (chip - step) % chips, 1)
+    plane = rep_gather(line, 2)
+    other = core_send(plane)
+    full = jnp.zeros((kinds, chips, 2) + plane.shape[2:], piece.dtype)
+    full = lax.dynamic_update_slice_in_dim(full, plane[:, :, None], core, 2)
+    full = lax.dynamic_update_slice_in_dim(full, other[:, :, None], 1 - core, 2)
+    return full.reshape(kinds, D, columns)
+
+
+def reduce_weights(grads):
+    kinds = len(grads)
+    size = lax.axis_size("rep")
+    chips = lax.axis_size("shard") // 2
+    chip, core = lax.axis_index("shard") // 2, lax.axis_index("shard") % 2
+    rows = D // (2 * chips * size)
+    stack = jnp.stack([low(g) for g in grads]).reshape(kinds, chips, 2, size, rows, D)
+    mine = lax.dynamic_index_in_dim(stack, core, 2, keepdims=False)
+    theirs = lax.dynamic_index_in_dim(stack, 1 - core, 2, keepdims=False)
+    both = low(mine.astype(jnp.float32) + core_send(theirs).astype(jnp.float32))
+    line = rep_reduce(both, 2)
+    total = lax.dynamic_index_in_dim(line, chip, 1, keepdims=False).astype(jnp.float32)
+    for step in range(1, chips):
+        part = lax.dynamic_index_in_dim(line, (chip + step) % chips, 1, keepdims=False)
+        total = total + line_send(part, step).astype(jnp.float32)
+    return rep_gather(low(total), 1).reshape(kinds, size * rows, D).astype(jnp.float32)
 
 
 def shards(
@@ -370,10 +441,12 @@
     proj_bias,
     expand_bias,
 ):
-    row_count = tokens.shape[0]
+    row_count, enc_rows = tokens.shape[0], enc_states.shape[0]
     span = SEQ // row_count
     width = D // span
     count = lax.axis_size("shard")
+    size = lax.axis_size("rep")
+    rep_pos = lax.axis_index("rep")
     shard_pos = lax.axis_index("shard")
     local_pos = shard_pos % span
     local_seq = shard_pos // span
@@ -381,7 +454,9 @@
     if count != span:
         groups = [[g * span + i for i in range(span)] for g in range(count // span)]
     weight_rows = self_qkv.shape[0]
+    part_rows = weight_rows // size
     hidden = expand_bias.shape[0]
+    shard_width = norm_gain.shape[1]
 
     def gather(value, groups=None):
         return lax.all_gather(value, "shard", axis=0, tiled=True, axis_index_groups=groups)
@@ -392,33 +467,44 @@
     def swap(value):
         return lax.all_to_all(value, "shard", 0, 0, tiled=True)
 
-    tokens_all = gather(tokens, groups)
-    blocks = self_qkv.reshape(weight_rows, 3, span, width).transpose(2, 0, 1, 3)
-    blocks = jnp.tile(blocks.reshape(span, weight_rows, 3 * width), (count // span, 1, 1))
-    qkv_weight = swap(blocks).reshape(D, 3 * width)
+    def own_part(weight):
+        return lax.dynamic_slice_in_dim(weight, rep_pos * part_rows, part_rows, axis=0)
+
+    def by_pairs(weight, kinds):
+        blocks = weight.reshape(part_rows, kinds, span, width).transpose(2, 0, 1, 3)
+        return blocks.reshape(span, part_rows, kinds * width)
+
+    rows_all = gather(jnp.concatenate([tokens, enc_states], axis=0), groups)
+    rows_all = rows_all.reshape(span, row_count + enc_rows, D)
+    blocks = jnp.concatenate([by_pairs(own_part(self_qkv), 3), by_pairs(own_part(cross_memory), 2)], axis=2)
+    blocks = jnp.tile(blocks, (count // span, 1, 1))
     small = jnp.concatenate([norm_gain, norm_bias, proj_bias], axis=0)
-    small_all = lax.all_gather(small, "shard", axis=1, tiled=True).astype(jnp.float32)
+    small_count = small.shape[0]
+    small = jnp.pad(small, ((0, 16 - small_count), (0, 5 * width - shard_width)))
+    blocks = jnp.concatenate([blocks, jnp.broadcast_to(small, (count,) + small.shape)], axis=1)
+    swapped = swap(blocks)
+    small_all = swapped[:, part_rows : part_rows + small_count, :shard_width].astype(jnp.float32)
+    small_all = small_all.transpose(1, 0, 2).reshape(small_count, D)
     gain_rows, shift_rows, bias_rows = small_all[:3], small_all[3:6], small_all[6:]
-    memory_weight = cross_memory.reshape(weight_rows, 2, span, width).transpose(0, 2, 1, 3)
-    memory_weight = memory_weight.reshape(weight_rows, 2 * D)
-    pack = gather(jnp.concatenate([self_out, cross_query, cross_out, memory_weight], axis=1))
-    attn_proj, query_in, cross_proj = pack[:, :D], pack[:, D : 2 * D], pack[:, 2 * D : 3 * D]
-    memory_in = pack[:, 3 * D :]
-    expand_local = swap(expand_weight.reshape(weight_rows, count, hidden).transpose(1, 0, 2)).reshape(D, hidden)
+    head_weight = rep_gather(swapped[:, :part_rows], 1).reshape(D, 5 * width)
+    qkv_weight, memory_weight = head_weight[:, : 3 * width], head_weight[:, 3 * width :]
+    plain = gather_weights(jnp.stack([own_part(self_out), own_part(cross_query), own_part(cross_out)]))
+    attn_proj, query_in, cross_proj = plain[0], plain[1], plain[2]
+    expand_part = own_part(expand_weight).reshape(part_rows, count, hidden).transpose(1, 0, 2)
+    expand_local = rep_gather(swap(expand_part), 1).reshape(D, hidden)
 
     seq_segments = lax.dynamic_slice_in_dim(segments, local_seq * SEQ, SEQ)
-    x_all = tokens_all.astype(jnp.float32)
-    input_one_all = low(norm_apply(x_all, gain_rows[0], shift_rows[0]))
-    own_bias = lax.dynamic_slice_in_dim(bias_rows[:2], local_pos * width, width, axis=1)
-    qkv_bias = jnp.concatenate([own_bias[0], jnp.zeros((width,), jnp.float32), own_bias[1]])
-    qkv = low(dot(input_one_all, qkv_weight) + qkv_bias)
+    x_all = rows_all[:, :row_count].astype(jnp.float32)
+    input_one_all = low(norm_apply(x_all, gain_rows[0], shift_rows[0])).reshape(SEQ, D)
+    own_bias = lax.dynamic_slice_in_dim(bias_rows, local_pos * width, width, axis=1)
+    zero_bias = jnp.zeros((width,), jnp.float32)
+    qkv = low(dot(input_one_all, qkv_weight) + jnp.concatenate([own_bias[0], zero_bias, own_bias[1]]))
     att_low, att_full, lse = self_forward(qkv, seq_segments)
     attended = lax.all_to_all(att_low, "shard", 0, 1, tiled=True, axis_index_groups=groups)
 
-    pair_bias = bias_rows[4].reshape(span, width)
-    pair_bias = jnp.stack([jnp.zeros_like(pair_bias), pair_bias], axis=1).reshape(2 * D)
-    memory_own = low(dot(enc_states, memory_in) + pair_bias)
-    memory_all = gather(memory_own, groups)
+    enc_all = rows_all[:, row_count:].reshape(span * enc_rows, D)
+    memory_pair = low(dot(enc_all, memory_weight) + jnp.concatenate([zero_bias, own_bias[4]]))
+    memory_all = gather(memory_pair, groups)
     enc_count = lax.dynamic_slice_in_dim(enc_lengths, local_seq, 1)
 
     residual_in = tokens.astype(jnp.float32)
@@ -440,6 +526,9 @@
     grad_shrink = dot_tn(act, grad_all)
     grad_expand = dot_tn(input_three_all, grad_pre)
     grad_hidden_bias = column_sums(grad_pre)
+    total_shrink = rep_gather(rep_reduce(low(grad_shrink).reshape(size, hidden // size, D), 0), 0)
+    own_expand = swap(rep_reduce(low(grad_expand).reshape(count, size, part_rows, hidden), 1))
+    total_expand = rep_gather(own_expand.transpose(1, 0, 2).reshape(part_rows, count * hidden), 0)
 
     grad_out = cotangent.astype(jnp.float32)
     norm_three = jax.vjp(norm_apply, hidden_two, gain_rows[2], shift_rows[2])[1](grad_in_three)
@@ -449,8 +538,8 @@
     grad_context = low(dot_nt(grad_two_low, cross_proj))
     grad_cross_q, memory_part = cross_backward(cross_q, memory_all, grad_context, enc_count)
     mem_grads = scatter(memory_part, groups)
-    grad_memory = dot_tn(enc_states, mem_grads)
-    grad_enc = dot_nt(mem_grads, memory_in)
+    grad_memory = dot_tn(enc_all, mem_grads)
+    grad_enc = scatter(low(dot_nt(mem_grads, memory_weight)), groups).astype(jnp.float32)
     grad_query_in = dot_tn(input_two, grad_cross_q)
     grad_in_two = dot_nt(grad_cross_q, query_in)
     norm_two = jax.vjp(norm_apply, hidden_one, gain_rows[1], shift_rows[1])[1](grad_in_two)
@@ -458,20 +547,30 @@
     grad_one_low = low(grad_one)
     grad_attn_proj = dot_tn(attended, grad_one_low)
     grad_attn = low(dot_nt(grad_one_low, attn_proj))
+    total_query, total_cross = reduce_weights([grad_query_in, grad_cross_proj])
+    (total_proj,) = reduce_weights([grad_attn_proj])
 
     grad_att_heads = lax.all_to_all(grad_attn, "shard", 1, 0, tiled=True, axis_index_groups=groups)
     delta = jnp.sum((grad_att_heads.astype(jnp.float32) * att_full).reshape(SEQ, 2, HD), axis=-1).T
     grad_qkv = self_backward(qkv, grad_att_heads, lse.T, delta, seq_segments)
     grad_in_one = scatter(low(dot_nt(grad_qkv, qkv_weight)), groups).astype(jnp.float32)
-    grad_attn_in = low(dot_tn(input_one_all, grad_qkv))
+    grad_attn_in = dot_tn(input_one_all, grad_qkv)
     norm_one = jax.vjp(norm_apply, residual_in, gain_rows[0], shift_rows[0])[1](grad_in_one)
     grad_tokens = grad_one + norm_one[0]
 
+    heads_grad = low(jnp.concatenate([grad_attn_in, grad_memory], axis=1))
+    own_heads = swap(rep_reduce(heads_grad.reshape(count, size, part_rows, 5 * width), 1))
+    own_heads = own_heads.reshape(count // span, span, part_rows, 5 * width)
+    own_heads = own_heads[0] if count == span else low(jnp.sum(own_heads.astype(jnp.float32), axis=0))
+    total_heads = rep_gather(own_heads.transpose(1, 0, 2), 0).reshape(weight_rows, span, 5, width)
+    total_heads = total_heads.transpose(0, 2, 1, 3).reshape(weight_rows, 5 * D).astype(jnp.float32)
+
     qkv_sums = column_sums(grad_qkv)
     zero_row = jnp.zeros((D,), jnp.float32)
-    bias_zero = lax.dynamic_update_slice_in_dim(zero_row, qkv_sums[:width], local_pos * width, 0)
-    bias_one = lax.dynamic_update_slice_in_dim(zero_row, qkv_sums[2 * width :], local_pos * width, 0)
-    memory_sums = column_sums(mem_grads).reshape(span, 2, width)[:, 1].reshape(D)
+
+    def at_own(values):
+        return lax.dynamic_update_slice_in_dim(zero_row, values, local_pos * width, 0)
+
     small_grads = jnp.stack(
         [
             norm_one[1],
@@ -480,59 +579,42 @@
             norm_one[2],
             norm_two[2],
             norm_three[2],
-            bias_zero,
-            bias_one,
+            at_own(qkv_sums[:width]),
+            at_own(qkv_sums[2 * width :]),
             column_sums(grad_one_low),
             column_sums(grad_cross_q),
-            memory_sums,
+            at_own(column_sums(mem_grads)[width:]),
             column_sums(grad_two_low),
             column_sums(cotangent),
         ]
     )
-    small_count = small_grads.shape[0]
-    shard_width = D // count
-    pack_width = 5 * D
-    extra = 8
-    small_rows = low(small_grads).reshape(small_count, count, shard_width).transpose(1, 0, 2)
-    small_rows = small_rows.reshape(count, small_count * shard_width)
-    small_rows = jnp.pad(small_rows, ((0, 0), (0, extra * pack_width - small_count * shard_width)))
-    small_rows = small_rows.reshape(count, extra, pack_width)
-    grad_pack = low(jnp.concatenate([grad_attn_proj, grad_query_in, grad_cross_proj, grad_memory], axis=1))
-    grad_pack = jnp.concatenate([grad_pack.reshape(count, weight_rows, pack_width), small_rows], axis=1)
-    owned_pack = scatter(grad_pack.reshape(count * (weight_rows + extra), pack_width))
-    owned_qkv = swap(grad_attn_in.reshape(count, weight_rows, 3 * width))
-    owned_qkv = owned_qkv.astype(jnp.float32).reshape(count // span, span, weight_rows, 3 * width)
-    owned_qkv = low(jnp.sum(owned_qkv, axis=0))
-    owned_expand = swap(low(grad_expand).reshape(count, weight_rows, hidden))
-    total_shrink, total_hidden_bias = lax.psum((low(grad_shrink), low(grad_hidden_bias)), "rep")
-    total_expand = lax.psum(owned_expand, "rep")
-    total_pack, total_qkv = lax.psum((owned_pack, owned_qkv), "rep")
-    total_expand = total_expand.transpose(1, 0, 2).reshape(weight_rows, count * hidden)
-    total_qkv = total_qkv.reshape(span, weight_rows, 3, width).transpose(1, 2, 0, 3)
-    total_qkv = total_qkv.reshape(weight_rows, 3 * D)
-    total_memory = total_pack[:weight_rows, 3 * D :].reshape(weight_rows, span, 2, width)
-    total_memory = total_memory.transpose(0, 2, 1, 3).reshape(weight_rows, 2 * D)
-    total_small = total_pack[weight_rows:].reshape(-1)[: small_count * shard_width]
-    total_small = total_small.reshape(small_count, shard_width)
-
-    def wide(value):
-        return value.astype(jnp.float32)
+    small_grads = small_grads.reshape(small_count, count, shard_width).transpose(1, 0, 2)
+    hidden_rows = hidden // shard_width
+    hidden_grads = jnp.zeros((count, hidden_rows, shard_width), jnp.float32)
+    hidden_grads = lax.dynamic_update_slice_in_dim(
+        hidden_grads, grad_hidden_bias.reshape(1, hidden_rows, shard_width), shard_pos, 0
+    )
+    small_grads = low(jnp.concatenate([small_grads, hidden_grads], axis=1))
+    small_grads = jnp.broadcast_to(small_grads, (size,) + small_grads.shape)
+    small_grads = small_grads.reshape((size * count,) + small_grads.shape[2:])
+    small_grads = lax.all_to_all(small_grads, ("rep", "shard"), 0, 0, tiled=True)
+    total_small = jnp.sum(small_grads.astype(jnp.float32), axis=0)
 
     return (
         low(result),
         grad_tokens,
         grad_enc,
-        wide(total_qkv),
-        wide(total_pack[:weight_rows, :D]),
-        wide(total_pack[:weight_rows, D : 2 * D]),
-        wide(total_memory),
-        wide(total_pack[:weight_rows, 2 * D : 3 * D]),
-        wide(total_expand),
-        wide(total_shrink),
-        wide(total_small[:3]),
-        wide(total_small[3:6]),
-        wide(total_small[6:]),
-        wide(total_hidden_bias),
+        total_heads[:, : 3 * D],
+        total_proj,
+        total_query,
+        total_heads[:, 3 * D :],
+        total_cross,
+        total_expand.reshape(weight_rows, count * hidden).astype(jnp.float32),
+        total_shrink.reshape(hidden, D).astype(jnp.float32),
+        total_small[:3],
+        total_small[3:6],
+        total_small[6:small_count],
+        total_small[small_count:].reshape(hidden),
     )
 
 

time: 1000 us -> 718 us (0.72)
  the two profiles are of different devices: /device:TPU:12 before, /device:TPU:1 now
where the time goes in v2:
time: 718 us; the launch traced here: 706 us
  waiting for transfers between devices  244 us (34%)
  starting transfers between devices  113 us (16%)
  matrix products  95.3 us (13%)
  local copies, waits for them, and re-layouts  92.5 us (13%)
  Pallas kernels  61 us (8%)
  other arithmetic  54 us (8%)
  blocking collectives  29.5 us (4%)
  between operations  16.1 us (2%)
    ppermute x39, waiting for transfers between devices, rep_send(): return lax.ppermute(value, 'rep', [(i, i ^ step) for i in range(size)])  113 us
    all_to_all x3, waiting for transfers between devices, swap(): return lax.all_to_all(value, 'shard', 0, 0, tiled=True)  38.7 us
    ppermute x39, starting transfers between devices, rep_send(): return lax.ppermute(value, 'rep', [(i, i ^ step) for i in range(size)])  37.5 us
    all_gather x4, waiting for transfers between devices, gather(): lax.all_gather(value, 'shard', axis=0, tiled=True, axis_index_groups=groups)  36.5 us
    dot_general x7, matrix products, dot(): return jnp.dot(left, right, preferred_element_type=jnp.float32)  35.3 us
    dot_general x7, matrix products, dot_nt(): lax.dot_general(left, right, (((1,), (1,)), ((), ())), preferred_element_...  33.5 us
    all_to_all x1, blocking collectives, swap(): return lax.all_to_all(value, 'shard', 0, 0, tiled=True)  29.5 us
    dot_general x7, matrix products, dot_tn(): lax.dot_general(left, right, (((0,), (0,)), ((), ())), preferred_element_...  26.4 us
  transfers between devices with their start and end apart: 66, of which 31 were waited for; matrix products, arithmetic and copies ran while one was open for 28% of the time, Pallas kernels for 7%

profile of v2, /device:TPU:1, one launch (start us, length us, event | category | flops | bytes accessed | tf_op | source)
XLA Modules:
  0.0 705.9 jit_solution(5016275982745435978)
XLA Ops:
  30.8 7.5 %collective-permute-done.4 = bf16[3,32,1024]{2,1,0:T(8,128)(2,1)} collective-permute-done((bf16[3,32,1024]{2,1,0:T(8,128)(2,1)}, bf16[3,32,1024]{2,1,0:T(8,128)(2,1)}, u32[]{:S(2)}, u32[]{:S(2)}) %collective-permute-start.4) | collective-permute-done | bytes 196640 | tf_op jit(solution)/shard_map/ppermute | solution.py:389
  48.3 27.6 %all-to-all-done = bf16[8,48,640]{2,1,0:T(8,128)(2,1)} async-done(((bf16[8,48,640]{2,1,0:T(8,128)(2,1)}), bf16[8,48,640]{2,1,0:T(8,128)(2,1)}, u32[]{:S(2)}, u32[]{:S(2)}) %all-to-all-start) | async-done | bytes 491552 | tf_op jit(solution)/shard_map/all_to_all | solution.py:468
  112.3 18.5 %shard_map.263 = (bf16[2048,128]{1,0:T(8,128)(2,1)S(1)}, f32[2048,128]{1,0:T(8,128)S(1)}, f32[2048,2]{1,0:T(8,128)S(1)}) custom-call(s32[2,4]{1,0:T(2,128)S(1)} %pad_add_fusion.ends, bf16[2048,384]{1,0:T(8,128)(2,1)S(1)} %add_convert_fusion.q_ref.k_ref.v_ref, bf16[2048,384]{1,0:T(8,128)(2,1)S(1)} %add_convert_fusion.q_ref.k_ref.v_ref, ...), custom_call_target="tpu_custom_call" | custom-call | flops 2147483648 | bytes 2097152 | tf_op jit(solution)/shard_map/pallas_call | solution.py:142
  135.6 21.3 %all-to-all-start.1 = ((bf16[8,256,128]{1,2,0:T(8,128)(2,1)}), bf16[8,256,128]{1,2,0:T(8,128)(2,1)}, u32[]{:S(2)}, u32[]{:S(2)}) async-start(bf16[8,256,128]{1,2,0:T(8,128)(2,1)} %copy.220), calls=%async_computation.1 | async-start | bytes 1048576 | tf_op jit(solution)/shard_map/all_to_all | solution.py:503
  176.9 8.6 %shard_map.264 = bf16[256,1024]{1,0:T(8,128)(2,1)} custom-call(s32[1]{0:T(128)S(6)} %copy.321.length, bf16[256,1024]{1,0:T(8,128)(2,1)} %fusion.30.q_ref, bf16[4096,256]{1,0:T(8,128)(2,1)} %all-gather.7.cloned.1.call-done.m_ref), custom_call_target="tpu_custom_call" | custom-call | flops 1073741824 | bytes 3145728 | tf_op jit(solution)/shard_map/pallas_call | solution.py:290
  192.7 29.5 %all_to_all.63 = bf16[8,32,1024]{2,1,0:T(8,128)(2,1)S(1)} all-to-all(bf16[8,32,1024]{2,1,0:T(8,128)(2,1)S(1)} %copy.228), channel_id=1, replica_groups=mesh['rep'=4,'shard'=8] {'shard'}, dimensions={0} | all-to-all | bytes 1048576 | tf_op jit(solution)/shard_map/all_to_all | solution.py:468
  236.0 9.1 %collective-permute-done.12 = bf16[8,32,1024]{2,1,0:T(8,128)(2,1)S(1)} collective-permute-done((bf16[8,32,1024]{2,1,0:T(8,128)(2,1)S(1)}, bf16[8,32,1024]{2,1,0:T(8,128)(2,1)S(1)}, u32[]{:S(2)}, u32[]{:S(2)}) %collective-permute-start.12) | collective-permute-done | bytes 524320 | tf_op jit(solution)/shard_map/ppermute | solution.py:357
  246.6 10.7 %fusion.105 = f32[2048,1024]{1,0:T(8,128)} fusion(bf16[2048,1024]{1,0:T(8,128)(2,1)} %all-gather.9.cloned.1.call-done, bf16[1024,1024]{1,0:T(8,128)(2,1)} %bitcast.63), kind=kOutput, calls=%fused_computation.283 | convolution fusion | flops 4294967296 | bytes 14680064 | tf_op jit(solution)/shard_map/dot_general | solution.py:40
  257.3 35.9 %all-gather.11.cloned.1.call-done = bf16[2048,1024]{1,0:T(8,128)(2,1)} async-done(((bf16[256,1024]{1,0:T(8,128)(2,1)}), bf16[2048,1024]{1,0:T(8,128)(2,1)}) %all-gather.11.cloned.1.call-update) | async-done | bytes 4194320 | tf_op jit(solution)/shard_map/all_gather | solution.py:462
  293.2 12.7 %convert_reduce_fusion.1 = (f32[1024]{0:T(1024)S(1)}, bf16[2048,1024]{1,0:T(8,128)(2,1)S(1)}) fusion(f32[2048,1024]{1,0:T(8,128)} %fusion.105, f32[1024]{0:T(1024)S(1)} %convert_element_type.340, bf16[2048,1024]{1,0:T(8,128)(2,1)} %all-gather.11.cloned.1.call-done, bf16[1024,1024]{1,0:T(8,128)(2,1)S(1)} %copy-done), kind=kOutput, calls=%fused_computation.17 | convolution fusion | flops 4343200768 | bytes 18882560 | tf_op jit(solution)/shard_map/dot_general | solution.py:44
  307.8 7.8 %convolution_convert_fusion.1 = bf16[2048,1024]{1,0:T(8,128)(2,1)} fusion(bf16[2048,1024]{1,0:T(8,128)(2,1)S(1)} %get-tuple-element.38, bf16[1024,1024]{1,0:T(8,128)(2,1)} %bitcast.63), kind=kOutput, calls=%fused_computation.26 | convolution fusion | flops 4297064448 | bytes 10485760 | tf_op jit(solution)/shard_map/dot_general | solution.py:44
  315.9 11.2 %convolution_convert_fusion.2 = bf16[2048,1024]{1,0:T(8,128)(2,1)} fusion(bf16[1024,1024]{1,0:T(8,128)(2,1)S(1)} %copy-done, f32[2048,1024]{1,0:T(8,128)} %fusion.105, f32[1024]{0:T(1024)S(1)} %convert_element_type.340), kind=kOutput, calls=%fused_computation.27 | convolution fusion | flops 4318035968 | bytes 14684160 | tf_op jit(solution)/shard_map/dot_general | solution.py:40
  327.1 10.9 %convolution_convert_fusion.3 = bf16[1024,1024]{1,0:T(8,128)(2,1)S(1)} fusion(bf16[2048,1024]{1,0:T(8,128)(2,1)} %all-gather.11.cloned.1.call-done, f32[2048,1024]{1,0:T(8,128)} %fusion.105, f32[1024]{0:T(1024)S(1)} %convert_element_type.340), kind=kOutput, calls=%fused_computation.45 | convolution fusion | flops 4316987392 | bytes 14684160 | tf_op jit(solution)/shard_map/dot_general | solution.py:48
  353.7 9.9 %collective-permute-done.47 = bf16[256,1024]{1,0:T(8,128)(2,1)S(1)} collective-permute-done((bf16[256,1024]{1,0:T(8,128)(2,1)S(1)}, bf16[256,1024]{1,0:T(8,128)(2,1)S(1)}, u32[]{:S(2)}, u32[]{:S(2)}) %collective-permute-start.47) | collective-permute-done | bytes 524320 | tf_op jit(solution)/shard_map/ppermute | solution.py:357
  377.9 8.3 %collective-permute-done.41 = bf16[8,32,1024]{2,1,0:T(8,128)(2,1)} collective-permute-done((bf16[8,32,1024]{2,1,0:T(8,128)(2,1)}, bf16[8,32,1024]{2,1,0:T(8,128)(2,1)}, u32[]{:S(2)}, u32[]{:S(2)}) %collective-permute-start.41) | collective-permute-done | bytes 524320 | tf_op jit(solution)/shard_map/ppermute | solution.py:357
  397.5 12.1 %collective-permute-done.49 = bf16[256,1024]{1,0:T(8,128)(2,1)S(1)} collective-permute-done((bf16[256,1024]{1,0:T(8,128)(2,1)}, bf16[256,1024]{1,0:T(8,128)(2,1)S(1)}, u32[]{:S(2)}, u32[]{:S(2)}) %collective-permute-start.49) | collective-permute-done | bytes 524320 | tf_op jit(solution)/shard_map/ppermute | solution.py:357
  424.4 7.3 %collective-permute-done.42 = bf16[32,8192]{1,0:T(8,128)(2,1)} collective-permute-done((bf16[32,8192]{1,0:T(8,128)(2,1)}, bf16[32,8192]{1,0:T(8,128)(2,1)}, u32[]{:S(2)}, u32[]{:S(2)}) %collective-permute-start.42) | collective-permute-done | bytes 524320 | tf_op jit(solution)/shard_map/ppermute | solution.py:357
  441.0 14.5 %shard_map.265 = (bf16[256,1024]{1,0:T(8,128)(2,1)}, bf16[4096,256]{1,0:T(8,128)(2,1)}) custom-call(s32[1]{0:T(128)S(6)} %copy.321.length, bf16[256,1024]{1,0:T(8,128)(2,1)} %fusion.30.q_ref, bf16[4096,256]{1,0:T(8,128)(2,1)} %all-gather.7.cloned.1.call-done.m_ref, bf16[256,1024]{1,0:T(8,128)(2,1)} %convolution_convert_fusion.11.g_ref), custom_call_target="tpu_custom_call" | custom-call | flops 2684354560 | bytes 5767168 | tf_op jit(solution)/shard_map/pallas_call | solution.py:342
  472.1 24.8 %reduce-scatter.12.cloned.1.call-done = bf16[512,256]{1,0:T(8,128)(2,1)} async-done(((bf16[4096,256]{1,0:T(8,128)(2,1)}), bf16[512,256]{1,0:T(8,128)(2,1)}) %reduce-scatter.12.cloned.1.call-update) | async-done | bytes 262160 | tf_op jit(solution)/shard_map/reduce_scatter | solution.py:465
  511.4 19.4 %shard_map.266 = bf16[2048,384]{1,0:T(8,128)(2,1)S(1)} custom-call(s32[2,4]{1,0:T(2,128)S(1)} %pad_add_fusion.ends, bf16[2048,384]{1,0:T(8,128)(2,1)S(1)} %copy-done.9, bf16[2048,384]{1,0:T(8,128)(2,1)S(1)} %copy-done.9, bf16[2048,384]{1,0:T(8,128)(2,1)S(1)} %copy-done.9, bf16[2048,128]{1,0:T(8,128)(2,1)S(1)} %bitcast.367, f32[2,2048]{1,0:T(2,128)S(1)} %bitcast.369, ...), custom_call_target="tpu_custom_call" | custom-call | flops 5368709120 | bytes 3670016 | tf_op jit(solution)/shard_map/pallas_call | solution.py:253
  585.8 10.6 %collective-permute-done.27 = bf16[1,32,1024]{2,1,0:T(8,128)(2,1)S(1)} collective-permute-done((bf16[1,32,1024]{2,1,0:T(8,128)(2,1)S(1)}, bf16[1,32,1024]{2,1,0:T(8,128)(2,1)S(1)}, u32[]{:S(2)}, u32[]{:S(2)}) %collective-permute-start.27) | collective-permute-done | bytes 65568 | tf_op jit(solution)/shard_map/ppermute | solution.py:357
  596.5 8.4 %collective-permute-done.32 = bf16[2,4,32,1024]{3,2,1,0:T(8,128)(2,1)S(1)} collective-permute-done((bf16[2,4,32,1024]{3,2,1,0:T(8,128)(2,1)S(1)}, bf16[2,4,32,1024]{3,2,1,0:T(8,128)(2,1)S(1)}, u32[]{:S(2)}, u32[]{:S(2)}) %collective-permute-start.32) | collective-permute-done | bytes 524320 | tf_op jit(solution)/shard_map/ppermute | solution.py:357
  635.2 12.1 %all-to-all-start.4 = ((bf16[8,32,640]{2,1,0:T(8,128)(2,1)}), bf16[8,32,640]{2,1,0:T(8,128)(2,1)S(1)}, u32[]{:S(2)}, u32[]{:S(2)}) async-start(bf16[8,32,640]{2,1,0:T(8,128)(2,1)} %fusion.56), calls=%async_computation.9 | async-start | bytes 655360 | tf_op jit(solution)/shard_map/all_to_all | solution.py:468
  648.5 8.8 %all-to-all-done.4 = bf16[8,32,640]{2,1,0:T(8,128)(2,1)S(1)} async-done(((bf16[8,32,640]{2,1,0:T(8,128)(2,1)}), bf16[8,32,640]{2,1,0:T(8,128)(2,1)S(1)}, u32[]{:S(2)}, u32[]{:S(2)}) %all-to-all-start.4) | async-done | bytes 327712 | tf_op jit(solution)/shard_map/all_to_all | solution.py:468
  (428 shorter events, 342.2 us)
Async XLA Ops:
  7.2 87.2 %all-gather.5.cloned.1.call-start = ((), (), s32[]{:S(2)}) async-start(), calls=%async_computation.12 | async-start | bytes 5898240 | tf_op jit(solution)/shard_map/all_gather | solution.py:462
  20.7 55.2 %all-to-all-start = ((bf16[8,48,640]{2,1,0:T(8,128)(2,1)}), bf16[8,48,640]{2,1,0:T(8,128)(2,1)}, u32[]{:S(2)}, u32[]{:S(2)}) async-start(bf16[8,48,640]{2,1,0:T(8,128)(2,1)} %pad_maximum_fusion.1), calls=%async_computation | async-start | bytes 983040 | tf_op jit(solution)/shard_map/all_to_all | solution.py:468
  26.3 150.7 %all-gather.7.cloned.1.call-start = ((), (), s32[]{:S(2)}) async-start(), calls=%async_computation.13 | async-start | bytes 2359296 | tf_op jit(solution)/shard_map/all_gather | solution.py:462
  41.6 41.8 %collective-permute-start.6 = (bf16[3,4,32,1024]{3,2,1,0:T(8,128)(2,1)}, bf16[3,4,32,1024]{3,2,1,0:T(8,128)(2,1)}, u32[]{:S(2)}, u32[]{:S(2)}) collective-permute-start(bf16[3,4,32,1024]{3,2,1,0:T(8,128)(2,1)} %bitcast_dynamic-update-slice_fusion.24), channel_id=1, source_target_pairs={{0,8},{8,0},{16,24},{24,16},{1,9},{9,1},{17,25},{25,17},{2,10},{10... | collective-permute-start | bytes 2359304 | tf_op jit(solution)/shard_map/ppermute | solution.py:357
  42.8 42.8 %collective-permute-start.7 = (bf16[3,4,32,1024]{3,2,1,0:T(8,128)(2,1)}, bf16[3,4,32,1024]{3,2,1,0:T(8,128)(2,1)}, u32[]{:S(2)}, u32[]{:S(2)}) collective-permute-start(bf16[3,4,32,1024]{3,2,1,0:T(8,128)(2,1)} %bitcast_dynamic-update-slice_fusion.24), channel_id=1, source_target_pairs={{0,16},{8,24},{16,0},{24,8},{1,17},{9,25},{17,1},{25,9},{2,18},{10... | collective-permute-start | bytes 2359304 | tf_op jit(solution)/shard_map/ppermute | solution.py:357
  44.0 43.7 %collective-permute-start.8 = (bf16[3,4,32,1024]{3,2,1,0:T(8,128)(2,1)}, bf16[3,4,32,1024]{3,2,1,0:T(8,128)(2,1)}, u32[]{:S(2)}, u32[]{:S(2)}) collective-permute-start(bf16[3,4,32,1024]{3,2,1,0:T(8,128)(2,1)} %bitcast_dynamic-update-slice_fusion.24), channel_id=1, source_target_pairs={{0,24},{8,16},{16,8},{24,0},{1,25},{9,17},{17,9},{25,1},{2,26},{10... | collective-permute-start | bytes 2359304 | tf_op jit(solution)/shard_map/ppermute | solution.py:357
  89.8 70.8 %collective-permute-start.9 = (bf16[3,4,4,32,1024]{4,3,2,1,0:T(8,128)(2,1)}, bf16[3,4,4,32,1024]{4,3,2,1,0:T(8,128)(2,1)}, u32[]{:S(2)}, u32[]{:S(2)}) collective-permute-start(bf16[3,4,4,32,1024]{4,3,2,1,0:T(8,128)(2,1)} %bitcast_dynamic-update-slice_fusion.5), channel_id=1, source_target_pairs={{0,1},{1,0},{2,3},{3,2},{4,5},{5,4},{6,7},{7,6},{8,9},{9,8},{10,11... | collective-permute-start | bytes 9437192 | tf_op jit(solution)/shard_map/ppermute | solution.py:384
  135.6 35.9 %all-to-all-start.1 = ((bf16[8,256,128]{1,2,0:T(8,128)(2,1)}), bf16[8,256,128]{1,2,0:T(8,128)(2,1)}, u32[]{:S(2)}, u32[]{:S(2)}) async-start(bf16[8,256,128]{1,2,0:T(8,128)(2,1)} %copy.220), calls=%async_computation.1 | async-start | bytes 1048576 | tf_op jit(solution)/shard_map/all_to_all | solution.py:503
  157.0 89.6 %all-gather.9.cloned.1.call-start = ((), (), s32[]{:S(2)}) async-start(), calls=%async_computation.14 | async-start | bytes 4718592 | tf_op jit(solution)/shard_map/all_gather | solution.py:462
  190.4 102.8 %all-gather.11.cloned.1.call-start = ((), (), s32[]{:S(2)}) async-start(), calls=%async_computation.16 | async-start | bytes 4718592 | tf_op jit(solution)/shard_map/all_gather | solution.py:462
  191.0 242.6 %reduce-scatter.8.cloned.1.call-start = ((), (), s32[]{:S(2)}) async-start(), calls=%async_computation.17 | async-start | bytes 4718592 | tf_op jit(solution)/shard_map/reduce_scatter | solution.py:465
  315.6 119.4 %reduce-scatter.6.cloned.1.call-start = ((), (), s32[]{:S(2)}) async-start(), calls=%async_computation.15 | async-start | bytes 4718592 | tf_op jit(solution)/shard_map/reduce_scatter | solution.py:465
  347.4 29.6 %collective-permute-start.39 = (bf16[8,32,1024]{2,1,0:T(8,128)(2,1)}, bf16[8,32,1024]{2,1,0:T(8,128)(2,1)}, u32[]{:S(2)}, u32[]{:S(2)}) collective-permute-start(bf16[8,32,1024]{2,1,0:T(8,128)(2,1)} %get-tuple-element.55), channel_id=1, source_target_pairs={{0,8},{8,0},{16,24},{24,16},{1,9},{9,1},{17,25},{25,17},{2,10},{10... | collective-permute-start | bytes 1572872 | tf_op jit(solution)/shard_map/ppermute | solution.py:357
  351.6 34.7 %collective-permute-start.41 = (bf16[8,32,1024]{2,1,0:T(8,128)(2,1)}, bf16[8,32,1024]{2,1,0:T(8,128)(2,1)}, u32[]{:S(2)}, u32[]{:S(2)}) collective-permute-start(bf16[8,32,1024]{2,1,0:T(8,128)(2,1)} %get-tuple-element.56), channel_id=1, source_target_pairs={{0,24},{8,16},{16,8},{24,0},{1,25},{9,17},{17,9},{25,1},{2,26},{10... | collective-permute-start | bytes 1572872 | tf_op jit(solution)/shard_map/ppermute | solution.py:357
  366.7 29.9 %collective-permute-start.48 = (bf16[256,1024]{1,0:T(8,128)(2,1)}, bf16[256,1024]{1,0:T(8,128)(2,1)S(1)}, u32[]{:S(2)}, u32[]{:S(2)}) collective-permute-start(bf16[256,1024]{1,0:T(8,128)(2,1)} %get-tuple-element.40), channel_id=1, source_target_pairs={{0,8},{8,0},{16,24},{24,16},{1,9},{9,1},{17,25},{25,17},{2,10},{10... | collective-permute-start | bytes 1572872 | tf_op jit(solution)/shard_map/ppermute | solution.py:357
  376.5 33.1 %collective-permute-start.49 = (bf16[256,1024]{1,0:T(8,128)(2,1)}, bf16[256,1024]{1,0:T(8,128)(2,1)S(1)}, u32[]{:S(2)}, u32[]{:S(2)}) collective-permute-start(bf16[256,1024]{1,0:T(8,128)(2,1)} %get-tuple-element.40), channel_id=1, source_target_pairs={{0,16},{8,24},{16,0},{24,8},{1,17},{9,25},{17,1},{25,9},{2,18},{10... | collective-permute-start | bytes 1572872 | tf_op jit(solution)/shard_map/ppermute | solution.py:357
  376.9 33.6 %collective-permute-start.50 = (bf16[256,1024]{1,0:T(8,128)(2,1)}, bf16[256,1024]{1,0:T(8,128)(2,1)S(1)}, u32[]{:S(2)}, u32[]{:S(2)}) collective-permute-start(bf16[256,1024]{1,0:T(8,128)(2,1)} %get-tuple-element.40), channel_id=1, source_target_pairs={{0,24},{8,16},{16,8},{24,0},{1,25},{9,17},{17,9},{25,1},{2,26},{10... | collective-permute-start | bytes 1572872 | tf_op jit(solution)/shard_map/ppermute | solution.py:357
  394.2 102.6 %reduce-scatter.12.cloned.1.call-start = ((), (), s32[]{:S(2)}) async-start(), calls=%async_computation.19 | async-start | bytes 2359296 | tf_op jit(solution)/shard_map/reduce_scatter | solution.py:465
  419.7 35.8 %collective-permute-start.43 = (bf16[32,8192]{1,0:T(8,128)(2,1)}, bf16[32,8192]{1,0:T(8,128)(2,1)}, u32[]{:S(2)}, u32[]{:S(2)}) collective-permute-start(bf16[32,8192]{1,0:T(8,128)(2,1)} %bitcast.207), channel_id=1, source_target_pairs={{0,16},{8,24},{16,0},{24,8},{1,17},{9,25},{17,1},{25,9},{2,18},{10... | collective-permute-start | bytes 1572872 | tf_op jit(solution)/shard_map/ppermute | solution.py:357
  420.2 37.3 %collective-permute-start.44 = (bf16[32,8192]{1,0:T(8,128)(2,1)}, bf16[32,8192]{1,0:T(8,128)(2,1)}, u32[]{:S(2)}, u32[]{:S(2)}) collective-permute-start(bf16[32,8192]{1,0:T(8,128)(2,1)} %bitcast.207), channel_id=1, source_target_pairs={{0,24},{8,16},{16,8},{24,0},{1,25},{9,17},{17,9},{25,1},{2,26},{10... | collective-permute-start | bytes 1572872 | tf_op jit(solution)/shard_map/ppermute | solution.py:357
  466.0 41.2 %all-to-all-start.3 = ((bf16[256,8,128]{2,0,1:T(8,128)(2,1)}), bf16[256,8,128]{2,0,1:T(8,128)(2,1)S(1)}, u32[]{:S(2)}, u32[]{:S(2)}) async-start(bf16[256,8,128]{2,0,1:T(8,128)(2,1)} %bitcast.366), calls=%async_computation.5 | async-start | bytes 1048576 | tf_op jit(solution)/shard_map/all_to_all | solution.py:553
  472.1 203.4 %reduce-scatter.14.cloned.1.call-start = ((), (), s32[]{:S(2)}) async-start(), calls=%async_computation.20 | async-start | bytes 1179648 | tf_op jit(solution)/shard_map/reduce_scatter | solution.py:465
  499.4 177.6 %reduce-scatter.10.cloned.1.call-start = ((), (), s32[]{:S(2)}) async-start(), calls=%async_computation.18 | async-start | bytes 4718592 | tf_op jit(solution)/shard_map/reduce_scatter | solution.py:465
  542.6 36.2 %collective-permute-start.29 = (bf16[2,4,4,32,1024]{4,3,2,1,0:T(8,128)(2,1)}, bf16[2,4,4,32,1024]{4,3,2,1,0:T(8,128)(2,1)}, u32[]{:S(2)}, u32[]{:S(2)}) collective-permute-start(bf16[2,4,4,32,1024]{4,3,2,1,0:T(8,128)(2,1)} %fusion.15), channel_id=1, source_target_pairs={{0,1},{1,0},{2,3},{3,2},{4,5},{5,4},{6,7},{7,6},{8,9},{9,8},{10,11... | collective-permute-start | bytes 6291464 | tf_op jit(solution)/shard_map/ppermute | solution.py:384
  (94 other events, 1278.6 us)
Sparse Core Ops, SparseCore 0:
  10.3 78.4 all-gather.4
  99.2 45.4 all-gather.6
  190.5 56.0 all-gather.8
  248.0 45.0 all-gather.10
  315.8 46.1 reduce-scatter.7
  364.1 56.5 reduce-scatter.5
  455.7 41.1 reduce-scatter.11
  499.6 30.0 reduce-scatter.13
  536.4 53.1 reduce-scatter.9

commit v3 on v2

--- a/solution.py
+++ b/solution.py
@@ -1,3 +1,5 @@
+import functools
+
 import jax
 import jax.numpy as jnp
 from jax import lax
@@ -15,6 +17,8 @@
 NEGATIVE = -1e30
 SCALE = HD**-0.5
 BLOCK = 512
+GELU = 0.7978845608028654
+LITTLE = pl.CostEstimate(flops=1000, bytes_accessed=1000, transcendentals=0)
 
 
 def norm_apply(rows, gain, shift):
@@ -46,6 +50,10 @@
 
 def dot_tn(left, right):
     return lax.dot_general(left, right, (((0,), (0,)), ((), ())), preferred_element_type=jnp.float32)
+
+
+def after(value, *earlier):
+    return lax.optimization_barrier((value, earlier))[0]
 
 
 def head_halves(rows, scale=None):
@@ -148,9 +156,7 @@
             jax.ShapeDtypeStruct((count, 2), jnp.float32),
         ),
         compiler_params=pltpu.CompilerParams(vmem_limit_bytes=40 * 2**20),
-        cost_estimate=pl.CostEstimate(
-            flops=4 * count * count * PAIR, bytes_accessed=8 * count * PAIR, transcendentals=count * count
-        ),
+        cost_estimate=LITTLE,
     )(block_ends(segments, rows), qkv, qkv, qkv, col, row)
 
 
@@ -255,9 +261,7 @@
         grid_spec=grid_spec,
         out_shape=jax.ShapeDtypeStruct((count, 3 * PAIR), jnp.bfloat16),
         compiler_params=pltpu.CompilerParams(vmem_limit_bytes=40 * 2**20),
-        cost_estimate=pl.CostEstimate(
-            flops=10 * count * count * PAIR, bytes_accessed=14 * count * PAIR, transcendentals=count * count
-        ),
+        cost_estimate=LITTLE,
     )(block_ends(segments, rows), qkv, qkv, qkv, grad_att, lse, delta, col, row)
 
 
@@ -291,9 +295,7 @@
         cross_forward_kernel,
         grid_spec=grid_spec,
         out_shape=jax.ShapeDtypeStruct((count, D), jnp.bfloat16),
-        cost_estimate=pl.CostEstimate(
-            flops=8 * count * states * D, bytes_accessed=4 * count * D + 4 * states * D, transcendentals=count * states * H
-        ),
+        cost_estimate=LITTLE,
     )(length, queries, memory)
 
 
@@ -346,10 +348,130 @@
             jax.ShapeDtypeStruct((count, D), jnp.bfloat16),
             jax.ShapeDtypeStruct((states * (D // PAIR), 2 * PAIR), jnp.bfloat16),
         ),
-        cost_estimate=pl.CostEstimate(
-            flops=20 * count * states * D, bytes_accessed=6 * count * D + 8 * states * D, transcendentals=count * states * H
+        cost_estimate=LITTLE,
+    )(length, queries, memory, grads)
+
+
+def front_kernel(x_ref, e_ref, gain, shift, qkv_w, qkv_b, mem_w, mem_b, one_ref, qkv_ref, enc_ref, mem_ref):
+    rows = x_ref[0].astype(jnp.float32)
+    centered = rows - jnp.mean(rows, axis=-1, keepdims=True)
+    inverse = lax.rsqrt(jnp.mean(centered * centered, axis=-1, keepdims=True) + EPS)
+    one = low(centered * inverse * gain[...] + shift[...])
+    one_ref[...] = one
+    qkv_ref[...] = low(dot(one, qkv_w[...]) + qkv_b[...])
+    enc_ref[...] = e_ref[0]
+    mem_ref[...] = low(dot(e_ref[0], mem_w[...]) + mem_b[...])
+
+
+def front(rows_all, row_count, gain, shift, qkv_w, qkv_b, mem_w, mem_b):
+    span, both, _ = rows_all.shape
+    enc_rows = both - row_count
+    whole = lambda i: (0, 0)
+    return pl.pallas_call(
+        front_kernel,
+        grid=(span,),
+        in_specs=[
+            pl.BlockSpec((1, row_count, D), lambda i: (i, 0, 0)),
+            pl.BlockSpec((1, enc_rows, D), lambda i: (i, row_count // enc_rows, 0)),
+            pl.BlockSpec((1, D), whole),
+            pl.BlockSpec((1, D), whole),
+            pl.BlockSpec(qkv_w.shape, whole),
+            pl.BlockSpec((1, qkv_w.shape[1]), whole),
+            pl.BlockSpec(mem_w.shape, whole),
+            pl.BlockSpec((1, mem_w.shape[1]), whole),
+        ],
+        out_specs=[
+            pl.BlockSpec((row_count, D), lambda i: (i, 0)),
+            pl.BlockSpec((row_count, qkv_w.shape[1]), lambda i: (i, 0)),
+            pl.BlockSpec((enc_rows, D), lambda i: (i, 0)),
+            pl.BlockSpec((enc_rows, mem_w.shape[1]), lambda i: (i, 0)),
+        ],
+        out_shape=(
+            jax.ShapeDtypeStruct((span * row_count, D), jnp.bfloat16),
+            jax.ShapeDtypeStruct((span * row_count, qkv_w.shape[1]), jnp.bfloat16),
+            jax.ShapeDtypeStruct((span * enc_rows, D), jnp.bfloat16),
+            jax.ShapeDtypeStruct((span * enc_rows, mem_w.shape[1]), jnp.bfloat16),
         ),
-    )(length, queries, memory, grads)
+        compiler_params=pltpu.CompilerParams(vmem_limit_bytes=32 * 2**20),
+        cost_estimate=LITTLE,
+    )(rows_all, rows_all, gain[None], shift[None], qkv_w, qkv_b[None], mem_w, mem_b[None])
+
+
+def gain_kernel(x_ref, g_ref, out_ref):
+    rows = x_ref[0].astype(jnp.float32)
+    centered = rows - jnp.mean(rows, axis=-1, keepdims=True)
+    inverse = lax.rsqrt(jnp.mean(centered * centered, axis=-1, keepdims=True) + EPS)
+    grads = g_ref[...].astype(jnp.float32)
+
+    @pl.when(pl.program_id(0) == 0)
+    def _():
+        out_ref[...] = jnp.zeros_like(out_ref)
+
+    out_ref[0:1, :] += jnp.sum(grads * (centered * inverse), axis=0, keepdims=True)
+    out_ref[1:2, :] += jnp.sum(grads, axis=0, keepdims=True)
+
+
+def gain_sums(rows_all, row_count, grads):
+    span = rows_all.shape[0]
+    return pl.pallas_call(
+        gain_kernel,
+        grid=(span,),
+        in_specs=[
+            pl.BlockSpec((1, row_count, D), lambda i: (i, 0, 0)),
+            pl.BlockSpec((row_count, D), lambda i: (i, 0)),
+        ],
+        out_specs=pl.BlockSpec((2, D), lambda i: (0, 0)),
+        out_shape=jax.ShapeDtypeStruct((2, D), jnp.float32),
+        cost_estimate=LITTLE,
+    )(rows_all, grads)
+
+
+def feed_kernel(x_ref, w_ref, b_ref, ga_ref, act_ref, pre_ref, in_ref, sum_ref):
+    v = dot(x_ref[...], w_ref[...]) + b_ref[...]
+    square = v * v
+    half = 0.5 + 0.5 * jnp.tanh(v * (GELU + GELU * 0.044715 * square))
+    act_ref[...] = low(v * half)
+    slope = half + (v * half) * (1.0 - half) * (2.0 * GELU + 6.0 * GELU * 0.044715 * square)
+    grad = low(ga_ref[...] * slope)
+    pre_ref[...] = grad
+    in_ref[...] = low(dot_nt(grad, w_ref[...]))
+
+    @pl.when(pl.program_id(0) == 0)
+    def _():
+        sum_ref[...] = jnp.zeros_like(sum_ref)
+
+    sum_ref[...] += jnp.sum(grad.astype(jnp.float32), axis=0, keepdims=True)
+
+
+def feed(rows, weight, bias, grad_act):
+    count, hidden = grad_act.shape
+    tile = 256
+    whole = lambda i: (0, 0)
+    block = lambda i: (i, 0)
+    return pl.pallas_call(
+        feed_kernel,
+        grid=(count // tile,),
+        in_specs=[
+            pl.BlockSpec((tile, D), block),
+            pl.BlockSpec((D, hidden), whole),
+            pl.BlockSpec((1, hidden), whole),
+            pl.BlockSpec((tile, hidden), block),
+        ],
+        out_specs=[
+            pl.BlockSpec((tile, hidden), block),
+            pl.BlockSpec((tile, hidden), block),
+            pl.BlockSpec((tile, D), block),
+            pl.BlockSpec((1, hidden), whole),
+        ],
+        out_shape=(
+            jax.ShapeDtypeStruct((count, hidden), jnp.bfloat16),
+            jax.ShapeDtypeStruct((count, hidden), jnp.bfloat16),
+            jax.ShapeDtypeStruct((count, D), jnp.bfloat16),
+            jax.ShapeDtypeStruct((1, hidden), jnp.float32),
+        ),
+        compiler_params=pltpu.CompilerParams(vmem_limit_bytes=58 * 2**20),
+        cost_estimate=LITTLE,
+    )(rows, weight, bias[None], grad_act)
 
 
 def rep_send(value, step):
@@ -357,26 +479,73 @@
     return lax.ppermute(value, "rep", [(i, i ^ step) for i in range(size)])
 
 
-def rep_gather(value, axis):
+def rep_start(value):
+    return [value] + [rep_send(value, step) for step in range(1, lax.axis_size("rep"))]
+
+
+def rep_place(parts, axis):
     size, me = lax.axis_size("rep"), lax.axis_index("rep")
-    parts = [value] + [rep_send(value, step) for step in range(1, size)]
-    shape = value.shape[:axis] + (size,) + value.shape[axis:]
-    out = jnp.zeros(shape, value.dtype)
+    value = parts[0]
+    out = jnp.zeros(value.shape[:axis] + (size,) + value.shape[axis:], value.dtype)
     for step, part in enumerate(parts):
         out = lax.dynamic_update_slice_in_dim(out, jnp.expand_dims(part, axis), me ^ step, axis)
     return out
 
 
+def spread_kernel(place, *refs):
+    out_ref = refs[-1]
+    for step, part in enumerate(refs[:-1]):
+        out_ref[pl.ds(place[0] ^ step, 1)] = part[...].astype(out_ref.dtype)[None]
+
+
+def spread(parts, first, last, dtype):
+    size, columns = len(parts), parts[0].shape[1]
+    rows = last - first
+    if rows % 32 or first % rows or parts[0].shape[0] % 16:
+        return rep_place([part[first:last] for part in parts], 0).astype(dtype)
+    tile = rows // 2
+    grid_spec = pltpu.PrefetchScalarGridSpec(
+        num_scalar_prefetch=1,
+        grid=(2,),
+        in_specs=[pl.BlockSpec((tile, columns), lambda i, e: (first // tile + i, 0))] * size,
+        out_specs=pl.BlockSpec((size, tile, columns), lambda i, e: (0, i, 0)),
+    )
+    return pl.pallas_call(
+        spread_kernel,
+        grid_spec=grid_spec,
+        out_shape=jax.ShapeDtypeStruct((size, rows, columns), dtype),
+        compiler_params=pltpu.CompilerParams(vmem_limit_bytes=40 * 2**20),
+        cost_estimate=LITTLE,
+    )(lax.axis_index("rep")[None], *parts)
+
+
+def rep_gather(value, axis):
+    return rep_place(rep_start(value), axis)
+
+
+def rep_swap(parts):
+    return lax.all_to_all(parts, "rep", 0, 0, tiled=True)
+
+
+def rep_split(parts, axis):
+    size, me = lax.axis_size("rep"), lax.axis_index("rep")
+    picks = [lax.dynamic_index_in_dim(parts, me ^ step, axis, keepdims=False) for step in range(size)]
+    return [picks[0]] + [rep_send(low(picks[step]), step) for step in range(1, size)]
+
+
+def sum_first(parts):
+    return low(jnp.sum(parts.astype(jnp.float32), axis=0))
+
+
+def add_up(parts):
+    total = parts[0].astype(jnp.float32)
+    for part in parts[1:]:
+        total = total + part.astype(jnp.float32)
+    return low(total)
+
+
 def rep_reduce(parts, axis):
-    size, me = lax.axis_size("rep"), lax.axis_index("rep")
-
-    def pick(step):
-        return lax.dynamic_index_in_dim(parts, me ^ step, axis, keepdims=False)
-
-    total = pick(0).astype(jnp.float32)
-    for step in range(1, size):
-        total = total + rep_send(low(pick(step)), step).astype(jnp.float32)
-    return low(total)
+    return add_up(rep_split(parts, axis))
 
 
 def core_send(value):
@@ -384,43 +553,218 @@
     return lax.ppermute(value, "shard", [(i, i ^ 1) for i in range(size)])
 
 
-def line_send(value, step):
+def line_send(value, step, group=None):
     size = lax.axis_size("shard")
-    return lax.ppermute(value, "shard", [(i, (i + 2 * step) % size) for i in range(size)])
-
-
-def gather_weights(piece):
+    group = group or size
+    route = [(i, i // group * group + (i + 2 * step) % group) for i in range(size)]
+    return lax.ppermute(value, "shard", route)
+
+
+def line_scatter_start(value, group=None):
+    group = group or lax.axis_size("shard")
+    core = lax.axis_index("shard") % 2
+    value = value.reshape((group // 2, 2, value.shape[0] // group) + value.shape[1:])
+    mine = lax.dynamic_index_in_dim(value, core, 1, keepdims=False)
+    theirs = lax.dynamic_index_in_dim(value, 1 - core, 1, keepdims=False)
+    return [mine, core_send(theirs)]
+
+
+def line_scatter_middle(both, group=None):
+    group = group or lax.axis_size("shard")
+    chips = group // 2
+    chip = lax.axis_index("shard") % group // 2
+    line = add_up(both)
+    parts = [lax.dynamic_index_in_dim(line, (chip + step) % chips, 0, keepdims=False) for step in range(chips)]
+    return [parts[0]] + [line_send(parts[step], step, group) for step in range(1, chips)]
+
+
+def columns_kernel(place, *refs):
+    out_ref = refs[-1]
+    rows = out_ref.shape[1]
+    for step, part in enumerate(refs[:-1]):
+        for block in range(part.shape[0] // rows):
+            wide = part[block * rows : (block + 1) * rows, :].astype(out_ref.dtype)
+            out_ref[pl.ds(place[0] ^ step, 1), :, block * D : (block + 1) * D] = wide[None]
+
+
+def spread_columns(parts, first, blocks, rows):
+    size, me = len(parts), lax.axis_index("rep")
+    if rows % 16:
+        parts = [part[first:].reshape(blocks, rows, -1).transpose(1, 0, 2).reshape(rows, -1) for part in parts]
+        return rep_place(parts, 0).astype(jnp.float32).reshape(size * rows, -1)
+    halves = 2
+    taken = blocks * rows // halves
+    grid_spec = pltpu.PrefetchScalarGridSpec(
+        num_scalar_prefetch=1,
+        grid=(halves,),
+        in_specs=[pl.BlockSpec((taken, D), lambda i, e: (first // taken + i, 0))] * size,
+        out_specs=pl.BlockSpec((size, rows, blocks * D // halves), lambda i, e: (0, 0, i)),
+    )
+    out = pl.pallas_call(
+        columns_kernel,
+        grid_spec=grid_spec,
+        out_shape=jax.ShapeDtypeStruct((size, rows, blocks * D), jnp.float32),
+        compiler_params=pltpu.CompilerParams(vmem_limit_bytes=40 * 2**20),
+        cost_estimate=LITTLE,
+    )(me[None], *parts)
+    return out.reshape(size * rows, blocks * D)
+
+
+def heads_kernel(span, place, *refs):
+    qkv_ref, memory_ref = refs[-2:]
+    rows, width = qkv_ref.shape[1], D // span
+    for step, part in enumerate(refs[:-2]):
+        take = pl.ds(place[0] ^ step, 1)
+        for block in range(span):
+            wide = part[block * rows : (block + 1) * rows, :].astype(jnp.float32)[None]
+            for kind in range(5):
+                out, at = (qkv_ref, kind) if kind < 3 else (memory_ref, kind - 3)
+                columns = slice(at * D + block * width, at * D + (block + 1) * width)
+                out[take, :, columns] = wide[:, :, kind * width : (kind + 1) * width]
+
+
+def spread_heads(parts, span, rows, width):
+    size, me = len(parts), lax.axis_index("rep")
+    if rows % 16:
+        full = rep_place([part[: span * rows].reshape(span, rows, 5, width) for part in parts], 0)
+        full = full.transpose(0, 2, 3, 1, 4).reshape(size * rows, 5 * D).astype(jnp.float32)
+        return full[:, : 3 * D], full[:, 3 * D :]
+    grid_spec = pltpu.PrefetchScalarGridSpec(
+        num_scalar_prefetch=1,
+        grid=(1,),
+        in_specs=[pl.BlockSpec((span * rows, 5 * width), lambda i, e: (0, 0))] * size,
+        out_specs=[
+            pl.BlockSpec((size, rows, 3 * D), lambda i, e: (0, 0, 0)),
+            pl.BlockSpec((size, rows, 2 * D), lambda i, e: (0, 0, 0)),
+        ],
+    )
+    qkv, memory = pl.pallas_call(
+        functools.partial(heads_kernel, span),
+        grid_spec=grid_spec,
+        out_shape=(
+            jax.ShapeDtypeStruct((size, rows, 3 * D), jnp.float32),
+            jax.ShapeDtypeStruct((size, rows, 2 * D), jnp.float32),
+        ),
+        compiler_params=pltpu.CompilerParams(vmem_limit_bytes=40 * 2**20),
+        cost_estimate=LITTLE,
+    )(me[None], *parts)
+    return qkv.reshape(size * rows, 3 * D), memory.reshape(size * rows, 2 * D)
+
+
+def weight_line(piece):
     kinds, rows, columns = piece.shape
     chips = lax.axis_size("shard") // 2
-    chip, core = lax.axis_index("shard") // 2, lax.axis_index("shard") % 2
+    chip = lax.axis_index("shard") // 2
     line = jnp.zeros((kinds, chips, rows, columns), piece.dtype)
     for step in range(chips):
         part = line_send(piece, step) if step else piece
         line = lax.dynamic_update_slice_in_dim(line, part[:, None], (chip - step) % chips, 1)
-    plane = rep_gather(line, 2)
-    other = core_send(plane)
-    full = jnp.zeros((kinds, chips, 2) + plane.shape[2:], piece.dtype)
-    full = lax.dynamic_update_slice_in_dim(full, plane[:, :, None], core, 2)
-    full = lax.dynamic_update_slice_in_dim(full, other[:, :, None], 1 - core, 2)
-    return full.reshape(kinds, D, columns)
-
-
-def reduce_weights(grads):
-    kinds = len(grads)
-    size = lax.axis_size("rep")
+    return line
+
+
+def join_kernel(place, *refs):
+    outs = refs[-3:]
+    parts = refs[:-3]
+    size = len(parts) // 2
+    for core in range(2):
+        side = place[1] ^ core
+        for step in range(size):
+            for kind in range(3):
+                outs[kind][0, pl.ds(side, 1), pl.ds(place[0] ^ step, 1)] = parts[core * size + step][kind][None]
+
+
+def weight_join(mine, other):
+    size = len(mine)
+    _, chips, rows, _ = mine[0].shape
+    core = lax.axis_index("shard") % 2
+    if rows % 16:
+        first = core == 0
+        plane, next_plane = rep_place(mine, 2), rep_place(other, 2)
+        low_core, high_core = jnp.where(first, plane, next_plane), jnp.where(first, next_plane, plane)
+        full = jnp.stack([low_core, high_core], axis=2).reshape(3, D, D)
+        return full[0], full[1], full[2]
+    grid_spec = pltpu.PrefetchScalarGridSpec(
+        num_scalar_prefetch=1,
+        grid=(chips,),
+        in_specs=[pl.BlockSpec((3, 1, rows, D), lambda i, e: (0, i, 0, 0))] * (2 * size),
+        out_specs=[pl.BlockSpec((1, 2, size, rows, D), lambda i, e: (i, 0, 0, 0, 0))] * 3,
+    )
+    outs = pl.pallas_call(
+        join_kernel,
+        grid_spec=grid_spec,
+        out_shape=(jax.ShapeDtypeStruct((chips, 2, size, rows, D), jnp.bfloat16),) * 3,
+        compiler_params=pltpu.CompilerParams(vmem_limit_bytes=40 * 2**20),
+        cost_estimate=LITTLE,
+    )(jnp.stack([lax.axis_index("rep"), core]), *mine, *other)
+    return tuple(out.reshape(D, D) for out in outs)
+
+
+def plain_kernel(core, a_ref, b_ref, c_ref, ga_ref, gb_ref, gc_ref, mine_ref, theirs_ref):
+    width = a_ref.shape[1] // 2
+    for kind, (left, right) in enumerate(((a_ref, ga_ref), (b_ref, gb_ref), (c_ref, gc_ref))):
+        for side, out in enumerate((mine_ref, theirs_ref)):
+            place = pl.ds(pl.multiple_of((core[0] ^ side) * width, width), width)
+            out[kind, 0] = low(dot_tn(left[:, place], right[...])).reshape(out.shape[2:])
+
+
+def plain_grads(lefts, rights):
+    size, chips = lax.axis_size("rep"), lax.axis_size("shard") // 2
+    core = lax.axis_index("shard") % 2
+    rows = D // (2 * chips * size)
+    if rows % 16:
+        stack = jnp.stack([low(dot_tn(left, right)) for left, right in zip(lefts, rights)])
+        stack = stack.reshape(3, chips, 2, size, rows, D)
+        return [lax.dynamic_index_in_dim(stack, core ^ side, 2, keepdims=False) for side in range(2)]
+    count = lefts[0].shape[0]
+    grid_spec = pltpu.PrefetchScalarGridSpec(
+        num_scalar_prefetch=1,
+        grid=(chips,),
+        in_specs=[pl.BlockSpec((count, D // chips), lambda i, e: (0, i))] * 3
+        + [pl.BlockSpec((count, D), lambda i, e: (0, 0))] * 3,
+        out_specs=[pl.BlockSpec((3, 1, size, rows, D), lambda i, e: (0, i, 0, 0, 0))] * 2,
+    )
+    return pl.pallas_call(
+        plain_kernel,
+        grid_spec=grid_spec,
+        out_shape=(jax.ShapeDtypeStruct((3, chips, size, rows, D), jnp.bfloat16),) * 2,
+        compiler_params=pltpu.CompilerParams(vmem_limit_bytes=40 * 2**20),
+        cost_estimate=LITTLE,
+    )(core[None], *lefts, *rights)
+
+
+def split_kernel(place, mine_ref, other_ref, *outs):
+    for step, out in enumerate(outs):
+        take = pl.ds(place[0] ^ step, 1)
+        total = mine_ref[:, 0, take].astype(jnp.float32) + other_ref[:, 0, take].astype(jnp.float32)
+        out[...] = low(total)
+
+
+def core_sum_split(mine, other):
+    kinds, chips, size, rows, _ = mine.shape
+    if rows % 16:
+        total = add_up([mine, other])
+        me = lax.axis_index("rep")
+        return [lax.dynamic_index_in_dim(total, me ^ step, 2, keepdims=False) for step in range(size)]
+    grid_spec = pltpu.PrefetchScalarGridSpec(
+        num_scalar_prefetch=1,
+        grid=(chips,),
+        in_specs=[pl.BlockSpec((kinds, 1, size, rows, D), lambda i, e: (0, i, 0, 0, 0))] * 2,
+        out_specs=[pl.BlockSpec((kinds, 1, rows, D), lambda i, e: (0, i, 0, 0))] * size,
+    )
+    return pl.pallas_call(
+        split_kernel,
+        grid_spec=grid_spec,
+        out_shape=(jax.ShapeDtypeStruct((kinds, chips, rows, D), jnp.bfloat16),) * size,
+        compiler_params=pltpu.CompilerParams(vmem_limit_bytes=40 * 2**20),
+        cost_estimate=LITTLE,
+    )(lax.axis_index("rep")[None], mine, other)
+
+
+def reduce_line(line):
     chips = lax.axis_size("shard") // 2
-    chip, core = lax.axis_index("shard") // 2, lax.axis_index("shard") % 2
-    rows = D // (2 * chips * size)
-    stack = jnp.stack([low(g) for g in grads]).reshape(kinds, chips, 2, size, rows, D)
-    mine = lax.dynamic_index_in_dim(stack, core, 2, keepdims=False)
-    theirs = lax.dynamic_index_in_dim(stack, 1 - core, 2, keepdims=False)
-    both = low(mine.astype(jnp.float32) + core_send(theirs).astype(jnp.float32))
-    line = rep_reduce(both, 2)
-    total = lax.dynamic_index_in_dim(line, chip, 1, keepdims=False).astype(jnp.float32)
-    for step in range(1, chips):
-        part = lax.dynamic_index_in_dim(line, (chip + step) % chips, 1, keepdims=False)
-        total = total + line_send(part, step).astype(jnp.float32)
-    return rep_gather(low(total), 1).reshape(kinds, size * rows, D).astype(jnp.float32)
+    chip = lax.axis_index("shard") // 2
+    parts = [lax.dynamic_index_in_dim(line, (chip + step) % chips, 1, keepdims=False) for step in range(chips)]
+    return [parts[0]] + [line_send(parts[step], step) for step in range(1, chips)]
 
 
 def shards(
@@ -475,38 +819,49 @@
         return blocks.reshape(span, part_rows, kinds * width)
 
     rows_all = gather(jnp.concatenate([tokens, enc_states], axis=0), groups)
-    rows_all = rows_all.reshape(span, row_count + enc_rows, D)
     blocks = jnp.concatenate([by_pairs(own_part(self_qkv), 3), by_pairs(own_part(cross_memory), 2)], axis=2)
     blocks = jnp.tile(blocks, (count // span, 1, 1))
     small = jnp.concatenate([norm_gain, norm_bias, proj_bias], axis=0)
     small_count = small.shape[0]
-    small = jnp.pad(small, ((0, 16 - small_count), (0, 5 * width - shard_width)))
+    small_rows = -(-small.size // (5 * width))
+    small = jnp.pad(small.reshape(-1), (0, small_rows * 5 * width - small.size)).reshape(small_rows, 5 * width)
     blocks = jnp.concatenate([blocks, jnp.broadcast_to(small, (count,) + small.shape)], axis=1)
     swapped = swap(blocks)
-    small_all = swapped[:, part_rows : part_rows + small_count, :shard_width].astype(jnp.float32)
-    small_all = small_all.transpose(1, 0, 2).reshape(small_count, D)
+    small_all = swapped[:, part_rows:].reshape(count, small_rows * 5 * width)[:, : small_count * shard_width]
+    small_all = small_all.reshape(count, small_count, shard_width)
+    small_all = small_all.transpose(1, 0, 2).reshape(small_count, D).astype(jnp.float32)
     gain_rows, shift_rows, bias_rows = small_all[:3], small_all[3:6], small_all[6:]
     head_weight = rep_gather(swapped[:, :part_rows], 1).reshape(D, 5 * width)
     qkv_weight, memory_weight = head_weight[:, : 3 * width], head_weight[:, 3 * width :]
-    plain = gather_weights(jnp.stack([own_part(self_out), own_part(cross_query), own_part(cross_out)]))
-    attn_proj, query_in, cross_proj = plain[0], plain[1], plain[2]
+    plain_part = jnp.stack([own_part(self_out), own_part(cross_query), own_part(cross_out)])
+    plain_line = weight_line(after(plain_part, swapped))
+    rows_all, plain_line, head_weight = lax.optimization_barrier((rows_all, plain_line, head_weight))
+    plain_mine = rep_start(plain_line)
     expand_part = own_part(expand_weight).reshape(part_rows, count, hidden).transpose(1, 0, 2)
-    expand_local = rep_gather(swap(expand_part), 1).reshape(D, hidden)
-
+    expand_swapped = swap(after(expand_part, rows_all))
+    grad_all = gather(after(cotangent, rows_all))
+
+    rows_all = rows_all.reshape(span, row_count + enc_rows, D)
     seq_segments = lax.dynamic_slice_in_dim(segments, local_seq * SEQ, SEQ)
-    x_all = rows_all[:, :row_count].astype(jnp.float32)
-    input_one_all = low(norm_apply(x_all, gain_rows[0], shift_rows[0])).reshape(SEQ, D)
     own_bias = lax.dynamic_slice_in_dim(bias_rows, local_pos * width, width, axis=1)
     zero_bias = jnp.zeros((width,), jnp.float32)
-    qkv = low(dot(input_one_all, qkv_weight) + jnp.concatenate([own_bias[0], zero_bias, own_bias[1]]))
+    qkv_bias = jnp.concatenate([own_bias[0], zero_bias, own_bias[1]])
+    memory_bias = jnp.concatenate([zero_bias, own_bias[4]])
+    input_one_all, qkv, enc_all, memory_pair = front(
+        rows_all, row_count, gain_rows[0], shift_rows[0], qkv_weight, qkv_bias, memory_weight, memory_bias
+    )
     att_low, att_full, lse = self_forward(qkv, seq_segments)
+    att_low, expand_swapped = lax.optimization_barrier((att_low, expand_swapped))
     attended = lax.all_to_all(att_low, "shard", 0, 1, tiled=True, axis_index_groups=groups)
 
-    enc_all = rows_all[:, row_count:].reshape(span * enc_rows, D)
-    memory_pair = low(dot(enc_all, memory_weight) + jnp.concatenate([zero_bias, own_bias[4]]))
-    memory_all = gather(memory_pair, groups)
+    memory_all = gather(after(memory_pair, grad_all, att_low), groups)
     enc_count = lax.dynamic_slice_in_dim(enc_lengths, local_seq, 1)
-
+    plain_other = [core_send(part) for part in plain_mine]
+
+    plain_mine, plain_other = after((plain_mine, plain_other), att_low)
+    attn_proj, query_in, cross_proj = weight_join(plain_mine, plain_other)
+    attended, attn_proj, query_in, cross_proj = lax.optimization_barrier((attended, attn_proj, query_in, cross_proj))
+    expand_parts = rep_start(after(expand_swapped, attended).reshape(count * part_rows, hidden))
     residual_in = tokens.astype(jnp.float32)
     hidden_one = residual_in + dot(attended, attn_proj) + bias_rows[2]
     input_two = low(norm_apply(hidden_one, gain_rows[1], shift_rows[1]))
@@ -515,57 +870,73 @@
     hidden_two = hidden_one + dot(context, cross_proj) + bias_rows[5]
     input_three = low(norm_apply(hidden_two, gain_rows[2], shift_rows[2]))
 
-    grad_all = gather(cotangent)
-    input_three_all = gather(input_three)
-    pre_act = dot(input_three_all, expand_local) + expand_bias.astype(jnp.float32)
-    act = low(gelu_apply(pre_act))
-    grad_act = dot_nt(grad_all, shrink_weight)
-    grad_pre = low(jax.vjp(gelu_apply, pre_act)[1](grad_act)[0])
-    grad_in_three = scatter(low(dot_nt(grad_pre, expand_local))).astype(jnp.float32)
-    result = hidden_two + scatter(low(dot(act, shrink_weight))).astype(jnp.float32) + bias_rows[6]
-    grad_shrink = dot_tn(act, grad_all)
-    grad_expand = dot_tn(input_three_all, grad_pre)
-    grad_hidden_bias = column_sums(grad_pre)
-    total_shrink = rep_gather(rep_reduce(low(grad_shrink).reshape(size, hidden // size, D), 0), 0)
-    own_expand = swap(rep_reduce(low(grad_expand).reshape(count, size, part_rows, hidden), 1))
-    total_expand = rep_gather(own_expand.transpose(1, 0, 2).reshape(part_rows, count * hidden), 0)
+    input_three_all = gather(after(input_three, grad_all))
+    expand_parts, grad_all_now = after((expand_parts, grad_all), input_three)
+    expand_local = spread(expand_parts, 0, count * part_rows, jnp.bfloat16)
+    expand_local = expand_local.reshape(size, count, part_rows, hidden).transpose(1, 0, 2, 3).reshape(D, hidden)
+    grad_act = dot_nt(grad_all_now, shrink_weight)
+    input_three_all, grad_act, expand_local = lax.optimization_barrier((input_three_all, grad_act, expand_local))
+    act, grad_pre, grad_in_three_low, hidden_sums = feed(
+        input_three_all, expand_local, expand_bias.astype(jnp.float32), grad_act
+    )
+    grad_hidden_bias = hidden_sums[0]
+    grad_in_three = scatter(grad_in_three_low)
+
+    part_hidden = hidden // size
+    grad_expand = low(dot_tn(input_three_all, grad_pre)).reshape(count, size, part_rows, hidden)
+    expand_grad_parts = rep_split(grad_expand, 1)
+    act_late = after(act, grad_expand)
+    grad_shrink = low(dot_tn(act_late, grad_all)).reshape(size, part_hidden, D)
+    shrink_parts = rep_split(grad_shrink, 0)
+    result_part = low(dot(after(act, grad_shrink), shrink_weight))
+    expand_sum = add_up(expand_grad_parts)
+    grad_in_three, shrink_parts[0], expand_sum, result_part = lax.optimization_barrier(
+        (grad_in_three, shrink_parts[0], expand_sum, result_part)
+    )
+    own_expand = swap(expand_sum)
+    result_sum = scatter(result_part)
+    grad_in_three = grad_in_three.astype(jnp.float32)
 
     grad_out = cotangent.astype(jnp.float32)
     norm_three = jax.vjp(norm_apply, hidden_two, gain_rows[2], shift_rows[2])[1](grad_in_three)
     grad_two = grad_out + norm_three[0]
     grad_two_low = low(grad_two)
-    grad_cross_proj = dot_tn(context, grad_two_low)
     grad_context = low(dot_nt(grad_two_low, cross_proj))
     grad_cross_q, memory_part = cross_backward(cross_q, memory_all, grad_context, enc_count)
     mem_grads = scatter(memory_part, groups)
-    grad_memory = dot_tn(enc_all, mem_grads)
-    grad_enc = scatter(low(dot_nt(mem_grads, memory_weight)), groups).astype(jnp.float32)
-    grad_query_in = dot_tn(input_two, grad_cross_q)
     grad_in_two = dot_nt(grad_cross_q, query_in)
     norm_two = jax.vjp(norm_apply, hidden_one, gain_rows[1], shift_rows[1])[1](grad_in_two)
     grad_one = grad_two + norm_two[0]
     grad_one_low = low(grad_one)
-    grad_attn_proj = dot_tn(attended, grad_one_low)
     grad_attn = low(dot_nt(grad_one_low, attn_proj))
-    total_query, total_cross = reduce_weights([grad_query_in, grad_cross_proj])
-    (total_proj,) = reduce_weights([grad_attn_proj])
-
+    shrink_sum = add_up(after(shrink_parts, grad_cross_q))
+    own_expand = own_expand.reshape(part_hidden, D)
+    own_feed = jnp.concatenate([shrink_sum, own_expand], axis=0)
+    grad_attn, own_feed = lax.optimization_barrier((grad_attn, own_feed))
     grad_att_heads = lax.all_to_all(grad_attn, "shard", 1, 0, tiled=True, axis_index_groups=groups)
+    feed_gather = rep_start(own_feed)
+
+    lefts, rights = after(((attended, input_two, context), (grad_one_low, grad_cross_q, grad_two_low)), grad_attn)
+    plain_own, plain_theirs = plain_grads(lefts, rights)
+    plain_theirs = core_send(plain_theirs)
+    grad_att_heads, plain_own = lax.optimization_barrier((grad_att_heads, plain_own))
+
     delta = jnp.sum((grad_att_heads.astype(jnp.float32) * att_full).reshape(SEQ, 2, HD), axis=-1).T
+    plain_rep = core_sum_split(*after((plain_own, plain_theirs), delta))
+    delta, plain_rep = lax.optimization_barrier((delta, list(plain_rep)))
+    plain_rep = [plain_rep[0]] + [rep_send(plain_rep[step], step) for step in range(1, size)]
     grad_qkv = self_backward(qkv, grad_att_heads, lse.T, delta, seq_segments)
-    grad_in_one = scatter(low(dot_nt(grad_qkv, qkv_weight)), groups).astype(jnp.float32)
-    grad_attn_in = dot_tn(input_one_all, grad_qkv)
-    norm_one = jax.vjp(norm_apply, residual_in, gain_rows[0], shift_rows[0])[1](grad_in_one)
-    grad_tokens = grad_one + norm_one[0]
-
+    grad_in_one_low = low(dot_nt(grad_qkv, qkv_weight))
+    grad_in_one = scatter(grad_in_one_low, groups)
+
+    input_one_late, mem_grads_late, grad_qkv_late, rows_late = after(
+        (input_one_all, mem_grads, grad_qkv, rows_all), grad_in_one_low
+    )
+    grad_attn_in = dot_tn(input_one_late, grad_qkv_late)
+    grad_memory = dot_tn(enc_all, mem_grads_late)
     heads_grad = low(jnp.concatenate([grad_attn_in, grad_memory], axis=1))
-    own_heads = swap(rep_reduce(heads_grad.reshape(count, size, part_rows, 5 * width), 1))
-    own_heads = own_heads.reshape(count // span, span, part_rows, 5 * width)
-    own_heads = own_heads[0] if count == span else low(jnp.sum(own_heads.astype(jnp.float32), axis=0))
-    total_heads = rep_gather(own_heads.transpose(1, 0, 2), 0).reshape(weight_rows, span, 5, width)
-    total_heads = total_heads.transpose(0, 2, 1, 3).reshape(weight_rows, 5 * D).astype(jnp.float32)
-
-    qkv_sums = column_sums(grad_qkv)
+    gain_shift = gain_sums(rows_late, row_count, grad_in_one_low)
+    qkv_sums = column_sums(grad_qkv_late)
     zero_row = jnp.zeros((D,), jnp.float32)
 
     def at_own(values):
@@ -573,48 +944,78 @@
 
     small_grads = jnp.stack(
         [
-            norm_one[1],
+            gain_shift[0],
             norm_two[1],
             norm_three[1],
-            norm_one[2],
+            gain_shift[1],
             norm_two[2],
             norm_three[2],
             at_own(qkv_sums[:width]),
             at_own(qkv_sums[2 * width :]),
             column_sums(grad_one_low),
             column_sums(grad_cross_q),
-            at_own(column_sums(mem_grads)[width:]),
+            at_own(column_sums(mem_grads_late)[width:]),
             column_sums(grad_two_low),
             column_sums(cotangent),
         ]
     )
     small_grads = small_grads.reshape(small_count, count, shard_width).transpose(1, 0, 2)
-    hidden_rows = hidden // shard_width
-    hidden_grads = jnp.zeros((count, hidden_rows, shard_width), jnp.float32)
-    hidden_grads = lax.dynamic_update_slice_in_dim(
-        hidden_grads, grad_hidden_bias.reshape(1, hidden_rows, shard_width), shard_pos, 0
-    )
+    small_grads = small_grads.reshape(count, small_count * shard_width)
+    hidden_grads = jnp.zeros((count, hidden), jnp.float32)
+    hidden_grads = lax.dynamic_update_slice_in_dim(hidden_grads, grad_hidden_bias[None], shard_pos, 0)
     small_grads = low(jnp.concatenate([small_grads, hidden_grads], axis=1))
-    small_grads = jnp.broadcast_to(small_grads, (size,) + small_grads.shape)
-    small_grads = small_grads.reshape((size * count,) + small_grads.shape[2:])
-    small_grads = lax.all_to_all(small_grads, ("rep", "shard"), 0, 0, tiled=True)
-    total_small = jnp.sum(small_grads.astype(jnp.float32), axis=0)
+    small_size = small_grads.shape[1]
+    extra = -(-small_size // (5 * width))
+    small_grads = jnp.pad(small_grads, ((0, 0), (0, extra * 5 * width - small_size)))
+    small_grads = small_grads.reshape(count, extra, 5 * width)
+    heads_parts = heads_grad.reshape(count, size, part_rows, 5 * width).transpose(1, 0, 2, 3)
+    heads_sum = sum_first(rep_swap(heads_parts))
+    own_heads = swap(jnp.concatenate([heads_sum, small_grads], axis=1))
+    own_small = sum_first(own_heads[:, part_rows:])
+    own_heads = own_heads[:, :part_rows].reshape(count // span, span, part_rows, 5 * width)
+    own_heads = own_heads[0] if count == span else sum_first(own_heads)
+    heads_gather = rep_start(jnp.concatenate([own_heads.reshape(span * part_rows, 5 * width), own_small], axis=0))
+
+    plain_line_parts = reduce_line(add_up(after(plain_rep, grad_in_one_low)))
+    own_plain = add_up(plain_line_parts).reshape(3 * part_rows, D)
+    plain_gather = rep_start(own_plain)
+    enc_parts = line_scatter_start(low(dot_nt(mem_grads_late, memory_weight)), span)
+    grad_enc = add_up(line_scatter_middle(enc_parts, span)).astype(jnp.float32)
+    result = hidden_two + after(result_sum, grad_in_one_low).astype(jnp.float32) + bias_rows[6]
+
+    feed_gather = after(feed_gather, heads_grad)
+    total_shrink = spread(feed_gather, 0, part_hidden, jnp.float32)
+    total_expand = spread_columns(feed_gather, part_hidden, count, part_rows)
+    total_plain = [
+        spread(plain_gather, kind * part_rows, (kind + 1) * part_rows, jnp.float32).reshape(weight_rows, D)
+        for kind in range(3)
+    ]
+    total_proj, total_query, total_cross = total_plain
+    total_small = sum(part[span * part_rows :].astype(jnp.float32) for part in heads_gather)
+    total_small = total_small.reshape(-1)[:small_size]
+    total_hidden_bias = total_small[small_count * shard_width :]
+    total_small = total_small[: small_count * shard_width].reshape(small_count, shard_width)
+    total_qkv, total_memory = spread_heads(heads_gather, span, part_rows, width)
+
+    grad_in_one = grad_in_one.astype(jnp.float32)
+    norm_one = jax.vjp(lambda rows: norm_apply(rows, gain_rows[0], shift_rows[0]), residual_in)[1](grad_in_one)
+    grad_tokens = grad_one + norm_one[0]
 
     return (
         low(result),
         grad_tokens,
         grad_enc,
-        total_heads[:, : 3 * D],
+        total_qkv,
         total_proj,
         total_query,
-        total_heads[:, 3 * D :],
+        total_memory,
         total_cross,
         total_expand.reshape(weight_rows, count * hidden).astype(jnp.float32),
         total_shrink.reshape(hidden, D).astype(jnp.float32),
         total_small[:3],
         total_small[3:6],
-        total_small[6:small_count],
-        total_small[small_count:].reshape(hidden),
+        total_small[6:],
+        total_hidden_bias,
     )
 
 

time: 718 us -> 609 us (0.85)
  the two profiles are of different devices: /device:TPU:1 before, /device:TPU:12 now
where the time goes in v3:
time: 609 us; the launch traced here: 598 us
  waiting for transfers between devices  199 us (33%)
  Pallas kernels  121 us (20%)
  starting transfers between devices  92.9 us (15%)
  local copies, waits for them, and re-layouts  68.8 us (11%)
  matrix products  53.9 us (9%)
  other arithmetic  46.1 us (8%)
  between operations  16.1 us (3%)
    ppermute x27, waiting for transfers between devices, rep_send(): return lax.ppermute(value, 'rep', [(i, i ^ step) for i in range(size)])  89.3 us
    ppermute x9, waiting for transfers between devices, line_send(): return lax.ppermute(value, 'shard', route)  45 us
    unnamed x151, local copies, waits for them, and re-layouts  34.3 us
    ppermute x27, starting transfers between devices, rep_send(): return lax.ppermute(value, 'rep', [(i, i ^ step) for i in range(size)])  32 us
    all_to_all x4, starting transfers between devices, swap(): return lax.all_to_all(value, 'shard', 0, 0, tiled=True)  25.9 us
    dot_general x4, matrix products, dot_tn(): lax.dot_general(left, right, (((0,), (0,)), ((), ())), preferred_element_...  21.1 us
    dot_general x6, matrix products, dot_nt(): lax.dot_general(left, right, (((1,), (1,)), ((), ())), preferred_element_...  19.9 us
    pallas_call x1, Pallas kernels, self_backward(): pl.pallas_call(self_backward_kernel, grid_spec=grid_spec, out_shape=jax.S...  19.2 us
  transfers between devices with their start and end apart: 57, of which 21 were waited for; matrix products, arithmetic and copies ran while one was open for 20% of the time, Pallas kernels for 13%

profile of v3, /device:TPU:12, one launch (start us, length us, event | category | flops | bytes accessed | tf_op | source)
XLA Modules:
  0.0 597.7 jit_solution(1930755446976208000)
XLA Ops:
  20.5 19.1 %all-to-all-done = bf16[8,35,640]{2,1,0:T(8,128)(2,1)S(1)} async-done(((bf16[8,35,640]{2,1,0:T(8,128)(2,1)}), bf16[8,35,640]{2,1,0:T(8,128)(2,1)S(1)}, u32[]{:S(2)}, u32[]{:S(2)}) %all-to-all-start) | async-done | bytes 358432 | tf_op jit(solution)/shard_map/all_to_all | solution.py:812
  51.6 27.7 %collective-permute-done = bf16[3,32,1024]{2,1,0:T(8,128)(2,1)S(1)} collective-permute-done((bf16[3,32,1024]{2,1,0:T(8,128)(2,1)S(1)}, bf16[3,32,1024]{2,1,0:T(8,128)(2,1)S(1)}, u32[]{:S(2)}, u32[]{:S(2)}) %collective-permute-start) | collective-permute-done | bytes 196640 | tf_op jit(solution)/shard_map/ppermute | solution.py:560
  107.7 7.0 %shard_map.263 = (bf16[2048,1024]{1,0:T(8,128)(2,1)S(1)}, bf16[2048,384]{1,0:T(8,128)(2,1)S(1)}, bf16[512,1024]{1,0:T(8,128)(2,1)S(1)}, bf16[512,256]{1,0:T(8,128)(2,1)}) custom-call(bf16[8,320,1024]{2,1,0:T(8,128)(2,1)S(1)} %bitcast.256, bf16[8,320,1024]{2,1,0:T(8,128)(2,1)S(1)} %bitcast.257, f32[1,1024]{1,0:T(1,128)S(1)} %bitcast.276, ...), custom_call_target="tpu_custom_call" | custom-call | flops 1000 | bytes 1000 | tf_op jit(solution)/shard_map/pallas_call | solution.py:370
  117.7 18.5 %shard_map.264 = (bf16[2048,128]{1,0:T(8,128)(2,1)S(1)}, f32[2048,128]{1,0:T(8,128)S(1)}, f32[2048,2]{1,0:T(8,128)S(1)}) custom-call(s32[2,4]{1,0:T(2,128)S(1)} %pad_add_fusion.ends, bf16[2048,384]{1,0:T(8,128)(2,1)S(1)} %get-tuple-element.110.q_ref.k_ref.v_ref, bf16[2048,384]{1,0:T(8,128)(2,1)S(1)} %get-tuple-element.110.q_ref.k_ref.v_ref, ...), custom_call_target="tpu_custom_call" | custom-call | flops 1000 | bytes 1000 | tf_op jit(solution)/shard_map/pallas_call | solution.py:150
  149.9 8.8 %all-to-all-start.2 = ((bf16[8,256,128]{2,1,0:T(8,128)(2,1)}), bf16[8,256,128]{2,1,0:T(8,128)(2,1)}, u32[]{:S(2)}, u32[]{:S(2)}) async-start(bf16[8,256,128]{2,1,0:T(8,128)(2,1)} %bitcast.269), calls=%async_computation.2 | async-start | bytes 1048576 | tf_op jit(solution)/shard_map/all_to_all | solution.py:855
  159.1 9.0 %collective-permute-done.8.refs_3_ = bf16[3,4,32,1024]{3,2,1,0:T(8,128)(2,1)} collective-permute-done((bf16[3,4,32,1024]{3,2,1,0:T(8,128)(2,1)}, bf16[3,4,32,1024]{3,2,1,0:T(8,128)(2,1)}, u32[]{:S(2)}, u32[]{:S(2)}) %collective-permute-start.8) | collective-permute-done | bytes 786464 | tf_op jit(solution)/shard_map/ppermute | solution.py:479
  168.1 16.1 %collective-permute-done.7.refs_2_ = bf16[3,4,32,1024]{3,2,1,0:T(8,128)(2,1)} collective-permute-done((bf16[3,4,32,1024]{3,2,1,0:T(8,128)(2,1)}, bf16[3,4,32,1024]{3,2,1,0:T(8,128)(2,1)}, u32[]{:S(2)}, u32[]{:S(2)}) %collective-permute-start.7) | collective-permute-done | bytes 786464 | tf_op jit(solution)/shard_map/ppermute | solution.py:479
  204.4 8.6 %shard_map.266.c_ref = bf16[256,1024]{1,0:T(8,128)(2,1)} custom-call(s32[1]{0:T(128)S(6)} %copy.124.length, bf16[256,1024]{1,0:T(8,128)(2,1)} %fusion.5.q_ref, bf16[4096,256]{1,0:T(8,128)(2,1)} %all-gather.9.cloned.1.call-done.m_ref), custom_call_target="tpu_custom_call" | custom-call | flops 1000 | bytes 1000 | tf_op jit(solution)/shard_map/pallas_call | solution.py:294
  222.0 11.8 %collective-permute-done.15.refs_3_ = bf16[256,1024]{1,0:T(8,128)(2,1)S(1)} collective-permute-done((bf16[256,1024]{1,0:T(8,128)(2,1)}, bf16[256,1024]{1,0:T(8,128)(2,1)S(1)}, u32[]{:S(2)}, u32[]{:S(2)}) %collective-permute-start.15) | collective-permute-done | bytes 524320 | tf_op jit(solution)/shard_map/ppermute | solution.py:479
  233.8 10.4 %collective-permute-done.14.refs_2_ = bf16[256,1024]{1,0:T(8,128)(2,1)S(1)} collective-permute-done((bf16[256,1024]{1,0:T(8,128)(2,1)}, bf16[256,1024]{1,0:T(8,128)(2,1)S(1)}, u32[]{:S(2)}, u32[]{:S(2)}) %collective-permute-start.14) | collective-permute-done | bytes 524320 | tf_op jit(solution)/shard_map/ppermute | solution.py:479
  248.5 7.1 %fusion.43.ga_ref = f32[2048,1024]{1,0:T(8,128)} fusion(bf16[2048,1024]{1,0:T(8,128)(2,1)S(1)} %copy-done.62, bf16[1024,1024]{1,0:T(8,128)(2,1)S(1)} %copy-done), kind=kOutput, calls=%fused_computation.177 | convolution fusion | flops 4294967296 | bytes 14680064 | tf_op jit(solution)/shard_map/dot_general | solution.py:48
  255.6 10.2 %all-gather.11.cloned.1.call-done.x_ref = bf16[2048,1024]{1,0:T(8,128)(2,1)} async-done(((bf16[256,1024]{1,0:T(8,128)(2,1)}), bf16[2048,1024]{1,0:T(8,128)(2,1)}) %all-gather.11.cloned.1.call-update) | async-done | bytes 4194320 | tf_op jit(solution)/shard_map/all_gather | solution.py:806
  265.7 18.1 %shard_map.268 = (bf16[2048,1024]{1,0:T(8,128)(2,1)}, bf16[2048,1024]{1,0:T(8,128)(2,1)}, bf16[2048,1024]{1,0:T(8,128)(2,1)}, f32[1,1024]{1,0:T(1,128)}) custom-call(bf16[2048,1024]{1,0:T(8,128)(2,1)} %all-gather.11.cloned.1.call-done.x_ref, bf16[1024,1024]{1,0:T(8,128)(2,1)} %bitcast.282, f32[1,1024]{1,0:T(1,128)} %bitcast.304, f32[2048,1024]{1,0:T(8,128)} %fusion.43.ga_ref), custom_call_target="tpu_custom_call" | custom-call | flops 1000 | bytes 1000 | tf_op jit(solution)/shard_map/pallas_call | solution.py:451
  284.4 8.2 %convolution_convert_fusion.3 = bf16[1024,1024]{1,0:T(8,128)(2,1)S(1)} fusion(bf16[2048,1024]{1,0:T(8,128)(2,1)} %all-gather.11.cloned.1.call-done.x_ref, bf16[2048,1024]{1,0:T(8,128)(2,1)} %get-tuple-element.146), kind=kOutput, calls=%fused_computation.4 | convolution fusion | flops 4296015872 | bytes 10485760 | tf_op jit(solution)/shard_map/dot_general | solution.py:52
  314.6 10.7 %collective-permute-done.18 = bf16[8,32,1024]{2,1,0:T(8,128)(2,1)} collective-permute-done((bf16[8,32,1024]{2,1,0:T(8,128)(2,1)}, bf16[8,32,1024]{2,1,0:T(8,128)(2,1)}, u32[]{:S(2)}, u32[]{:S(2)}) %collective-permute-start.18) | collective-permute-done | bytes 524320 | tf_op jit(solution)/shard_map/ppermute | solution.py:479
  336.9 14.5 %shard_map.269 = (bf16[256,1024]{1,0:T(8,128)(2,1)}, bf16[4096,256]{1,0:T(8,128)(2,1)}) custom-call(s32[1]{0:T(128)S(6)} %copy.124.length, bf16[256,1024]{1,0:T(8,128)(2,1)} %fusion.5.q_ref, bf16[4096,256]{1,0:T(8,128)(2,1)} %all-gather.9.cloned.1.call-done.m_ref, bf16[256,1024]{1,0:T(8,128)(2,1)} %convolution_convert_fusion.8.g_ref), custom_call_target="tpu_custom_call" | custom-call | flops 1000 | bytes 1000 | tf_op jit(solution)/shard_map/pallas_call | solution.py:344
  355.8 8.0 %all-to-all-start.3 = ((bf16[8,32,1024]{2,1,0:T(8,128)(2,1)}), bf16[8,32,1024]{2,1,0:T(8,128)(2,1)}, u32[]{:S(2)}, u32[]{:S(2)}) async-start(bf16[8,32,1024]{2,1,0:T(8,128)(2,1)} %fusion.15), calls=%async_computation.5 | async-start | bytes 1048576 | tf_op jit(solution)/shard_map/all_to_all | solution.py:812
  367.7 11.8 %collective-permute-done.20 = bf16[256,1024]{1,0:T(8,128)(2,1)} collective-permute-done((bf16[256,1024]{1,0:T(8,128)(2,1)}, bf16[256,1024]{1,0:T(8,128)(2,1)}, u32[]{:S(2)}, u32[]{:S(2)}) %collective-permute-start.20) | collective-permute-done | bytes 524320 | tf_op jit(solution)/shard_map/ppermute | solution.py:479
  407.3 15.1 %all-to-all-done.4 = bf16[256,8,128]{2,0,1:T(8,128)(2,1)S(1)} async-done(((bf16[256,8,128]{2,0,1:T(8,128)(2,1)}), bf16[256,8,128]{2,0,1:T(8,128)(2,1)S(1)}, u32[]{:S(2)}, u32[]{:S(2)}) %all-to-all-start.4) | async-done | bytes 524320 | tf_op jit(solution)/shard_map/all_to_all | solution.py:916
  438.7 19.2 %shard_map.272 = bf16[2048,384]{1,0:T(8,128)(2,1)S(1)} custom-call(s32[2,4]{1,0:T(2,128)S(1)} %pad_add_fusion.ends, bf16[2048,384]{1,0:T(8,128)(2,1)S(1)} %copy-done.3, bf16[2048,384]{1,0:T(8,128)(2,1)S(1)} %copy-done.3, bf16[2048,384]{1,0:T(8,128)(2,1)S(1)} %copy-done.3, bf16[2048,128]{1,0:T(8,128)(2,1)S(1)} %bitcast.260, f32[2,2048]{1,0:T(2,128)S(1)} %bitcast.273, ...), custom_call_target="tpu_custom_call" | custom-call | flops 1000 | bytes 1000 | tf_op jit(solution)/shard_map/pallas_call | solution.py:259
  471.4 9.1 %shard_map.273 = f32[2,1024]{1,0:T(2,128)} custom-call(bf16[8,320,1024]{2,1,0:T(8,128)(2,1)} %bitcast.255, bf16[2048,1024]{1,0:T(8,128)(2,1)} %convolution_convert_fusion.g_ref), custom_call_target="tpu_custom_call" | custom-call | flops 1000 | bytes 1000 | tf_op jit(solution)/shard_map/pallas_call | solution.py:416
  497.3 9.4 %all-to-all-done.5 = bf16[4,8,32,640]{3,2,1,0:T(8,128)(2,1)} async-done(((bf16[4,8,32,640]{3,2,1,0:T(8,128)(2,1)}), bf16[4,8,32,640]{3,2,1,0:T(8,128)(2,1)}, u32[]{:S(2)}, u32[]{:S(2)}) %all-to-all-start.5) | async-done | bytes 1310752 | tf_op jit(solution)/shard_map/all_to_all | solution.py:527
  522.9 17.3 %collective-permute-done.35 = bf16[3,32,1024]{2,1,0:T(8,128)(2,1)S(1)} collective-permute-done((bf16[3,32,1024]{2,1,0:T(8,128)(2,1)}, bf16[3,32,1024]{2,1,0:T(8,128)(2,1)S(1)}, u32[]{:S(2)}, u32[]{:S(2)}) %collective-permute-start.35) | collective-permute-done | bytes 196640 | tf_op jit(solution)/shard_map/ppermute | solution.py:560
  564.5 9.9 %collective-permute-done.37.refs_2_ = bf16[96,1024]{1,0:T(8,128)(2,1)S(1)} collective-permute-done((bf16[96,1024]{1,0:T(8,128)(2,1)S(1)}, bf16[96,1024]{1,0:T(8,128)(2,1)S(1)}, u32[]{:S(2)}, u32[]{:S(2)}) %collective-permute-start.37) | collective-permute-done | bytes 196640 | tf_op jit(solution)/shard_map/ppermute | solution.py:479
  (398 shorter events, 276.0 us)
Async XLA Ops:
  7.2 82.8 %all-gather.5.cloned.1.call-start = ((), (), s32[]{:S(2)}) async-start(), calls=%async_computation.11 | async-start | bytes 5898240 | tf_op jit(solution)/shard_map/all_gather | solution.py:806
  18.7 127.6 %all-gather.7.cloned.1.call-start = ((), (), s32[]{:S(2)}) async-start(), calls=%async_computation.12 | async-start | bytes 4718592 | tf_op jit(solution)/shard_map/all_gather | solution.py:806
  39.6 42.5 %collective-permute-start.2 = (bf16[3,32,1024]{2,1,0:T(8,128)(2,1)S(1)}, bf16[3,32,1024]{2,1,0:T(8,128)(2,1)S(1)}, u32[]{:S(2)}, u32[]{:S(2)}) collective-permute-start(bf16[3,32,1024]{2,1,0:T(8,128)(2,1)S(1)} %pad_maximum_fusion.6), channel_id=1, source_target_pairs={{0,6},{1,7},{2,0},{3,1},{4,2},{5,3},{6,4},{7,5},{8,14},{9,15},{10,... | collective-permute-start | bytes 589832 | tf_op jit(solution)/shard_map/ppermute | solution.py:560
  40.9 40.4 %collective-permute-start.1 = (bf16[3,32,1024]{2,1,0:T(8,128)(2,1)S(1)}, bf16[3,32,1024]{2,1,0:T(8,128)(2,1)S(1)}, u32[]{:S(2)}, u32[]{:S(2)}) collective-permute-start(bf16[3,32,1024]{2,1,0:T(8,128)(2,1)S(1)} %pad_maximum_fusion.6), channel_id=1, source_target_pairs={{0,4},{1,5},{2,6},{3,7},{4,0},{5,1},{6,2},{7,3},{8,12},{9,13},{10,... | collective-permute-start | bytes 589832 | tf_op jit(solution)/shard_map/ppermute | solution.py:560
  42.9 36.3 %collective-permute-start = (bf16[3,32,1024]{2,1,0:T(8,128)(2,1)S(1)}, bf16[3,32,1024]{2,1,0:T(8,128)(2,1)S(1)}, u32[]{:S(2)}, u32[]{:S(2)}) collective-permute-start(bf16[3,32,1024]{2,1,0:T(8,128)(2,1)S(1)} %pad_maximum_fusion.6), channel_id=1, source_target_pairs={{0,2},{1,3},{2,4},{3,5},{4,6},{5,7},{6,0},{7,1},{8,10},{9,11},{10,... | collective-permute-start | bytes 589832 | tf_op jit(solution)/shard_map/ppermute | solution.py:560
  45.9 37.7 %collective-permute-start.4 = (bf16[8,32,640]{2,1,0:T(8,128)(2,1)S(1)}, bf16[8,32,640]{2,1,0:T(8,128)(2,1)S(1)}, u32[]{:S(2)}, u32[]{:S(2)}) collective-permute-start(bf16[8,32,640]{2,1,0:T(8,128)(2,1)S(1)} %slice.198), channel_id=1, source_target_pairs={{0,16},{8,24},{16,0},{24,8},{1,17},{9,25},{17,1},{25,9},{2,18},{10... | collective-permute-start | bytes 983048 | tf_op jit(solution)/shard_map/ppermute | solution.py:479
  46.4 36.3 %collective-permute-start.3 = (bf16[8,32,640]{2,1,0:T(8,128)(2,1)S(1)}, bf16[8,32,640]{2,1,0:T(8,128)(2,1)S(1)}, u32[]{:S(2)}, u32[]{:S(2)}) collective-permute-start(bf16[8,32,640]{2,1,0:T(8,128)(2,1)S(1)} %slice.198), channel_id=1, source_target_pairs={{0,8},{8,0},{16,24},{24,16},{1,9},{9,1},{17,25},{25,17},{2,10},{10... | collective-permute-start | bytes 983048 | tf_op jit(solution)/shard_map/ppermute | solution.py:479
  95.8 44.3 %all-to-all-start.1 = ((bf16[8,32,1024]{2,1,0:T(8,128)(2,1)}), bf16[8,32,1024]{2,1,0:T(8,128)(2,1)}, u32[]{:S(2)}, u32[]{:S(2)}) async-start(bf16[8,32,1024]{2,1,0:T(8,128)(2,1)} %copy.72), calls=%async_computation.1 | async-start | bytes 1048576 | tf_op jit(solution)/shard_map/all_to_all | solution.py:812
  102.1 102.2 %all-gather.9.cloned.1.call-start = ((), (), s32[]{:S(2)}) async-start(), calls=%async_computation.13 | async-start | bytes 2359296 | tf_op jit(solution)/shard_map/all_gather | solution.py:806
  147.9 36.3 %collective-permute-start.7 = (bf16[3,4,32,1024]{3,2,1,0:T(8,128)(2,1)}, bf16[3,4,32,1024]{3,2,1,0:T(8,128)(2,1)}, u32[]{:S(2)}, u32[]{:S(2)}) collective-permute-start(bf16[3,4,32,1024]{3,2,1,0:T(8,128)(2,1)} %bitcast_dynamic-update-slice_fusion.7.refs_0_), channel_id=1, source_target_pairs={{0,16},{8,24},{16,0},{24,8},{1,17},{9,25},{17,1},{25,9},{2,18},{10... | collective-permute-start | bytes 2359304 | tf_op jit(solution)/shard_map/ppermute | solution.py:479
  149.4 34.9 %collective-permute-start.6 = (bf16[3,4,32,1024]{3,2,1,0:T(8,128)(2,1)}, bf16[3,4,32,1024]{3,2,1,0:T(8,128)(2,1)}, u32[]{:S(2)}, u32[]{:S(2)}) collective-permute-start(bf16[3,4,32,1024]{3,2,1,0:T(8,128)(2,1)} %bitcast_dynamic-update-slice_fusion.7.refs_0_), channel_id=1, source_target_pairs={{0,8},{8,0},{16,24},{24,16},{1,9},{9,1},{17,25},{25,17},{2,10},{10... | collective-permute-start | bytes 2359304 | tf_op jit(solution)/shard_map/ppermute | solution.py:479
  149.9 46.3 %all-to-all-start.2 = ((bf16[8,256,128]{2,1,0:T(8,128)(2,1)}), bf16[8,256,128]{2,1,0:T(8,128)(2,1)}, u32[]{:S(2)}, u32[]{:S(2)}) async-start(bf16[8,256,128]{2,1,0:T(8,128)(2,1)} %bitcast.269), calls=%async_computation.2 | async-start | bytes 1048576 | tf_op jit(solution)/shard_map/all_to_all | solution.py:855
  158.7 107.1 %all-gather.11.cloned.1.call-start = ((), (), s32[]{:S(2)}) async-start(), calls=%async_computation.14 | async-start | bytes 4718592 | tf_op jit(solution)/shard_map/all_gather | solution.py:806
  217.8 113.1 %reduce-scatter.5.cloned.1.call-start = ((), (), s32[]{:S(2)}) async-start(), calls=%async_computation.15 | async-start | bytes 4718592 | tf_op jit(solution)/shard_map/reduce_scatter | solution.py:809
  283.9 180.7 %reduce-scatter.11.cloned.1.call-start = ((), (), s32[]{:S(2)}) async-start(), calls=%async_computation.18 | async-start | bytes 2359296 | tf_op jit(solution)/shard_map/reduce_scatter | solution.py:809
  351.5 230.6 %reduce-scatter.7.cloned.1.call-start = ((), (), s32[]{:S(2)}) async-start(), calls=%async_computation.16 | async-start | bytes 4718592 | tf_op jit(solution)/shard_map/reduce_scatter | solution.py:809
  402.0 182.3 %reduce-scatter.9.cloned.1.call-start = ((), (), s32[]{:S(2)}) async-start(), calls=%async_computation.17 | async-start | bytes 4718592 | tf_op jit(solution)/shard_map/reduce_scatter | solution.py:809
  404.9 143.5 %collective-permute-start.41 = (bf16[512,1024]{1,0:T(8,128)(2,1)S(1)}, bf16[512,1024]{1,0:T(8,128)(2,1)}, u32[]{:S(2)}, u32[]{:S(2)}) collective-permute-start(bf16[512,1024]{1,0:T(8,128)(2,1)S(1)} %pad_maximum_fusion.1.refs_0_), channel_id=1, source_target_pairs={{0,24},{8,16},{16,8},{24,0},{1,25},{9,17},{17,9},{25,1},{2,26},{10... | collective-permute-start | bytes 3145736 | tf_op jit(solution)/shard_map/ppermute | solution.py:479
  406.5 142.0 %collective-permute-start.40 = (bf16[512,1024]{1,0:T(8,128)(2,1)S(1)}, bf16[512,1024]{1,0:T(8,128)(2,1)}, u32[]{:S(2)}, u32[]{:S(2)}) collective-permute-start(bf16[512,1024]{1,0:T(8,128)(2,1)S(1)} %pad_maximum_fusion.1.refs_0_), channel_id=1, source_target_pairs={{0,16},{8,24},{16,0},{24,8},{1,17},{9,25},{17,1},{25,9},{2,18},{10... | collective-permute-start | bytes 3145736 | tf_op jit(solution)/shard_map/ppermute | solution.py:479
  435.2 57.6 %collective-permute-start.30 = (bf16[3,4,32,1024]{3,2,1,0:T(8,128)(2,1)}, bf16[3,4,32,1024]{3,2,1,0:T(8,128)(2,1)}, u32[]{:S(2)}, u32[]{:S(2)}) collective-permute-start(bf16[3,4,32,1024]{3,2,1,0:T(8,128)(2,1)} %get-tuple-element.189), channel_id=1, source_target_pairs={{0,8},{8,0},{16,24},{24,16},{1,9},{9,1},{17,25},{25,17},{2,10},{10... | collective-permute-start | bytes 2359304 | tf_op jit(solution)/shard_map/ppermute | solution.py:479
  435.5 58.7 %collective-permute-start.31 = (bf16[3,4,32,1024]{3,2,1,0:T(8,128)(2,1)}, bf16[3,4,32,1024]{3,2,1,0:T(8,128)(2,1)}, u32[]{:S(2)}, u32[]{:S(2)}) collective-permute-start(bf16[3,4,32,1024]{3,2,1,0:T(8,128)(2,1)} %get-tuple-element.190), channel_id=1, source_target_pairs={{0,16},{8,24},{16,0},{24,8},{1,17},{9,25},{17,1},{25,9},{2,18},{10... | collective-permute-start | bytes 2359304 | tf_op jit(solution)/shard_map/ppermute | solution.py:479
  437.3 56.9 %collective-permute-start.32 = (bf16[3,4,32,1024]{3,2,1,0:T(8,128)(2,1)}, bf16[3,4,32,1024]{3,2,1,0:T(8,128)(2,1)}, u32[]{:S(2)}, u32[]{:S(2)}) collective-permute-start(bf16[3,4,32,1024]{3,2,1,0:T(8,128)(2,1)} %get-tuple-element.191), channel_id=1, source_target_pairs={{0,24},{8,16},{16,8},{24,0},{1,25},{9,17},{17,9},{25,1},{2,26},{10... | collective-permute-start | bytes 2359304 | tf_op jit(solution)/shard_map/ppermute | solution.py:479
  492.7 57.3 %collective-permute-start.39 = (bf16[512,1024]{1,0:T(8,128)(2,1)S(1)}, bf16[512,1024]{1,0:T(8,128)(2,1)S(1)}, u32[]{:S(2)}, u32[]{:S(2)}) collective-permute-start(bf16[512,1024]{1,0:T(8,128)(2,1)S(1)} %pad_maximum_fusion.1.refs_0_), channel_id=1, source_target_pairs={{0,8},{8,0},{16,24},{24,16},{1,9},{9,1},{17,25},{25,17},{2,10},{10... | collective-permute-start | bytes 3145736 | tf_op jit(solution)/shard_map/ppermute | solution.py:479
  510.8 35.7 %all-to-all-start.6 = ((bf16[8,37,640]{2,1,0:T(8,128)(2,1)}), bf16[8,37,640]{2,1,0:T(8,128)(2,1)}, u32[]{:S(2)}, u32[]{:S(2)}) async-start(bf16[8,37,640]{2,1,0:T(8,128)(2,1)} %pad_maximum_fusion.4), calls=%async_computation.10 | async-start | bytes 819200 | tf_op jit(solution)/shard_map/all_to_all | solution.py:812
  (98 other events, 1370.3 us)
Sparse Core Ops, SparseCore 0:
  10.2 77.9 all-gather.4
  90.1 56.1 all-gather.6
  148.5 42.6 all-gather.8
  217.9 47.7 all-gather.10
  284.0 46.8 reduce-scatter.4
  351.6 41.6 reduce-scatter.10
  395.6 57.9 reduce-scatter.6
  464.7 51.9 reduce-scatter.8

commit v4 on v3

--- a/solution.py
+++ b/solution.py
@@ -155,13 +155,13 @@
             jax.ShapeDtypeStruct((count, PAIR), jnp.float32),
             jax.ShapeDtypeStruct((count, 2), jnp.float32),
         ),
-        compiler_params=pltpu.CompilerParams(vmem_limit_bytes=40 * 2**20),
+        compiler_params=pltpu.CompilerParams(vmem_limit_bytes=58 * 2**20),
         cost_estimate=LITTLE,
     )(block_ends(segments, rows), qkv, qkv, qkv, col, row)
 
 
 def self_backward_kernel(
-    ends, q_ref, k_ref, v_ref, go_ref, lse_ref, delta_ref, seg_col, seg_row, grad_ref, acc_q, acc_k, acc_v
+    ends, q_ref, k_ref, v_ref, go_ref, lse_ref, o_ref, seg_col, seg_row, grad_ref, acc_q, acc_k, acc_v, delta_ref
 ):
     step = pl.program_id(0)
     blocks = pl.num_programs(0)
@@ -170,6 +170,15 @@
     @pl.when(step == 0)
     def _():
         acc_q[...] = jnp.zeros_like(acc_q)
+        lane = lax.broadcasted_iota(jnp.int32, (8, PAIR), 1) // HD
+        pick = (lane == lax.broadcasted_iota(jnp.int32, (8, PAIR), 0)).astype(jnp.float32)
+        delta_ref[...] = lax.dot_general(
+            pick,
+            go_ref[...].astype(jnp.float32) * o_ref[...],
+            (((1,), (1,)), ((), ())),
+            precision=lax.Precision.HIGHEST,
+            preferred_element_type=jnp.float32,
+        )
 
     keys = k_ref[...]
     values = v_ref[...]
@@ -230,7 +239,7 @@
     grad_ref[own, 2 * PAIR : 3 * PAIR] = low(acc_v[...])
 
 
-def self_backward(qkv, grad_att, lse, delta, segments):
+def self_backward(qkv, grad_att, lse, attended, segments):
     count = qkv.shape[0]
     rows = BLOCK
     col = segments[:, None]
@@ -245,7 +254,7 @@
             pl.BlockSpec((rows, PAIR), lambda i, e: (i, 2)),
             pl.BlockSpec((count, PAIR), whole),
             pl.BlockSpec((2, count), whole),
-            pl.BlockSpec((2, count), whole),
+            pl.BlockSpec((count, PAIR), whole),
             pl.BlockSpec((rows, 1), lambda i, e: (i, 0)),
             pl.BlockSpec((1, count), whole),
         ],
@@ -254,15 +263,16 @@
             pltpu.VMEM((count, PAIR), jnp.float32),
             pltpu.VMEM((rows, PAIR), jnp.float32),
             pltpu.VMEM((rows, PAIR), jnp.float32),
+            pltpu.VMEM((8, count), jnp.float32),
         ],
     )
     return pl.pallas_call(
         self_backward_kernel,
         grid_spec=grid_spec,
         out_shape=jax.ShapeDtypeStruct((count, 3 * PAIR), jnp.bfloat16),
-        compiler_params=pltpu.CompilerParams(vmem_limit_bytes=40 * 2**20),
-        cost_estimate=LITTLE,
-    )(block_ends(segments, rows), qkv, qkv, qkv, grad_att, lse, delta, col, row)
+        compiler_params=pltpu.CompilerParams(vmem_limit_bytes=58 * 2**20),
+        cost_estimate=LITTLE,
+    )(block_ends(segments, rows), qkv, qkv, qkv, grad_att, lse, attended, col, row)
 
 
 def cross_forward_kernel(length, q_ref, m_ref, out_ref):
@@ -392,38 +402,9 @@
             jax.ShapeDtypeStruct((span * enc_rows, D), jnp.bfloat16),
             jax.ShapeDtypeStruct((span * enc_rows, mem_w.shape[1]), jnp.bfloat16),
         ),
-        compiler_params=pltpu.CompilerParams(vmem_limit_bytes=32 * 2**20),
+        compiler_params=pltpu.CompilerParams(vmem_limit_bytes=58 * 2**20),
         cost_estimate=LITTLE,
     )(rows_all, rows_all, gain[None], shift[None], qkv_w, qkv_b[None], mem_w, mem_b[None])
-
-
-def gain_kernel(x_ref, g_ref, out_ref):
-    rows = x_ref[0].astype(jnp.float32)
-    centered = rows - jnp.mean(rows, axis=-1, keepdims=True)
-    inverse = lax.rsqrt(jnp.mean(centered * centered, axis=-1, keepdims=True) + EPS)
-    grads = g_ref[...].astype(jnp.float32)
-
-    @pl.when(pl.program_id(0) == 0)
-    def _():
-        out_ref[...] = jnp.zeros_like(out_ref)
-
-    out_ref[0:1, :] += jnp.sum(grads * (centered * inverse), axis=0, keepdims=True)
-    out_ref[1:2, :] += jnp.sum(grads, axis=0, keepdims=True)
-
-
-def gain_sums(rows_all, row_count, grads):
-    span = rows_all.shape[0]
-    return pl.pallas_call(
-        gain_kernel,
-        grid=(span,),
-        in_specs=[
-            pl.BlockSpec((1, row_count, D), lambda i: (i, 0, 0)),
-            pl.BlockSpec((row_count, D), lambda i: (i, 0)),
-        ],
-        out_specs=pl.BlockSpec((2, D), lambda i: (0, 0)),
-        out_shape=jax.ShapeDtypeStruct((2, D), jnp.float32),
-        cost_estimate=LITTLE,
-    )(rows_all, grads)
 
 
 def feed_kernel(x_ref, w_ref, b_ref, ga_ref, act_ref, pre_ref, in_ref, sum_ref):
@@ -445,7 +426,7 @@
 
 def feed(rows, weight, bias, grad_act):
     count, hidden = grad_act.shape
-    tile = 256
+    tile = 512
     whole = lambda i: (0, 0)
     block = lambda i: (i, 0)
     return pl.pallas_call(
@@ -472,6 +453,193 @@
         compiler_params=pltpu.CompilerParams(vmem_limit_bytes=58 * 2**20),
         cost_estimate=LITTLE,
     )(rows, weight, bias[None], grad_act)
+
+
+def expand_kernel(replica, x_ref, g_ref, *refs):
+    keep, outs = refs[-1], refs[:-1]
+    size, rows = len(outs), outs[0].shape[1]
+    owners = x_ref.shape[1] // (size * rows)
+    keep[...] = low(dot_tn(x_ref[...], g_ref[...])).reshape(keep.shape)
+    step = pl.program_id(0) * owners
+    for owner in range(owners):
+        for other, out in enumerate(outs):
+            out[pl.ds(step + owner, 1)] = keep[owner, pl.ds(replica[0] ^ other, 1)]
+
+
+def expand_grads(rows_in, grads, owners, part_rows):
+    size, me = lax.axis_size("rep"), lax.axis_index("rep")
+    count, hidden = grads.shape
+    if part_rows % 16:
+        full = low(dot_tn(rows_in, grads)).reshape(owners, size, part_rows, hidden)
+        return [lax.dynamic_index_in_dim(full, me ^ step, 1, keepdims=False) for step in range(size)]
+    tile = 2
+    grid_spec = pltpu.PrefetchScalarGridSpec(
+        num_scalar_prefetch=1,
+        grid=(owners // tile,),
+        in_specs=[
+            pl.BlockSpec((count, tile * size * part_rows), lambda i, e: (0, i)),
+            pl.BlockSpec((count, hidden), lambda i, e: (0, 0)),
+        ],
+        out_specs=[pl.BlockSpec((owners, part_rows, hidden), lambda i, e: (0, 0, 0))] * size,
+        scratch_shapes=[pltpu.VMEM((tile, size, part_rows, hidden), jnp.bfloat16)],
+    )
+    return pl.pallas_call(
+        expand_kernel,
+        grid_spec=grid_spec,
+        out_shape=(jax.ShapeDtypeStruct((owners, part_rows, hidden), jnp.bfloat16),) * size,
+        compiler_params=pltpu.CompilerParams(vmem_limit_bytes=58 * 2**20),
+        cost_estimate=LITTLE,
+    )(me[None], rows_in, grads)
+
+
+def shrink_kernel(replica, a_ref, g_ref, *outs):
+    for step, out in enumerate(outs):
+
+        @pl.when(pl.program_id(0) == step)
+        def _():
+            out[...] = low(dot_tn(a_ref[...], g_ref[...]))
+
+
+def shrink_grads(act, grads):
+    size, me = lax.axis_size("rep"), lax.axis_index("rep")
+    count, hidden = act.shape
+    part = hidden // size
+    if part % 128:
+        full = low(dot_tn(act, grads)).reshape(size, part, D)
+        return [lax.dynamic_index_in_dim(full, me ^ step, 0, keepdims=False) for step in range(size)]
+    grid_spec = pltpu.PrefetchScalarGridSpec(
+        num_scalar_prefetch=1,
+        grid=(size,),
+        in_specs=[
+            pl.BlockSpec((count, part), lambda i, e: (0, e[0] ^ i)),
+            pl.BlockSpec((count, D), lambda i, e: (0, 0)),
+        ],
+        out_specs=[pl.BlockSpec((part, D), lambda i, e: (0, 0))] * size,
+    )
+    return pl.pallas_call(
+        shrink_kernel,
+        grid_spec=grid_spec,
+        out_shape=(jax.ShapeDtypeStruct((part, D), jnp.bfloat16),) * size,
+        compiler_params=pltpu.CompilerParams(vmem_limit_bytes=58 * 2**20),
+        cost_estimate=LITTLE,
+    )(me[None], act, grads)
+
+
+def product_kernel(a_ref, b_ref, out_ref):
+    out_ref[...] = low(dot(a_ref[...], b_ref[...]))
+
+
+def product(left, right):
+    count, depth = left.shape
+    tile = 512
+    return pl.pallas_call(
+        product_kernel,
+        grid=(count // tile,),
+        in_specs=[pl.BlockSpec((tile, depth), lambda i: (i, 0)), pl.BlockSpec(right.shape, lambda i: (0, 0))],
+        out_specs=pl.BlockSpec((tile, right.shape[1]), lambda i: (i, 0)),
+        out_shape=jax.ShapeDtypeStruct((count, right.shape[1]), jnp.bfloat16),
+        compiler_params=pltpu.CompilerParams(vmem_limit_bytes=58 * 2**20),
+        cost_estimate=LITTLE,
+    )(left, right)
+
+
+def back_kernel(g_ref, w_ref, one_ref, out_ref, sum_ref, own_ref):
+    @pl.when(pl.program_id(0) == 0)
+    def _():
+        sum_ref[...] = jnp.zeros_like(sum_ref)
+        own_ref[...] = jnp.zeros_like(own_ref)
+
+    grads = dot_nt(g_ref[...], w_ref[...])
+    out_ref[...] = low(grads)
+    sum_ref[0:1, :] += jnp.sum(grads * one_ref[...].astype(jnp.float32), axis=0, keepdims=True)
+    sum_ref[1:2, :] += jnp.sum(grads, axis=0, keepdims=True)
+    own_ref[...] += jnp.sum(g_ref[...].astype(jnp.float32), axis=0, keepdims=True)
+
+
+def back(grads, weight, rows_in):
+    count, width = grads.shape
+    tile = 256
+    return pl.pallas_call(
+        back_kernel,
+        grid=(count // tile,),
+        in_specs=[
+            pl.BlockSpec((tile, width), lambda i: (i, 0)),
+            pl.BlockSpec(weight.shape, lambda i: (0, 0)),
+            pl.BlockSpec((tile, D), lambda i: (i, 0)),
+        ],
+        out_specs=[
+            pl.BlockSpec((tile, D), lambda i: (i, 0)),
+            pl.BlockSpec((2, D), lambda i: (0, 0)),
+            pl.BlockSpec((1, width), lambda i: (0, 0)),
+        ],
+        out_shape=(
+            jax.ShapeDtypeStruct((count, D), jnp.bfloat16),
+            jax.ShapeDtypeStruct((2, D), jnp.float32),
+            jax.ShapeDtypeStruct((1, width), jnp.float32),
+        ),
+        compiler_params=pltpu.CompilerParams(vmem_limit_bytes=58 * 2**20),
+        cost_estimate=LITTLE,
+    )(grads, weight, rows_in)
+
+
+def heads_grads_kernel(x_ref, g_ref, e_ref, m_ref, out_ref):
+    width = g_ref.shape[1]
+    shape = out_ref.shape[1:3]
+    for owner in range(shape[0]):
+        place = slice(owner * x_ref.shape[1] // shape[0], (owner + 1) * x_ref.shape[1] // shape[0])
+        left = low(dot_tn(x_ref[:, place], g_ref[...]))
+        right = low(dot_tn(e_ref[:, place], m_ref[...]))
+        for replica in range(out_ref.shape[0]):
+            rows = slice(replica * shape[1], (replica + 1) * shape[1])
+            out_ref[replica, owner, :, :width] = left[rows, :]
+            out_ref[replica, owner, :, width:] = right[rows, :]
+
+
+def heads_grads(rows_in, grads, enc, enc_grads, owners, part_rows):
+    size = lax.axis_size("rep")
+    width, enc_width = grads.shape[1], enc_grads.shape[1]
+    if part_rows % 16:
+        both = low(jnp.concatenate([dot_tn(rows_in, grads), dot_tn(enc, enc_grads)], axis=1))
+        return both.reshape(owners, size, part_rows, width + enc_width).transpose(1, 0, 2, 3)
+    tile = 2
+    return pl.pallas_call(
+        heads_grads_kernel,
+        grid=(owners // tile,),
+        in_specs=[
+            pl.BlockSpec((rows_in.shape[0], tile * size * part_rows), lambda i: (0, i)),
+            pl.BlockSpec(grads.shape, lambda i: (0, 0)),
+            pl.BlockSpec((enc.shape[0], tile * size * part_rows), lambda i: (0, i)),
+            pl.BlockSpec(enc_grads.shape, lambda i: (0, 0)),
+        ],
+        out_specs=pl.BlockSpec((size, tile, part_rows, width + enc_width), lambda i: (0, i, 0, 0)),
+        out_shape=jax.ShapeDtypeStruct((size, owners, part_rows, width + enc_width), jnp.bfloat16),
+        compiler_params=pltpu.CompilerParams(vmem_limit_bytes=58 * 2**20),
+        cost_estimate=LITTLE,
+    )(rows_in, grads, enc, enc_grads)
+
+
+def last_kernel(x_ref, e_ref, one_ref, gain, out_ref):
+    rows = x_ref[...].astype(jnp.float32)
+    centered = rows - jnp.mean(rows, axis=-1, keepdims=True)
+    inverse = lax.rsqrt(jnp.mean(centered * centered, axis=-1, keepdims=True) + EPS)
+    x_hat = centered * inverse
+    grads = e_ref[...].astype(jnp.float32) * gain[...]
+    inner = jnp.mean(grads * x_hat, axis=-1, keepdims=True)
+    out_ref[...] = one_ref[...] + inverse * (grads - jnp.mean(grads, axis=-1, keepdims=True) - x_hat * inner)
+
+
+def last(rows, grads, grad_one, gain):
+    count = rows.shape[0]
+    tile = 128
+    block = pl.BlockSpec((tile, D), lambda i: (i, 0))
+    return pl.pallas_call(
+        last_kernel,
+        grid=(count // tile,),
+        in_specs=[block, block, block, pl.BlockSpec((1, D), lambda i: (0, 0))],
+        out_specs=block,
+        out_shape=jax.ShapeDtypeStruct((count, D), jnp.float32),
+        cost_estimate=LITTLE,
+    )(rows, grads, grad_one, gain[None])
 
 
 def rep_send(value, step):
@@ -514,7 +682,7 @@
         spread_kernel,
         grid_spec=grid_spec,
         out_shape=jax.ShapeDtypeStruct((size, rows, columns), dtype),
-        compiler_params=pltpu.CompilerParams(vmem_limit_bytes=40 * 2**20),
+        compiler_params=pltpu.CompilerParams(vmem_limit_bytes=58 * 2**20),
         cost_estimate=LITTLE,
     )(lax.axis_index("rep")[None], *parts)
 
@@ -604,7 +772,7 @@
         columns_kernel,
         grid_spec=grid_spec,
         out_shape=jax.ShapeDtypeStruct((size, rows, blocks * D), jnp.float32),
-        compiler_params=pltpu.CompilerParams(vmem_limit_bytes=40 * 2**20),
+        compiler_params=pltpu.CompilerParams(vmem_limit_bytes=58 * 2**20),
         cost_estimate=LITTLE,
     )(me[None], *parts)
     return out.reshape(size * rows, blocks * D)
@@ -645,7 +813,7 @@
             jax.ShapeDtypeStruct((size, rows, 3 * D), jnp.float32),
             jax.ShapeDtypeStruct((size, rows, 2 * D), jnp.float32),
         ),
-        compiler_params=pltpu.CompilerParams(vmem_limit_bytes=40 * 2**20),
+        compiler_params=pltpu.CompilerParams(vmem_limit_bytes=58 * 2**20),
         cost_estimate=LITTLE,
     )(me[None], *parts)
     return qkv.reshape(size * rows, 3 * D), memory.reshape(size * rows, 2 * D)
@@ -693,7 +861,7 @@
         join_kernel,
         grid_spec=grid_spec,
         out_shape=(jax.ShapeDtypeStruct((chips, 2, size, rows, D), jnp.bfloat16),) * 3,
-        compiler_params=pltpu.CompilerParams(vmem_limit_bytes=40 * 2**20),
+        compiler_params=pltpu.CompilerParams(vmem_limit_bytes=58 * 2**20),
         cost_estimate=LITTLE,
     )(jnp.stack([lax.axis_index("rep"), core]), *mine, *other)
     return tuple(out.reshape(D, D) for out in outs)
@@ -727,8 +895,8 @@
         plain_kernel,
         grid_spec=grid_spec,
         out_shape=(jax.ShapeDtypeStruct((3, chips, size, rows, D), jnp.bfloat16),) * 2,
-        compiler_params=pltpu.CompilerParams(vmem_limit_bytes=40 * 2**20),
-        cost_estimate=LITTLE,
+        compiler_params=pltpu.CompilerParams(vmem_limit_bytes=58 * 2**20),
+        cost_estimate=pl.CostEstimate(flops=6 * count * D * D, bytes_accessed=20 * count * D, transcendentals=0),
     )(core[None], *lefts, *rights)
 
 
@@ -755,7 +923,7 @@
         split_kernel,
         grid_spec=grid_spec,
         out_shape=(jax.ShapeDtypeStruct((kinds, chips, rows, D), jnp.bfloat16),) * size,
-        compiler_params=pltpu.CompilerParams(vmem_limit_bytes=40 * 2**20),
+        compiler_params=pltpu.CompilerParams(vmem_limit_bytes=58 * 2**20),
         cost_estimate=LITTLE,
     )(lax.axis_index("rep")[None], mine, other)
 
@@ -835,11 +1003,10 @@
     qkv_weight, memory_weight = head_weight[:, : 3 * width], head_weight[:, 3 * width :]
     plain_part = jnp.stack([own_part(self_out), own_part(cross_query), own_part(cross_out)])
     plain_line = weight_line(after(plain_part, swapped))
-    rows_all, plain_line, head_weight = lax.optimization_barrier((rows_all, plain_line, head_weight))
     plain_mine = rep_start(plain_line)
+    rows_all, head_weight, _ = lax.optimization_barrier((rows_all, head_weight, plain_line))
     expand_part = own_part(expand_weight).reshape(part_rows, count, hidden).transpose(1, 0, 2)
     expand_swapped = swap(after(expand_part, rows_all))
-    grad_all = gather(after(cotangent, rows_all))
 
     rows_all = rows_all.reshape(span, row_count + enc_rows, D)
     seq_segments = lax.dynamic_slice_in_dim(segments, local_seq * SEQ, SEQ)
@@ -850,17 +1017,19 @@
     input_one_all, qkv, enc_all, memory_pair = front(
         rows_all, row_count, gain_rows[0], shift_rows[0], qkv_weight, qkv_bias, memory_weight, memory_bias
     )
+    qkv, plain_mine[1], plain_mine[2] = lax.optimization_barrier((qkv, plain_mine[1], plain_mine[2]))
     att_low, att_full, lse = self_forward(qkv, seq_segments)
-    att_low, expand_swapped = lax.optimization_barrier((att_low, expand_swapped))
+    att_low, expand_swapped, plain_mine = lax.optimization_barrier((att_low, expand_swapped, plain_mine))
     attended = lax.all_to_all(att_low, "shard", 0, 1, tiled=True, axis_index_groups=groups)
 
-    memory_all = gather(after(memory_pair, grad_all, att_low), groups)
+    memory_all = gather(memory_pair, groups)
     enc_count = lax.dynamic_slice_in_dim(enc_lengths, local_seq, 1)
     plain_other = [core_send(part) for part in plain_mine]
 
     plain_mine, plain_other = after((plain_mine, plain_other), att_low)
     attn_proj, query_in, cross_proj = weight_join(plain_mine, plain_other)
     attended, attn_proj, query_in, cross_proj = lax.optimization_barrier((attended, attn_proj, query_in, cross_proj))
+    grad_all = gather(after(cotangent, memory_all, att_low))
     expand_parts = rep_start(after(expand_swapped, attended).reshape(count * part_rows, hidden))
     residual_in = tokens.astype(jnp.float32)
     hidden_one = residual_in + dot(attended, attn_proj) + bias_rows[2]
@@ -883,17 +1052,20 @@
     grad_in_three = scatter(grad_in_three_low)
 
     part_hidden = hidden // size
-    grad_expand = low(dot_tn(input_three_all, grad_pre)).reshape(count, size, part_rows, hidden)
-    expand_grad_parts = rep_split(grad_expand, 1)
-    act_late = after(act, grad_expand)
-    grad_shrink = low(dot_tn(act_late, grad_all)).reshape(size, part_hidden, D)
-    shrink_parts = rep_split(grad_shrink, 0)
-    result_part = low(dot(after(act, grad_shrink), shrink_weight))
+
+    def send_parts(parts):
+        return [parts[0]] + [rep_send(parts[step], step) for step in range(1, size)]
+
+    rows_late, grad_pre_late = after((input_three_all, grad_pre), grad_in_three_low)
+    expand_grad_parts = expand_grads(rows_late, grad_pre_late, count, part_rows)
+    shrink_parts = send_parts(shrink_grads(after(act, expand_grad_parts[0]), grad_all))
+    expand_grad_parts = send_parts(expand_grad_parts)
+    result_part = product(after(act, shrink_parts[0]), shrink_weight)
     expand_sum = add_up(expand_grad_parts)
-    grad_in_three, shrink_parts[0], expand_sum, result_part = lax.optimization_barrier(
-        (grad_in_three, shrink_parts[0], expand_sum, result_part)
-    )
     own_expand = swap(expand_sum)
+    grad_in_three, shrink_parts[0], result_part = lax.optimization_barrier(
+        (grad_in_three, shrink_parts[0], result_part)
+    )
     result_sum = scatter(result_part)
     grad_in_three = grad_in_three.astype(jnp.float32)
 
@@ -902,41 +1074,41 @@
     grad_two = grad_out + norm_three[0]
     grad_two_low = low(grad_two)
     grad_context = low(dot_nt(grad_two_low, cross_proj))
+    grad_context, own_expand = lax.optimization_barrier((grad_context, own_expand))
     grad_cross_q, memory_part = cross_backward(cross_q, memory_all, grad_context, enc_count)
+    grad_cross_q, memory_part, shrink_parts = lax.optimization_barrier((grad_cross_q, memory_part, shrink_parts))
     mem_grads = scatter(memory_part, groups)
     grad_in_two = dot_nt(grad_cross_q, query_in)
     norm_two = jax.vjp(norm_apply, hidden_one, gain_rows[1], shift_rows[1])[1](grad_in_two)
     grad_one = grad_two + norm_two[0]
     grad_one_low = low(grad_one)
     grad_attn = low(dot_nt(grad_one_low, attn_proj))
-    shrink_sum = add_up(after(shrink_parts, grad_cross_q))
+    shrink_sum = add_up(shrink_parts)
     own_expand = own_expand.reshape(part_hidden, D)
     own_feed = jnp.concatenate([shrink_sum, own_expand], axis=0)
     grad_attn, own_feed = lax.optimization_barrier((grad_attn, own_feed))
     grad_att_heads = lax.all_to_all(grad_attn, "shard", 1, 0, tiled=True, axis_index_groups=groups)
-    feed_gather = rep_start(own_feed)
 
     lefts, rights = after(((attended, input_two, context), (grad_one_low, grad_cross_q, grad_two_low)), grad_attn)
     plain_own, plain_theirs = plain_grads(lefts, rights)
     plain_theirs = core_send(plain_theirs)
     grad_att_heads, plain_own = lax.optimization_barrier((grad_att_heads, plain_own))
 
-    delta = jnp.sum((grad_att_heads.astype(jnp.float32) * att_full).reshape(SEQ, 2, HD), axis=-1).T
-    plain_rep = core_sum_split(*after((plain_own, plain_theirs), delta))
-    delta, plain_rep = lax.optimization_barrier((delta, list(plain_rep)))
-    plain_rep = [plain_rep[0]] + [rep_send(plain_rep[step], step) for step in range(1, size)]
-    grad_qkv = self_backward(qkv, grad_att_heads, lse.T, delta, seq_segments)
-    grad_in_one_low = low(dot_nt(grad_qkv, qkv_weight))
+    feed_gather = rep_start(own_feed)
+    grad_qkv = self_backward(qkv, grad_att_heads, lse.T, att_full, seq_segments)
+    grad_qkv, feed_gather, plain_theirs = lax.optimization_barrier((grad_qkv, feed_gather, plain_theirs))
+    heads_parts = heads_grads(input_one_all, grad_qkv, enc_all, mem_grads, count, part_rows)
+    heads_swapped = rep_swap(heads_parts)
+    grad_in_one_low, one_sums, qkv_sums = back(after(grad_qkv, heads_parts), qkv_weight, input_one_all)
+    plain_rep = send_parts(core_sum_split(*after((plain_own, plain_theirs), heads_parts)))
+    grad_in_one_low, heads_swapped, plain_rep[0] = lax.optimization_barrier(
+        (grad_in_one_low, heads_swapped, plain_rep[0])
+    )
     grad_in_one = scatter(grad_in_one_low, groups)
 
-    input_one_late, mem_grads_late, grad_qkv_late, rows_late = after(
-        (input_one_all, mem_grads, grad_qkv, rows_all), grad_in_one_low
-    )
-    grad_attn_in = dot_tn(input_one_late, grad_qkv_late)
-    grad_memory = dot_tn(enc_all, mem_grads_late)
-    heads_grad = low(jnp.concatenate([grad_attn_in, grad_memory], axis=1))
-    gain_shift = gain_sums(rows_late, row_count, grad_in_one_low)
-    qkv_sums = column_sums(grad_qkv_late)
+    mem_grads_late = after(mem_grads, grad_in_one_low)
+    qkv_sums = qkv_sums[0]
+    gain_shift = [(one_sums[0] - shift_rows[0] * one_sums[1]) / gain_rows[0], one_sums[1]]
     zero_row = jnp.zeros((D,), jnp.float32)
 
     def at_own(values):
@@ -968,22 +1140,20 @@
     extra = -(-small_size // (5 * width))
     small_grads = jnp.pad(small_grads, ((0, 0), (0, extra * 5 * width - small_size)))
     small_grads = small_grads.reshape(count, extra, 5 * width)
-    heads_parts = heads_grad.reshape(count, size, part_rows, 5 * width).transpose(1, 0, 2, 3)
-    heads_sum = sum_first(rep_swap(heads_parts))
+    heads_sum = sum_first(after(heads_swapped, grad_in_one_low))
     own_heads = swap(jnp.concatenate([heads_sum, small_grads], axis=1))
     own_small = sum_first(own_heads[:, part_rows:])
     own_heads = own_heads[:, :part_rows].reshape(count // span, span, part_rows, 5 * width)
     own_heads = own_heads[0] if count == span else sum_first(own_heads)
     heads_gather = rep_start(jnp.concatenate([own_heads.reshape(span * part_rows, 5 * width), own_small], axis=0))
 
-    plain_line_parts = reduce_line(add_up(after(plain_rep, grad_in_one_low)))
+    plain_line_parts = reduce_line(add_up(after(plain_rep, own_heads)))
     own_plain = add_up(plain_line_parts).reshape(3 * part_rows, D)
     plain_gather = rep_start(own_plain)
     enc_parts = line_scatter_start(low(dot_nt(mem_grads_late, memory_weight)), span)
     grad_enc = add_up(line_scatter_middle(enc_parts, span)).astype(jnp.float32)
     result = hidden_two + after(result_sum, grad_in_one_low).astype(jnp.float32) + bias_rows[6]
 
-    feed_gather = after(feed_gather, heads_grad)
     total_shrink = spread(feed_gather, 0, part_hidden, jnp.float32)
     total_expand = spread_columns(feed_gather, part_hidden, count, part_rows)
     total_plain = [
@@ -997,9 +1167,7 @@
     total_small = total_small[: small_count * shard_width].reshape(small_count, shard_width)
     total_qkv, total_memory = spread_heads(heads_gather, span, part_rows, width)
 
-    grad_in_one = grad_in_one.astype(jnp.float32)
-    norm_one = jax.vjp(lambda rows: norm_apply(rows, gain_rows[0], shift_rows[0]), residual_in)[1](grad_in_one)
-    grad_tokens = grad_one + norm_one[0]
+    grad_tokens = last(tokens, grad_in_one, grad_one, gain_rows[0])
 
     return (
         low(result),

time: 609 us -> 557 us (0.915)
  the two profiles are of different devices: /device:TPU:12 before, /device:TPU:0 now
where the time goes in v4:
time: 557 us; the launch traced here: 548 us
  waiting for transfers between devices  186 us (33%)
  Pallas kernels  174 us (31%)
  starting transfers between devices  92.5 us (17%)
  local copies, waits for them, and re-layouts  31.4 us (6%)
  other arithmetic  29.1 us (5%)
  matrix products  18.6 us (3%)
  between operations  16.3 us (3%)
    ppermute x9, waiting for transfers between devices, line_send(): return lax.ppermute(value, 'shard', route)  55.7 us
    ppermute x27, waiting for transfers between devices, rep_send(): return lax.ppermute(value, 'rep', [(i, i ^ step) for i in range(size)])  45.4 us
    ppermute x27, starting transfers between devices, rep_send(): return lax.ppermute(value, 'rep', [(i, i ^ step) for i in range(size)])  33.8 us
    all_to_all x4, waiting for transfers between devices, swap(): return lax.all_to_all(value, 'shard', 0, 0, tiled=True)  31.7 us
    pallas_call x1, Pallas kernels, self_backward(): pl.pallas_call(self_backward_kernel, grid_spec=grid_spec, out_shape=jax.S...  23 us
    all_gather x4, waiting for transfers between devices, gather(): lax.all_gather(value, 'shard', axis=0, tiled=True, axis_index_groups=groups)  22.4 us
    pallas_call x1, Pallas kernels, self_forward(): pl.pallas_call(self_forward_kernel, grid_spec=grid_spec, out_shape=(jax.S...  20.6 us
    all_to_all x4, starting transfers between devices, swap(): return lax.all_to_all(value, 'shard', 0, 0, tiled=True)  18.4 us
  transfers between devices with their start and end apart: 57, of which 28 were waited for; matrix products, arithmetic and copies ran while one was open for 12% of the time, Pallas kernels for 27%

profile of v4, /device:TPU:0, one launch (start us, length us, event | category | flops | bytes accessed | tf_op | source)
XLA Modules:
  0.0 547.7 jit_solution(6812662320163575390)
XLA Ops:
  21.7 20.2 %all-to-all-done = bf16[8,35,640]{2,1,0:T(8,128)(2,1)S(1)} async-done(((bf16[8,35,640]{2,1,0:T(8,128)(2,1)}), bf16[8,35,640]{2,1,0:T(8,128)(2,1)S(1)}, u32[]{:S(2)}, u32[]{:S(2)}) %all-to-all-start) | async-done | bytes 358432 | tf_op jit(solution)/shard_map/all_to_all | solution.py:980
  51.2 20.7 %collective-permute-done.3 = bf16[3,32,1024]{2,1,0:T(8,128)(2,1)S(1)} collective-permute-done((bf16[3,32,1024]{2,1,0:T(8,128)(2,1)S(1)}, bf16[3,32,1024]{2,1,0:T(8,128)(2,1)S(1)}, u32[]{:S(2)}, u32[]{:S(2)}) %collective-permute-start.3) | collective-permute-done | bytes 196640 | tf_op jit(solution)/shard_map/ppermute | solution.py:728
  74.4 8.2 %collective-permute-done.4 = bf16[3,32,1024]{2,1,0:T(8,128)(2,1)S(1)} collective-permute-done((bf16[3,32,1024]{2,1,0:T(8,128)(2,1)S(1)}, bf16[3,32,1024]{2,1,0:T(8,128)(2,1)S(1)}, u32[]{:S(2)}, u32[]{:S(2)}) %collective-permute-start.4) | collective-permute-done | bytes 196640 | tf_op jit(solution)/shard_map/ppermute | solution.py:728
  85.2 8.1 %all-gather.5.cloned.1.call-done = bf16[2560,1024]{1,0:T(8,128)(2,1)} async-done(((bf16[320,1024]{1,0:T(8,128)(2,1)}), bf16[2560,1024]{1,0:T(8,128)(2,1)}) %all-gather.5.cloned.1.call-update) | async-done | bytes 5242896 | tf_op jit(solution)/shard_map/all_gather | solution.py:974
  93.2 9.9 %shard_map.263 = (bf16[2048,1024]{1,0:T(8,128)(2,1)}, bf16[2048,384]{1,0:T(8,128)(2,1)}, bf16[512,1024]{1,0:T(8,128)(2,1)}, bf16[512,256]{1,0:T(8,128)(2,1)}) custom-call(bf16[8,320,1024]{2,1,0:T(8,128)(2,1)} %bitcast.210, bf16[8,320,1024]{2,1,0:T(8,128)(2,1)} %bitcast.211, f32[1,1024]{1,0:T(1,128)} %bitcast.248, f32[1,1024]{1,0:T(1,128)} %bitcast.252, ...), custom_call_target="tpu_custom_call" | custom-call | flops 1000 | bytes 1000 | tf_op jit(solution)/shard_map/pallas_call | solution.py:380
  114.8 14.3 %collective-permute-done.7.refs_2_ = bf16[3,4,32,1024]{3,2,1,0:T(8,128)(2,1)S(1)} collective-permute-done((bf16[3,4,32,1024]{3,2,1,0:T(8,128)(2,1)S(1)}, bf16[3,4,32,1024]{3,2,1,0:T(8,128)(2,1)S(1)}, u32[]{:S(2)}, u32[]{:S(2)}) %collective-permute-start.7) | collective-permute-done | bytes 786464 | tf_op jit(solution)/shard_map/ppermute | solution.py:647
  131.2 20.6 %shard_map.264 = (bf16[2048,128]{1,0:T(8,128)(2,1)}, f32[2048,128]{1,0:T(8,128)}, f32[2048,2]{1,0:T(8,128)}) custom-call(s32[2,4]{1,0:T(2,128)} %pad_add_fusion.ends, bf16[2048,384]{1,0:T(8,128)(2,1)} %get-tuple-element.131.q_ref.k_ref.v_ref, bf16[2048,384]{1,0:T(8,128)(2,1)} %get-tuple-element.131.q_ref.k_ref.v_ref, ...), custom_call_target="tpu_custom_call" | custom-call | flops 1000 | bytes 1000 | tf_op jit(solution)/shard_map/pallas_call | solution.py:150
  156.9 11.2 %all-gather.11.cloned.1.call-start = ((), (), s32[]{:S(2)}) async-start(), calls=%async_computation.14 | async-start | bytes 4718592 | tf_op jit(solution)/shard_map/all_gather | solution.py:974
  187.8 8.6 %shard_map.266.c_ref = bf16[256,1024]{1,0:T(8,128)(2,1)} custom-call(s32[1]{0:T(128)S(6)} %copy.114.length, bf16[256,1024]{1,0:T(8,128)(2,1)} %fusion.2.q_ref, bf16[4096,256]{1,0:T(8,128)(2,1)} %all-gather.7.cloned.1.call-done.m_ref), custom_call_target="tpu_custom_call" | custom-call | flops 1000 | bytes 1000 | tf_op jit(solution)/shard_map/pallas_call | solution.py:304
  200.3 7.6 %all-gather.9.cloned.1.call-done.g_ref = bf16[2048,1024]{1,0:T(8,128)(2,1)} async-done(((bf16[256,1024]{1,0:T(8,128)(2,1)}), bf16[2048,1024]{1,0:T(8,128)(2,1)}) %all-gather.9.cloned.1.call-update) | async-done | bytes 4194320 | tf_op jit(solution)/shard_map/all_gather | solution.py:974
  212.1 11.6 %collective-permute-done.15.refs_3_ = bf16[256,1024]{1,0:T(8,128)(2,1)S(1)} collective-permute-done((bf16[256,1024]{1,0:T(8,128)(2,1)S(1)}, bf16[256,1024]{1,0:T(8,128)(2,1)S(1)}, u32[]{:S(2)}, u32[]{:S(2)}) %collective-permute-start.15) | collective-permute-done | bytes 524320 | tf_op jit(solution)/shard_map/ppermute | solution.py:647
  223.7 10.5 %collective-permute-done.14.refs_2_ = bf16[256,1024]{1,0:T(8,128)(2,1)S(1)} collective-permute-done((bf16[256,1024]{1,0:T(8,128)(2,1)S(1)}, bf16[256,1024]{1,0:T(8,128)(2,1)S(1)}, u32[]{:S(2)}, u32[]{:S(2)}) %collective-permute-start.14) | collective-permute-done | bytes 524320 | tf_op jit(solution)/shard_map/ppermute | solution.py:647
  241.1 7.1 %fusion.30.ga_ref = f32[2048,1024]{1,0:T(8,128)} fusion(bf16[2048,1024]{1,0:T(8,128)(2,1)S(1)} %copy-done.9, bf16[1024,1024]{1,0:T(8,128)(2,1)S(1)} %copy-done.15), kind=kOutput, calls=%fused_computation.138 | convolution fusion | flops 4294967296 | bytes 14680064 | tf_op jit(solution)/shard_map/dot_general | solution.py:48
  255.0 16.0 %shard_map.268 = (bf16[2048,1024]{1,0:T(8,128)(2,1)}, bf16[2048,1024]{1,0:T(8,128)(2,1)}, bf16[2048,1024]{1,0:T(8,128)(2,1)}, f32[1,1024]{1,0:T(1,128)}) custom-call(bf16[2048,1024]{1,0:T(8,128)(2,1)} %all-gather.11.cloned.1.call-done.x_ref, bf16[1024,1024]{1,0:T(8,128)(2,1)} %bitcast.213, f32[1,1024]{1,0:T(1,128)} %bitcast.255, f32[2048,1024]{1,0:T(8,128)} %fusion.30.ga_ref), custom_call_target="tpu_custom_call" | custom-call | flops 1000 | bytes 1000 | tf_op jit(solution)/shard_map/pallas_call | solution.py:432
  271.0 9.3 %shard_map.269 = (bf16[8,32,1024]{2,1,0:T(8,128)(2,1)}, bf16[8,32,1024]{2,1,0:T(8,128)(2,1)}, bf16[8,32,1024]{2,1,0:T(8,128)(2,1)}, bf16[8,32,1024]{2,1,0:T(8,128)(2,1)}) custom-call(s32[1]{0:T(128)} %bitcast.39.place.replica, bf16[2048,1024]{1,0:T(8,128)(2,1)} %all-gather.11.cloned.1.call-done.x_ref, bf16[2048,1024]{1,0:T(8,128)(2,1)} %get-tuple-element.173.g_ref), custom_call_target="tpu_custom_call" | custom-call | flops 1000 | bytes 1000 | tf_op jit(solution)/shard_map/pallas_call | solution.py:486
  283.8 9.2 %shard_map.270 = (bf16[256,1024]{1,0:T(8,128)(2,1)}, bf16[256,1024]{1,0:T(8,128)(2,1)}, bf16[256,1024]{1,0:T(8,128)(2,1)}, bf16[256,1024]{1,0:T(8,128)(2,1)}) custom-call(s32[1]{0:T(128)} %bitcast.39.place.replica, bf16[2048,1024]{1,0:T(8,128)(2,1)} %get-tuple-element.177.a_ref, bf16[2048,1024]{1,0:T(8,128)(2,1)} %all-gather.9.cloned.1.call-done.g_ref), custom_call_target="tpu_custom_call" | custom-call | flops 1000 | bytes 1000 | tf_op jit(solution)/shard_map/pallas_call | solution.py:519
  293.0 8.5 %shard_map.271 = bf16[2048,1024]{1,0:T(8,128)(2,1)} custom-call(bf16[2048,1024]{1,0:T(8,128)(2,1)} %get-tuple-element.177.a_ref, bf16[1024,1024]{1,0:T(8,128)(2,1)} %b_ref.1), custom_call_target="tpu_custom_call" | custom-call | flops 1000 | bytes 1000 | tf_op jit(solution)/shard_map/pallas_call | solution.py:535
  329.9 14.5 %shard_map.272 = (bf16[256,1024]{1,0:T(8,128)(2,1)}, bf16[4096,256]{1,0:T(8,128)(2,1)}) custom-call(s32[1]{0:T(128)S(6)} %copy.114.length, bf16[256,1024]{1,0:T(8,128)(2,1)} %fusion.2.q_ref, bf16[4096,256]{1,0:T(8,128)(2,1)} %all-gather.7.cloned.1.call-done.m_ref, bf16[256,1024]{1,0:T(8,128)(2,1)} %convolution_convert_fusion.2.g_ref), custom_call_target="tpu_custom_call" | custom-call | flops 1000 | bytes 1000 | tf_op jit(solution)/shard_map/pallas_call | solution.py:354
  371.1 16.9 %all-to-all-done.4 = bf16[256,8,128]{2,0,1:T(8,128)(2,1)} async-done(((bf16[256,8,128]{2,0,1:T(8,128)(2,1)}), bf16[256,8,128]{2,0,1:T(8,128)(2,1)}, u32[]{:S(2)}, u32[]{:S(2)}) %all-to-all-start.4) | async-done | bytes 524320 | tf_op jit(solution)/shard_map/all_to_all | solution.py:1090
  388.0 23.0 %shard_map.274.g_ref = bf16[2048,384]{1,0:T(8,128)(2,1)} custom-call(s32[2,4]{1,0:T(2,128)} %pad_add_fusion.ends, bf16[2048,384]{1,0:T(8,128)(2,1)} %get-tuple-element.131.q_ref.k_ref.v_ref, bf16[2048,384]{1,0:T(8,128)(2,1)} %get-tuple-element.131.q_ref.k_ref.v_ref, bf16[2048,384]{1,0:T(8,128)(2,1)} %get-tuple-element.131.q_ref.k_ref.v_ref, ...), custom_call_target="tpu_custom_call" | custom-call | flops 1000 | bytes 1000 | tf_op jit(solution)/shard_map/pallas_call | solution.py:269
  421.7 9.0 %shard_map.276 = (bf16[2048,1024]{1,0:T(8,128)(2,1)}, f32[2,1024]{1,0:T(2,128)}, f32[1,384]{1,0:T(1,128)}) custom-call(bf16[2048,384]{1,0:T(8,128)(2,1)} %shard_map.274.g_ref, bf16[1024,384]{1,0:T(8,128)(2,1)} %slice.206.qkv_w.w_ref, bf16[2048,1024]{1,0:T(8,128)(2,1)} %get-tuple-element.210.x_ref.one_ref), custom_call_target="tpu_custom_call" | custom-call | flops 1000 | bytes 1000 | tf_op jit(solution)/shard_map/pallas_call | solution.py:562
  465.5 8.6 %all-to-all-done.6 = bf16[8,37,640]{2,1,0:T(8,128)(2,1)S(1)} async-done(((bf16[8,37,640]{2,1,0:T(8,128)(2,1)}), bf16[8,37,640]{2,1,0:T(8,128)(2,1)S(1)}, u32[]{:S(2)}, u32[]{:S(2)}) %all-to-all-start.6) | async-done | bytes 378912 | tf_op jit(solution)/shard_map/all_to_all | solution.py:980
  483.8 12.5 %collective-permute-done.28 = bf16[64,1024]{1,0:T(8,128)(2,1)S(1)} collective-permute-done((bf16[64,1024]{1,0:T(8,128)(2,1)S(1)}, bf16[64,1024]{1,0:T(8,128)(2,1)S(1)}, u32[]{:S(2)}, u32[]{:S(2)}) %collective-permute-start.28) | collective-permute-done | bytes 131104 | tf_op jit(solution)/shard_map/ppermute | solution.py:728
  506.9 10.8 %collective-permute-done.37 = bf16[3,32,1024]{2,1,0:T(8,128)(2,1)S(1)} collective-permute-done((bf16[3,32,1024]{2,1,0:T(8,128)(2,1)S(1)}, bf16[3,32,1024]{2,1,0:T(8,128)(2,1)S(1)}, u32[]{:S(2)}, u32[]{:S(2)}) %collective-permute-start.37) | collective-permute-done | bytes 196640 | tf_op jit(solution)/shard_map/ppermute | solution.py:728
  (344 shorter events, 234.4 us)
Async XLA Ops:
  7.2 86.0 %all-gather.5.cloned.1.call-start = ((), (), s32[]{:S(2)}) async-start(), calls=%async_computation.11 | async-start | bytes 5898240 | tf_op jit(solution)/shard_map/all_gather | solution.py:974
  19.7 132.1 %all-gather.7.cloned.1.call-start = ((), (), s32[]{:S(2)}) async-start(), calls=%async_computation.12 | async-start | bytes 2359296 | tf_op jit(solution)/shard_map/all_gather | solution.py:974
  41.9 40.7 %collective-permute-start.5 = (bf16[3,32,1024]{2,1,0:T(8,128)(2,1)S(1)}, bf16[3,32,1024]{2,1,0:T(8,128)(2,1)S(1)}, u32[]{:S(2)}, u32[]{:S(2)}) collective-permute-start(bf16[3,32,1024]{2,1,0:T(8,128)(2,1)S(1)} %pad_maximum_fusion.5), channel_id=1, source_target_pairs={{0,6},{1,7},{2,0},{3,1},{4,2},{5,3},{6,4},{7,5},{8,14},{9,15},{10,... | collective-permute-start | bytes 589832 | tf_op jit(solution)/shard_map/ppermute | solution.py:728
  45.4 37.2 %collective-permute-start.4 = (bf16[3,32,1024]{2,1,0:T(8,128)(2,1)S(1)}, bf16[3,32,1024]{2,1,0:T(8,128)(2,1)S(1)}, u32[]{:S(2)}, u32[]{:S(2)}) collective-permute-start(bf16[3,32,1024]{2,1,0:T(8,128)(2,1)S(1)} %pad_maximum_fusion.5), channel_id=1, source_target_pairs={{0,4},{1,5},{2,6},{3,7},{4,0},{5,1},{6,2},{7,3},{8,12},{9,13},{10,... | collective-permute-start | bytes 589832 | tf_op jit(solution)/shard_map/ppermute | solution.py:728
  46.0 36.8 %collective-permute-start.1 = (bf16[8,32,640]{2,1,0:T(8,128)(2,1)S(1)}, bf16[8,32,640]{2,1,0:T(8,128)(2,1)S(1)}, u32[]{:S(2)}, u32[]{:S(2)}) collective-permute-start(bf16[8,32,640]{2,1,0:T(8,128)(2,1)S(1)} %slice.201), channel_id=1, source_target_pairs={{0,16},{8,24},{16,0},{24,8},{1,17},{9,25},{17,1},{25,9},{2,18},{10... | collective-permute-start | bytes 983048 | tf_op jit(solution)/shard_map/ppermute | solution.py:647
  104.7 47.2 %all-to-all-start.1 = ((bf16[8,32,1024]{2,1,0:T(8,128)(2,1)}), bf16[8,32,1024]{2,1,0:T(8,128)(2,1)S(1)}, u32[]{:S(2)}, u32[]{:S(2)}) async-start(bf16[8,32,1024]{2,1,0:T(8,128)(2,1)} %copy.69), calls=%async_computation.1 | async-start | bytes 1048576 | tf_op jit(solution)/shard_map/all_to_all | solution.py:980
  109.1 98.8 %all-gather.9.cloned.1.call-start = ((), (), s32[]{:S(2)}) async-start(), calls=%async_computation.13 | async-start | bytes 4718592 | tf_op jit(solution)/shard_map/all_gather | solution.py:974
  112.2 39.6 %collective-permute-start.8 = (bf16[3,4,32,1024]{3,2,1,0:T(8,128)(2,1)S(1)}, bf16[3,4,32,1024]{3,2,1,0:T(8,128)(2,1)}, u32[]{:S(2)}, u32[]{:S(2)}) collective-permute-start(bf16[3,4,32,1024]{3,2,1,0:T(8,128)(2,1)S(1)} %bitcast_dynamic-update-slice_fusion.7.refs_0_), channel_id=1, source_target_pairs={{0,24},{8,16},{16,8},{24,0},{1,25},{9,17},{17,9},{25,1},{2,26},{10... | collective-permute-start | bytes 2359304 | tf_op jit(solution)/shard_map/ppermute | solution.py:647
  156.9 98.0 %all-gather.11.cloned.1.call-start = ((), (), s32[]{:S(2)}) async-start(), calls=%async_computation.14 | async-start | bytes 4718592 | tf_op jit(solution)/shard_map/all_gather | solution.py:974
  207.9 112.0 %reduce-scatter.5.cloned.1.call-start = ((), (), s32[]{:S(2)}) async-start(), calls=%async_computation.15 | async-start | bytes 4718592 | tf_op jit(solution)/shard_map/reduce_scatter | solution.py:977
  301.5 42.9 %collective-permute-start.19 = (bf16[256,1024]{1,0:T(8,128)(2,1)}, bf16[256,1024]{1,0:T(8,128)(2,1)}, u32[]{:S(2)}, u32[]{:S(2)}) collective-permute-start(bf16[256,1024]{1,0:T(8,128)(2,1)} %get-tuple-element.187), channel_id=1, source_target_pairs={{0,8},{8,0},{16,24},{24,16},{1,9},{9,1},{17,25},{25,17},{2,10},{10... | collective-permute-start | bytes 1572872 | tf_op jit(solution)/shard_map/ppermute | solution.py:647
  302.8 41.6 %collective-permute-start.20 = (bf16[256,1024]{1,0:T(8,128)(2,1)}, bf16[256,1024]{1,0:T(8,128)(2,1)}, u32[]{:S(2)}, u32[]{:S(2)}) collective-permute-start(bf16[256,1024]{1,0:T(8,128)(2,1)} %get-tuple-element.188), channel_id=1, source_target_pairs={{0,16},{8,24},{16,0},{24,8},{1,17},{9,25},{17,1},{25,9},{2,18},{10... | collective-permute-start | bytes 1572872 | tf_op jit(solution)/shard_map/ppermute | solution.py:647
  304.3 40.1 %collective-permute-start.21 = (bf16[256,1024]{1,0:T(8,128)(2,1)}, bf16[256,1024]{1,0:T(8,128)(2,1)}, u32[]{:S(2)}, u32[]{:S(2)}) collective-permute-start(bf16[256,1024]{1,0:T(8,128)(2,1)} %get-tuple-element.189), channel_id=1, source_target_pairs={{0,24},{8,16},{16,8},{24,0},{1,25},{9,17},{17,9},{25,1},{2,26},{10... | collective-permute-start | bytes 1572872 | tf_op jit(solution)/shard_map/ppermute | solution.py:647
  314.0 97.1 %reduce-scatter.9.cloned.1.call-start = ((), (), s32[]{:S(2)}) async-start(), calls=%async_computation.17 | async-start | bytes 2359296 | tf_op jit(solution)/shard_map/reduce_scatter | solution.py:977
  344.5 191.2 %reduce-scatter.7.cloned.1.call-start = ((), (), s32[]{:S(2)}) async-start(), calls=%async_computation.16 | async-start | bytes 4718592 | tf_op jit(solution)/shard_map/reduce_scatter | solution.py:977
  360.1 50.9 %collective-permute-start.25 = (bf16[3,4,4,32,1024]{4,3,2,1,0:T(8,128)(2,1)}, bf16[3,4,4,32,1024]{4,3,2,1,0:T(8,128)(2,1)}, u32[]{:S(2)}, u32[]{:S(2)}) collective-permute-start(bf16[3,4,4,32,1024]{4,3,2,1,0:T(8,128)(2,1)} %get-tuple-element.208), channel_id=1, source_target_pairs={{0,1},{1,0},{2,3},{3,2},{4,5},{5,4},{6,7},{7,6},{8,9},{9,8},{10,11... | collective-permute-start | bytes 9437192 | tf_op jit(solution)/shard_map/ppermute | solution.py:721
  360.1 50.9 %collective-permute-start.24 = (bf16[512,1024]{1,0:T(8,128)(2,1)S(1)}, bf16[512,1024]{1,0:T(8,128)(2,1)S(1)}, u32[]{:S(2)}, u32[]{:S(2)}) collective-permute-start(bf16[512,1024]{1,0:T(8,128)(2,1)S(1)} %pad_maximum_fusion.refs_0_), channel_id=1, source_target_pairs={{0,24},{8,16},{16,8},{24,0},{1,25},{9,17},{17,9},{25,1},{2,26},{10... | collective-permute-start | bytes 3145736 | tf_op jit(solution)/shard_map/ppermute | solution.py:647
  362.6 48.5 %collective-permute-start.23 = (bf16[512,1024]{1,0:T(8,128)(2,1)S(1)}, bf16[512,1024]{1,0:T(8,128)(2,1)}, u32[]{:S(2)}, u32[]{:S(2)}) collective-permute-start(bf16[512,1024]{1,0:T(8,128)(2,1)S(1)} %pad_maximum_fusion.refs_0_), channel_id=1, source_target_pairs={{0,16},{8,24},{16,0},{24,8},{1,17},{9,25},{17,1},{25,9},{2,18},{10... | collective-permute-start | bytes 3145736 | tf_op jit(solution)/shard_map/ppermute | solution.py:647
  363.1 47.9 %collective-permute-start.22 = (bf16[512,1024]{1,0:T(8,128)(2,1)S(1)}, bf16[512,1024]{1,0:T(8,128)(2,1)}, u32[]{:S(2)}, u32[]{:S(2)}) collective-permute-start(bf16[512,1024]{1,0:T(8,128)(2,1)S(1)} %pad_maximum_fusion.refs_0_), channel_id=1, source_target_pairs={{0,8},{8,0},{16,24},{24,16},{1,9},{9,1},{17,25},{25,17},{2,10},{10... | collective-permute-start | bytes 3145736 | tf_op jit(solution)/shard_map/ppermute | solution.py:647
  421.7 116.1 %reduce-scatter.11.cloned.1.call-start = ((), (), s32[]{:S(2)}) async-start(), calls=%async_computation.18 | async-start | bytes 4718592 | tf_op jit(solution)/shard_map/reduce_scatter | solution.py:977
  442.2 35.3 %collective-permute-start.34 = (bf16[3,4,32,1024]{3,2,1,0:T(8,128)(2,1)}, bf16[3,4,32,1024]{3,2,1,0:T(8,128)(2,1)}, u32[]{:S(2)}, u32[]{:S(2)}) collective-permute-start(bf16[3,4,32,1024]{3,2,1,0:T(8,128)(2,1)} %get-tuple-element.231), channel_id=1, source_target_pairs={{0,16},{8,24},{16,0},{24,8},{1,17},{9,25},{17,1},{25,9},{2,18},{10... | collective-permute-start | bytes 2359304 | tf_op jit(solution)/shard_map/ppermute | solution.py:647
  480.3 40.7 %collective-permute-start.32 = (bf16[261,640]{1,0:T(8,128)(2,1)S(1)}, bf16[261,640]{1,0:T(8,128)(2,1)S(1)}, u32[]{:S(2)}, u32[]{:S(2)}) collective-permute-start(bf16[261,640]{1,0:T(8,128)(2,1)S(1)} %pad_maximum_fusion.4.refs_0_), channel_id=1, source_target_pairs={{0,24},{8,16},{16,8},{24,0},{1,25},{9,17},{17,9},{25,1},{2,26},{10... | collective-permute-start | bytes 1002248 | tf_op jit(solution)/shard_map/ppermute | solution.py:647
  482.0 39.5 %collective-permute-start.31 = (bf16[261,640]{1,0:T(8,128)(2,1)S(1)}, bf16[261,640]{1,0:T(8,128)(2,1)S(1)}, u32[]{:S(2)}, u32[]{:S(2)}) collective-permute-start(bf16[261,640]{1,0:T(8,128)(2,1)S(1)} %pad_maximum_fusion.4.refs_0_), channel_id=1, source_target_pairs={{0,16},{8,24},{16,0},{24,8},{1,17},{9,25},{17,1},{25,9},{2,18},{10... | collective-permute-start | bytes 1002248 | tf_op jit(solution)/shard_map/ppermute | solution.py:647
  482.5 39.0 %collective-permute-start.30 = (bf16[261,640]{1,0:T(8,128)(2,1)S(1)}, bf16[261,640]{1,0:T(8,128)(2,1)S(1)}, u32[]{:S(2)}, u32[]{:S(2)}) collective-permute-start(bf16[261,640]{1,0:T(8,128)(2,1)S(1)} %pad_maximum_fusion.4.refs_0_), channel_id=1, source_target_pairs={{0,8},{8,0},{16,24},{24,16},{1,9},{9,1},{17,25},{25,17},{2,10},{10... | collective-permute-start | bytes 1002248 | tf_op jit(solution)/shard_map/ppermute | solution.py:647
  (79 other events, 1140.9 us)
Sparse Core Ops, SparseCore 0:
  10.2 82.9 all-gather.4
  103.3 39.5 all-gather.6
  152.0 55.8 all-gather.8
  209.9 44.9 all-gather.10
  271.1 48.7 reduce-scatter.4
  344.6 38.1 reduce-scatter.8
  385.1 51.2 reduce-scatter.6
  438.7 75.4 reduce-scatter.10

commit v5 on v4

--- a/solution.py
+++ b/solution.py
@@ -68,36 +68,37 @@
     step = pl.program_id(0)
     rows = q_ref.shape[0]
     queries = head_halves(q_ref[...], SCALE)
-    query_seg = seg_col[...]
+    query_seg = seg_row[...]
     last_seg = ends[1, step]
 
     def piece(index, state, masked, diagonal):
-        keys = k_ref[pl.ds(index * rows, rows), :]
-        values = v_ref[pl.ds(index * rows, rows), :]
+        place = pl.ds(pl.multiple_of(index * rows, rows), rows)
+        keys = k_ref[place, :]
+        values = v_ref[place, :]
         keep = None
         if masked:
-            keep = seg_row[:, pl.ds(index * rows, rows)] == query_seg
+            keep = seg_col[place, :] == query_seg
             if diagonal:
-                key_pos = lax.broadcasted_iota(jnp.int32, (rows, rows), 1)
-                query_pos = lax.broadcasted_iota(jnp.int32, (rows, rows), 0)
+                key_pos = lax.broadcasted_iota(jnp.int32, (rows, rows), 0)
+                query_pos = lax.broadcasted_iota(jnp.int32, (rows, rows), 1)
                 keep = keep & (key_pos <= query_pos)
-        after = []
+        after_piece = []
         for head in range(2):
             top, total, acc = state[head]
-            scores = dot_nt(queries[head], keys)
+            scores = dot_nt(keys, queries[head])
             if masked:
                 scores = jnp.where(keep, scores, NEGATIVE)
-            top_new = jnp.maximum(top, jnp.max(scores, axis=1, keepdims=True))
+            top_new = jnp.maximum(top, jnp.max(scores, axis=0, keepdims=True))
             expo = jnp.exp(scores - top_new)
             fade = jnp.exp(top - top_new)
-            after.append(
+            after_piece.append(
                 (
                     top_new,
-                    total * fade + jnp.sum(expo, axis=1, keepdims=True),
-                    acc * fade + dot(low(expo), values),
+                    total * fade + jnp.sum(expo, axis=0, keepdims=True),
+                    acc * fade + dot_tn(values, low(expo)),
                 )
             )
-        return tuple(after)
+        return tuple(after_piece)
 
     def before(index, state):
         return lax.cond(
@@ -108,18 +109,20 @@
         )
 
     blank = (
-        jnp.full((rows, 1), NEGATIVE, jnp.float32),
-        jnp.zeros((rows, 1), jnp.float32),
-        jnp.zeros((rows, PAIR), jnp.float32),
+        jnp.full((1, rows), NEGATIVE, jnp.float32),
+        jnp.zeros((1, rows), jnp.float32),
+        jnp.zeros((PAIR, rows), jnp.float32),
     )
     state = lax.fori_loop(0, step, before, (blank, blank))
     state = piece(step, state, True, True)
-    lane = lax.broadcasted_iota(jnp.int32, (rows, PAIR), 1)
-    joined = jnp.where(lane < HD, state[0][2] / state[0][1], state[1][2] / state[1][1])
+    parts = [
+        (state[head][2] * (1.0 / state[head][1]))[head * HD : (head + 1) * HD] for head in range(2)
+    ]
+    joined = jnp.concatenate(parts, axis=0).T
     full_ref[...] = joined
     low_ref[...] = low(joined)
-    lse_ref[:, 0:1] = state[0][0] + jnp.log(state[0][1])
-    lse_ref[:, 1:2] = state[1][0] + jnp.log(state[1][1])
+    lse_ref[0:1, :] = state[0][0] + jnp.log(state[0][1])
+    lse_ref[1:2, :] = state[1][0] + jnp.log(state[1][1])
 
 
 def block_ends(segments, rows):
@@ -138,13 +141,13 @@
             pl.BlockSpec((rows, PAIR), lambda i, e: (i, 0)),
             pl.BlockSpec((count, PAIR), lambda i, e: (0, 1)),
             pl.BlockSpec((count, PAIR), lambda i, e: (0, 2)),
-            pl.BlockSpec((rows, 1), lambda i, e: (i, 0)),
-            pl.BlockSpec((1, count), lambda i, e: (0, 0)),
+            pl.BlockSpec((count, 1), lambda i, e: (0, 0)),
+            pl.BlockSpec((1, rows), lambda i, e: (0, i)),
         ],
         out_specs=[
             pl.BlockSpec((rows, PAIR), lambda i, e: (i, 0)),
             pl.BlockSpec((rows, PAIR), lambda i, e: (i, 0)),
-            pl.BlockSpec((rows, 2), lambda i, e: (i, 0)),
+            pl.BlockSpec((2, rows), lambda i, e: (0, i)),
         ],
     )
     return pl.pallas_call(
@@ -153,7 +156,7 @@
         out_shape=(
             jax.ShapeDtypeStruct((count, PAIR), jnp.bfloat16),
             jax.ShapeDtypeStruct((count, PAIR), jnp.float32),
-            jax.ShapeDtypeStruct((count, 2), jnp.float32),
+            jax.ShapeDtypeStruct((2, count), jnp.float32),
         ),
         compiler_params=pltpu.CompilerParams(vmem_limit_bytes=58 * 2**20),
         cost_estimate=LITTLE,
@@ -207,11 +210,11 @@
             grad_probs = dot_nt(values, grads[head])
             grad_scores = low(probs * (grad_probs - delta_ref[head : head + 1, place]))
             part_k = dot(grad_scores, queries[head])
-            part_q = dot_tn(grad_scores, key_halves[head])
+            part_q = dot_tn(key_halves[head], grad_scores)
             sum_q = part_q if sum_q is None else sum_q + part_q
             sum_k = part_k if sum_k is None else sum_k + part_k
             sum_v = part_v if sum_v is None else sum_v + part_v
-        acc_q[place, :] += sum_q
+        acc_q[:, place] += sum_q
         if diagonal:
             acc_k[...] = sum_k
             acc_v[...] = sum_v
@@ -234,7 +237,7 @@
             piece(index, True, False)
 
     own = pl.ds(pl.multiple_of(step * rows, rows), rows)
-    grad_ref[own, 0:PAIR] = low(acc_q[own, :])
+    grad_ref[own, 0:PAIR] = low(acc_q[:, own].T)
     grad_ref[own, PAIR : 2 * PAIR] = low(acc_k[...])
     grad_ref[own, 2 * PAIR : 3 * PAIR] = low(acc_v[...])
 
@@ -260,7 +263,7 @@
         ],
         out_specs=pl.BlockSpec((count, 3 * PAIR), whole),
         scratch_shapes=[
-            pltpu.VMEM((count, PAIR), jnp.float32),
+            pltpu.VMEM((PAIR, count), jnp.float32),
             pltpu.VMEM((rows, PAIR), jnp.float32),
             pltpu.VMEM((rows, PAIR), jnp.float32),
             pltpu.VMEM((8, count), jnp.float32),
@@ -362,49 +365,37 @@
     )(length, queries, memory, grads)
 
 
-def front_kernel(x_ref, e_ref, gain, shift, qkv_w, qkv_b, mem_w, mem_b, one_ref, qkv_ref, enc_ref, mem_ref):
-    rows = x_ref[0].astype(jnp.float32)
+def front_kernel(x_ref, gain, shift, qkv_w, qkv_b, one_ref, qkv_ref):
+    rows = x_ref[...].astype(jnp.float32)
     centered = rows - jnp.mean(rows, axis=-1, keepdims=True)
     inverse = lax.rsqrt(jnp.mean(centered * centered, axis=-1, keepdims=True) + EPS)
     one = low(centered * inverse * gain[...] + shift[...])
     one_ref[...] = one
     qkv_ref[...] = low(dot(one, qkv_w[...]) + qkv_b[...])
-    enc_ref[...] = e_ref[0]
-    mem_ref[...] = low(dot(e_ref[0], mem_w[...]) + mem_b[...])
-
-
-def front(rows_all, row_count, gain, shift, qkv_w, qkv_b, mem_w, mem_b):
-    span, both, _ = rows_all.shape
-    enc_rows = both - row_count
+
+
+def front(rows, gain, shift, qkv_w, qkv_b):
+    count, tile = rows.shape[0], 256
     whole = lambda i: (0, 0)
+    block = lambda i: (i, 0)
     return pl.pallas_call(
         front_kernel,
-        grid=(span,),
+        grid=(count // tile,),
         in_specs=[
-            pl.BlockSpec((1, row_count, D), lambda i: (i, 0, 0)),
-            pl.BlockSpec((1, enc_rows, D), lambda i: (i, row_count // enc_rows, 0)),
+            pl.BlockSpec((tile, D), block),
             pl.BlockSpec((1, D), whole),
             pl.BlockSpec((1, D), whole),
             pl.BlockSpec(qkv_w.shape, whole),
             pl.BlockSpec((1, qkv_w.shape[1]), whole),
-            pl.BlockSpec(mem_w.shape, whole),
-            pl.BlockSpec((1, mem_w.shape[1]), whole),
-        ],
-        out_specs=[
-            pl.BlockSpec((row_count, D), lambda i: (i, 0)),
-            pl.BlockSpec((row_count, qkv_w.shape[1]), lambda i: (i, 0)),
-            pl.BlockSpec((enc_rows, D), lambda i: (i, 0)),
-            pl.BlockSpec((enc_rows, mem_w.shape[1]), lambda i: (i, 0)),
-        ],
+        ],
+        out_specs=[pl.BlockSpec((tile, D), block), pl.BlockSpec((tile, qkv_w.shape[1]), block)],
         out_shape=(
-            jax.ShapeDtypeStruct((span * row_count, D), jnp.bfloat16),
-            jax.ShapeDtypeStruct((span * row_count, qkv_w.shape[1]), jnp.bfloat16),
-            jax.ShapeDtypeStruct((span * enc_rows, D), jnp.bfloat16),
-            jax.ShapeDtypeStruct((span * enc_rows, mem_w.shape[1]), jnp.bfloat16),
+            jax.ShapeDtypeStruct((count, D), jnp.bfloat16),
+            jax.ShapeDtypeStruct((count, qkv_w.shape[1]), jnp.bfloat16),
         ),
         compiler_params=pltpu.CompilerParams(vmem_limit_bytes=58 * 2**20),
         cost_estimate=LITTLE,
-    )(rows_all, rows_all, gain[None], shift[None], qkv_w, qkv_b[None], mem_w, mem_b[None])
+    )(rows, gain[None], shift[None], qkv_w, qkv_b[None])
 
 
 def feed_kernel(x_ref, w_ref, b_ref, ga_ref, act_ref, pre_ref, in_ref, sum_ref):
@@ -819,13 +810,15 @@
     return qkv.reshape(size * rows, 3 * D), memory.reshape(size * rows, 2 * D)
 
 
-def weight_line(piece):
-    kinds, rows, columns = piece.shape
-    chips = lax.axis_size("shard") // 2
-    chip = lax.axis_index("shard") // 2
-    line = jnp.zeros((kinds, chips, rows, columns), piece.dtype)
-    for step in range(chips):
-        part = line_send(piece, step) if step else piece
+def line_start(piece):
+    return [piece] + [line_send(piece, step) for step in range(1, lax.axis_size("shard") // 2)]
+
+
+def line_place(parts):
+    chips, chip = len(parts), lax.axis_index("shard") // 2
+    kinds, rows, columns = parts[0].shape
+    line = jnp.zeros((kinds, chips, rows, columns), parts[0].dtype)
+    for step, part in enumerate(parts):
         line = lax.dynamic_update_slice_in_dim(line, part[:, None], (chip - step) % chips, 1)
     return line
 
@@ -986,7 +979,6 @@
         blocks = weight.reshape(part_rows, kinds, span, width).transpose(2, 0, 1, 3)
         return blocks.reshape(span, part_rows, kinds * width)
 
-    rows_all = gather(jnp.concatenate([tokens, enc_states], axis=0), groups)
     blocks = jnp.concatenate([by_pairs(own_part(self_qkv), 3), by_pairs(own_part(cross_memory), 2)], axis=2)
     blocks = jnp.tile(blocks, (count // span, 1, 1))
     small = jnp.concatenate([norm_gain, norm_bias, proj_bias], axis=0)
@@ -995,42 +987,42 @@
     small = jnp.pad(small.reshape(-1), (0, small_rows * 5 * width - small.size)).reshape(small_rows, 5 * width)
     blocks = jnp.concatenate([blocks, jnp.broadcast_to(small, (count,) + small.shape)], axis=1)
     swapped = swap(blocks)
+    plain_parts = line_start(jnp.stack([own_part(self_out), own_part(cross_query), own_part(cross_out)]))
+    enc_all = gather(enc_states, groups)
+    swapped, plain_parts, enc_all = lax.optimization_barrier((swapped, plain_parts, enc_all))
+    rows_all = gather(after(tokens, plain_parts, enc_all), groups)
     small_all = swapped[:, part_rows:].reshape(count, small_rows * 5 * width)[:, : small_count * shard_width]
     small_all = small_all.reshape(count, small_count, shard_width)
     small_all = small_all.transpose(1, 0, 2).reshape(small_count, D).astype(jnp.float32)
     gain_rows, shift_rows, bias_rows = small_all[:3], small_all[3:6], small_all[6:]
     head_weight = rep_gather(swapped[:, :part_rows], 1).reshape(D, 5 * width)
     qkv_weight, memory_weight = head_weight[:, : 3 * width], head_weight[:, 3 * width :]
-    plain_part = jnp.stack([own_part(self_out), own_part(cross_query), own_part(cross_out)])
-    plain_line = weight_line(after(plain_part, swapped))
-    plain_mine = rep_start(plain_line)
-    rows_all, head_weight, _ = lax.optimization_barrier((rows_all, head_weight, plain_line))
-    expand_part = own_part(expand_weight).reshape(part_rows, count, hidden).transpose(1, 0, 2)
-    expand_swapped = swap(after(expand_part, rows_all))
-
-    rows_all = rows_all.reshape(span, row_count + enc_rows, D)
-    seq_segments = lax.dynamic_slice_in_dim(segments, local_seq * SEQ, SEQ)
+    qkv_weight, memory_weight = head_weight[:, : 3 * width], head_weight[:, 3 * width :]
     own_bias = lax.dynamic_slice_in_dim(bias_rows, local_pos * width, width, axis=1)
     zero_bias = jnp.zeros((width,), jnp.float32)
+    memory_pair = low(dot(enc_all, memory_weight) + jnp.concatenate([zero_bias, own_bias[4]]))
+    plain_mine = rep_start(line_place(after(plain_parts, head_weight)))
+    rows_all, qkv_weight, memory_weight, plain_mine[1], plain_mine[2] = lax.optimization_barrier(
+        (rows_all, qkv_weight, memory_weight, plain_mine[1], plain_mine[2])
+    )
+    memory_all = gather(after(memory_pair, rows_all), groups)
+    expand_part = own_part(after(expand_weight, rows_all)).reshape(part_rows, count, hidden).transpose(1, 0, 2)
+    expand_swapped = swap(expand_part)
+
+    seq_segments = lax.dynamic_slice_in_dim(segments, local_seq * SEQ, SEQ)
     qkv_bias = jnp.concatenate([own_bias[0], zero_bias, own_bias[1]])
-    memory_bias = jnp.concatenate([zero_bias, own_bias[4]])
-    input_one_all, qkv, enc_all, memory_pair = front(
-        rows_all, row_count, gain_rows[0], shift_rows[0], qkv_weight, qkv_bias, memory_weight, memory_bias
-    )
-    qkv, plain_mine[1], plain_mine[2] = lax.optimization_barrier((qkv, plain_mine[1], plain_mine[2]))
+    input_one_all, qkv = front(rows_all, gain_rows[0], shift_rows[0], qkv_weight, qkv_bias)
     att_low, att_full, lse = self_forward(qkv, seq_segments)
-    att_low, expand_swapped, plain_mine = lax.optimization_barrier((att_low, expand_swapped, plain_mine))
+    att_low, memory_all, plain_mine, expand_swapped = lax.optimization_barrier(
+        (att_low, memory_all, plain_mine, expand_swapped)
+    )
+    grad_all = gather(after(cotangent, memory_all))
+    plain_other = [core_send(part) for part in plain_mine]
+    attn_proj, query_in, cross_proj = weight_join(plain_mine, plain_other)
     attended = lax.all_to_all(att_low, "shard", 0, 1, tiled=True, axis_index_groups=groups)
 
-    memory_all = gather(memory_pair, groups)
     enc_count = lax.dynamic_slice_in_dim(enc_lengths, local_seq, 1)
-    plain_other = [core_send(part) for part in plain_mine]
-
-    plain_mine, plain_other = after((plain_mine, plain_other), att_low)
-    attn_proj, query_in, cross_proj = weight_join(plain_mine, plain_other)
-    attended, attn_proj, query_in, cross_proj = lax.optimization_barrier((attended, attn_proj, query_in, cross_proj))
-    grad_all = gather(after(cotangent, memory_all, att_low))
-    expand_parts = rep_start(after(expand_swapped, attended).reshape(count * part_rows, hidden))
+
     residual_in = tokens.astype(jnp.float32)
     hidden_one = residual_in + dot(attended, attn_proj) + bias_rows[2]
     input_two = low(norm_apply(hidden_one, gain_rows[1], shift_rows[1]))
@@ -1039,8 +1031,9 @@
     hidden_two = hidden_one + dot(context, cross_proj) + bias_rows[5]
     input_three = low(norm_apply(hidden_two, gain_rows[2], shift_rows[2]))
 
-    input_three_all = gather(after(input_three, grad_all))
-    expand_parts, grad_all_now = after((expand_parts, grad_all), input_three)
+    input_three_all = gather(input_three)
+    expand_parts = rep_start(expand_swapped.reshape(count * part_rows, hidden))
+    grad_all_now = after(grad_all, input_three)
     expand_local = spread(expand_parts, 0, count * part_rows, jnp.bfloat16)
     expand_local = expand_local.reshape(size, count, part_rows, hidden).transpose(1, 0, 2, 3).reshape(D, hidden)
     grad_act = dot_nt(grad_all_now, shrink_weight)
@@ -1095,7 +1088,7 @@
     grad_att_heads, plain_own = lax.optimization_barrier((grad_att_heads, plain_own))
 
     feed_gather = rep_start(own_feed)
-    grad_qkv = self_backward(qkv, grad_att_heads, lse.T, att_full, seq_segments)
+    grad_qkv = self_backward(qkv, grad_att_heads, lse, att_full, seq_segments)
     grad_qkv, feed_gather, plain_theirs = lax.optimization_barrier((grad_qkv, feed_gather, plain_theirs))
     heads_parts = heads_grads(input_one_all, grad_qkv, enc_all, mem_grads, count, part_rows)
     heads_swapped = rep_swap(heads_parts)

time: 557 us -> 543 us (0.975)
  the two profiles are of different devices: /device:TPU:0 before, /device:TPU:12 now
where the time goes in v5:
time: 543 us; the launch traced here: 534 us
  Pallas kernels  167 us (31%)
  waiting for transfers between devices  157 us (29%)
  starting transfers between devices  89 us (16%)
  local copies, waits for them, and re-layouts  32.3 us (6%)
  other arithmetic  26.3 us (5%)
  matrix products  24.3 us (4%)
  blocking collectives  21.9 us (4%)
  between operations  15.8 us (3%)
    ppermute x9, waiting for transfers between devices, line_send(): return lax.ppermute(value, 'shard', route)  63.4 us
    ppermute x27, waiting for transfers between devices, rep_send(): return lax.ppermute(value, 'rep', [(i, i ^ step) for i in range(size)])  55.4 us
    ppermute x27, starting transfers between devices, rep_send(): return lax.ppermute(value, 'rep', [(i, i ^ step) for i in range(size)])  32.1 us
    all_to_all x4, starting transfers between devices, swap(): return lax.all_to_all(value, 'shard', 0, 0, tiled=True)  23.6 us
    all_to_all x1, blocking collectives, shards(): lax.all_to_all(grad_attn, 'shard', 1, 0, tiled=True, axis_index_groups=gr...  21.9 us
    pallas_call x1, Pallas kernels, self_backward(): pl.pallas_call(self_backward_kernel, grid_spec=grid_spec, out_shape=jax.S...  21.5 us
    all_gather x5, waiting for transfers between devices, gather(): lax.all_gather(value, 'shard', axis=0, tiled=True, axis_index_groups=groups)  21.5 us
    dot_general x5, matrix products, dot_nt(): lax.dot_general(left, right, (((1,), (1,)), ((), ())), preferred_element_...  16.5 us
  transfers between devices with their start and end apart: 57, of which 28 were waited for; matrix products, arithmetic and copies ran while one was open for 13% of the time, Pallas kernels for 28%

profile of v5, /device:TPU:12, one launch (start us, length us, event | category | flops | bytes accessed | tf_op | source)
XLA Modules:
  0.0 533.6 jit_solution(15902321767664140837)
XLA Ops:
  22.8 24.2 %collective-permute-done = bf16[3,32,1024]{2,1,0:T(8,128)(2,1)S(1)} collective-permute-done((bf16[3,32,1024]{2,1,0:T(8,128)(2,1)S(1)}, bf16[3,32,1024]{2,1,0:T(8,128)(2,1)S(1)}, u32[]{:S(2)}, u32[]{:S(2)}) %collective-permute-start) | collective-permute-done | bytes 196640 | tf_op jit(solution)/shard_map/ppermute | solution.py:719
  57.9 6.9 %collective-permute-done.3 = bf16[8,32,640]{2,1,0:T(8,128)(2,1)S(1)} collective-permute-done((bf16[8,32,640]{2,1,0:T(8,128)(2,1)S(1)}, bf16[8,32,640]{2,1,0:T(8,128)(2,1)S(1)}, u32[]{:S(2)}, u32[]{:S(2)}) %collective-permute-start.3) | collective-permute-done | bytes 327712 | tf_op jit(solution)/shard_map/ppermute | solution.py:638
  64.8 6.8 %collective-permute-done.4 = bf16[8,32,640]{2,1,0:T(8,128)(2,1)S(1)} collective-permute-done((bf16[8,32,640]{2,1,0:T(8,128)(2,1)S(1)}, bf16[8,32,640]{2,1,0:T(8,128)(2,1)S(1)}, u32[]{:S(2)}, u32[]{:S(2)}) %collective-permute-start.4) | collective-permute-done | bytes 327712 | tf_op jit(solution)/shard_map/ppermute | solution.py:638
  76.7 12.4 %collective-permute-done.6.refs_1_ = bf16[3,4,32,1024]{3,2,1,0:T(8,128)(2,1)} collective-permute-done((bf16[3,4,32,1024]{3,2,1,0:T(8,128)(2,1)S(1)}, bf16[3,4,32,1024]{3,2,1,0:T(8,128)(2,1)}, u32[]{:S(2)}, u32[]{:S(2)}) %collective-permute-start.6) | collective-permute-done | bytes 786464 | tf_op jit(solution)/shard_map/ppermute | solution.py:638
  90.3 8.6 %all-gather.8.cloned.1.call-done.x_ref = bf16[2048,1024]{1,0:T(8,128)(2,1)} async-done(((bf16[256,1024]{1,0:T(8,128)(2,1)}), bf16[2048,1024]{1,0:T(8,128)(2,1)}) %all-gather.8.cloned.1.call-update) | async-done | bytes 4194320 | tf_op jit(solution)/shard_map/all_gather | solution.py:967
  110.7 9.2 %shard_map.263 = (bf16[2048,1024]{1,0:T(8,128)(2,1)}, bf16[2048,384]{1,0:T(8,128)(2,1)}) custom-call(bf16[2048,1024]{1,0:T(8,128)(2,1)} %all-gather.8.cloned.1.call-done.x_ref, f32[1,1024]{1,0:T(1,128)} %bitcast.250, f32[1,1024]{1,0:T(1,128)} %bitcast.254, bf16[1024,384]{1,0:T(8,128)(2,1)} %slice.201.qkv_w.w_ref, f32[1,384]{1,0:T(1,128)} %broadcast_in_dim.102.qkv_b), custom_call_target="tpu_custom_call" | custom-call | flops 1000 | bytes 1000 | tf_op jit(solution)/shard_map/pallas_call | solution.py:381
  119.9 15.6 %shard_map.264 = (bf16[2048,128]{1,0:T(8,128)(2,1)}, f32[2048,128]{1,0:T(8,128)}, f32[2,2048]{1,0:T(2,128)}) custom-call(s32[2,4]{1,0:T(2,128)} %pad_add_fusion.ends, bf16[2048,384]{1,0:T(8,128)(2,1)} %get-tuple-element.134.q_ref.k_ref.v_ref, bf16[2048,384]{1,0:T(8,128)(2,1)} %get-tuple-element.134.q_ref.k_ref.v_ref, ...), custom_call_target="tpu_custom_call" | custom-call | flops 1000 | bytes 1000 | tf_op jit(solution)/shard_map/pallas_call | solution.py:153
  143.2 11.0 %all-gather.12.cloned.1.call-start = ((), (), s32[]{:S(2)}) async-start(), calls=%async_computation.14 | async-start | bytes 4718592 | tf_op jit(solution)/shard_map/all_gather | solution.py:967
  172.7 8.6 %shard_map.266.c_ref = bf16[256,1024]{1,0:T(8,128)(2,1)} custom-call(s32[1]{0:T(128)S(6)} %copy.114.length, bf16[256,1024]{1,0:T(8,128)(2,1)} %fusion.2.q_ref, bf16[4096,256]{1,0:T(8,128)(2,1)} %all-gather.10.cloned.1.call-done.m_ref), custom_call_target="tpu_custom_call" | custom-call | flops 1000 | bytes 1000 | tf_op jit(solution)/shard_map/pallas_call | solution.py:307
  189.5 10.7 %collective-permute-done.13.refs_1_ = bf16[256,1024]{1,0:T(8,128)(2,1)S(1)} collective-permute-done((bf16[256,1024]{1,0:T(8,128)(2,1)S(1)}, bf16[256,1024]{1,0:T(8,128)(2,1)S(1)}, u32[]{:S(2)}, u32[]{:S(2)}) %collective-permute-start.13) | collective-permute-done | bytes 524320 | tf_op jit(solution)/shard_map/ppermute | solution.py:638
  200.1 11.6 %collective-permute-done.14.refs_2_ = bf16[256,1024]{1,0:T(8,128)(2,1)S(1)} collective-permute-done((bf16[256,1024]{1,0:T(8,128)(2,1)S(1)}, bf16[256,1024]{1,0:T(8,128)(2,1)S(1)}, u32[]{:S(2)}, u32[]{:S(2)}) %collective-permute-start.14) | collective-permute-done | bytes 524320 | tf_op jit(solution)/shard_map/ppermute | solution.py:638
  219.2 10.8 %fusion.31.ga_ref = f32[2048,1024]{1,0:T(8,128)} fusion(bf16[2048,1024]{1,0:T(8,128)(2,1)} %all-gather.14.cloned.1.call-done.g_ref, bf16[1024,1024]{1,0:T(8,128)(2,1)} %b_ref.1), kind=kOutput, calls=%fused_computation.139 | convolution fusion | flops 4294967296 | bytes 14680064 | tf_op jit(solution)/shard_map/dot_general | solution.py:48
  230.0 10.0 %all-gather.12.cloned.1.call-done.x_ref = bf16[2048,1024]{1,0:T(8,128)(2,1)} async-done(((bf16[256,1024]{1,0:T(8,128)(2,1)}), bf16[2048,1024]{1,0:T(8,128)(2,1)}) %all-gather.12.cloned.1.call-update) | async-done | bytes 4194320 | tf_op jit(solution)/shard_map/all_gather | solution.py:967
  240.0 16.0 %shard_map.268 = (bf16[2048,1024]{1,0:T(8,128)(2,1)}, bf16[2048,1024]{1,0:T(8,128)(2,1)}, bf16[2048,1024]{1,0:T(8,128)(2,1)}, f32[1,1024]{1,0:T(1,128)}) custom-call(bf16[2048,1024]{1,0:T(8,128)(2,1)} %all-gather.12.cloned.1.call-done.x_ref, bf16[1024,1024]{1,0:T(8,128)(2,1)} %bitcast.215, f32[1,1024]{1,0:T(1,128)} %bitcast.257, f32[2048,1024]{1,0:T(8,128)} %fusion.31.ga_ref), custom_call_target="tpu_custom_call" | custom-call | flops 1000 | bytes 1000 | tf_op jit(solution)/shard_map/pallas_call | solution.py:423
  256.1 9.2 %shard_map.269 = (bf16[8,32,1024]{2,1,0:T(8,128)(2,1)}, bf16[8,32,1024]{2,1,0:T(8,128)(2,1)}, bf16[8,32,1024]{2,1,0:T(8,128)(2,1)}, bf16[8,32,1024]{2,1,0:T(8,128)(2,1)}) custom-call(s32[1]{0:T(128)} %bitcast.37.place.replica, bf16[2048,1024]{1,0:T(8,128)(2,1)} %all-gather.12.cloned.1.call-done.x_ref, bf16[2048,1024]{1,0:T(8,128)(2,1)} %get-tuple-element.159.g_ref), custom_call_target="tpu_custom_call" | custom-call | flops 1000 | bytes 1000 | tf_op jit(solution)/shard_map/pallas_call | solution.py:477
  268.8 9.2 %shard_map.270 = (bf16[256,1024]{1,0:T(8,128)(2,1)}, bf16[256,1024]{1,0:T(8,128)(2,1)}, bf16[256,1024]{1,0:T(8,128)(2,1)}, bf16[256,1024]{1,0:T(8,128)(2,1)}) custom-call(s32[1]{0:T(128)} %bitcast.37.place.replica, bf16[2048,1024]{1,0:T(8,128)(2,1)} %get-tuple-element.163.a_ref, bf16[2048,1024]{1,0:T(8,128)(2,1)} %all-gather.14.cloned.1.call-done.g_ref), custom_call_target="tpu_custom_call" | custom-call | flops 1000 | bytes 1000 | tf_op jit(solution)/shard_map/pallas_call | solution.py:510
  277.9 8.8 %shard_map.271 = bf16[2048,1024]{1,0:T(8,128)(2,1)} custom-call(bf16[2048,1024]{1,0:T(8,128)(2,1)} %get-tuple-element.163.a_ref, bf16[1024,1024]{1,0:T(8,128)(2,1)} %b_ref.1), custom_call_target="tpu_custom_call" | custom-call | flops 1000 | bytes 1000 | tf_op jit(solution)/shard_map/pallas_call | solution.py:526
  313.9 14.5 %shard_map.272 = (bf16[256,1024]{1,0:T(8,128)(2,1)}, bf16[4096,256]{1,0:T(8,128)(2,1)}) custom-call(s32[1]{0:T(128)S(6)} %copy.114.length, bf16[256,1024]{1,0:T(8,128)(2,1)} %fusion.2.q_ref, bf16[4096,256]{1,0:T(8,128)(2,1)} %all-gather.10.cloned.1.call-done.m_ref, bf16[256,1024]{1,0:T(8,128)(2,1)} %convolution_convert_fusion.2.g_ref), custom_call_target="tpu_custom_call" | custom-call | flops 1000 | bytes 1000 | tf_op jit(solution)/shard_map/pallas_call | solution.py:357
  350.6 21.9 %all_to_all.63 = bf16[256,8,128]{2,0,1:T(8,128)(2,1)} all-to-all(bf16[256,8,128]{2,0,1:T(8,128)(2,1)S(1)} %copy_bitcast_fusion.1), channel_id=1, replica_groups=mesh['rep'=4,'shard'=8] {'shard'}, dimensions={1} | all-to-all | bytes 1048576 | tf_op jit(solution)/shard_map/all_to_all | solution.py:1083
  372.5 21.5 %shard_map.274.g_ref = bf16[2048,384]{1,0:T(8,128)(2,1)} custom-call(s32[2,4]{1,0:T(2,128)} %pad_add_fusion.ends, bf16[2048,384]{1,0:T(8,128)(2,1)} %get-tuple-element.134.q_ref.k_ref.v_ref, bf16[2048,384]{1,0:T(8,128)(2,1)} %get-tuple-element.134.q_ref.k_ref.v_ref, bf16[2048,384]{1,0:T(8,128)(2,1)} %get-tuple-element.134.q_ref.k_ref.v_ref, ...), custom_call_target="tpu_custom_call" | custom-call | flops 1000 | bytes 1000 | tf_op jit(solution)/shard_map/pallas_call | solution.py:272
  397.2 6.7 %shard_map.275 = bf16[4,8,32,640]{3,2,1,0:T(8,128)(2,1)} custom-call(bf16[2048,1024]{1,0:T(8,128)(2,1)} %get-tuple-element.196.x_ref.one_ref, bf16[2048,384]{1,0:T(8,128)(2,1)} %shard_map.274.g_ref, bf16[512,1024]{1,0:T(8,128)(2,1)} %all-gather.6.cloned.1.call-done.e_ref, bf16[512,256]{1,0:T(8,128)(2,1)} %reduce-scatter.9.cloned.1.call-done.m_ref), custom_call_target="tpu_custom_call" | custom-call | flops 1000 | bytes 1000 | tf_op jit(solution)/shard_map/pallas_call | solution.py:596
  408.0 8.9 %shard_map.276 = (bf16[2048,1024]{1,0:T(8,128)(2,1)}, f32[2,1024]{1,0:T(2,128)}, f32[1,384]{1,0:T(1,128)}) custom-call(bf16[2048,384]{1,0:T(8,128)(2,1)} %shard_map.274.g_ref, bf16[1024,384]{1,0:T(8,128)(2,1)} %slice.201.qkv_w.w_ref, bf16[2048,1024]{1,0:T(8,128)(2,1)} %get-tuple-element.196.x_ref.one_ref), custom_call_target="tpu_custom_call" | custom-call | flops 1000 | bytes 1000 | tf_op jit(solution)/shard_map/pallas_call | solution.py:553
  433.5 6.7 %all-to-all-start.6 = ((bf16[8,37,640]{2,1,0:T(8,128)(2,1)}), bf16[8,37,640]{2,1,0:T(8,128)(2,1)S(1)}, u32[]{:S(2)}, u32[]{:S(2)}) async-start(bf16[8,37,640]{2,1,0:T(8,128)(2,1)} %pad_maximum_fusion.2), calls=%async_computation.10 | async-start | bytes 819200 | tf_op jit(solution)/shard_map/all_to_all | solution.py:973
  487.7 14.2 %collective-permute-done.37 = bf16[3,32,1024]{2,1,0:T(8,128)(2,1)S(1)} collective-permute-done((bf16[3,32,1024]{2,1,0:T(8,128)(2,1)S(1)}, bf16[3,32,1024]{2,1,0:T(8,128)(2,1)S(1)}, u32[]{:S(2)}, u32[]{:S(2)}) %collective-permute-start.37) | collective-permute-done | bytes 196640 | tf_op jit(solution)/shard_map/ppermute | solution.py:719
  (359 shorter events, 233.5 us)
Async XLA Ops:
  7.2 46.1 %all-gather.6.cloned.1.call-start = ((), (), s32[]{:S(2)}) async-start(), calls=%async_computation.11 | async-start | bytes 1179648 | tf_op jit(solution)/shard_map/all_gather | solution.py:967
  11.3 42.1 %all-to-all-start = ((bf16[8,35,640]{2,1,0:T(8,128)(2,1)}), bf16[8,35,640]{2,1,0:T(8,128)(2,1)S(1)}, u32[]{:S(2)}, u32[]{:S(2)}) async-start(bf16[8,35,640]{2,1,0:T(8,128)(2,1)} %pad_maximum_fusion.1), calls=%async_computation | async-start | bytes 819200 | tf_op jit(solution)/shard_map/all_to_all | solution.py:973
  16.6 82.3 %all-gather.8.cloned.1.call-start = ((), (), s32[]{:S(2)}) async-start(), calls=%async_computation.12 | async-start | bytes 4718592 | tf_op jit(solution)/shard_map/all_gather | solution.py:967
  53.4 85.1 %all-gather.10.cloned.1.call-start = ((), (), s32[]{:S(2)}) async-start(), calls=%async_computation.13 | async-start | bytes 2359296 | tf_op jit(solution)/shard_map/all_gather | solution.py:967
  100.5 35.1 %all-to-all-start.1 = ((bf16[8,32,1024]{2,1,0:T(8,128)(2,1)}), bf16[8,32,1024]{2,1,0:T(8,128)(2,1)S(1)}, u32[]{:S(2)}, u32[]{:S(2)}) async-start(bf16[8,32,1024]{2,1,0:T(8,128)(2,1)} %copy.67), calls=%async_computation.1 | async-start | bytes 1048576 | tf_op jit(solution)/shard_map/all_to_all | solution.py:973
  105.9 113.3 %all-gather.14.cloned.1.call-start = ((), (), s32[]{:S(2)}) async-start(), calls=%async_computation.15 | async-start | bytes 4718592 | tf_op jit(solution)/shard_map/all_gather | solution.py:967
  143.2 96.9 %all-gather.12.cloned.1.call-start = ((), (), s32[]{:S(2)}) async-start(), calls=%async_computation.14 | async-start | bytes 4718592 | tf_op jit(solution)/shard_map/all_gather | solution.py:967
  185.2 117.9 %reduce-scatter.5.cloned.1.call-start = ((), (), s32[]{:S(2)}) async-start(), calls=%async_computation.16 | async-start | bytes 4718592 | tf_op jit(solution)/shard_map/reduce_scatter | solution.py:970
  286.8 41.7 %collective-permute-start.19 = (bf16[256,1024]{1,0:T(8,128)(2,1)}, bf16[256,1024]{1,0:T(8,128)(2,1)}, u32[]{:S(2)}, u32[]{:S(2)}) collective-permute-start(bf16[256,1024]{1,0:T(8,128)(2,1)} %get-tuple-element.173), channel_id=1, source_target_pairs={{0,8},{8,0},{16,24},{24,16},{1,9},{9,1},{17,25},{25,17},{2,10},{10... | collective-permute-start | bytes 1572872 | tf_op jit(solution)/shard_map/ppermute | solution.py:638
  288.2 40.2 %collective-permute-start.20 = (bf16[256,1024]{1,0:T(8,128)(2,1)}, bf16[256,1024]{1,0:T(8,128)(2,1)}, u32[]{:S(2)}, u32[]{:S(2)}) collective-permute-start(bf16[256,1024]{1,0:T(8,128)(2,1)} %get-tuple-element.174), channel_id=1, source_target_pairs={{0,16},{8,24},{16,0},{24,8},{1,17},{9,25},{17,1},{25,9},{2,18},{10... | collective-permute-start | bytes 1572872 | tf_op jit(solution)/shard_map/ppermute | solution.py:638
  288.8 39.7 %collective-permute-start.21 = (bf16[256,1024]{1,0:T(8,128)(2,1)}, bf16[256,1024]{1,0:T(8,128)(2,1)}, u32[]{:S(2)}, u32[]{:S(2)}) collective-permute-start(bf16[256,1024]{1,0:T(8,128)(2,1)} %get-tuple-element.175), channel_id=1, source_target_pairs={{0,24},{8,16},{16,8},{24,0},{1,25},{9,17},{17,9},{25,1},{2,26},{10... | collective-permute-start | bytes 1572872 | tf_op jit(solution)/shard_map/ppermute | solution.py:638
  301.6 95.7 %reduce-scatter.9.cloned.1.call-start = ((), (), s32[]{:S(2)}) async-start(), calls=%async_computation.18 | async-start | bytes 2359296 | tf_op jit(solution)/shard_map/reduce_scatter | solution.py:970
  328.5 193.4 %reduce-scatter.7.cloned.1.call-start = ((), (), s32[]{:S(2)}) async-start(), calls=%async_computation.17 | async-start | bytes 4718592 | tf_op jit(solution)/shard_map/reduce_scatter | solution.py:970
  345.9 51.3 %collective-permute-start.25 = (bf16[3,4,4,32,1024]{4,3,2,1,0:T(8,128)(2,1)}, bf16[3,4,4,32,1024]{4,3,2,1,0:T(8,128)(2,1)}, u32[]{:S(2)}, u32[]{:S(2)}) collective-permute-start(bf16[3,4,4,32,1024]{4,3,2,1,0:T(8,128)(2,1)} %get-tuple-element.194), channel_id=1, source_target_pairs={{0,1},{1,0},{2,3},{3,2},{4,5},{5,4},{6,7},{7,6},{8,9},{9,8},{10,11... | collective-permute-start | bytes 9437192 | tf_op jit(solution)/shard_map/ppermute | solution.py:712
  345.9 48.1 %collective-permute-start.22 = (bf16[512,1024]{1,0:T(8,128)(2,1)S(1)}, bf16[512,1024]{1,0:T(8,128)(2,1)S(1)}, u32[]{:S(2)}, u32[]{:S(2)}) collective-permute-start(bf16[512,1024]{1,0:T(8,128)(2,1)S(1)} %pad_maximum_fusion.refs_0_), channel_id=1, source_target_pairs={{0,8},{8,0},{16,24},{24,16},{1,9},{9,1},{17,25},{25,17},{2,10},{10... | collective-permute-start | bytes 3145736 | tf_op jit(solution)/shard_map/ppermute | solution.py:638
  347.6 47.7 %collective-permute-start.23 = (bf16[512,1024]{1,0:T(8,128)(2,1)S(1)}, bf16[512,1024]{1,0:T(8,128)(2,1)S(1)}, u32[]{:S(2)}, u32[]{:S(2)}) collective-permute-start(bf16[512,1024]{1,0:T(8,128)(2,1)S(1)} %pad_maximum_fusion.refs_0_), channel_id=1, source_target_pairs={{0,16},{8,24},{16,0},{24,8},{1,17},{9,25},{17,1},{25,9},{2,18},{10... | collective-permute-start | bytes 3145736 | tf_op jit(solution)/shard_map/ppermute | solution.py:638
  348.0 47.2 %collective-permute-start.24 = (bf16[512,1024]{1,0:T(8,128)(2,1)S(1)}, bf16[512,1024]{1,0:T(8,128)(2,1)S(1)}, u32[]{:S(2)}, u32[]{:S(2)}) collective-permute-start(bf16[512,1024]{1,0:T(8,128)(2,1)S(1)} %pad_maximum_fusion.refs_0_), channel_id=1, source_target_pairs={{0,24},{8,16},{16,8},{24,0},{1,25},{9,17},{17,9},{25,1},{2,26},{10... | collective-permute-start | bytes 3145736 | tf_op jit(solution)/shard_map/ppermute | solution.py:638
  408.0 116.1 %reduce-scatter.11.cloned.1.call-start = ((), (), s32[]{:S(2)}) async-start(), calls=%async_computation.19 | async-start | bytes 4718592 | tf_op jit(solution)/shard_map/reduce_scatter | solution.py:970
  425.0 32.5 %collective-permute-start.33 = (bf16[3,4,32,1024]{3,2,1,0:T(8,128)(2,1)}, bf16[3,4,32,1024]{3,2,1,0:T(8,128)(2,1)}, u32[]{:S(2)}, u32[]{:S(2)}) collective-permute-start(bf16[3,4,32,1024]{3,2,1,0:T(8,128)(2,1)} %get-tuple-element.216), channel_id=1, source_target_pairs={{0,8},{8,0},{16,24},{24,16},{1,9},{9,1},{17,25},{25,17},{2,10},{10... | collective-permute-start | bytes 2359304 | tf_op jit(solution)/shard_map/ppermute | solution.py:638
  425.9 35.9 %collective-permute-start.34 = (bf16[3,4,32,1024]{3,2,1,0:T(8,128)(2,1)}, bf16[3,4,32,1024]{3,2,1,0:T(8,128)(2,1)}, u32[]{:S(2)}, u32[]{:S(2)}) collective-permute-start(bf16[3,4,32,1024]{3,2,1,0:T(8,128)(2,1)} %get-tuple-element.217), channel_id=1, source_target_pairs={{0,16},{8,24},{16,0},{24,8},{1,17},{9,25},{17,1},{25,9},{2,18},{10... | collective-permute-start | bytes 2359304 | tf_op jit(solution)/shard_map/ppermute | solution.py:638
  427.8 34.5 %collective-permute-start.35 = (bf16[3,4,32,1024]{3,2,1,0:T(8,128)(2,1)}, bf16[3,4,32,1024]{3,2,1,0:T(8,128)(2,1)}, u32[]{:S(2)}, u32[]{:S(2)}) collective-permute-start(bf16[3,4,32,1024]{3,2,1,0:T(8,128)(2,1)} %get-tuple-element.218), channel_id=1, source_target_pairs={{0,24},{8,16},{16,8},{24,0},{1,25},{9,17},{17,9},{25,1},{2,26},{10... | collective-permute-start | bytes 2359304 | tf_op jit(solution)/shard_map/ppermute | solution.py:638
  465.9 40.3 %collective-permute-start.30 = (bf16[261,640]{1,0:T(8,128)(2,1)S(1)}, bf16[261,640]{1,0:T(8,128)(2,1)S(1)}, u32[]{:S(2)}, u32[]{:S(2)}) collective-permute-start(bf16[261,640]{1,0:T(8,128)(2,1)S(1)} %pad_maximum_fusion.3.refs_0_), channel_id=1, source_target_pairs={{0,8},{8,0},{16,24},{24,16},{1,9},{9,1},{17,25},{25,17},{2,10},{10... | collective-permute-start | bytes 1002248 | tf_op jit(solution)/shard_map/ppermute | solution.py:638
  466.5 41.0 %collective-permute-start.31 = (bf16[261,640]{1,0:T(8,128)(2,1)S(1)}, bf16[261,640]{1,0:T(8,128)(2,1)S(1)}, u32[]{:S(2)}, u32[]{:S(2)}) collective-permute-start(bf16[261,640]{1,0:T(8,128)(2,1)S(1)} %pad_maximum_fusion.3.refs_0_), channel_id=1, source_target_pairs={{0,16},{8,24},{16,0},{24,8},{1,17},{9,25},{17,1},{25,9},{2,18},{10... | collective-permute-start | bytes 1002248 | tf_op jit(solution)/shard_map/ppermute | solution.py:638
  474.4 33.1 %collective-permute-start.32 = (bf16[261,640]{1,0:T(8,128)(2,1)S(1)}, bf16[261,640]{1,0:T(8,128)(2,1)S(1)}, u32[]{:S(2)}, u32[]{:S(2)}) collective-permute-start(bf16[261,640]{1,0:T(8,128)(2,1)S(1)} %pad_maximum_fusion.3.refs_0_), channel_id=1, source_target_pairs={{0,24},{8,16},{16,8},{24,0},{1,25},{9,17},{17,9},{25,1},{2,26},{10... | collective-permute-start | bytes 1002248 | tf_op jit(solution)/shard_map/ppermute | solution.py:638
  (86 other events, 1113.8 us)
Sparse Core Ops, SparseCore 0:
  9.7 32.2 all-gather.5
  53.5 45.4 all-gather.7
  101.1 37.2 all-gather.9
  139.9 49.7 all-gather.13
  191.7 48.2 all-gather.11
  256.2 46.9 reduce-scatter.4
  328.6 39.2 reduce-scatter.8
  370.3 50.1 reduce-scatter.6
  422.9 84.8 reduce-scatter.10

commit v6 on v5

--- a/solution.py
+++ b/solution.py
@@ -274,7 +274,7 @@
         grid_spec=grid_spec,
         out_shape=jax.ShapeDtypeStruct((count, 3 * PAIR), jnp.bfloat16),
         compiler_params=pltpu.CompilerParams(vmem_limit_bytes=58 * 2**20),
-        cost_estimate=LITTLE,
+        cost_estimate=pl.CostEstimate(flops=16 * 10**9, bytes_accessed=4 * 2**20, transcendentals=0),
     )(block_ends(segments, rows), qkv, qkv, qkv, grad_att, lse, attended, col, row)
 
 
@@ -735,6 +735,33 @@
     line = add_up(both)
     parts = [lax.dynamic_index_in_dim(line, (chip + step) % chips, 0, keepdims=False) for step in range(chips)]
     return [parts[0]] + [line_send(parts[step], step, group) for step in range(1, chips)]
+
+
+def kinds_kernel(place, *refs):
+    outs = refs[-3:]
+    rows = outs[0].shape[1]
+    for step, part in enumerate(refs[:-3]):
+        for kind, out in enumerate(outs):
+            out[pl.ds(place[0] ^ step, 1)] = part[kind * rows : (kind + 1) * rows, :].astype(out.dtype)[None]
+
+
+def spread_kinds(parts, rows):
+    size = len(parts)
+    if rows % 16:
+        return [rep_place([part[k * rows : (k + 1) * rows] for part in parts], 0).astype(jnp.float32) for k in range(3)]
+    whole = lambda i, e: (0, 0)
+    grid_spec = pltpu.PrefetchScalarGridSpec(
+        num_scalar_prefetch=1,
+        grid=(1,),
+        in_specs=[pl.BlockSpec(parts[0].shape, whole)] * size,
+        out_specs=[pl.BlockSpec((size, rows, D), lambda i, e: (0, 0, 0))] * 3,
+    )
+    return pl.pallas_call(
+        kinds_kernel,
+        grid_spec=grid_spec,
+        out_shape=(jax.ShapeDtypeStruct((size, rows, D), jnp.float32),) * 3,
+        cost_estimate=LITTLE,
+    )(lax.axis_index("rep")[None], *parts)
 
 
 def columns_kernel(place, *refs):
@@ -1089,10 +1116,9 @@
 
     feed_gather = rep_start(own_feed)
     grad_qkv = self_backward(qkv, grad_att_heads, lse, att_full, seq_segments)
-    grad_qkv, feed_gather, plain_theirs = lax.optimization_barrier((grad_qkv, feed_gather, plain_theirs))
     heads_parts = heads_grads(input_one_all, grad_qkv, enc_all, mem_grads, count, part_rows)
     heads_swapped = rep_swap(heads_parts)
-    grad_in_one_low, one_sums, qkv_sums = back(after(grad_qkv, heads_parts), qkv_weight, input_one_all)
+    grad_in_one_low, one_sums, qkv_sums = back(after(grad_qkv, heads_parts, feed_gather), qkv_weight, input_one_all)
     plain_rep = send_parts(core_sum_split(*after((plain_own, plain_theirs), heads_parts)))
     grad_in_one_low, heads_swapped, plain_rep[0] = lax.optimization_barrier(
         (grad_in_one_low, heads_swapped, plain_rep[0])
@@ -1149,11 +1175,6 @@
 
     total_shrink = spread(feed_gather, 0, part_hidden, jnp.float32)
     total_expand = spread_columns(feed_gather, part_hidden, count, part_rows)
-    total_plain = [
-        spread(plain_gather, kind * part_rows, (kind + 1) * part_rows, jnp.float32).reshape(weight_rows, D)
-        for kind in range(3)
-    ]
-    total_proj, total_query, total_cross = total_plain
     total_small = sum(part[span * part_rows :].astype(jnp.float32) for part in heads_gather)
     total_small = total_small.reshape(-1)[:small_size]
     total_hidden_bias = total_small[small_count * shard_width :]
@@ -1161,6 +1182,8 @@
     total_qkv, total_memory = spread_heads(heads_gather, span, part_rows, width)
 
     grad_tokens = last(tokens, grad_in_one, grad_one, gain_rows[0])
+    plain_gather = after(plain_gather, grad_tokens, result)
+    total_proj, total_query, total_cross = [part.reshape(weight_rows, D) for part in spread_kinds(plain_gather, part_rows)]
 
     return (
         low(result),

time: 543 us -> 538 us (level)
  blocking collectives: 21.9 us -> 0 us
  waiting for transfers between devices: 157 us -> 178 us
    all_to_all x1 -> x0, blocking collectives: 21.9 us -> none  [shards(): lax.all_to_all(grad_attn, 'shard', 1, 0, tiled=True, axis_index_groups=gr...]
    ppermute x27, waiting for transfers between devices: 55.4 us -> 64.6 us  [rep_send(): return lax.ppermute(value, 'rep', [(i, i ^ step) for i in range(size)])]
    all_to_all x0 -> x1, waiting for transfers between devices: none -> 8.88 us  [shards(): lax.all_to_all(grad_attn, 'shard', 1, 0, tiled=True, axis_index_groups=gr...]
    all_to_all x0 -> x1, starting transfers between devices: none -> 7.38 us  [shards(): lax.all_to_all(grad_attn, 'shard', 1, 0, tiled=True, axis_index_groups=gr...]
    unnamed x127 -> x119, local copies, waits for them, and re-layouts: 15.1 us -> 11.5 us
    convert_element_type x8 -> x7, other arithmetic: 11.6 us -> 9.39 us  [low(): return values.astype(jnp.bfloat16)]
  transfers between devices with their start and end apart: 57 -> 58, of which waited for: 28 -> 27; matrix products, arithmetic and copies ran while one was open for 13% -> 13% of each run, Pallas kernels for 28% -> 28%
where the time goes in v6:
time: 538 us; the launch traced here: 529 us
  waiting for transfers between devices  178 us (33%)
  Pallas kernels  164 us (30%)
  starting transfers between devices  93.7 us (17%)
  local copies, waits for them, and re-layouts  28.6 us (5%)
  other arithmetic  26.5 us (5%)
  matrix products  22.5 us (4%)
  between operations  15.9 us (3%)
    ppermute x9, waiting for transfers between devices, line_send(): return lax.ppermute(value, 'shard', route)  66.1 us
    ppermute x27, waiting for transfers between devices, rep_send(): return lax.ppermute(value, 'rep', [(i, i ^ step) for i in range(size)])  64.6 us
    ppermute x27, starting transfers between devices, rep_send(): return lax.ppermute(value, 'rep', [(i, i ^ step) for i in range(size)])  30.1 us
    all_to_all x4, starting transfers between devices, swap(): return lax.all_to_all(value, 'shard', 0, 0, tiled=True)  22.1 us
    all_gather x5, waiting for transfers between devices, gather(): lax.all_gather(value, 'shard', axis=0, tiled=True, axis_index_groups=groups)  21.5 us
    pallas_call x1, Pallas kernels, self_backward(): pl.pallas_call(self_backward_kernel, grid_spec=grid_spec, out_shape=jax.S...  21.5 us
    pallas_call x1, Pallas kernels, feed(): pl.pallas_call(feed_kernel, grid=(count // tile,), in_specs=[pl.BlockSpec...  16 us
    pallas_call x1, Pallas kernels, self_forward(): pl.pallas_call(self_forward_kernel, grid_spec=grid_spec, out_shape=(jax.S...  15.7 us
  transfers between devices with their start and end apart: 58, of which 27 were waited for; matrix products, arithmetic and copies ran while one was open for 13% of the time, Pallas kernels for 28%

profile of v6, /device:TPU:12, one launch (start us, length us, event | category | flops | bytes accessed | tf_op | source)
XLA Modules:
  0.0 529.0 jit_solution(5202709455379819319)
XLA Ops:
  22.8 24.2 %collective-permute-done = bf16[3,32,1024]{2,1,0:T(8,128)(2,1)S(1)} collective-permute-done((bf16[3,32,1024]{2,1,0:T(8,128)(2,1)S(1)}, bf16[3,32,1024]{2,1,0:T(8,128)(2,1)S(1)}, u32[]{:S(2)}, u32[]{:S(2)}) %collective-permute-start) | collective-permute-done | bytes 196640 | tf_op jit(solution)/shard_map/ppermute | solution.py:719
  57.9 6.9 %collective-permute-done.3 = bf16[8,32,640]{2,1,0:T(8,128)(2,1)S(1)} collective-permute-done((bf16[8,32,640]{2,1,0:T(8,128)(2,1)S(1)}, bf16[8,32,640]{2,1,0:T(8,128)(2,1)S(1)}, u32[]{:S(2)}, u32[]{:S(2)}) %collective-permute-start.3) | collective-permute-done | bytes 327712 | tf_op jit(solution)/shard_map/ppermute | solution.py:638
  76.7 12.4 %collective-permute-done.6.refs_1_ = bf16[3,4,32,1024]{3,2,1,0:T(8,128)(2,1)} collective-permute-done((bf16[3,4,32,1024]{3,2,1,0:T(8,128)(2,1)S(1)}, bf16[3,4,32,1024]{3,2,1,0:T(8,128)(2,1)}, u32[]{:S(2)}, u32[]{:S(2)}) %collective-permute-start.6) | collective-permute-done | bytes 786464 | tf_op jit(solution)/shard_map/ppermute | solution.py:638
  90.3 8.6 %all-gather.8.cloned.1.call-done.x_ref = bf16[2048,1024]{1,0:T(8,128)(2,1)} async-done(((bf16[256,1024]{1,0:T(8,128)(2,1)}), bf16[2048,1024]{1,0:T(8,128)(2,1)}) %all-gather.8.cloned.1.call-update) | async-done | bytes 4194320 | tf_op jit(solution)/shard_map/all_gather | solution.py:994
  110.7 9.2 %shard_map.263 = (bf16[2048,1024]{1,0:T(8,128)(2,1)}, bf16[2048,384]{1,0:T(8,128)(2,1)}) custom-call(bf16[2048,1024]{1,0:T(8,128)(2,1)} %all-gather.8.cloned.1.call-done.x_ref, f32[1,1024]{1,0:T(1,128)} %bitcast.241, f32[1,1024]{1,0:T(1,128)} %bitcast.245, bf16[1024,384]{1,0:T(8,128)(2,1)} %slice.201.qkv_w.w_ref, f32[1,384]{1,0:T(1,128)} %broadcast_in_dim.100.qkv_b), custom_call_target="tpu_custom_call" | custom-call | flops 1000 | bytes 1000 | tf_op jit(solution)/shard_map/pallas_call | solution.py:381
  119.9 15.7 %shard_map.264 = (bf16[2048,128]{1,0:T(8,128)(2,1)}, f32[2048,128]{1,0:T(8,128)}, f32[2,2048]{1,0:T(2,128)}) custom-call(s32[2,4]{1,0:T(2,128)} %pad_add_fusion.ends, bf16[2048,384]{1,0:T(8,128)(2,1)} %get-tuple-element.135.q_ref.k_ref.v_ref, bf16[2048,384]{1,0:T(8,128)(2,1)} %get-tuple-element.135.q_ref.k_ref.v_ref, ...), custom_call_target="tpu_custom_call" | custom-call | flops 1000 | bytes 1000 | tf_op jit(solution)/shard_map/pallas_call | solution.py:153
  143.2 11.0 %all-gather.12.cloned.1.call-start = ((), (), s32[]{:S(2)}) async-start(), calls=%async_computation.14 | async-start | bytes 4718592 | tf_op jit(solution)/shard_map/all_gather | solution.py:994
  172.7 8.6 %shard_map.266.c_ref = bf16[256,1024]{1,0:T(8,128)(2,1)} custom-call(s32[1]{0:T(128)S(6)} %copy.114.length, bf16[256,1024]{1,0:T(8,128)(2,1)} %fusion.2.q_ref, bf16[4096,256]{1,0:T(8,128)(2,1)} %all-gather.10.cloned.1.call-done.m_ref), custom_call_target="tpu_custom_call" | custom-call | flops 1000 | bytes 1000 | tf_op jit(solution)/shard_map/pallas_call | solution.py:307
  189.4 10.7 %collective-permute-done.13.refs_1_ = bf16[256,1024]{1,0:T(8,128)(2,1)S(1)} collective-permute-done((bf16[256,1024]{1,0:T(8,128)(2,1)S(1)}, bf16[256,1024]{1,0:T(8,128)(2,1)S(1)}, u32[]{:S(2)}, u32[]{:S(2)}) %collective-permute-start.13) | collective-permute-done | bytes 524320 | tf_op jit(solution)/shard_map/ppermute | solution.py:638
  200.1 11.6 %collective-permute-done.14.refs_2_ = bf16[256,1024]{1,0:T(8,128)(2,1)S(1)} collective-permute-done((bf16[256,1024]{1,0:T(8,128)(2,1)S(1)}, bf16[256,1024]{1,0:T(8,128)(2,1)S(1)}, u32[]{:S(2)}, u32[]{:S(2)}) %collective-permute-start.14) | collective-permute-done | bytes 524320 | tf_op jit(solution)/shard_map/ppermute | solution.py:638
  219.2 10.8 %fusion.31.ga_ref = f32[2048,1024]{1,0:T(8,128)} fusion(bf16[2048,1024]{1,0:T(8,128)(2,1)} %all-gather.14.cloned.1.call-done.g_ref, bf16[1024,1024]{1,0:T(8,128)(2,1)} %b_ref.1), kind=kOutput, calls=%fused_computation.139 | convolution fusion | flops 4294967296 | bytes 14680064 | tf_op jit(solution)/shard_map/dot_general | solution.py:48
  230.0 10.0 %all-gather.12.cloned.1.call-done.x_ref = bf16[2048,1024]{1,0:T(8,128)(2,1)} async-done(((bf16[256,1024]{1,0:T(8,128)(2,1)}), bf16[2048,1024]{1,0:T(8,128)(2,1)}) %all-gather.12.cloned.1.call-update) | async-done | bytes 4194320 | tf_op jit(solution)/shard_map/all_gather | solution.py:994
  240.0 16.0 %shard_map.268 = (bf16[2048,1024]{1,0:T(8,128)(2,1)}, bf16[2048,1024]{1,0:T(8,128)(2,1)}, bf16[2048,1024]{1,0:T(8,128)(2,1)}, f32[1,1024]{1,0:T(1,128)}) custom-call(bf16[2048,1024]{1,0:T(8,128)(2,1)} %all-gather.12.cloned.1.call-done.x_ref, bf16[1024,1024]{1,0:T(8,128)(2,1)} %bitcast.215, f32[1,1024]{1,0:T(1,128)} %bitcast.251, f32[2048,1024]{1,0:T(8,128)} %fusion.31.ga_ref), custom_call_target="tpu_custom_call" | custom-call | flops 1000 | bytes 1000 | tf_op jit(solution)/shard_map/pallas_call | solution.py:423
  256.1 9.2 %shard_map.269 = (bf16[8,32,1024]{2,1,0:T(8,128)(2,1)}, bf16[8,32,1024]{2,1,0:T(8,128)(2,1)}, bf16[8,32,1024]{2,1,0:T(8,128)(2,1)}, bf16[8,32,1024]{2,1,0:T(8,128)(2,1)}) custom-call(s32[1]{0:T(128)} %bitcast.37.place.replica, bf16[2048,1024]{1,0:T(8,128)(2,1)} %all-gather.12.cloned.1.call-done.x_ref, bf16[2048,1024]{1,0:T(8,128)(2,1)} %get-tuple-element.160.g_ref), custom_call_target="tpu_custom_call" | custom-call | flops 1000 | bytes 1000 | tf_op jit(solution)/shard_map/pallas_call | solution.py:477
  268.7 9.2 %shard_map.270 = (bf16[256,1024]{1,0:T(8,128)(2,1)}, bf16[256,1024]{1,0:T(8,128)(2,1)}, bf16[256,1024]{1,0:T(8,128)(2,1)}, bf16[256,1024]{1,0:T(8,128)(2,1)}) custom-call(s32[1]{0:T(128)} %bitcast.37.place.replica, bf16[2048,1024]{1,0:T(8,128)(2,1)} %get-tuple-element.164.a_ref, bf16[2048,1024]{1,0:T(8,128)(2,1)} %all-gather.14.cloned.1.call-done.g_ref), custom_call_target="tpu_custom_call" | custom-call | flops 1000 | bytes 1000 | tf_op jit(solution)/shard_map/pallas_call | solution.py:510
  277.9 8.8 %shard_map.271 = bf16[2048,1024]{1,0:T(8,128)(2,1)} custom-call(bf16[2048,1024]{1,0:T(8,128)(2,1)} %get-tuple-element.164.a_ref, bf16[1024,1024]{1,0:T(8,128)(2,1)} %b_ref.1), custom_call_target="tpu_custom_call" | custom-call | flops 1000 | bytes 1000 | tf_op jit(solution)/shard_map/pallas_call | solution.py:526
  313.9 14.5 %shard_map.272 = (bf16[256,1024]{1,0:T(8,128)(2,1)}, bf16[4096,256]{1,0:T(8,128)(2,1)}) custom-call(s32[1]{0:T(128)S(6)} %copy.114.length, bf16[256,1024]{1,0:T(8,128)(2,1)} %fusion.2.q_ref, bf16[4096,256]{1,0:T(8,128)(2,1)} %all-gather.10.cloned.1.call-done.m_ref, bf16[256,1024]{1,0:T(8,128)(2,1)} %convolution_convert_fusion.2.g_ref), custom_call_target="tpu_custom_call" | custom-call | flops 1000 | bytes 1000 | tf_op jit(solution)/shard_map/pallas_call | solution.py:357
  338.8 7.4 %all-to-all-start.4 = ((bf16[256,8,128]{2,0,1:T(8,128)(2,1)}), bf16[256,8,128]{2,0,1:T(8,128)(2,1)}, u32[]{:S(2)}, u32[]{:S(2)}) async-start(bf16[256,8,128]{2,0,1:T(8,128)(2,1)} %copy_bitcast_fusion.1), calls=%async_computation.6 | async-start | bytes 1048576 | tf_op jit(solution)/shard_map/all_to_all | solution.py:1110
  357.1 8.9 %all-to-all-done.4 = bf16[256,8,128]{2,0,1:T(8,128)(2,1)} async-done(((bf16[256,8,128]{2,0,1:T(8,128)(2,1)}), bf16[256,8,128]{2,0,1:T(8,128)(2,1)}, u32[]{:S(2)}, u32[]{:S(2)}) %all-to-all-start.4) | async-done | bytes 524320 | tf_op jit(solution)/shard_map/all_to_all | solution.py:1110
  366.0 21.5 %shard_map.274.g_ref = bf16[2048,384]{1,0:T(8,128)(2,1)} custom-call(s32[2,4]{1,0:T(2,128)} %pad_add_fusion.ends, bf16[2048,384]{1,0:T(8,128)(2,1)} %get-tuple-element.135.q_ref.k_ref.v_ref, bf16[2048,384]{1,0:T(8,128)(2,1)} %get-tuple-element.135.q_ref.k_ref.v_ref, bf16[2048,384]{1,0:T(8,128)(2,1)} %get-tuple-element.135.q_ref.k_ref.v_ref, ...), custom_call_target="tpu_custom_call" | custom-call | flops 16000000000 | bytes 4194304 | tf_op jit(solution)/shard_map/pallas_call | solution.py:272
  398.6 11.9 %collective-permute-done.23.refs_2_ = bf16[512,1024]{1,0:T(8,128)(2,1)} collective-permute-done((bf16[512,1024]{1,0:T(8,128)(2,1)S(1)}, bf16[512,1024]{1,0:T(8,128)(2,1)}, u32[]{:S(2)}, u32[]{:S(2)}) %collective-permute-start.23) | collective-permute-done | bytes 1048608 | tf_op jit(solution)/shard_map/ppermute | solution.py:638
  410.5 9.0 %shard_map.276 = (bf16[2048,1024]{1,0:T(8,128)(2,1)}, f32[2,1024]{1,0:T(2,128)}, f32[1,384]{1,0:T(1,128)}) custom-call(bf16[2048,384]{1,0:T(8,128)(2,1)} %shard_map.274.g_ref, bf16[1024,384]{1,0:T(8,128)(2,1)} %slice.201.qkv_w.w_ref, bf16[2048,1024]{1,0:T(8,128)(2,1)} %get-tuple-element.194.x_ref.one_ref), custom_call_target="tpu_custom_call" | custom-call | flops 1000 | bytes 1000 | tf_op jit(solution)/shard_map/pallas_call | solution.py:553
  473.3 8.1 %collective-permute-done.29 = bf16[64,1024]{1,0:T(8,128)(2,1)S(1)} collective-permute-done((bf16[64,1024]{1,0:T(8,128)(2,1)S(1)}, bf16[64,1024]{1,0:T(8,128)(2,1)S(1)}, u32[]{:S(2)}, u32[]{:S(2)}) %collective-permute-start.29) | collective-permute-done | bytes 131104 | tf_op jit(solution)/shard_map/ppermute | solution.py:719
  486.4 15.2 %collective-permute-done.37 = bf16[3,32,1024]{2,1,0:T(8,128)(2,1)S(1)} collective-permute-done((bf16[3,32,1024]{2,1,0:T(8,128)(2,1)S(1)}, bf16[3,32,1024]{2,1,0:T(8,128)(2,1)S(1)}, u32[]{:S(2)}, u32[]{:S(2)}) %collective-permute-start.37) | collective-permute-done | bytes 196640 | tf_op jit(solution)/shard_map/ppermute | solution.py:719
  (350 shorter events, 233.8 us)
Async XLA Ops:
  7.2 46.1 %all-gather.6.cloned.1.call-start = ((), (), s32[]{:S(2)}) async-start(), calls=%async_computation.11 | async-start | bytes 1179648 | tf_op jit(solution)/shard_map/all_gather | solution.py:994
  11.3 42.1 %all-to-all-start = ((bf16[8,35,640]{2,1,0:T(8,128)(2,1)}), bf16[8,35,640]{2,1,0:T(8,128)(2,1)S(1)}, u32[]{:S(2)}, u32[]{:S(2)}) async-start(bf16[8,35,640]{2,1,0:T(8,128)(2,1)} %pad_maximum_fusion.1), calls=%async_computation | async-start | bytes 819200 | tf_op jit(solution)/shard_map/all_to_all | solution.py:1000
  16.6 82.3 %all-gather.8.cloned.1.call-start = ((), (), s32[]{:S(2)}) async-start(), calls=%async_computation.12 | async-start | bytes 4718592 | tf_op jit(solution)/shard_map/all_gather | solution.py:994
  20.9 32.5 %collective-permute-start.2 = (bf16[3,32,1024]{2,1,0:T(8,128)(2,1)S(1)}, bf16[3,32,1024]{2,1,0:T(8,128)(2,1)S(1)}, u32[]{:S(2)}, u32[]{:S(2)}) collective-permute-start(bf16[3,32,1024]{2,1,0:T(8,128)(2,1)S(1)} %pad_maximum_fusion.4), channel_id=1, source_target_pairs={{0,6},{1,7},{2,0},{3,1},{4,2},{5,3},{6,4},{7,5},{8,14},{9,15},{10,... | collective-permute-start | bytes 589832 | tf_op jit(solution)/shard_map/ppermute | solution.py:719
  53.4 85.0 %all-gather.10.cloned.1.call-start = ((), (), s32[]{:S(2)}) async-start(), calls=%async_computation.13 | async-start | bytes 2359296 | tf_op jit(solution)/shard_map/all_gather | solution.py:994
  100.5 35.1 %all-to-all-start.1 = ((bf16[8,32,1024]{2,1,0:T(8,128)(2,1)}), bf16[8,32,1024]{2,1,0:T(8,128)(2,1)S(1)}, u32[]{:S(2)}, u32[]{:S(2)}) async-start(bf16[8,32,1024]{2,1,0:T(8,128)(2,1)} %copy.67), calls=%async_computation.1 | async-start | bytes 1048576 | tf_op jit(solution)/shard_map/all_to_all | solution.py:1000
  105.9 113.3 %all-gather.14.cloned.1.call-start = ((), (), s32[]{:S(2)}) async-start(), calls=%async_computation.15 | async-start | bytes 4718592 | tf_op jit(solution)/shard_map/all_gather | solution.py:994
  143.2 96.9 %all-gather.12.cloned.1.call-start = ((), (), s32[]{:S(2)}) async-start(), calls=%async_computation.14 | async-start | bytes 4718592 | tf_op jit(solution)/shard_map/all_gather | solution.py:994
  185.2 117.9 %reduce-scatter.5.cloned.1.call-start = ((), (), s32[]{:S(2)}) async-start(), calls=%async_computation.16 | async-start | bytes 4718592 | tf_op jit(solution)/shard_map/reduce_scatter | solution.py:997
  286.7 41.7 %collective-permute-start.19 = (bf16[256,1024]{1,0:T(8,128)(2,1)}, bf16[256,1024]{1,0:T(8,128)(2,1)}, u32[]{:S(2)}, u32[]{:S(2)}) collective-permute-start(bf16[256,1024]{1,0:T(8,128)(2,1)} %get-tuple-element.174), channel_id=1, source_target_pairs={{0,8},{8,0},{16,24},{24,16},{1,9},{9,1},{17,25},{25,17},{2,10},{10... | collective-permute-start | bytes 1572872 | tf_op jit(solution)/shard_map/ppermute | solution.py:638
  288.2 40.3 %collective-permute-start.20 = (bf16[256,1024]{1,0:T(8,128)(2,1)}, bf16[256,1024]{1,0:T(8,128)(2,1)}, u32[]{:S(2)}, u32[]{:S(2)}) collective-permute-start(bf16[256,1024]{1,0:T(8,128)(2,1)} %get-tuple-element.175), channel_id=1, source_target_pairs={{0,16},{8,24},{16,0},{24,8},{1,17},{9,25},{17,1},{25,9},{2,18},{10... | collective-permute-start | bytes 1572872 | tf_op jit(solution)/shard_map/ppermute | solution.py:638
  288.8 39.7 %collective-permute-start.21 = (bf16[256,1024]{1,0:T(8,128)(2,1)}, bf16[256,1024]{1,0:T(8,128)(2,1)}, u32[]{:S(2)}, u32[]{:S(2)}) collective-permute-start(bf16[256,1024]{1,0:T(8,128)(2,1)} %get-tuple-element.176), channel_id=1, source_target_pairs={{0,24},{8,16},{16,8},{24,0},{1,25},{9,17},{17,9},{25,1},{2,26},{10... | collective-permute-start | bytes 1572872 | tf_op jit(solution)/shard_map/ppermute | solution.py:638
  301.5 86.0 %reduce-scatter.9.cloned.1.call-start = ((), (), s32[]{:S(2)}) async-start(), calls=%async_computation.18 | async-start | bytes 2359296 | tf_op jit(solution)/shard_map/reduce_scatter | solution.py:997
  328.5 185.7 %reduce-scatter.7.cloned.1.call-start = ((), (), s32[]{:S(2)}) async-start(), calls=%async_computation.17 | async-start | bytes 4718592 | tf_op jit(solution)/shard_map/reduce_scatter | solution.py:997
  353.4 66.1 %collective-permute-start.25 = (bf16[3,4,4,32,1024]{4,3,2,1,0:T(8,128)(2,1)}, bf16[3,4,4,32,1024]{4,3,2,1,0:T(8,128)(2,1)}, u32[]{:S(2)}, u32[]{:S(2)}) collective-permute-start(bf16[3,4,4,32,1024]{4,3,2,1,0:T(8,128)(2,1)} %get-tuple-element.200), channel_id=1, source_target_pairs={{0,1},{1,0},{2,3},{3,2},{4,5},{5,4},{6,7},{7,6},{8,9},{9,8},{10,11... | collective-permute-start | bytes 9437192 | tf_op jit(solution)/shard_map/ppermute | solution.py:712
  353.6 45.0 %collective-permute-start.22 = (bf16[512,1024]{1,0:T(8,128)(2,1)S(1)}, bf16[512,1024]{1,0:T(8,128)(2,1)S(1)}, u32[]{:S(2)}, u32[]{:S(2)}) collective-permute-start(bf16[512,1024]{1,0:T(8,128)(2,1)S(1)} %pad_maximum_fusion.refs_0_), channel_id=1, source_target_pairs={{0,8},{8,0},{16,24},{24,16},{1,9},{9,1},{17,25},{25,17},{2,10},{10... | collective-permute-start | bytes 3145736 | tf_op jit(solution)/shard_map/ppermute | solution.py:638
  354.9 55.6 %collective-permute-start.23 = (bf16[512,1024]{1,0:T(8,128)(2,1)S(1)}, bf16[512,1024]{1,0:T(8,128)(2,1)}, u32[]{:S(2)}, u32[]{:S(2)}) collective-permute-start(bf16[512,1024]{1,0:T(8,128)(2,1)S(1)} %pad_maximum_fusion.refs_0_), channel_id=1, source_target_pairs={{0,16},{8,24},{16,0},{24,8},{1,17},{9,25},{17,1},{25,9},{2,18},{10... | collective-permute-start | bytes 3145736 | tf_op jit(solution)/shard_map/ppermute | solution.py:638
  355.5 55.0 %collective-permute-start.24 = (bf16[512,1024]{1,0:T(8,128)(2,1)S(1)}, bf16[512,1024]{1,0:T(8,128)(2,1)}, u32[]{:S(2)}, u32[]{:S(2)}) collective-permute-start(bf16[512,1024]{1,0:T(8,128)(2,1)S(1)} %pad_maximum_fusion.refs_0_), channel_id=1, source_target_pairs={{0,24},{8,16},{16,8},{24,0},{1,25},{9,17},{17,9},{25,1},{2,26},{10... | collective-permute-start | bytes 3145736 | tf_op jit(solution)/shard_map/ppermute | solution.py:638
  398.5 117.9 %reduce-scatter.11.cloned.1.call-start = ((), (), s32[]{:S(2)}) async-start(), calls=%async_computation.19 | async-start | bytes 4718592 | tf_op jit(solution)/shard_map/reduce_scatter | solution.py:997
  426.0 34.8 %collective-permute-start.34 = (bf16[3,4,32,1024]{3,2,1,0:T(8,128)(2,1)}, bf16[3,4,32,1024]{3,2,1,0:T(8,128)(2,1)}, u32[]{:S(2)}, u32[]{:S(2)}) collective-permute-start(bf16[3,4,32,1024]{3,2,1,0:T(8,128)(2,1)} %get-tuple-element.216), channel_id=1, source_target_pairs={{0,16},{8,24},{16,0},{24,8},{1,17},{9,25},{17,1},{25,9},{2,18},{10... | collective-permute-start | bytes 2359304 | tf_op jit(solution)/shard_map/ppermute | solution.py:638
  426.1 34.7 %collective-permute-start.35 = (bf16[3,4,32,1024]{3,2,1,0:T(8,128)(2,1)}, bf16[3,4,32,1024]{3,2,1,0:T(8,128)(2,1)}, u32[]{:S(2)}, u32[]{:S(2)}) collective-permute-start(bf16[3,4,32,1024]{3,2,1,0:T(8,128)(2,1)} %get-tuple-element.217), channel_id=1, source_target_pairs={{0,24},{8,16},{16,8},{24,0},{1,25},{9,17},{17,9},{25,1},{2,26},{10... | collective-permute-start | bytes 2359304 | tf_op jit(solution)/shard_map/ppermute | solution.py:638
  464.9 40.2 %collective-permute-start.30 = (bf16[261,640]{1,0:T(8,128)(2,1)S(1)}, bf16[261,640]{1,0:T(8,128)(2,1)S(1)}, u32[]{:S(2)}, u32[]{:S(2)}) collective-permute-start(bf16[261,640]{1,0:T(8,128)(2,1)S(1)} %pad_maximum_fusion.3.refs_0_), channel_id=1, source_target_pairs={{0,8},{8,0},{16,24},{24,16},{1,9},{9,1},{17,25},{25,17},{2,10},{10... | collective-permute-start | bytes 1002248 | tf_op jit(solution)/shard_map/ppermute | solution.py:638
  466.7 40.5 %collective-permute-start.31 = (bf16[261,640]{1,0:T(8,128)(2,1)S(1)}, bf16[261,640]{1,0:T(8,128)(2,1)S(1)}, u32[]{:S(2)}, u32[]{:S(2)}) collective-permute-start(bf16[261,640]{1,0:T(8,128)(2,1)S(1)} %pad_maximum_fusion.3.refs_0_), channel_id=1, source_target_pairs={{0,16},{8,24},{16,0},{24,8},{1,17},{9,25},{17,1},{25,9},{2,18},{10... | collective-permute-start | bytes 1002248 | tf_op jit(solution)/shard_map/ppermute | solution.py:638
  473.1 34.1 %collective-permute-start.32 = (bf16[261,640]{1,0:T(8,128)(2,1)S(1)}, bf16[261,640]{1,0:T(8,128)(2,1)S(1)}, u32[]{:S(2)}, u32[]{:S(2)}) collective-permute-start(bf16[261,640]{1,0:T(8,128)(2,1)S(1)} %pad_maximum_fusion.3.refs_0_), channel_id=1, source_target_pairs={{0,24},{8,16},{16,8},{24,0},{1,25},{9,17},{17,9},{25,1},{2,26},{10... | collective-permute-start | bytes 1002248 | tf_op jit(solution)/shard_map/ppermute | solution.py:638
  (83 other events, 1194.0 us)
Sparse Core Ops, SparseCore 0:
  9.7 32.2 all-gather.5
  53.5 45.4 all-gather.7
  101.1 37.2 all-gather.9
  139.9 49.7 all-gather.13
  191.7 48.2 all-gather.11
  256.2 46.9 reduce-scatter.4
  328.6 42.2 reduce-scatter.8
  373.2 47.6 reduce-scatter.6
  424.8 83.6 reduce-scatter.10

commit v7 on v6

--- a/solution.py
+++ b/solution.py
@@ -1016,8 +1016,7 @@
     swapped = swap(blocks)
     plain_parts = line_start(jnp.stack([own_part(self_out), own_part(cross_query), own_part(cross_out)]))
     enc_all = gather(enc_states, groups)
-    swapped, plain_parts, enc_all = lax.optimization_barrier((swapped, plain_parts, enc_all))
-    rows_all = gather(after(tokens, plain_parts, enc_all), groups)
+    rows_all = gather(after(tokens, swapped, enc_all, plain_parts[1], plain_parts[-1]), groups)
     small_all = swapped[:, part_rows:].reshape(count, small_rows * 5 * width)[:, : small_count * shard_width]
     small_all = small_all.reshape(count, small_count, shard_width)
     small_all = small_all.transpose(1, 0, 2).reshape(small_count, D).astype(jnp.float32)

time: 538 us -> 529 us (0.983)
  waiting for transfers between devices: 178 us -> 170 us
    ppermute x9, waiting for transfers between devices: 66.1 us -> 60 us  [line_send(): return lax.ppermute(value, 'shard', route)]
    unnamed x119 -> x115, local copies, waits for them, and re-layouts: 11.5 us -> 11.1 us
  transfers between devices with their start and end apart: 58 -> 58, of which waited for: 27 -> 26; matrix products, arithmetic and copies ran while one was open for 13% -> 13% of each run, Pallas kernels for 28% -> 28%
where the time goes in v7:
time: 529 us; the launch traced here: 521 us
  waiting for transfers between devices  170 us (32%)
  Pallas kernels  164 us (31%)
  starting transfers between devices  92.3 us (17%)
  local copies, waits for them, and re-layouts  29.1 us (6%)
  other arithmetic  26.5 us (5%)
  matrix products  22.4 us (4%)
  between operations  15.9 us (3%)
    ppermute x27, waiting for transfers between devices, rep_send(): return lax.ppermute(value, 'rep', [(i, i ^ step) for i in range(size)])  64.6 us
    ppermute x9, waiting for transfers between devices, line_send(): return lax.ppermute(value, 'shard', route)  60 us
    ppermute x27, starting transfers between devices, rep_send(): return lax.ppermute(value, 'rep', [(i, i ^ step) for i in range(size)])  30.1 us
    all_to_all x4, starting transfers between devices, swap(): return lax.all_to_all(value, 'shard', 0, 0, tiled=True)  22.8 us
    pallas_call x1, Pallas kernels, self_backward(): pl.pallas_call(self_backward_kernel, grid_spec=grid_spec, out_shape=jax.S...  21.5 us
    all_gather x5, waiting for transfers between devices, gather(): lax.all_gather(value, 'shard', axis=0, tiled=True, axis_index_groups=groups)  20.2 us
    pallas_call x1, Pallas kernels, feed(): pl.pallas_call(feed_kernel, grid=(count // tile,), in_specs=[pl.BlockSpec...  16 us
    pallas_call x1, Pallas kernels, self_forward(): pl.pallas_call(self_forward_kernel, grid_spec=grid_spec, out_shape=(jax.S...  15.7 us
  transfers between devices with their start and end apart: 58, of which 26 were waited for; matrix products, arithmetic and copies ran while one was open for 13% of the time, Pallas kernels for 28%

profile of v7, /device:TPU:12, one launch (start us, length us, event | category | flops | bytes accessed | tf_op | source)
XLA Modules:
  0.0 520.5 jit_solution(10798412937637161349)
XLA Ops:
  20.5 22.3 %collective-permute-done = bf16[3,32,1024]{2,1,0:T(8,128)(2,1)S(1)} collective-permute-done((bf16[3,32,1024]{2,1,0:T(8,128)(2,1)S(1)}, bf16[3,32,1024]{2,1,0:T(8,128)(2,1)S(1)}, u32[]{:S(2)}, u32[]{:S(2)}) %collective-permute-start) | collective-permute-done | bytes 196640 | tf_op jit(solution)/shard_map/ppermute | solution.py:719
  49.0 6.9 %collective-permute-done.2 = bf16[8,32,640]{2,1,0:T(8,128)(2,1)S(1)} collective-permute-done((bf16[8,32,640]{2,1,0:T(8,128)(2,1)S(1)}, bf16[8,32,640]{2,1,0:T(8,128)(2,1)S(1)}, u32[]{:S(2)}, u32[]{:S(2)}) %collective-permute-start.2) | collective-permute-done | bytes 327712 | tf_op jit(solution)/shard_map/ppermute | solution.py:638
  68.9 12.4 %collective-permute-done.6.refs_1_ = bf16[3,4,32,1024]{3,2,1,0:T(8,128)(2,1)} collective-permute-done((bf16[3,4,32,1024]{3,2,1,0:T(8,128)(2,1)S(1)}, bf16[3,4,32,1024]{3,2,1,0:T(8,128)(2,1)}, u32[]{:S(2)}, u32[]{:S(2)}) %collective-permute-start.6) | collective-permute-done | bytes 786464 | tf_op jit(solution)/shard_map/ppermute | solution.py:638
  82.4 7.3 %all-gather.8.cloned.1.call-done.x_ref = bf16[2048,1024]{1,0:T(8,128)(2,1)} async-done(((bf16[256,1024]{1,0:T(8,128)(2,1)}), bf16[2048,1024]{1,0:T(8,128)(2,1)}) %all-gather.8.cloned.1.call-update) | async-done | bytes 4194320 | tf_op jit(solution)/shard_map/all_gather | solution.py:994
  102.1 9.1 %shard_map.263 = (bf16[2048,1024]{1,0:T(8,128)(2,1)}, bf16[2048,384]{1,0:T(8,128)(2,1)}) custom-call(bf16[2048,1024]{1,0:T(8,128)(2,1)} %all-gather.8.cloned.1.call-done.x_ref, f32[1,1024]{1,0:T(1,128)} %bitcast.243, f32[1,1024]{1,0:T(1,128)} %bitcast.247, bf16[1024,384]{1,0:T(8,128)(2,1)} %slice.202.qkv_w.w_ref, f32[1,384]{1,0:T(1,128)} %broadcast_in_dim.100.qkv_b), custom_call_target="tpu_custom_call" | custom-call | flops 1000 | bytes 1000 | tf_op jit(solution)/shard_map/pallas_call | solution.py:381
  111.3 15.7 %shard_map.264 = (bf16[2048,128]{1,0:T(8,128)(2,1)}, f32[2048,128]{1,0:T(8,128)}, f32[2,2048]{1,0:T(2,128)}) custom-call(s32[2,4]{1,0:T(2,128)} %pad_add_fusion.ends, bf16[2048,384]{1,0:T(8,128)(2,1)} %get-tuple-element.123.q_ref.k_ref.v_ref, bf16[2048,384]{1,0:T(8,128)(2,1)} %get-tuple-element.123.q_ref.k_ref.v_ref, ...), custom_call_target="tpu_custom_call" | custom-call | flops 1000 | bytes 1000 | tf_op jit(solution)/shard_map/pallas_call | solution.py:153
  134.6 11.0 %all-gather.12.cloned.1.call-start = ((), (), s32[]{:S(2)}) async-start(), calls=%async_computation.14 | async-start | bytes 4718592 | tf_op jit(solution)/shard_map/all_gather | solution.py:994
  164.1 8.6 %shard_map.266.c_ref = bf16[256,1024]{1,0:T(8,128)(2,1)} custom-call(s32[1]{0:T(128)S(6)} %copy.118.length, bf16[256,1024]{1,0:T(8,128)(2,1)} %fusion.2.q_ref, bf16[4096,256]{1,0:T(8,128)(2,1)} %all-gather.10.cloned.1.call-done.m_ref), custom_call_target="tpu_custom_call" | custom-call | flops 1000 | bytes 1000 | tf_op jit(solution)/shard_map/pallas_call | solution.py:307
  180.9 10.7 %collective-permute-done.13.refs_1_ = bf16[256,1024]{1,0:T(8,128)(2,1)S(1)} collective-permute-done((bf16[256,1024]{1,0:T(8,128)(2,1)S(1)}, bf16[256,1024]{1,0:T(8,128)(2,1)S(1)}, u32[]{:S(2)}, u32[]{:S(2)}) %collective-permute-start.13) | collective-permute-done | bytes 524320 | tf_op jit(solution)/shard_map/ppermute | solution.py:638
  191.6 11.6 %collective-permute-done.14.refs_2_ = bf16[256,1024]{1,0:T(8,128)(2,1)S(1)} collective-permute-done((bf16[256,1024]{1,0:T(8,128)(2,1)S(1)}, bf16[256,1024]{1,0:T(8,128)(2,1)S(1)}, u32[]{:S(2)}, u32[]{:S(2)}) %collective-permute-start.14) | collective-permute-done | bytes 524320 | tf_op jit(solution)/shard_map/ppermute | solution.py:638
  210.7 10.8 %fusion.32.ga_ref = f32[2048,1024]{1,0:T(8,128)} fusion(bf16[2048,1024]{1,0:T(8,128)(2,1)} %all-gather.14.cloned.1.call-done.g_ref, bf16[1024,1024]{1,0:T(8,128)(2,1)} %b_ref.1), kind=kOutput, calls=%fused_computation.140 | convolution fusion | flops 4294967296 | bytes 14680064 | tf_op jit(solution)/shard_map/dot_general | solution.py:48
  221.4 10.0 %all-gather.12.cloned.1.call-done.x_ref = bf16[2048,1024]{1,0:T(8,128)(2,1)} async-done(((bf16[256,1024]{1,0:T(8,128)(2,1)}), bf16[2048,1024]{1,0:T(8,128)(2,1)}) %all-gather.12.cloned.1.call-update) | async-done | bytes 4194320 | tf_op jit(solution)/shard_map/all_gather | solution.py:994
  231.5 16.0 %shard_map.268 = (bf16[2048,1024]{1,0:T(8,128)(2,1)}, bf16[2048,1024]{1,0:T(8,128)(2,1)}, bf16[2048,1024]{1,0:T(8,128)(2,1)}, f32[1,1024]{1,0:T(1,128)}) custom-call(bf16[2048,1024]{1,0:T(8,128)(2,1)} %all-gather.12.cloned.1.call-done.x_ref, bf16[1024,1024]{1,0:T(8,128)(2,1)} %bitcast.217, f32[1,1024]{1,0:T(1,128)} %bitcast.253, f32[2048,1024]{1,0:T(8,128)} %fusion.32.ga_ref), custom_call_target="tpu_custom_call" | custom-call | flops 1000 | bytes 1000 | tf_op jit(solution)/shard_map/pallas_call | solution.py:423
  247.5 9.2 %shard_map.269 = (bf16[8,32,1024]{2,1,0:T(8,128)(2,1)}, bf16[8,32,1024]{2,1,0:T(8,128)(2,1)}, bf16[8,32,1024]{2,1,0:T(8,128)(2,1)}, bf16[8,32,1024]{2,1,0:T(8,128)(2,1)}) custom-call(s32[1]{0:T(128)} %bitcast.38.place.replica, bf16[2048,1024]{1,0:T(8,128)(2,1)} %all-gather.12.cloned.1.call-done.x_ref, bf16[2048,1024]{1,0:T(8,128)(2,1)} %get-tuple-element.148.g_ref), custom_call_target="tpu_custom_call" | custom-call | flops 1000 | bytes 1000 | tf_op jit(solution)/shard_map/pallas_call | solution.py:477
  260.2 9.2 %shard_map.270 = (bf16[256,1024]{1,0:T(8,128)(2,1)}, bf16[256,1024]{1,0:T(8,128)(2,1)}, bf16[256,1024]{1,0:T(8,128)(2,1)}, bf16[256,1024]{1,0:T(8,128)(2,1)}) custom-call(s32[1]{0:T(128)} %bitcast.38.place.replica, bf16[2048,1024]{1,0:T(8,128)(2,1)} %get-tuple-element.152.a_ref, bf16[2048,1024]{1,0:T(8,128)(2,1)} %all-gather.14.cloned.1.call-done.g_ref), custom_call_target="tpu_custom_call" | custom-call | flops 1000 | bytes 1000 | tf_op jit(solution)/shard_map/pallas_call | solution.py:510
  269.4 8.8 %shard_map.271 = bf16[2048,1024]{1,0:T(8,128)(2,1)} custom-call(bf16[2048,1024]{1,0:T(8,128)(2,1)} %get-tuple-element.152.a_ref, bf16[1024,1024]{1,0:T(8,128)(2,1)} %b_ref.1), custom_call_target="tpu_custom_call" | custom-call | flops 1000 | bytes 1000 | tf_op jit(solution)/shard_map/pallas_call | solution.py:526
  305.4 14.6 %shard_map.272 = (bf16[256,1024]{1,0:T(8,128)(2,1)}, bf16[4096,256]{1,0:T(8,128)(2,1)}) custom-call(s32[1]{0:T(128)S(6)} %copy.118.length, bf16[256,1024]{1,0:T(8,128)(2,1)} %fusion.2.q_ref, bf16[4096,256]{1,0:T(8,128)(2,1)} %all-gather.10.cloned.1.call-done.m_ref, bf16[256,1024]{1,0:T(8,128)(2,1)} %convolution_convert_fusion.2.g_ref), custom_call_target="tpu_custom_call" | custom-call | flops 1000 | bytes 1000 | tf_op jit(solution)/shard_map/pallas_call | solution.py:357
  330.2 7.4 %all-to-all-start.4 = ((bf16[256,8,128]{2,0,1:T(8,128)(2,1)}), bf16[256,8,128]{2,0,1:T(8,128)(2,1)}, u32[]{:S(2)}, u32[]{:S(2)}) async-start(bf16[256,8,128]{2,0,1:T(8,128)(2,1)} %copy_bitcast_fusion.1), calls=%async_computation.6 | async-start | bytes 1048576 | tf_op jit(solution)/shard_map/all_to_all | solution.py:1109
  348.6 8.9 %all-to-all-done.4 = bf16[256,8,128]{2,0,1:T(8,128)(2,1)} async-done(((bf16[256,8,128]{2,0,1:T(8,128)(2,1)}), bf16[256,8,128]{2,0,1:T(8,128)(2,1)}, u32[]{:S(2)}, u32[]{:S(2)}) %all-to-all-start.4) | async-done | bytes 524320 | tf_op jit(solution)/shard_map/all_to_all | solution.py:1109
  357.4 21.5 %shard_map.274.g_ref = bf16[2048,384]{1,0:T(8,128)(2,1)} custom-call(s32[2,4]{1,0:T(2,128)} %pad_add_fusion.ends, bf16[2048,384]{1,0:T(8,128)(2,1)} %get-tuple-element.123.q_ref.k_ref.v_ref, bf16[2048,384]{1,0:T(8,128)(2,1)} %get-tuple-element.123.q_ref.k_ref.v_ref, bf16[2048,384]{1,0:T(8,128)(2,1)} %get-tuple-element.123.q_ref.k_ref.v_ref, ...), custom_call_target="tpu_custom_call" | custom-call | flops 16000000000 | bytes 4194304 | tf_op jit(solution)/shard_map/pallas_call | solution.py:272
  390.1 11.9 %collective-permute-done.23.refs_2_ = bf16[512,1024]{1,0:T(8,128)(2,1)} collective-permute-done((bf16[512,1024]{1,0:T(8,128)(2,1)S(1)}, bf16[512,1024]{1,0:T(8,128)(2,1)}, u32[]{:S(2)}, u32[]{:S(2)}) %collective-permute-start.23) | collective-permute-done | bytes 1048608 | tf_op jit(solution)/shard_map/ppermute | solution.py:638
  402.0 8.9 %shard_map.276 = (bf16[2048,1024]{1,0:T(8,128)(2,1)}, f32[2,1024]{1,0:T(2,128)}, f32[1,384]{1,0:T(1,128)}) custom-call(bf16[2048,384]{1,0:T(8,128)(2,1)} %shard_map.274.g_ref, bf16[1024,384]{1,0:T(8,128)(2,1)} %slice.202.qkv_w.w_ref, bf16[2048,1024]{1,0:T(8,128)(2,1)} %get-tuple-element.182.x_ref.one_ref), custom_call_target="tpu_custom_call" | custom-call | flops 1000 | bytes 1000 | tf_op jit(solution)/shard_map/pallas_call | solution.py:553
  464.7 8.0 %collective-permute-done.29 = bf16[64,1024]{1,0:T(8,128)(2,1)S(1)} collective-permute-done((bf16[64,1024]{1,0:T(8,128)(2,1)S(1)}, bf16[64,1024]{1,0:T(8,128)(2,1)S(1)}, u32[]{:S(2)}, u32[]{:S(2)}) %collective-permute-start.29) | collective-permute-done | bytes 131104 | tf_op jit(solution)/shard_map/ppermute | solution.py:719
  477.9 15.1 %collective-permute-done.37 = bf16[3,32,1024]{2,1,0:T(8,128)(2,1)S(1)} collective-permute-done((bf16[3,32,1024]{2,1,0:T(8,128)(2,1)S(1)}, bf16[3,32,1024]{2,1,0:T(8,128)(2,1)S(1)}, u32[]{:S(2)}, u32[]{:S(2)}) %collective-permute-start.37) | collective-permute-done | bytes 196640 | tf_op jit(solution)/shard_map/ppermute | solution.py:719
  (346 shorter events, 228.6 us)
Async XLA Ops:
  7.2 37.7 %all-gather.6.cloned.1.call-start = ((), (), s32[]{:S(2)}) async-start(), calls=%async_computation.11 | async-start | bytes 1179648 | tf_op jit(solution)/shard_map/all_gather | solution.py:994
  11.3 33.6 %all-to-all-start = ((bf16[8,35,640]{2,1,0:T(8,128)(2,1)}), bf16[8,35,640]{2,1,0:T(8,128)(2,1)S(1)}, u32[]{:S(2)}, u32[]{:S(2)}) async-start(bf16[8,35,640]{2,1,0:T(8,128)(2,1)} %pad_maximum_fusion.1), calls=%async_computation | async-start | bytes 819200 | tf_op jit(solution)/shard_map/all_to_all | solution.py:1000
  16.6 73.1 %all-gather.8.cloned.1.call-start = ((), (), s32[]{:S(2)}) async-start(), calls=%async_computation.12 | async-start | bytes 4718592 | tf_op jit(solution)/shard_map/all_gather | solution.py:994
  45.0 84.8 %all-gather.10.cloned.1.call-start = ((), (), s32[]{:S(2)}) async-start(), calls=%async_computation.13 | async-start | bytes 2359296 | tf_op jit(solution)/shard_map/all_gather | solution.py:994
  91.3 35.7 %all-to-all-start.1 = ((bf16[8,32,1024]{2,1,0:T(8,128)(2,1)}), bf16[8,32,1024]{2,1,0:T(8,128)(2,1)S(1)}, u32[]{:S(2)}, u32[]{:S(2)}) async-start(bf16[8,32,1024]{2,1,0:T(8,128)(2,1)} %copy.70), calls=%async_computation.1 | async-start | bytes 1048576 | tf_op jit(solution)/shard_map/all_to_all | solution.py:1000
  97.4 113.3 %all-gather.14.cloned.1.call-start = ((), (), s32[]{:S(2)}) async-start(), calls=%async_computation.15 | async-start | bytes 4718592 | tf_op jit(solution)/shard_map/all_gather | solution.py:994
  134.6 96.9 %all-gather.12.cloned.1.call-start = ((), (), s32[]{:S(2)}) async-start(), calls=%async_computation.14 | async-start | bytes 4718592 | tf_op jit(solution)/shard_map/all_gather | solution.py:994
  176.7 117.9 %reduce-scatter.5.cloned.1.call-start = ((), (), s32[]{:S(2)}) async-start(), calls=%async_computation.16 | async-start | bytes 4718592 | tf_op jit(solution)/shard_map/reduce_scatter | solution.py:997
  278.2 41.7 %collective-permute-start.19 = (bf16[256,1024]{1,0:T(8,128)(2,1)}, bf16[256,1024]{1,0:T(8,128)(2,1)}, u32[]{:S(2)}, u32[]{:S(2)}) collective-permute-start(bf16[256,1024]{1,0:T(8,128)(2,1)} %get-tuple-element.162), channel_id=1, source_target_pairs={{0,8},{8,0},{16,24},{24,16},{1,9},{9,1},{17,25},{25,17},{2,10},{10... | collective-permute-start | bytes 1572872 | tf_op jit(solution)/shard_map/ppermute | solution.py:638
  279.7 40.3 %collective-permute-start.20 = (bf16[256,1024]{1,0:T(8,128)(2,1)}, bf16[256,1024]{1,0:T(8,128)(2,1)}, u32[]{:S(2)}, u32[]{:S(2)}) collective-permute-start(bf16[256,1024]{1,0:T(8,128)(2,1)} %get-tuple-element.163), channel_id=1, source_target_pairs={{0,16},{8,24},{16,0},{24,8},{1,17},{9,25},{17,1},{25,9},{2,18},{10... | collective-permute-start | bytes 1572872 | tf_op jit(solution)/shard_map/ppermute | solution.py:638
  280.2 39.7 %collective-permute-start.21 = (bf16[256,1024]{1,0:T(8,128)(2,1)}, bf16[256,1024]{1,0:T(8,128)(2,1)}, u32[]{:S(2)}, u32[]{:S(2)}) collective-permute-start(bf16[256,1024]{1,0:T(8,128)(2,1)} %get-tuple-element.164), channel_id=1, source_target_pairs={{0,24},{8,16},{16,8},{24,0},{1,25},{9,17},{17,9},{25,1},{2,26},{10... | collective-permute-start | bytes 1572872 | tf_op jit(solution)/shard_map/ppermute | solution.py:638
  293.0 85.9 %reduce-scatter.9.cloned.1.call-start = ((), (), s32[]{:S(2)}) async-start(), calls=%async_computation.18 | async-start | bytes 2359296 | tf_op jit(solution)/shard_map/reduce_scatter | solution.py:997
  320.0 185.7 %reduce-scatter.7.cloned.1.call-start = ((), (), s32[]{:S(2)}) async-start(), calls=%async_computation.17 | async-start | bytes 4718592 | tf_op jit(solution)/shard_map/reduce_scatter | solution.py:997
  344.9 66.0 %collective-permute-start.25 = (bf16[3,4,4,32,1024]{4,3,2,1,0:T(8,128)(2,1)}, bf16[3,4,4,32,1024]{4,3,2,1,0:T(8,128)(2,1)}, u32[]{:S(2)}, u32[]{:S(2)}) collective-permute-start(bf16[3,4,4,32,1024]{4,3,2,1,0:T(8,128)(2,1)} %get-tuple-element.188), channel_id=1, source_target_pairs={{0,1},{1,0},{2,3},{3,2},{4,5},{5,4},{6,7},{7,6},{8,9},{9,8},{10,11... | collective-permute-start | bytes 9437192 | tf_op jit(solution)/shard_map/ppermute | solution.py:712
  345.1 45.0 %collective-permute-start.22 = (bf16[512,1024]{1,0:T(8,128)(2,1)S(1)}, bf16[512,1024]{1,0:T(8,128)(2,1)S(1)}, u32[]{:S(2)}, u32[]{:S(2)}) collective-permute-start(bf16[512,1024]{1,0:T(8,128)(2,1)S(1)} %pad_maximum_fusion.refs_0_), channel_id=1, source_target_pairs={{0,8},{8,0},{16,24},{24,16},{1,9},{9,1},{17,25},{25,17},{2,10},{10... | collective-permute-start | bytes 3145736 | tf_op jit(solution)/shard_map/ppermute | solution.py:638
  346.4 55.6 %collective-permute-start.23 = (bf16[512,1024]{1,0:T(8,128)(2,1)S(1)}, bf16[512,1024]{1,0:T(8,128)(2,1)}, u32[]{:S(2)}, u32[]{:S(2)}) collective-permute-start(bf16[512,1024]{1,0:T(8,128)(2,1)S(1)} %pad_maximum_fusion.refs_0_), channel_id=1, source_target_pairs={{0,16},{8,24},{16,0},{24,8},{1,17},{9,25},{17,1},{25,9},{2,18},{10... | collective-permute-start | bytes 3145736 | tf_op jit(solution)/shard_map/ppermute | solution.py:638
  346.9 55.0 %collective-permute-start.24 = (bf16[512,1024]{1,0:T(8,128)(2,1)S(1)}, bf16[512,1024]{1,0:T(8,128)(2,1)}, u32[]{:S(2)}, u32[]{:S(2)}) collective-permute-start(bf16[512,1024]{1,0:T(8,128)(2,1)S(1)} %pad_maximum_fusion.refs_0_), channel_id=1, source_target_pairs={{0,24},{8,16},{16,8},{24,0},{1,25},{9,17},{17,9},{25,1},{2,26},{10... | collective-permute-start | bytes 3145736 | tf_op jit(solution)/shard_map/ppermute | solution.py:638
  385.7 30.4 %all-to-all-start.5 = ((bf16[4,8,32,640]{3,2,1,0:T(8,128)(2,1)}), bf16[4,8,32,640]{3,2,1,0:T(8,128)(2,1)}, u32[]{:S(2)}, u32[]{:S(2)}) async-start(bf16[4,8,32,640]{3,2,1,0:T(8,128)(2,1)} %shard_map.275), calls=%async_computation.8 | async-start | bytes 2621440 | tf_op jit(solution)/shard_map/all_to_all | solution.py:686
  390.0 117.8 %reduce-scatter.11.cloned.1.call-start = ((), (), s32[]{:S(2)}) async-start(), calls=%async_computation.19 | async-start | bytes 4718592 | tf_op jit(solution)/shard_map/reduce_scatter | solution.py:997
  417.5 34.8 %collective-permute-start.34 = (bf16[3,4,32,1024]{3,2,1,0:T(8,128)(2,1)}, bf16[3,4,32,1024]{3,2,1,0:T(8,128)(2,1)}, u32[]{:S(2)}, u32[]{:S(2)}) collective-permute-start(bf16[3,4,32,1024]{3,2,1,0:T(8,128)(2,1)} %get-tuple-element.204), channel_id=1, source_target_pairs={{0,16},{8,24},{16,0},{24,8},{1,17},{9,25},{17,1},{25,9},{2,18},{10... | collective-permute-start | bytes 2359304 | tf_op jit(solution)/shard_map/ppermute | solution.py:638
  417.5 34.7 %collective-permute-start.35 = (bf16[3,4,32,1024]{3,2,1,0:T(8,128)(2,1)}, bf16[3,4,32,1024]{3,2,1,0:T(8,128)(2,1)}, u32[]{:S(2)}, u32[]{:S(2)}) collective-permute-start(bf16[3,4,32,1024]{3,2,1,0:T(8,128)(2,1)} %get-tuple-element.205), channel_id=1, source_target_pairs={{0,24},{8,16},{16,8},{24,0},{1,25},{9,17},{17,9},{25,1},{2,26},{10... | collective-permute-start | bytes 2359304 | tf_op jit(solution)/shard_map/ppermute | solution.py:638
  456.4 40.2 %collective-permute-start.30 = (bf16[261,640]{1,0:T(8,128)(2,1)S(1)}, bf16[261,640]{1,0:T(8,128)(2,1)S(1)}, u32[]{:S(2)}, u32[]{:S(2)}) collective-permute-start(bf16[261,640]{1,0:T(8,128)(2,1)S(1)} %pad_maximum_fusion.3.refs_0_), channel_id=1, source_target_pairs={{0,8},{8,0},{16,24},{24,16},{1,9},{9,1},{17,25},{25,17},{2,10},{10... | collective-permute-start | bytes 1002248 | tf_op jit(solution)/shard_map/ppermute | solution.py:638
  458.1 40.5 %collective-permute-start.31 = (bf16[261,640]{1,0:T(8,128)(2,1)S(1)}, bf16[261,640]{1,0:T(8,128)(2,1)S(1)}, u32[]{:S(2)}, u32[]{:S(2)}) collective-permute-start(bf16[261,640]{1,0:T(8,128)(2,1)S(1)} %pad_maximum_fusion.3.refs_0_), channel_id=1, source_target_pairs={{0,16},{8,24},{16,0},{24,8},{1,17},{9,25},{17,1},{25,9},{2,18},{10... | collective-permute-start | bytes 1002248 | tf_op jit(solution)/shard_map/ppermute | solution.py:638
  464.5 34.1 %collective-permute-start.32 = (bf16[261,640]{1,0:T(8,128)(2,1)S(1)}, bf16[261,640]{1,0:T(8,128)(2,1)S(1)}, u32[]{:S(2)}, u32[]{:S(2)}) collective-permute-start(bf16[261,640]{1,0:T(8,128)(2,1)S(1)} %pad_maximum_fusion.3.refs_0_), channel_id=1, source_target_pairs={{0,24},{8,16},{16,8},{24,0},{1,25},{9,17},{17,9},{25,1},{2,26},{10... | collective-permute-start | bytes 1002248 | tf_op jit(solution)/shard_map/ppermute | solution.py:638
  (81 other events, 1148.2 us)
Sparse Core Ops, SparseCore 0:
  9.7 32.2 all-gather.5
  45.1 44.6 all-gather.7
  91.9 37.8 all-gather.9
  131.3 49.8 all-gather.13
  183.1 48.2 all-gather.11
  247.6 46.9 reduce-scatter.4
  320.1 42.2 reduce-scatter.8
  364.7 47.7 reduce-scatter.6
  416.3 83.6 reduce-scatter.10

commit v8 on v7

--- a/solution.py
+++ b/solution.py
@@ -1102,10 +1102,9 @@
     grad_one = grad_two + norm_two[0]
     grad_one_low = low(grad_one)
     grad_attn = low(dot_nt(grad_one_low, attn_proj))
-    shrink_sum = add_up(shrink_parts)
+    shrink_sum = add_up(after(shrink_parts, grad_attn))
     own_expand = own_expand.reshape(part_hidden, D)
     own_feed = jnp.concatenate([shrink_sum, own_expand], axis=0)
-    grad_attn, own_feed = lax.optimization_barrier((grad_attn, own_feed))
     grad_att_heads = lax.all_to_all(grad_attn, "shard", 1, 0, tiled=True, axis_index_groups=groups)
 
     lefts, rights = after(((attended, input_two, context), (grad_one_low, grad_cross_q, grad_two_low)), grad_attn)
@@ -1117,10 +1116,10 @@
     grad_qkv = self_backward(qkv, grad_att_heads, lse, att_full, seq_segments)
     heads_parts = heads_grads(input_one_all, grad_qkv, enc_all, mem_grads, count, part_rows)
     heads_swapped = rep_swap(heads_parts)
-    grad_in_one_low, one_sums, qkv_sums = back(after(grad_qkv, heads_parts, feed_gather), qkv_weight, input_one_all)
+    grad_in_one_low, one_sums, qkv_sums = back(after(grad_qkv, heads_parts), qkv_weight, input_one_all)
     plain_rep = send_parts(core_sum_split(*after((plain_own, plain_theirs), heads_parts)))
-    grad_in_one_low, heads_swapped, plain_rep[0] = lax.optimization_barrier(
-        (grad_in_one_low, heads_swapped, plain_rep[0])
+    grad_in_one_low, heads_swapped, plain_rep[0], feed_gather = lax.optimization_barrier(
+        (grad_in_one_low, heads_swapped, plain_rep[0], feed_gather)
     )
     grad_in_one = scatter(grad_in_one_low, groups)
 

time: 529 us -> 526 us (level)
  starting transfers between devices: 92.3 us -> 83.3 us
    ppermute x27, waiting for transfers between devices: 64.6 us -> 53.1 us  [rep_send(): return lax.ppermute(value, 'rep', [(i, i ^ step) for i in range(size)])]
    all_gather x5, starting transfers between devices: 11.1 us -> 0.37 us  [gather(): lax.all_gather(value, 'shard', axis=0, tiled=True, axis_index_groups=groups)]
    all_to_all x1, waiting for transfers between devices: 0.01 us -> 10.2 us  [shards(): lax.all_to_all(att_low, 'shard', 0, 1, tiled=True, axis_index_groups=groups)]
    all_to_all x1, waiting for transfers between devices: 0.01 us -> 6.14 us  [rep_swap(): return lax.all_to_all(parts, 'rep', 0, 0, tiled=True)]
    unnamed x115 -> x103, local copies, waits for them, and re-layouts: 11.1 us -> 10.4 us
  transfers between devices with their start and end apart: 58 -> 58, of which waited for: 26 -> 28; matrix products, arithmetic and copies ran while one was open for 13% -> 14% of each run, Pallas kernels for 28% -> 28%
where the time goes in v8:
time: 526 us; the launch traced here: 517 us
  waiting for transfers between devices  173 us (33%)
  Pallas kernels  164 us (31%)
  starting transfers between devices  83.3 us (16%)
  local copies, waits for them, and re-layouts  28.4 us (5%)
  other arithmetic  27 us (5%)
  matrix products  25.3 us (5%)
  between operations  15.8 us (3%)
    ppermute x9, waiting for transfers between devices, line_send(): return lax.ppermute(value, 'shard', route)  59.4 us
    ppermute x27, waiting for transfers between devices, rep_send(): return lax.ppermute(value, 'rep', [(i, i ^ step) for i in range(size)])  53.1 us
    ppermute x27, starting transfers between devices, rep_send(): return lax.ppermute(value, 'rep', [(i, i ^ step) for i in range(size)])  31.3 us
    all_to_all x4, starting transfers between devices, swap(): return lax.all_to_all(value, 'shard', 0, 0, tiled=True)  22.7 us
    pallas_call x1, Pallas kernels, self_backward(): pl.pallas_call(self_backward_kernel, grid_spec=grid_spec, out_shape=jax.S...  21.4 us
    all_gather x5, waiting for transfers between devices, gather(): lax.all_gather(value, 'shard', axis=0, tiled=True, axis_index_groups=groups)  21.4 us
    dot_general x5, matrix products, dot_nt(): lax.dot_general(left, right, (((1,), (1,)), ((), ())), preferred_element_...  17.5 us
    pallas_call x1, Pallas kernels, feed(): pl.pallas_call(feed_kernel, grid=(count // tile,), in_specs=[pl.BlockSpec...  16 us
  transfers between devices with their start and end apart: 58, of which 28 were waited for; matrix products, arithmetic and copies ran while one was open for 14% of the time, Pallas kernels for 28%

profile of v8, /device:TPU:12, one launch (start us, length us, event | category | flops | bytes accessed | tf_op | source)
XLA Modules:
  0.0 517.4 jit_solution(6451016243541296449)
XLA Ops:
  20.5 22.3 %collective-permute-done = bf16[3,32,1024]{2,1,0:T(8,128)(2,1)S(1)} collective-permute-done((bf16[3,32,1024]{2,1,0:T(8,128)(2,1)S(1)}, bf16[3,32,1024]{2,1,0:T(8,128)(2,1)S(1)}, u32[]{:S(2)}, u32[]{:S(2)}) %collective-permute-start) | collective-permute-done | bytes 196640 | tf_op jit(solution)/shard_map/ppermute | solution.py:719
  49.0 6.9 %collective-permute-done.2 = bf16[8,32,640]{2,1,0:T(8,128)(2,1)S(1)} collective-permute-done((bf16[8,32,640]{2,1,0:T(8,128)(2,1)S(1)}, bf16[8,32,640]{2,1,0:T(8,128)(2,1)S(1)}, u32[]{:S(2)}, u32[]{:S(2)}) %collective-permute-start.2) | collective-permute-done | bytes 327712 | tf_op jit(solution)/shard_map/ppermute | solution.py:638
  56.0 6.8 %collective-permute-done.3 = bf16[8,32,640]{2,1,0:T(8,128)(2,1)S(1)} collective-permute-done((bf16[8,32,640]{2,1,0:T(8,128)(2,1)S(1)}, bf16[8,32,640]{2,1,0:T(8,128)(2,1)S(1)}, u32[]{:S(2)}, u32[]{:S(2)}) %collective-permute-start.3) | collective-permute-done | bytes 327712 | tf_op jit(solution)/shard_map/ppermute | solution.py:638
  68.9 12.3 %collective-permute-done.6.refs_1_ = bf16[3,4,32,1024]{3,2,1,0:T(8,128)(2,1)} collective-permute-done((bf16[3,4,32,1024]{3,2,1,0:T(8,128)(2,1)S(1)}, bf16[3,4,32,1024]{3,2,1,0:T(8,128)(2,1)}, u32[]{:S(2)}, u32[]{:S(2)}) %collective-permute-start.6) | collective-permute-done | bytes 786464 | tf_op jit(solution)/shard_map/ppermute | solution.py:638
  82.4 7.3 %all-gather.8.cloned.1.call-done.x_ref = bf16[2048,1024]{1,0:T(8,128)(2,1)} async-done(((bf16[256,1024]{1,0:T(8,128)(2,1)}), bf16[2048,1024]{1,0:T(8,128)(2,1)}) %all-gather.8.cloned.1.call-update) | async-done | bytes 4194320 | tf_op jit(solution)/shard_map/all_gather | solution.py:994
  102.1 9.2 %shard_map.263 = (bf16[2048,1024]{1,0:T(8,128)(2,1)}, bf16[2048,384]{1,0:T(8,128)(2,1)}) custom-call(bf16[2048,1024]{1,0:T(8,128)(2,1)} %all-gather.8.cloned.1.call-done.x_ref, f32[1,1024]{1,0:T(1,128)} %bitcast.243, f32[1,1024]{1,0:T(1,128)} %bitcast.247, bf16[1024,384]{1,0:T(8,128)(2,1)} %slice.202.qkv_w.w_ref, f32[1,384]{1,0:T(1,128)} %broadcast_in_dim.100.qkv_b), custom_call_target="tpu_custom_call" | custom-call | flops 1000 | bytes 1000 | tf_op jit(solution)/shard_map/pallas_call | solution.py:381
  111.3 15.7 %shard_map.264 = (bf16[2048,128]{1,0:T(8,128)(2,1)}, f32[2048,128]{1,0:T(8,128)}, f32[2,2048]{1,0:T(2,128)}) custom-call(s32[2,4]{1,0:T(2,128)} %pad_add_fusion.ends, bf16[2048,384]{1,0:T(8,128)(2,1)} %get-tuple-element.129.q_ref.k_ref.v_ref, bf16[2048,384]{1,0:T(8,128)(2,1)} %get-tuple-element.129.q_ref.k_ref.v_ref, ...), custom_call_target="tpu_custom_call" | custom-call | flops 1000 | bytes 1000 | tf_op jit(solution)/shard_map/pallas_call | solution.py:153
  147.4 10.2 %all-to-all-done.2 = bf16[8,256,128]{2,1,0:T(8,128)(2,1)S(1)} async-done(((bf16[8,256,128]{2,1,0:T(8,128)(2,1)}), bf16[8,256,128]{2,1,0:T(8,128)(2,1)S(1)}, u32[]{:S(2)}, u32[]{:S(2)}) %all-to-all-start.2) | async-done | bytes 524320 | tf_op jit(solution)/shard_map/all_to_all | solution.py:1048
  163.6 8.6 %shard_map.266.c_ref = bf16[256,1024]{1,0:T(8,128)(2,1)} custom-call(s32[1]{0:T(128)S(6)} %copy.118.length, bf16[256,1024]{1,0:T(8,128)(2,1)} %fusion.2.q_ref, bf16[4096,256]{1,0:T(8,128)(2,1)} %all-gather.10.cloned.1.call-done.m_ref), custom_call_target="tpu_custom_call" | custom-call | flops 1000 | bytes 1000 | tf_op jit(solution)/shard_map/pallas_call | solution.py:307
  180.3 10.8 %collective-permute-done.13.refs_1_ = bf16[256,1024]{1,0:T(8,128)(2,1)S(1)} collective-permute-done((bf16[256,1024]{1,0:T(8,128)(2,1)S(1)}, bf16[256,1024]{1,0:T(8,128)(2,1)S(1)}, u32[]{:S(2)}, u32[]{:S(2)}) %collective-permute-start.13) | collective-permute-done | bytes 524320 | tf_op jit(solution)/shard_map/ppermute | solution.py:638
  191.1 11.0 %collective-permute-done.14.refs_2_ = bf16[256,1024]{1,0:T(8,128)(2,1)S(1)} collective-permute-done((bf16[256,1024]{1,0:T(8,128)(2,1)S(1)}, bf16[256,1024]{1,0:T(8,128)(2,1)S(1)}, u32[]{:S(2)}, u32[]{:S(2)}) %collective-permute-start.14) | collective-permute-done | bytes 524320 | tf_op jit(solution)/shard_map/ppermute | solution.py:638
  209.4 10.8 %fusion.32.ga_ref = f32[2048,1024]{1,0:T(8,128)} fusion(bf16[2048,1024]{1,0:T(8,128)(2,1)} %all-gather.14.cloned.1.call-done.g_ref, bf16[1024,1024]{1,0:T(8,128)(2,1)} %b_ref.1), kind=kOutput, calls=%fused_computation.140 | convolution fusion | flops 4294967296 | bytes 14680064 | tf_op jit(solution)/shard_map/dot_general | solution.py:48
  220.2 11.2 %all-gather.12.cloned.1.call-done.x_ref = bf16[2048,1024]{1,0:T(8,128)(2,1)} async-done(((bf16[256,1024]{1,0:T(8,128)(2,1)}), bf16[2048,1024]{1,0:T(8,128)(2,1)}) %all-gather.12.cloned.1.call-update) | async-done | bytes 4194320 | tf_op jit(solution)/shard_map/all_gather | solution.py:994
  231.5 16.0 %shard_map.268 = (bf16[2048,1024]{1,0:T(8,128)(2,1)}, bf16[2048,1024]{1,0:T(8,128)(2,1)}, bf16[2048,1024]{1,0:T(8,128)(2,1)}, f32[1,1024]{1,0:T(1,128)}) custom-call(bf16[2048,1024]{1,0:T(8,128)(2,1)} %all-gather.12.cloned.1.call-done.x_ref, bf16[1024,1024]{1,0:T(8,128)(2,1)} %bitcast.217, f32[1,1024]{1,0:T(1,128)} %bitcast.253, f32[2048,1024]{1,0:T(8,128)} %fusion.32.ga_ref), custom_call_target="tpu_custom_call" | custom-call | flops 1000 | bytes 1000 | tf_op jit(solution)/shard_map/pallas_call | solution.py:423
  247.5 9.2 %shard_map.269 = (bf16[8,32,1024]{2,1,0:T(8,128)(2,1)}, bf16[8,32,1024]{2,1,0:T(8,128)(2,1)}, bf16[8,32,1024]{2,1,0:T(8,128)(2,1)}, bf16[8,32,1024]{2,1,0:T(8,128)(2,1)}) custom-call(s32[1]{0:T(128)} %bitcast.38.place.replica, bf16[2048,1024]{1,0:T(8,128)(2,1)} %all-gather.12.cloned.1.call-done.x_ref, bf16[2048,1024]{1,0:T(8,128)(2,1)} %get-tuple-element.154.g_ref), custom_call_target="tpu_custom_call" | custom-call | flops 1000 | bytes 1000 | tf_op jit(solution)/shard_map/pallas_call | solution.py:477
  260.2 9.2 %shard_map.270 = (bf16[256,1024]{1,0:T(8,128)(2,1)}, bf16[256,1024]{1,0:T(8,128)(2,1)}, bf16[256,1024]{1,0:T(8,128)(2,1)}, bf16[256,1024]{1,0:T(8,128)(2,1)}) custom-call(s32[1]{0:T(128)} %bitcast.38.place.replica, bf16[2048,1024]{1,0:T(8,128)(2,1)} %get-tuple-element.158.a_ref, bf16[2048,1024]{1,0:T(8,128)(2,1)} %all-gather.14.cloned.1.call-done.g_ref), custom_call_target="tpu_custom_call" | custom-call | flops 1000 | bytes 1000 | tf_op jit(solution)/shard_map/pallas_call | solution.py:510
  269.4 8.9 %shard_map.271 = bf16[2048,1024]{1,0:T(8,128)(2,1)} custom-call(bf16[2048,1024]{1,0:T(8,128)(2,1)} %get-tuple-element.158.a_ref, bf16[1024,1024]{1,0:T(8,128)(2,1)} %b_ref.1), custom_call_target="tpu_custom_call" | custom-call | flops 1000 | bytes 1000 | tf_op jit(solution)/shard_map/pallas_call | solution.py:526
  305.4 14.6 %shard_map.272 = (bf16[256,1024]{1,0:T(8,128)(2,1)}, bf16[4096,256]{1,0:T(8,128)(2,1)}) custom-call(s32[1]{0:T(128)S(6)} %copy.118.length, bf16[256,1024]{1,0:T(8,128)(2,1)} %fusion.2.q_ref, bf16[4096,256]{1,0:T(8,128)(2,1)} %all-gather.10.cloned.1.call-done.m_ref, bf16[256,1024]{1,0:T(8,128)(2,1)} %convolution_convert_fusion.2.g_ref), custom_call_target="tpu_custom_call" | custom-call | flops 1000 | bytes 1000 | tf_op jit(solution)/shard_map/pallas_call | solution.py:357
  328.2 7.5 %all-to-all-start.4 = ((bf16[256,8,128]{2,0,1:T(8,128)(2,1)}), bf16[256,8,128]{2,0,1:T(8,128)(2,1)}, u32[]{:S(2)}, u32[]{:S(2)}) async-start(bf16[256,8,128]{2,0,1:T(8,128)(2,1)} %copy_bitcast_fusion.1), calls=%async_computation.6 | async-start | bytes 1048576 | tf_op jit(solution)/shard_map/all_to_all | solution.py:1108
  355.8 21.4 %shard_map.274.g_ref = bf16[2048,384]{1,0:T(8,128)(2,1)} custom-call(s32[2,4]{1,0:T(2,128)} %pad_add_fusion.ends, bf16[2048,384]{1,0:T(8,128)(2,1)} %get-tuple-element.129.q_ref.k_ref.v_ref, bf16[2048,384]{1,0:T(8,128)(2,1)} %get-tuple-element.129.q_ref.k_ref.v_ref, bf16[2048,384]{1,0:T(8,128)(2,1)} %get-tuple-element.129.q_ref.k_ref.v_ref, ...), custom_call_target="tpu_custom_call" | custom-call | flops 16000000000 | bytes 4194304 | tf_op jit(solution)/shard_map/pallas_call | solution.py:272
  377.3 6.8 %shard_map.275 = bf16[4,8,32,640]{3,2,1,0:T(8,128)(2,1)} custom-call(bf16[2048,1024]{1,0:T(8,128)(2,1)} %get-tuple-element.182.x_ref.one_ref, bf16[2048,384]{1,0:T(8,128)(2,1)} %shard_map.274.g_ref, bf16[512,1024]{1,0:T(8,128)(2,1)} %all-gather.6.cloned.1.call-done.e_ref, bf16[512,256]{1,0:T(8,128)(2,1)} %reduce-scatter.9.cloned.1.call-done.m_ref), custom_call_target="tpu_custom_call" | custom-call | flops 1000 | bytes 1000 | tf_op jit(solution)/shard_map/pallas_call | solution.py:596
  388.6 8.9 %shard_map.276 = (bf16[2048,1024]{1,0:T(8,128)(2,1)}, f32[2,1024]{1,0:T(2,128)}, f32[1,384]{1,0:T(1,128)}) custom-call(bf16[2048,384]{1,0:T(8,128)(2,1)} %shard_map.274.g_ref, bf16[1024,384]{1,0:T(8,128)(2,1)} %slice.202.qkv_w.w_ref, bf16[2048,1024]{1,0:T(8,128)(2,1)} %get-tuple-element.182.x_ref.one_ref), custom_call_target="tpu_custom_call" | custom-call | flops 1000 | bytes 1000 | tf_op jit(solution)/shard_map/pallas_call | solution.py:553
  460.7 7.2 %collective-permute-done.29 = bf16[64,1024]{1,0:T(8,128)(2,1)S(1)} collective-permute-done((bf16[64,1024]{1,0:T(8,128)(2,1)S(1)}, bf16[64,1024]{1,0:T(8,128)(2,1)S(1)}, u32[]{:S(2)}, u32[]{:S(2)}) %collective-permute-start.29) | collective-permute-done | bytes 131104 | tf_op jit(solution)/shard_map/ppermute | solution.py:719
  472.9 17.3 %collective-permute-done.37 = bf16[3,32,1024]{2,1,0:T(8,128)(2,1)S(1)} collective-permute-done((bf16[3,32,1024]{2,1,0:T(8,128)(2,1)S(1)}, bf16[3,32,1024]{2,1,0:T(8,128)(2,1)S(1)}, u32[]{:S(2)}, u32[]{:S(2)}) %collective-permute-start.37) | collective-permute-done | bytes 196640 | tf_op jit(solution)/shard_map/ppermute | solution.py:719
  (334 shorter events, 231.4 us)
Async XLA Ops:
  7.2 37.7 %all-gather.6.cloned.1.call-start = ((), (), s32[]{:S(2)}) async-start(), calls=%async_computation.11 | async-start | bytes 1179648 | tf_op jit(solution)/shard_map/all_gather | solution.py:994
  11.3 33.6 %all-to-all-start = ((bf16[8,35,640]{2,1,0:T(8,128)(2,1)}), bf16[8,35,640]{2,1,0:T(8,128)(2,1)S(1)}, u32[]{:S(2)}, u32[]{:S(2)}) async-start(bf16[8,35,640]{2,1,0:T(8,128)(2,1)} %pad_maximum_fusion.1), calls=%async_computation | async-start | bytes 819200 | tf_op jit(solution)/shard_map/all_to_all | solution.py:1000
  16.6 73.1 %all-gather.8.cloned.1.call-start = ((), (), s32[]{:S(2)}) async-start(), calls=%async_computation.12 | async-start | bytes 4718592 | tf_op jit(solution)/shard_map/all_gather | solution.py:994
  45.0 84.8 %all-gather.10.cloned.1.call-start = ((), (), s32[]{:S(2)}) async-start(), calls=%async_computation.13 | async-start | bytes 2359296 | tf_op jit(solution)/shard_map/all_gather | solution.py:994
  91.3 35.7 %all-to-all-start.1 = ((bf16[8,32,1024]{2,1,0:T(8,128)(2,1)}), bf16[8,32,1024]{2,1,0:T(8,128)(2,1)S(1)}, u32[]{:S(2)}, u32[]{:S(2)}) async-start(bf16[8,32,1024]{2,1,0:T(8,128)(2,1)} %copy.70), calls=%async_computation.1 | async-start | bytes 1048576 | tf_op jit(solution)/shard_map/all_to_all | solution.py:1000
  97.4 112.0 %all-gather.14.cloned.1.call-start = ((), (), s32[]{:S(2)}) async-start(), calls=%async_computation.15 | async-start | bytes 4718592 | tf_op jit(solution)/shard_map/all_gather | solution.py:994
  134.6 96.9 %all-gather.12.cloned.1.call-start = ((), (), s32[]{:S(2)}) async-start(), calls=%async_computation.14 | async-start | bytes 4718592 | tf_op jit(solution)/shard_map/all_gather | solution.py:994
  176.1 118.4 %reduce-scatter.5.cloned.1.call-start = ((), (), s32[]{:S(2)}) async-start(), calls=%async_computation.16 | async-start | bytes 4718592 | tf_op jit(solution)/shard_map/reduce_scatter | solution.py:997
  278.3 41.6 %collective-permute-start.19 = (bf16[256,1024]{1,0:T(8,128)(2,1)}, bf16[256,1024]{1,0:T(8,128)(2,1)}, u32[]{:S(2)}, u32[]{:S(2)}) collective-permute-start(bf16[256,1024]{1,0:T(8,128)(2,1)} %get-tuple-element.168), channel_id=1, source_target_pairs={{0,8},{8,0},{16,24},{24,16},{1,9},{9,1},{17,25},{25,17},{2,10},{10... | collective-permute-start | bytes 1572872 | tf_op jit(solution)/shard_map/ppermute | solution.py:638
  279.7 40.2 %collective-permute-start.20 = (bf16[256,1024]{1,0:T(8,128)(2,1)}, bf16[256,1024]{1,0:T(8,128)(2,1)}, u32[]{:S(2)}, u32[]{:S(2)}) collective-permute-start(bf16[256,1024]{1,0:T(8,128)(2,1)} %get-tuple-element.169), channel_id=1, source_target_pairs={{0,16},{8,24},{16,0},{24,8},{1,17},{9,25},{17,1},{25,9},{2,18},{10... | collective-permute-start | bytes 1572872 | tf_op jit(solution)/shard_map/ppermute | solution.py:638
  280.3 39.6 %collective-permute-start.21 = (bf16[256,1024]{1,0:T(8,128)(2,1)}, bf16[256,1024]{1,0:T(8,128)(2,1)}, u32[]{:S(2)}, u32[]{:S(2)}) collective-permute-start(bf16[256,1024]{1,0:T(8,128)(2,1)} %get-tuple-element.170), channel_id=1, source_target_pairs={{0,24},{8,16},{16,8},{24,0},{1,25},{9,17},{17,9},{25,1},{2,26},{10... | collective-permute-start | bytes 1572872 | tf_op jit(solution)/shard_map/ppermute | solution.py:638
  292.9 84.4 %reduce-scatter.9.cloned.1.call-start = ((), (), s32[]{:S(2)}) async-start(), calls=%async_computation.18 | async-start | bytes 2359296 | tf_op jit(solution)/shard_map/reduce_scatter | solution.py:997
  320.0 182.5 %reduce-scatter.7.cloned.1.call-start = ((), (), s32[]{:S(2)}) async-start(), calls=%async_computation.17 | async-start | bytes 4718592 | tf_op jit(solution)/shard_map/reduce_scatter | solution.py:997
  343.1 54.5 %collective-permute-start.22 = (bf16[3,4,4,32,1024]{4,3,2,1,0:T(8,128)(2,1)}, bf16[3,4,4,32,1024]{4,3,2,1,0:T(8,128)(2,1)}, u32[]{:S(2)}, u32[]{:S(2)}) collective-permute-start(bf16[3,4,4,32,1024]{4,3,2,1,0:T(8,128)(2,1)} %get-tuple-element.187), channel_id=1, source_target_pairs={{0,1},{1,0},{2,3},{3,2},{4,5},{5,4},{6,7},{7,6},{8,9},{9,8},{10,11... | collective-permute-start | bytes 9437192 | tf_op jit(solution)/shard_map/ppermute | solution.py:712
  346.1 56.7 %collective-permute-start.23 = (bf16[512,1024]{1,0:T(8,128)(2,1)S(1)}, bf16[512,1024]{1,0:T(8,128)(2,1)S(1)}, u32[]{:S(2)}, u32[]{:S(2)}) collective-permute-start(bf16[512,1024]{1,0:T(8,128)(2,1)S(1)} %pad_maximum_fusion.refs_0_), channel_id=1, source_target_pairs={{0,8},{8,0},{16,24},{24,16},{1,9},{9,1},{17,25},{25,17},{2,10},{10... | collective-permute-start | bytes 3145736 | tf_op jit(solution)/shard_map/ppermute | solution.py:638
  347.5 55.6 %collective-permute-start.24 = (bf16[512,1024]{1,0:T(8,128)(2,1)S(1)}, bf16[512,1024]{1,0:T(8,128)(2,1)}, u32[]{:S(2)}, u32[]{:S(2)}) collective-permute-start(bf16[512,1024]{1,0:T(8,128)(2,1)S(1)} %pad_maximum_fusion.refs_0_), channel_id=1, source_target_pairs={{0,16},{8,24},{16,0},{24,8},{1,17},{9,25},{17,1},{25,9},{2,18},{10... | collective-permute-start | bytes 3145736 | tf_op jit(solution)/shard_map/ppermute | solution.py:638
  348.1 55.1 %collective-permute-start.25 = (bf16[512,1024]{1,0:T(8,128)(2,1)S(1)}, bf16[512,1024]{1,0:T(8,128)(2,1)}, u32[]{:S(2)}, u32[]{:S(2)}) collective-permute-start(bf16[512,1024]{1,0:T(8,128)(2,1)S(1)} %pad_maximum_fusion.refs_0_), channel_id=1, source_target_pairs={{0,24},{8,16},{16,8},{24,0},{1,25},{9,17},{17,9},{25,1},{2,26},{10... | collective-permute-start | bytes 3145736 | tf_op jit(solution)/shard_map/ppermute | solution.py:638
  388.6 116.1 %reduce-scatter.11.cloned.1.call-start = ((), (), s32[]{:S(2)}) async-start(), calls=%async_computation.19 | async-start | bytes 4718592 | tf_op jit(solution)/shard_map/reduce_scatter | solution.py:997
  411.6 31.2 %collective-permute-start.33 = (bf16[3,4,32,1024]{3,2,1,0:T(8,128)(2,1)}, bf16[3,4,32,1024]{3,2,1,0:T(8,128)(2,1)}, u32[]{:S(2)}, u32[]{:S(2)}) collective-permute-start(bf16[3,4,32,1024]{3,2,1,0:T(8,128)(2,1)} %get-tuple-element.211), channel_id=1, source_target_pairs={{0,8},{8,0},{16,24},{24,16},{1,9},{9,1},{17,25},{25,17},{2,10},{10... | collective-permute-start | bytes 2359304 | tf_op jit(solution)/shard_map/ppermute | solution.py:638
  412.3 36.2 %collective-permute-start.34 = (bf16[3,4,32,1024]{3,2,1,0:T(8,128)(2,1)}, bf16[3,4,32,1024]{3,2,1,0:T(8,128)(2,1)}, u32[]{:S(2)}, u32[]{:S(2)}) collective-permute-start(bf16[3,4,32,1024]{3,2,1,0:T(8,128)(2,1)} %get-tuple-element.212), channel_id=1, source_target_pairs={{0,16},{8,24},{16,0},{24,8},{1,17},{9,25},{17,1},{25,9},{2,18},{10... | collective-permute-start | bytes 2359304 | tf_op jit(solution)/shard_map/ppermute | solution.py:638
  413.4 35.1 %collective-permute-start.35 = (bf16[3,4,32,1024]{3,2,1,0:T(8,128)(2,1)}, bf16[3,4,32,1024]{3,2,1,0:T(8,128)(2,1)}, u32[]{:S(2)}, u32[]{:S(2)}) collective-permute-start(bf16[3,4,32,1024]{3,2,1,0:T(8,128)(2,1)} %get-tuple-element.213), channel_id=1, source_target_pairs={{0,24},{8,16},{16,8},{24,0},{1,25},{9,17},{17,9},{25,1},{2,26},{10... | collective-permute-start | bytes 2359304 | tf_op jit(solution)/shard_map/ppermute | solution.py:638
  452.6 41.2 %collective-permute-start.30 = (bf16[261,640]{1,0:T(8,128)(2,1)S(1)}, bf16[261,640]{1,0:T(8,128)(2,1)S(1)}, u32[]{:S(2)}, u32[]{:S(2)}) collective-permute-start(bf16[261,640]{1,0:T(8,128)(2,1)S(1)} %pad_maximum_fusion.3.refs_0_), channel_id=1, source_target_pairs={{0,8},{8,0},{16,24},{24,16},{1,9},{9,1},{17,25},{25,17},{2,10},{10... | collective-permute-start | bytes 1002248 | tf_op jit(solution)/shard_map/ppermute | solution.py:638
  453.4 42.1 %collective-permute-start.31 = (bf16[261,640]{1,0:T(8,128)(2,1)S(1)}, bf16[261,640]{1,0:T(8,128)(2,1)S(1)}, u32[]{:S(2)}, u32[]{:S(2)}) collective-permute-start(bf16[261,640]{1,0:T(8,128)(2,1)S(1)} %pad_maximum_fusion.3.refs_0_), channel_id=1, source_target_pairs={{0,16},{8,24},{16,0},{24,8},{1,17},{9,25},{17,1},{25,9},{2,18},{10... | collective-permute-start | bytes 1002248 | tf_op jit(solution)/shard_map/ppermute | solution.py:638
  459.5 36.0 %collective-permute-start.32 = (bf16[261,640]{1,0:T(8,128)(2,1)S(1)}, bf16[261,640]{1,0:T(8,128)(2,1)S(1)}, u32[]{:S(2)}, u32[]{:S(2)}) collective-permute-start(bf16[261,640]{1,0:T(8,128)(2,1)S(1)} %pad_maximum_fusion.3.refs_0_), channel_id=1, source_target_pairs={{0,24},{8,16},{16,8},{24,0},{1,25},{9,17},{17,9},{25,1},{2,26},{10... | collective-permute-start | bytes 1002248 | tf_op jit(solution)/shard_map/ppermute | solution.py:638
  (75 other events, 1117.8 us)
Sparse Core Ops, SparseCore 0:
  9.7 32.2 all-gather.5
  45.1 44.6 all-gather.7
  91.9 37.7 all-gather.9
  131.2 49.8 all-gather.13
  183.1 48.2 all-gather.11
  247.6 46.8 reduce-scatter.4
  320.1 42.1 reduce-scatter.8
  364.6 47.9 reduce-scatter.6
  414.9 85.4 reduce-scatter.10

commit v9 on v8

--- a/solution.py
+++ b/solution.py
@@ -1093,9 +1093,10 @@
     grad_two = grad_out + norm_three[0]
     grad_two_low = low(grad_two)
     grad_context = low(dot_nt(grad_two_low, cross_proj))
-    grad_context, own_expand = lax.optimization_barrier((grad_context, own_expand))
     grad_cross_q, memory_part = cross_backward(cross_q, memory_all, grad_context, enc_count)
-    grad_cross_q, memory_part, shrink_parts = lax.optimization_barrier((grad_cross_q, memory_part, shrink_parts))
+    grad_cross_q, memory_part, shrink_parts, own_expand = lax.optimization_barrier(
+        (grad_cross_q, memory_part, shrink_parts, own_expand)
+    )
     mem_grads = scatter(memory_part, groups)
     grad_in_two = dot_nt(grad_cross_q, query_in)
     norm_two = jax.vjp(norm_apply, hidden_one, gain_rows[1], shift_rows[1])[1](grad_in_two)

time: 526 us -> 524 us (level)
  transfers between devices with their start and end apart: 58 -> 58, of which waited for: 28 -> 27; matrix products, arithmetic and copies ran while one was open for 14% -> 14% of each run, Pallas kernels for 28% -> 28%
where the time goes in v9:
time: 524 us; the launch traced here: 514 us
  waiting for transfers between devices  169 us (32%)
  Pallas kernels  164 us (31%)
  starting transfers between devices  84.3 us (16%)
  local copies, waits for them, and re-layouts  28.4 us (5%)
  other arithmetic  27 us (5%)
  matrix products  25.3 us (5%)
  between operations  15.8 us (3%)
    ppermute x9, waiting for transfers between devices, line_send(): return lax.ppermute(value, 'shard', route)  59.4 us
    ppermute x27, waiting for transfers between devices, rep_send(): return lax.ppermute(value, 'rep', [(i, i ^ step) for i in range(size)])  53.1 us
    ppermute x27, starting transfers between devices, rep_send(): return lax.ppermute(value, 'rep', [(i, i ^ step) for i in range(size)])  31.6 us
    all_to_all x4, starting transfers between devices, swap(): return lax.all_to_all(value, 'shard', 0, 0, tiled=True)  22.7 us
    pallas_call x1, Pallas kernels, self_backward(): pl.pallas_call(self_backward_kernel, grid_spec=grid_spec, out_shape=jax.S...  21.5 us
    all_gather x5, waiting for transfers between devices, gather(): lax.all_gather(value, 'shard', axis=0, tiled=True, axis_index_groups=groups)  21.4 us
    dot_general x5, matrix products, dot_nt(): lax.dot_general(left, right, (((1,), (1,)), ((), ())), preferred_element_...  17.5 us
    pallas_call x1, Pallas kernels, feed(): pl.pallas_call(feed_kernel, grid=(count // tile,), in_specs=[pl.BlockSpec...  16 us
  transfers between devices with their start and end apart: 58, of which 27 were waited for; matrix products, arithmetic and copies ran while one was open for 14% of the time, Pallas kernels for 28%

profile of v9, /device:TPU:12, one launch (start us, length us, event | category | flops | bytes accessed | tf_op | source)
XLA Modules:
  0.0 514.4 jit_solution(4458979661621496785)
XLA Ops:
  20.5 22.3 %collective-permute-done = bf16[3,32,1024]{2,1,0:T(8,128)(2,1)S(1)} collective-permute-done((bf16[3,32,1024]{2,1,0:T(8,128)(2,1)S(1)}, bf16[3,32,1024]{2,1,0:T(8,128)(2,1)S(1)}, u32[]{:S(2)}, u32[]{:S(2)}) %collective-permute-start) | collective-permute-done | bytes 196640 | tf_op jit(solution)/shard_map/ppermute | solution.py:719
  49.0 6.9 %collective-permute-done.2 = bf16[8,32,640]{2,1,0:T(8,128)(2,1)S(1)} collective-permute-done((bf16[8,32,640]{2,1,0:T(8,128)(2,1)S(1)}, bf16[8,32,640]{2,1,0:T(8,128)(2,1)S(1)}, u32[]{:S(2)}, u32[]{:S(2)}) %collective-permute-start.2) | collective-permute-done | bytes 327712 | tf_op jit(solution)/shard_map/ppermute | solution.py:638
  56.0 6.8 %collective-permute-done.3 = bf16[8,32,640]{2,1,0:T(8,128)(2,1)S(1)} collective-permute-done((bf16[8,32,640]{2,1,0:T(8,128)(2,1)S(1)}, bf16[8,32,640]{2,1,0:T(8,128)(2,1)S(1)}, u32[]{:S(2)}, u32[]{:S(2)}) %collective-permute-start.3) | collective-permute-done | bytes 327712 | tf_op jit(solution)/shard_map/ppermute | solution.py:638
  68.9 12.3 %collective-permute-done.6.refs_1_ = bf16[3,4,32,1024]{3,2,1,0:T(8,128)(2,1)} collective-permute-done((bf16[3,4,32,1024]{3,2,1,0:T(8,128)(2,1)S(1)}, bf16[3,4,32,1024]{3,2,1,0:T(8,128)(2,1)}, u32[]{:S(2)}, u32[]{:S(2)}) %collective-permute-start.6) | collective-permute-done | bytes 786464 | tf_op jit(solution)/shard_map/ppermute | solution.py:638
  82.4 7.3 %all-gather.8.cloned.1.call-done.x_ref = bf16[2048,1024]{1,0:T(8,128)(2,1)} async-done(((bf16[256,1024]{1,0:T(8,128)(2,1)}), bf16[2048,1024]{1,0:T(8,128)(2,1)}) %all-gather.8.cloned.1.call-update) | async-done | bytes 4194320 | tf_op jit(solution)/shard_map/all_gather | solution.py:994
  102.1 9.2 %shard_map.263 = (bf16[2048,1024]{1,0:T(8,128)(2,1)}, bf16[2048,384]{1,0:T(8,128)(2,1)}) custom-call(bf16[2048,1024]{1,0:T(8,128)(2,1)} %all-gather.8.cloned.1.call-done.x_ref, f32[1,1024]{1,0:T(1,128)} %bitcast.243, f32[1,1024]{1,0:T(1,128)} %bitcast.247, bf16[1024,384]{1,0:T(8,128)(2,1)} %slice.202.qkv_w.w_ref, f32[1,384]{1,0:T(1,128)} %broadcast_in_dim.100.qkv_b), custom_call_target="tpu_custom_call" | custom-call | flops 1000 | bytes 1000 | tf_op jit(solution)/shard_map/pallas_call | solution.py:381
  111.3 15.7 %shard_map.264 = (bf16[2048,128]{1,0:T(8,128)(2,1)}, f32[2048,128]{1,0:T(8,128)}, f32[2,2048]{1,0:T(2,128)}) custom-call(s32[2,4]{1,0:T(2,128)} %pad_add_fusion.ends, bf16[2048,384]{1,0:T(8,128)(2,1)} %get-tuple-element.128.q_ref.k_ref.v_ref, bf16[2048,384]{1,0:T(8,128)(2,1)} %get-tuple-element.128.q_ref.k_ref.v_ref, ...), custom_call_target="tpu_custom_call" | custom-call | flops 1000 | bytes 1000 | tf_op jit(solution)/shard_map/pallas_call | solution.py:153
  147.4 10.2 %all-to-all-done.2 = bf16[8,256,128]{2,1,0:T(8,128)(2,1)S(1)} async-done(((bf16[8,256,128]{2,1,0:T(8,128)(2,1)}), bf16[8,256,128]{2,1,0:T(8,128)(2,1)S(1)}, u32[]{:S(2)}, u32[]{:S(2)}) %all-to-all-start.2) | async-done | bytes 524320 | tf_op jit(solution)/shard_map/all_to_all | solution.py:1048
  163.6 8.6 %shard_map.266.c_ref = bf16[256,1024]{1,0:T(8,128)(2,1)} custom-call(s32[1]{0:T(128)S(6)} %copy.118.length, bf16[256,1024]{1,0:T(8,128)(2,1)} %fusion.2.q_ref, bf16[4096,256]{1,0:T(8,128)(2,1)} %all-gather.10.cloned.1.call-done.m_ref), custom_call_target="tpu_custom_call" | custom-call | flops 1000 | bytes 1000 | tf_op jit(solution)/shard_map/pallas_call | solution.py:307
  180.3 10.8 %collective-permute-done.13.refs_1_ = bf16[256,1024]{1,0:T(8,128)(2,1)S(1)} collective-permute-done((bf16[256,1024]{1,0:T(8,128)(2,1)S(1)}, bf16[256,1024]{1,0:T(8,128)(2,1)S(1)}, u32[]{:S(2)}, u32[]{:S(2)}) %collective-permute-start.13) | collective-permute-done | bytes 524320 | tf_op jit(solution)/shard_map/ppermute | solution.py:638
  191.1 11.0 %collective-permute-done.14.refs_2_ = bf16[256,1024]{1,0:T(8,128)(2,1)S(1)} collective-permute-done((bf16[256,1024]{1,0:T(8,128)(2,1)S(1)}, bf16[256,1024]{1,0:T(8,128)(2,1)S(1)}, u32[]{:S(2)}, u32[]{:S(2)}) %collective-permute-start.14) | collective-permute-done | bytes 524320 | tf_op jit(solution)/shard_map/ppermute | solution.py:638
  209.4 10.8 %fusion.32.ga_ref = f32[2048,1024]{1,0:T(8,128)} fusion(bf16[2048,1024]{1,0:T(8,128)(2,1)} %all-gather.14.cloned.1.call-done.g_ref, bf16[1024,1024]{1,0:T(8,128)(2,1)} %b_ref.1), kind=kOutput, calls=%fused_computation.140 | convolution fusion | flops 4294967296 | bytes 14680064 | tf_op jit(solution)/shard_map/dot_general | solution.py:48
  220.2 11.2 %all-gather.12.cloned.1.call-done.x_ref = bf16[2048,1024]{1,0:T(8,128)(2,1)} async-done(((bf16[256,1024]{1,0:T(8,128)(2,1)}), bf16[2048,1024]{1,0:T(8,128)(2,1)}) %all-gather.12.cloned.1.call-update) | async-done | bytes 4194320 | tf_op jit(solution)/shard_map/all_gather | solution.py:994
  231.5 16.0 %shard_map.268 = (bf16[2048,1024]{1,0:T(8,128)(2,1)}, bf16[2048,1024]{1,0:T(8,128)(2,1)}, bf16[2048,1024]{1,0:T(8,128)(2,1)}, f32[1,1024]{1,0:T(1,128)}) custom-call(bf16[2048,1024]{1,0:T(8,128)(2,1)} %all-gather.12.cloned.1.call-done.x_ref, bf16[1024,1024]{1,0:T(8,128)(2,1)} %bitcast.217, f32[1,1024]{1,0:T(1,128)} %bitcast.253, f32[2048,1024]{1,0:T(8,128)} %fusion.32.ga_ref), custom_call_target="tpu_custom_call" | custom-call | flops 1000 | bytes 1000 | tf_op jit(solution)/shard_map/pallas_call | solution.py:423
  247.5 9.2 %shard_map.269 = (bf16[8,32,1024]{2,1,0:T(8,128)(2,1)}, bf16[8,32,1024]{2,1,0:T(8,128)(2,1)}, bf16[8,32,1024]{2,1,0:T(8,128)(2,1)}, bf16[8,32,1024]{2,1,0:T(8,128)(2,1)}) custom-call(s32[1]{0:T(128)} %bitcast.38.place.replica, bf16[2048,1024]{1,0:T(8,128)(2,1)} %all-gather.12.cloned.1.call-done.x_ref, bf16[2048,1024]{1,0:T(8,128)(2,1)} %get-tuple-element.153.g_ref), custom_call_target="tpu_custom_call" | custom-call | flops 1000 | bytes 1000 | tf_op jit(solution)/shard_map/pallas_call | solution.py:477
  260.2 9.2 %shard_map.270 = (bf16[256,1024]{1,0:T(8,128)(2,1)}, bf16[256,1024]{1,0:T(8,128)(2,1)}, bf16[256,1024]{1,0:T(8,128)(2,1)}, bf16[256,1024]{1,0:T(8,128)(2,1)}) custom-call(s32[1]{0:T(128)} %bitcast.38.place.replica, bf16[2048,1024]{1,0:T(8,128)(2,1)} %get-tuple-element.157.a_ref, bf16[2048,1024]{1,0:T(8,128)(2,1)} %all-gather.14.cloned.1.call-done.g_ref), custom_call_target="tpu_custom_call" | custom-call | flops 1000 | bytes 1000 | tf_op jit(solution)/shard_map/pallas_call | solution.py:510
  269.4 8.9 %shard_map.271 = bf16[2048,1024]{1,0:T(8,128)(2,1)} custom-call(bf16[2048,1024]{1,0:T(8,128)(2,1)} %get-tuple-element.157.a_ref, bf16[1024,1024]{1,0:T(8,128)(2,1)} %b_ref.1), custom_call_target="tpu_custom_call" | custom-call | flops 1000 | bytes 1000 | tf_op jit(solution)/shard_map/pallas_call | solution.py:526
  301.3 14.6 %shard_map.272 = (bf16[256,1024]{1,0:T(8,128)(2,1)}, bf16[4096,256]{1,0:T(8,128)(2,1)}) custom-call(s32[1]{0:T(128)S(6)} %copy.118.length, bf16[256,1024]{1,0:T(8,128)(2,1)} %fusion.2.q_ref, bf16[4096,256]{1,0:T(8,128)(2,1)} %all-gather.10.cloned.1.call-done.m_ref, bf16[256,1024]{1,0:T(8,128)(2,1)} %convolution_convert_fusion.2.g_ref), custom_call_target="tpu_custom_call" | custom-call | flops 1000 | bytes 1000 | tf_op jit(solution)/shard_map/pallas_call | solution.py:357
  324.1 8.3 %all-to-all-start.4 = ((bf16[256,8,128]{2,0,1:T(8,128)(2,1)}), bf16[256,8,128]{2,0,1:T(8,128)(2,1)}, u32[]{:S(2)}, u32[]{:S(2)}) async-start(bf16[256,8,128]{2,0,1:T(8,128)(2,1)} %copy_bitcast_fusion.1), calls=%async_computation.6 | async-start | bytes 1048576 | tf_op jit(solution)/shard_map/all_to_all | solution.py:1109
  352.6 21.5 %shard_map.274.g_ref = bf16[2048,384]{1,0:T(8,128)(2,1)} custom-call(s32[2,4]{1,0:T(2,128)} %pad_add_fusion.ends, bf16[2048,384]{1,0:T(8,128)(2,1)} %get-tuple-element.128.q_ref.k_ref.v_ref, bf16[2048,384]{1,0:T(8,128)(2,1)} %get-tuple-element.128.q_ref.k_ref.v_ref, bf16[2048,384]{1,0:T(8,128)(2,1)} %get-tuple-element.128.q_ref.k_ref.v_ref, ...), custom_call_target="tpu_custom_call" | custom-call | flops 16000000000 | bytes 4194304 | tf_op jit(solution)/shard_map/pallas_call | solution.py:272
  374.1 6.8 %shard_map.275 = bf16[4,8,32,640]{3,2,1,0:T(8,128)(2,1)} custom-call(bf16[2048,1024]{1,0:T(8,128)(2,1)} %get-tuple-element.180.x_ref.one_ref, bf16[2048,384]{1,0:T(8,128)(2,1)} %shard_map.274.g_ref, bf16[512,1024]{1,0:T(8,128)(2,1)} %all-gather.6.cloned.1.call-done.e_ref, bf16[512,256]{1,0:T(8,128)(2,1)} %reduce-scatter.9.cloned.1.call-done.m_ref), custom_call_target="tpu_custom_call" | custom-call | flops 1000 | bytes 1000 | tf_op jit(solution)/shard_map/pallas_call | solution.py:596
  385.3 8.9 %shard_map.276 = (bf16[2048,1024]{1,0:T(8,128)(2,1)}, f32[2,1024]{1,0:T(2,128)}, f32[1,384]{1,0:T(1,128)}) custom-call(bf16[2048,384]{1,0:T(8,128)(2,1)} %shard_map.274.g_ref, bf16[1024,384]{1,0:T(8,128)(2,1)} %slice.202.qkv_w.w_ref, bf16[2048,1024]{1,0:T(8,128)(2,1)} %get-tuple-element.180.x_ref.one_ref), custom_call_target="tpu_custom_call" | custom-call | flops 1000 | bytes 1000 | tf_op jit(solution)/shard_map/pallas_call | solution.py:553
  458.1 7.2 %collective-permute-done.29 = bf16[64,1024]{1,0:T(8,128)(2,1)S(1)} collective-permute-done((bf16[64,1024]{1,0:T(8,128)(2,1)S(1)}, bf16[64,1024]{1,0:T(8,128)(2,1)S(1)}, u32[]{:S(2)}, u32[]{:S(2)}) %collective-permute-start.29) | collective-permute-done | bytes 131104 | tf_op jit(solution)/shard_map/ppermute | solution.py:719
  470.0 17.2 %collective-permute-done.37 = bf16[3,32,1024]{2,1,0:T(8,128)(2,1)S(1)} collective-permute-done((bf16[3,32,1024]{2,1,0:T(8,128)(2,1)S(1)}, bf16[3,32,1024]{2,1,0:T(8,128)(2,1)S(1)}, u32[]{:S(2)}, u32[]{:S(2)}) %collective-permute-start.37) | collective-permute-done | bytes 196640 | tf_op jit(solution)/shard_map/ppermute | solution.py:719
  (334 shorter events, 227.8 us)
Async XLA Ops:
  7.2 37.7 %all-gather.6.cloned.1.call-start = ((), (), s32[]{:S(2)}) async-start(), calls=%async_computation.11 | async-start | bytes 1179648 | tf_op jit(solution)/shard_map/all_gather | solution.py:994
  11.3 33.6 %all-to-all-start = ((bf16[8,35,640]{2,1,0:T(8,128)(2,1)}), bf16[8,35,640]{2,1,0:T(8,128)(2,1)S(1)}, u32[]{:S(2)}, u32[]{:S(2)}) async-start(bf16[8,35,640]{2,1,0:T(8,128)(2,1)} %pad_maximum_fusion.1), calls=%async_computation | async-start | bytes 819200 | tf_op jit(solution)/shard_map/all_to_all | solution.py:1000
  16.6 73.1 %all-gather.8.cloned.1.call-start = ((), (), s32[]{:S(2)}) async-start(), calls=%async_computation.12 | async-start | bytes 4718592 | tf_op jit(solution)/shard_map/all_gather | solution.py:994
  45.0 84.8 %all-gather.10.cloned.1.call-start = ((), (), s32[]{:S(2)}) async-start(), calls=%async_computation.13 | async-start | bytes 2359296 | tf_op jit(solution)/shard_map/all_gather | solution.py:994
  91.3 35.7 %all-to-all-start.1 = ((bf16[8,32,1024]{2,1,0:T(8,128)(2,1)}), bf16[8,32,1024]{2,1,0:T(8,128)(2,1)S(1)}, u32[]{:S(2)}, u32[]{:S(2)}) async-start(bf16[8,32,1024]{2,1,0:T(8,128)(2,1)} %copy.70), calls=%async_computation.1 | async-start | bytes 1048576 | tf_op jit(solution)/shard_map/all_to_all | solution.py:1000
  97.4 112.0 %all-gather.14.cloned.1.call-start = ((), (), s32[]{:S(2)}) async-start(), calls=%async_computation.15 | async-start | bytes 4718592 | tf_op jit(solution)/shard_map/all_gather | solution.py:994
  134.6 96.9 %all-gather.12.cloned.1.call-start = ((), (), s32[]{:S(2)}) async-start(), calls=%async_computation.14 | async-start | bytes 4718592 | tf_op jit(solution)/shard_map/all_gather | solution.py:994
  176.1 118.4 %reduce-scatter.5.cloned.1.call-start = ((), (), s32[]{:S(2)}) async-start(), calls=%async_computation.16 | async-start | bytes 4718592 | tf_op jit(solution)/shard_map/reduce_scatter | solution.py:997
  278.3 37.5 %collective-permute-start.16 = (bf16[256,1024]{1,0:T(8,128)(2,1)}, bf16[256,1024]{1,0:T(8,128)(2,1)}, u32[]{:S(2)}, u32[]{:S(2)}) collective-permute-start(bf16[256,1024]{1,0:T(8,128)(2,1)} %get-tuple-element.163), channel_id=1, source_target_pairs={{0,8},{8,0},{16,24},{24,16},{1,9},{9,1},{17,25},{25,17},{2,10},{10... | collective-permute-start | bytes 1572872 | tf_op jit(solution)/shard_map/ppermute | solution.py:638
  279.7 36.1 %collective-permute-start.17 = (bf16[256,1024]{1,0:T(8,128)(2,1)}, bf16[256,1024]{1,0:T(8,128)(2,1)}, u32[]{:S(2)}, u32[]{:S(2)}) collective-permute-start(bf16[256,1024]{1,0:T(8,128)(2,1)} %get-tuple-element.164), channel_id=1, source_target_pairs={{0,16},{8,24},{16,0},{24,8},{1,17},{9,25},{17,1},{25,9},{2,18},{10... | collective-permute-start | bytes 1572872 | tf_op jit(solution)/shard_map/ppermute | solution.py:638
  280.3 35.5 %collective-permute-start.18 = (bf16[256,1024]{1,0:T(8,128)(2,1)}, bf16[256,1024]{1,0:T(8,128)(2,1)}, u32[]{:S(2)}, u32[]{:S(2)}) collective-permute-start(bf16[256,1024]{1,0:T(8,128)(2,1)} %get-tuple-element.165), channel_id=1, source_target_pairs={{0,24},{8,16},{16,8},{24,0},{1,25},{9,17},{17,9},{25,1},{2,26},{10... | collective-permute-start | bytes 1572872 | tf_op jit(solution)/shard_map/ppermute | solution.py:638
  292.9 81.1 %reduce-scatter.9.cloned.1.call-start = ((), (), s32[]{:S(2)}) async-start(), calls=%async_computation.18 | async-start | bytes 2359296 | tf_op jit(solution)/shard_map/reduce_scatter | solution.py:997
  315.9 183.7 %reduce-scatter.7.cloned.1.call-start = ((), (), s32[]{:S(2)}) async-start(), calls=%async_computation.17 | async-start | bytes 4718592 | tf_op jit(solution)/shard_map/reduce_scatter | solution.py:997
  339.8 54.5 %collective-permute-start.22 = (bf16[3,4,4,32,1024]{4,3,2,1,0:T(8,128)(2,1)}, bf16[3,4,4,32,1024]{4,3,2,1,0:T(8,128)(2,1)}, u32[]{:S(2)}, u32[]{:S(2)}) collective-permute-start(bf16[3,4,4,32,1024]{4,3,2,1,0:T(8,128)(2,1)} %get-tuple-element.185), channel_id=1, source_target_pairs={{0,1},{1,0},{2,3},{3,2},{4,5},{5,4},{6,7},{7,6},{8,9},{9,8},{10,11... | collective-permute-start | bytes 9437192 | tf_op jit(solution)/shard_map/ppermute | solution.py:712
  342.8 56.7 %collective-permute-start.23 = (bf16[512,1024]{1,0:T(8,128)(2,1)S(1)}, bf16[512,1024]{1,0:T(8,128)(2,1)S(1)}, u32[]{:S(2)}, u32[]{:S(2)}) collective-permute-start(bf16[512,1024]{1,0:T(8,128)(2,1)S(1)} %pad_maximum_fusion.refs_0_), channel_id=1, source_target_pairs={{0,8},{8,0},{16,24},{24,16},{1,9},{9,1},{17,25},{25,17},{2,10},{10... | collective-permute-start | bytes 3145736 | tf_op jit(solution)/shard_map/ppermute | solution.py:638
  344.8 55.6 %collective-permute-start.24 = (bf16[512,1024]{1,0:T(8,128)(2,1)S(1)}, bf16[512,1024]{1,0:T(8,128)(2,1)}, u32[]{:S(2)}, u32[]{:S(2)}) collective-permute-start(bf16[512,1024]{1,0:T(8,128)(2,1)S(1)} %pad_maximum_fusion.refs_0_), channel_id=1, source_target_pairs={{0,16},{8,24},{16,0},{24,8},{1,17},{9,25},{17,1},{25,9},{2,18},{10... | collective-permute-start | bytes 3145736 | tf_op jit(solution)/shard_map/ppermute | solution.py:638
  344.8 55.6 %collective-permute-start.25 = (bf16[512,1024]{1,0:T(8,128)(2,1)S(1)}, bf16[512,1024]{1,0:T(8,128)(2,1)}, u32[]{:S(2)}, u32[]{:S(2)}) collective-permute-start(bf16[512,1024]{1,0:T(8,128)(2,1)S(1)} %pad_maximum_fusion.refs_0_), channel_id=1, source_target_pairs={{0,24},{8,16},{16,8},{24,0},{1,25},{9,17},{17,9},{25,1},{2,26},{10... | collective-permute-start | bytes 3145736 | tf_op jit(solution)/shard_map/ppermute | solution.py:638
  385.3 116.4 %reduce-scatter.11.cloned.1.call-start = ((), (), s32[]{:S(2)}) async-start(), calls=%async_computation.19 | async-start | bytes 4718592 | tf_op jit(solution)/shard_map/reduce_scatter | solution.py:997
  408.9 31.3 %collective-permute-start.33 = (bf16[3,4,32,1024]{3,2,1,0:T(8,128)(2,1)}, bf16[3,4,32,1024]{3,2,1,0:T(8,128)(2,1)}, u32[]{:S(2)}, u32[]{:S(2)}) collective-permute-start(bf16[3,4,32,1024]{3,2,1,0:T(8,128)(2,1)} %get-tuple-element.209), channel_id=1, source_target_pairs={{0,8},{8,0},{16,24},{24,16},{1,9},{9,1},{17,25},{25,17},{2,10},{10... | collective-permute-start | bytes 2359304 | tf_op jit(solution)/shard_map/ppermute | solution.py:638
  409.3 35.5 %collective-permute-start.34 = (bf16[3,4,32,1024]{3,2,1,0:T(8,128)(2,1)}, bf16[3,4,32,1024]{3,2,1,0:T(8,128)(2,1)}, u32[]{:S(2)}, u32[]{:S(2)}) collective-permute-start(bf16[3,4,32,1024]{3,2,1,0:T(8,128)(2,1)} %get-tuple-element.210), channel_id=1, source_target_pairs={{0,16},{8,24},{16,0},{24,8},{1,17},{9,25},{17,1},{25,9},{2,18},{10... | collective-permute-start | bytes 2359304 | tf_op jit(solution)/shard_map/ppermute | solution.py:638
  410.7 34.6 %collective-permute-start.35 = (bf16[3,4,32,1024]{3,2,1,0:T(8,128)(2,1)}, bf16[3,4,32,1024]{3,2,1,0:T(8,128)(2,1)}, u32[]{:S(2)}, u32[]{:S(2)}) collective-permute-start(bf16[3,4,32,1024]{3,2,1,0:T(8,128)(2,1)} %get-tuple-element.211), channel_id=1, source_target_pairs={{0,24},{8,16},{16,8},{24,0},{1,25},{9,17},{17,9},{25,1},{2,26},{10... | collective-permute-start | bytes 2359304 | tf_op jit(solution)/shard_map/ppermute | solution.py:638
  449.4 41.5 %collective-permute-start.30 = (bf16[261,640]{1,0:T(8,128)(2,1)S(1)}, bf16[261,640]{1,0:T(8,128)(2,1)S(1)}, u32[]{:S(2)}, u32[]{:S(2)}) collective-permute-start(bf16[261,640]{1,0:T(8,128)(2,1)S(1)} %pad_maximum_fusion.3.refs_0_), channel_id=1, source_target_pairs={{0,8},{8,0},{16,24},{24,16},{1,9},{9,1},{17,25},{25,17},{2,10},{10... | collective-permute-start | bytes 1002248 | tf_op jit(solution)/shard_map/ppermute | solution.py:638
  450.7 41.8 %collective-permute-start.31 = (bf16[261,640]{1,0:T(8,128)(2,1)S(1)}, bf16[261,640]{1,0:T(8,128)(2,1)S(1)}, u32[]{:S(2)}, u32[]{:S(2)}) collective-permute-start(bf16[261,640]{1,0:T(8,128)(2,1)S(1)} %pad_maximum_fusion.3.refs_0_), channel_id=1, source_target_pairs={{0,16},{8,24},{16,0},{24,8},{1,17},{9,25},{17,1},{25,9},{2,18},{10... | collective-permute-start | bytes 1002248 | tf_op jit(solution)/shard_map/ppermute | solution.py:638
  456.8 35.7 %collective-permute-start.32 = (bf16[261,640]{1,0:T(8,128)(2,1)S(1)}, bf16[261,640]{1,0:T(8,128)(2,1)S(1)}, u32[]{:S(2)}, u32[]{:S(2)}) collective-permute-start(bf16[261,640]{1,0:T(8,128)(2,1)S(1)} %pad_maximum_fusion.3.refs_0_), channel_id=1, source_target_pairs={{0,24},{8,16},{16,8},{24,0},{1,25},{9,17},{17,9},{25,1},{2,26},{10... | collective-permute-start | bytes 1002248 | tf_op jit(solution)/shard_map/ppermute | solution.py:638
  (75 other events, 1130.8 us)
Sparse Core Ops, SparseCore 0:
  9.7 32.2 all-gather.5
  45.1 44.6 all-gather.7
  91.9 37.7 all-gather.9
  131.2 49.8 all-gather.13
  183.1 48.2 all-gather.11
  247.6 46.8 reduce-scatter.4
  316.0 43.4 reduce-scatter.8
  361.7 48.8 reduce-scatter.6
  413.0 85.6 reduce-scatter.10
